TPU v7x, 32 devices: a whole 2x2x4 slice. The times are simulated.
32 devices in a mesh: section: 2 (over core), rep: 4 (over y, x), fsdp: 4 (over z).
Axes of the slice: x: 2, y: 2, z: 4, core: 2. Of those that a mesh axis runs over, the one named last changes fastest.
Arguments:
- layer_input: bfloat16 [2, 2, 1024, 8192], P('section', None, ('rep', 'fsdp')), may hold values from -600 to 600
- value_grad: bfloat16 [2, 2, 1024, 1024], P('section', None, ('rep', 'fsdp')), may hold values from -7 to 7
- value_weight: bfloat16 [2, 8192, 1024], P('section', 'fsdp'), may hold values from -2 to 2
- norm_gain: bfloat16 [2, 8192], P('section', 'fsdp'), may hold values from 0.25 to 1.75
- top_grad: bfloat16 [2, 1024, 8192], P(None, ('rep', 'fsdp')), may hold values from -6 to 6
Outputs:
- input_grad: bfloat16 [2, 2, 1024, 8192], P('section', None, ('rep', 'fsdp'))
- weight_grad: float32 [2, 8192, 1024], P('section', 'fsdp')
- gain_grad: float32 [2, 8192], P('section', 'fsdp')
All inputs are finite; a program needn't handle non-finite values.
Results may differ from a plain program's by a relative error of at most 0.0041.
Values may be sent and summed in bfloat16 or wider, within the bound.
No kernel may reach another device: no remote copies, remote signals or barrier semaphores. Data moves between devices by JAX's collectives and lax.ppermute only.
A program may use at most 128 MiB of HBM per device.

v0:
```python
import jax
import jax.numpy as jnp
from jax import lax
from jax.sharding import PartitionSpec as P

norm_eps = 1e-05


def shifted(value, axis, steps):
    count = lax.axis_size(axis)
    initial, last = (max(0, -steps), min(count, count - steps))
    return lax.ppermute(value, axis, [(source, source + steps) for source in range(initial, last)])


def local(layer_input, value_grad, value_weight, norm_gain, top_grad):
    groups = lax.axis_size("fsdp")
    micro_count = layer_input.shape[1]
    local_rows = layer_input.shape[2]
    feature_width = layer_input.shape[3]
    total_rows = micro_count * local_rows * lax.axis_size("rep") * groups
    norm_scale = float(total_rows) ** (-0.5)
    weight_shard = value_weight[0]
    gain_shard = norm_gain[0]
    gain_column_block = gain_shard.astype(jnp.float32)
    is_upper = lax.axis_index("section") == 1
    weight_total = jnp.zeros(weight_shard.shape, jnp.float32)
    gain_total = jnp.zeros(gain_shard.shape, jnp.float32)
    results = []
    for batch_index in range(micro_count):
        layer_rows = layer_input[0, batch_index]
        grad_rows = value_grad[0, batch_index]
        columns = lax.all_to_all(layer_rows, "fsdp", split_axis=1, concat_axis=0, tiled=True)
        grads_all = lax.all_gather(grad_rows, "fsdp", axis=0, tiled=True)
        column_entries = columns.astype(jnp.float32)
        row_vals = layer_rows.astype(jnp.float32)
        scale_own = lax.rsqrt(jnp.mean(row_vals * row_vals, axis=1) + norm_eps)
        scale_every_row = lax.all_gather(scale_own, "fsdp", axis=0, tiled=True)
        centered_columns = column_entries * scale_every_row[:, None]
        normalized_input = (centered_columns * gain_column_block).astype(jnp.bfloat16)
        weight_part = lax.dot_general(
            normalized_input,
            grads_all,
            (((0,), (0,)), ((), ())),
            preferred_element_type=jnp.float32,
        )
        normalized_gradient = lax.dot_general(
            grads_all, weight_shard, (((1,), (1,)), ((), ())), preferred_element_type=jnp.float32
        )
        gain_portion = jnp.sum(normalized_gradient * centered_columns, axis=0)
        centered_gradient = normalized_gradient * gain_column_block
        row_accumulated = lax.psum(jnp.sum(centered_gradient * centered_columns, axis=1), "fsdp")
        local_cols = (
            scale_every_row[:, None]
            * (centered_gradient - centered_columns * (row_accumulated / feature_width)[:, None])
        ).astype(jnp.bfloat16)
        local_piece = lax.all_to_all(local_cols, "fsdp", split_axis=0, concat_axis=1, tiled=True)
        weight_total = weight_total + weight_part
        gain_total = gain_total + gain_portion
        local_f = local_piece.astype(jnp.float32)
        upper = (top_grad[batch_index].astype(jnp.float32) + local_f).astype(jnp.bfloat16)
        passed = shifted(upper, "section", -1)
        lower = (passed.astype(jnp.float32) + local_f).astype(jnp.bfloat16)
        results.append(jnp.where(is_upper, upper, lower))
    weight_total, gain_total = lax.psum((weight_total, gain_total), "rep")
    input_grad = jnp.stack(results)[None]
    return (input_grad, (weight_total * norm_scale)[None], (gain_total * norm_scale)[None])


def solution(mesh):
    return jax.shard_map(
        local,
        mesh=mesh,
        in_specs=(
            P("section", None, ("rep", "fsdp"), None),
            P("section", None, ("rep", "fsdp"), None),
            P("section", "fsdp", None),
            P("section", "fsdp"),
            P(None, ("rep", "fsdp"), None),
        ),
        out_specs=(
            P("section", None, ("rep", "fsdp"), None),
            P("section", "fsdp", None),
            P("section", "fsdp"),
        ),
        check_vma=False,
    )
```

profile of v0, /device:TPU:0, one launch (start us, length us, event | category | flops | bytes accessed | tf_op | source)
XLA Modules:
  0.0 332.6 jit_solution(5759405734209134086)
XLA Ops:
  7.2 1.7 fusion.15
  8.8 0.8 all_to_all.40
  9.7 1.5 copy.8
  11.2 6.3 %all-to-all-start = ((bf16[64,4,2048]{2,0,1:T(8,128)(2,1)}), bf16[64,4,2048]{2,0,1:T(8,128)(2,1)}, u32[]{:S(2)}, u32[]{:S(2)}) async-start(bf16[64,4,2048]{2,0,1:T(8,128)(2,1)} %copy.8), calls=%async_computation | async-start | bytes 2097152 | tf_op jit(solution)/shard_map/all_to_all | solution.py:32
  17.5 0.8 all_to_all.44
  18.3 0.0 copy-start.1
  18.3 1.5 copy.10
  19.9 23.5 %all-to-all-done = bf16[64,4,2048]{2,0,1:T(8,128)(2,1)} async-done(((bf16[64,4,2048]{2,0,1:T(8,128)(2,1)}), bf16[64,4,2048]{2,0,1:T(8,128)(2,1)}, u32[]{:S(2)}, u32[]{:S(2)}) %all-to-all-start) | async-done | bytes 1048608 | tf_op jit(solution)/shard_map/all_to_all | solution.py:32
  43.4 3.5 %all-to-all-start.2 = ((bf16[64,4,2048]{2,0,1:T(8,128)(2,1)}), bf16[64,4,2048]{2,0,1:T(8,128)(2,1)S(1)}, u32[]{:S(2)}, u32[]{:S(2)}) async-start(bf16[64,4,2048]{2,0,1:T(8,128)(2,1)} %copy.10), calls=%async_computation.2 | async-start | bytes 2097152 | tf_op jit(solution)/shard_map/all_to_all | solution.py:32
  46.9 0.5 multiply_reduce_fusion.5
  47.5 0.6 dynamic-slice
  48.7 0.1 rsqrt_dynamic-update-slice_fusion.1
  48.8 0.1 rsqrt_dynamic-update-slice_fusion
  48.9 20.7 %all-reduce.3 = (f32[256]{0:T(256)S(1)}, f32[256]{0:T(256)S(1)}) all-reduce(f32[256]{0:T(256)S(1)} %rsqrt_dynamic-update-slice_fusion, f32[256]{0:T(256)S(1)} %rsqrt_dynamic-update-slice_fusion.1), channel_id=1, replica_groups=mesh['section'=2,'rep'=4,'fsdp'=4] {'fsdp'}, use_global_device_ids=true, to_apply=%add.1 | all-reduce | flops 512 | bytes 4096
  69.6 20.1 %all-gather = bf16[1,1,256,1024]{3,2,1,0:T(8,128)(2,1)S(1)} all-gather(bf16[1,1,64,1024]{3,2,1,0:T(8,128)(2,1)S(1)} %get-tuple-element.23), channel_id=2, replica_groups=mesh['section'=2,'rep'=4,'fsdp'=4] {'fsdp'}, dimensions={2}, use_global_device_ids=true | all-gather | bytes 655360 | tf_op jit(solution)/shard_map/all_gather | solution.py:33
  89.7 15.9 %all-gather.1 = bf16[1,1,256,1024]{3,2,1,0:T(8,128)(2,1)S(1)} all-gather(bf16[1,1,64,1024]{3,2,1,0:T(8,128)(2,1)S(1)} %get-tuple-element.24), channel_id=3, replica_groups=mesh['section'=2,'rep'=4,'fsdp'=4] {'fsdp'}, dimensions={2}, use_global_device_ids=true | all-gather | bytes 655360 | tf_op jit(solution)/shard_map/all_gather | solution.py:33
  105.6 0.8 copy-done.3
  106.4 4.8 %fusion = f32[256,2048]{1,0:T(8,128)} fusion(bf16[1,2048,1024]{2,1,0:T(8,128)(2,1)} %param.7, bf16[1,1,256,1024]{3,2,1,0:T(8,128)(2,1)S(1)} %all-gather.1), kind=kOutput, calls=%fused_computation.2 | convolution fusion | flops 1073741824 | bytes 6815744 | tf_op jit(solution)/shard_map/dot_general | solution.py:46
  111.2 0.0 all-to-all-done.2
  111.2 6.1 %multiply_reduce_fusion.1 = (f32[2048]{0:T(1024)S(1)}, f32[256]{0:T(256)S(1)}, f32[256]{0:T(256)S(1)}, f32[2048]{0:T(1024)S(1)}, f32[256,2048]{1,0:T(8,128)}) fusion(bf16[64,4,2048]{2,0,1:T(8,128)(2,1)} %all-to-all-done, f32[256]{0:T(256)S(1)} %get-tuple-element.12, f32[2048]{0:T(1024)S(1)} %bitcast.85, f32[256,2048]{1,0:T(8,128)} %fusion, ...), kind=kOutput, calls=%fused_computation.16 | convolution fusion | flops 1081077248 | bytes 11038720 | tf_op jit(solution)/shard_map/dot_general | solution.py:46
  117.4 9.7 %all-reduce.2 = (f32[256]{0:T(256)S(1)}, f32[256]{0:T(256)S(1)}) all-reduce(f32[256]{0:T(256)S(1)} %get-tuple-element.27, f32[256]{0:T(256)S(1)} %get-tuple-element.6), channel_id=1, replica_groups=mesh['section'=2,'rep'=4,'fsdp'=4] {'fsdp'}, use_global_device_ids=true, to_apply=%region_5.6 | all-reduce | flops 512 | bytes 4096 | tf_op jit(solution)/shard_map/psum | solution.py:51
  127.0 5.1 %multiply_convert_fusion = (bf16[256,2048]{1,0:T(8,128)(2,1)S(1)}, bf16[256,2048]{1,0:T(8,128)(2,1)}, bf16[256,2048]{1,0:T(8,128)(2,1)}, bf16[256,2048]{1,0:T(8,128)(2,1)S(1)}) fusion(bf16[64,4,2048]{2,0,1:T(8,128)(2,1)S(1)} %all-to-all-done.2, f32[256]{0:T(256)S(1)} %get-tuple-element.11, f32[2048]{0:T(1024)S(1)} %bitcast.86, f32[256]{0:T(256)S(1)} %get-tuple-element.30, ...), kind=kLoop, calls=%fused_computation.17 | loop fusion | flops 9437184 | bytes 10498048 | tf_op jit(solution)/shard_map/convert_element_type | solution.py:39
  132.2 3.5 %all-to-all-start.1 = ((bf16[4,64,2048]{2,1,0:T(8,128)(2,1)}), bf16[4,64,2048]{2,1,0:T(8,128)(2,1)S(1)}, u32[]{:S(2)}, u32[]{:S(2)}) async-start(bf16[4,64,2048]{2,1,0:T(8,128)(2,1)} %bitcast.84), calls=%async_computation.1 | async-start | bytes 2097152 | tf_op jit(solution)/shard_map/all_to_all | solution.py:56
  135.7 0.0 all-reduce.6.cloned.1.call-start
  135.7 2.4 fusion.12
  138.1 4.7 %convolution_add_fusion = f32[2048,1024]{1,0:T(8,128)} fusion(f32[2048,1024]{1,0:T(8,128)S(1)} %fusion.12, bf16[256,2048]{1,0:T(8,128)(2,1)S(1)} %get-tuple-element.19, bf16[1,1,256,1024]{3,2,1,0:T(8,128)(2,1)S(1)} %copy-done.4), kind=kOutput, calls=%fused_computation.1 | convolution fusion | flops 1075838976 | bytes 18350080 | tf_op jit(solution)/shard_map/dot_general | solution.py:40
  142.9 0.0 all-reduce.6.cloned.1.call-update
  142.9 10.2 %all-to-all-done.1 = bf16[4,64,2048]{2,1,0:T(8,128)(2,1)S(1)} async-done(((bf16[4,64,2048]{2,1,0:T(8,128)(2,1)}), bf16[4,64,2048]{2,1,0:T(8,128)(2,1)S(1)}, u32[]{:S(2)}, u32[]{:S(2)}) %all-to-all-start.1) | async-done | bytes 1048608 | tf_op jit(solution)/shard_map/all_to_all | solution.py:56
  153.0 4.4 %all-to-all-start.3 = ((bf16[4,64,2048]{2,1,0:T(8,128)(2,1)}), bf16[4,64,2048]{2,1,0:T(8,128)(2,1)}, u32[]{:S(2)}, u32[]{:S(2)}) async-start(bf16[4,64,2048]{2,1,0:T(8,128)(2,1)} %bitcast.14), calls=%async_computation.3 | async-start | bytes 2097152 | tf_op jit(solution)/shard_map/all_to_all | solution.py:56
  157.5 0.2 convert_bitcast_fusion.1
  157.7 0.2 copy.12
  157.9 19.4 %all-to-all-done.3 = bf16[4,64,2048]{2,1,0:T(8,128)(2,1)} async-done(((bf16[4,64,2048]{2,1,0:T(8,128)(2,1)}), bf16[4,64,2048]{2,1,0:T(8,128)(2,1)}, u32[]{:S(2)}, u32[]{:S(2)}) %all-to-all-start.3) | async-done | bytes 1048608 | tf_op jit(solution)/shard_map/all_to_all | solution.py:56
  177.4 1.5 convert_bitcast_fusion
  178.9 0.0 copy-start.2
  178.9 0.1 copy.13
  179.0 0.0 copy-start
  179.0 2.3 copy-done.2
  181.3 1.8 fusion.5
  183.1 1.3 collective-permute-start
  184.4 1.3 collective-permute-start.1
  185.7 10.5 %psum.31 = f32[2048]{0:T(1024)S(1)} all-reduce(f32[2048]{0:T(1024)S(1)} %add.39), channel_id=1, replica_groups=mesh['section'=2,'rep'=4,'fsdp'=4] {'rep'}, use_global_device_ids=true, to_apply=%region_9.10 | all-reduce | flops 2048 | bytes 16384 | tf_op jit(solution)/shard_map/psum | solution.py:64
  196.2 0.6 broadcast_multiply_fusion
  196.8 0.0 collective-permute-done
  196.8 0.0 collective-permute-done.1
  196.8 3.3 fusion.7
  200.2 1.5 maximum_bitcast_fusion
  201.7 115.4 %all-reduce.6.cloned.1.call-done = f32[2048,1024]{1,0:T(8,128)} async-done(((f32[2048,1024]{1,0:T(8,128)}), f32[2048,1024]{1,0:T(8,128)}) %all-reduce.6.cloned.1.call-update) | async-done | bytes 8388624 | tf_op jit(solution)/shard_map/psum | solution.py:64
  317.0 8.8 %multiply_bitcast_fusion = f32[1,2048,1024]{2,1,0:T(8,128)} fusion(f32[2048,1024]{1,0:T(8,128)} %all-reduce.6.cloned.1.call-done), kind=kLoop, calls=%fused_computation | loop fusion | flops 2097152 | bytes 16777216 | tf_op jit(solution)/shard_map/broadcast_in_dim | solution.py:66
  (19 shorter events, 0.1 us)
Async XLA Ops:
  11.2 32.1 %all-to-all-start = ((bf16[64,4,2048]{2,0,1:T(8,128)(2,1)}), bf16[64,4,2048]{2,0,1:T(8,128)(2,1)}, u32[]{:S(2)}, u32[]{:S(2)}) async-start(bf16[64,4,2048]{2,0,1:T(8,128)(2,1)} %copy.8), calls=%async_computation | async-start | bytes 2097152 | tf_op jit(solution)/shard_map/all_to_all | solution.py:32
  18.3 28.6 %copy-start.1 = (bf16[1,2,64,8192]{3,2,1,0:T(8,128)(2,1)S(1)}, bf16[1,2,64,8192]{3,2,1,0:T(8,128)(2,1)}, u32[]{:S(2)}) copy-start(bf16[1,2,64,8192]{3,2,1,0:T(8,128)(2,1)} %param.5) | copy-start | bytes 6291460
  19.9 27.6 %copy-start.7 = (bf16[1,2048]{1,0:T(2,128)(2,1)S(1)}, bf16[1,2048]{1,0:T(2,128)(2,1)}, u32[]{:S(2)}) copy-start(bf16[1,2048]{1,0:T(2,128)(2,1)} %param.8) | copy-start | bytes 12292
  19.9 27.6 %copy-start.8 = (u32[32]{0:T(128)S(1)}, u32[32]{0:T(128)}, u32[]{:S(2)}) copy-start(u32[32]{0:T(128)} %constant.28) | copy-start | bytes 388
  19.9 49.7 %copy-start.6 = (bf16[1,2,64,1024]{3,2,1,0:T(8,128)(2,1)S(1)}, bf16[1,2,64,1024]{3,2,1,0:T(8,128)(2,1)}, u32[]{:S(2)}) copy-start(bf16[1,2,64,1024]{3,2,1,0:T(8,128)(2,1)} %param.6) | copy-start | bytes 786436
  43.4 67.9 %all-to-all-start.2 = ((bf16[64,4,2048]{2,0,1:T(8,128)(2,1)}), bf16[64,4,2048]{2,0,1:T(8,128)(2,1)S(1)}, u32[]{:S(2)}, u32[]{:S(2)}) async-start(bf16[64,4,2048]{2,0,1:T(8,128)(2,1)} %copy.10), calls=%async_computation.2 | async-start | bytes 2097152 | tf_op jit(solution)/shard_map/all_to_all | solution.py:32
  89.7 21.5 %copy-start.5 = (bf16[1,1,256,1024]{3,2,1,0:T(8,128)(2,1)}, bf16[1,1,256,1024]{3,2,1,0:T(8,128)(2,1)S(1)}, u32[]{:S(2)}) copy-start(bf16[1,1,256,1024]{3,2,1,0:T(8,128)(2,1)S(1)} %all-gather) | copy-start | bytes 1572868
  105.6 0.8 copy-start.3
  132.2 20.9 %all-to-all-start.1 = ((bf16[4,64,2048]{2,1,0:T(8,128)(2,1)}), bf16[4,64,2048]{2,1,0:T(8,128)(2,1)S(1)}, u32[]{:S(2)}, u32[]{:S(2)}) async-start(bf16[4,64,2048]{2,1,0:T(8,128)(2,1)} %bitcast.84), calls=%async_computation.1 | async-start | bytes 2097152 | tf_op jit(solution)/shard_map/all_to_all | solution.py:56
  135.7 181.3 %all-reduce.6.cloned.1.call-start = ((), (), s32[]{:S(2)}) async-start(), calls=%async_computation.4 | async-start | bytes 16777216 | tf_op jit(solution)/shard_map/psum | solution.py:64
  135.7 2.4 copy-start.4
  153.0 24.3 %all-to-all-start.3 = ((bf16[4,64,2048]{2,1,0:T(8,128)(2,1)}), bf16[4,64,2048]{2,1,0:T(8,128)(2,1)}, u32[]{:S(2)}, u32[]{:S(2)}) async-start(bf16[4,64,2048]{2,1,0:T(8,128)(2,1)} %bitcast.14), calls=%async_computation.3 | async-start | bytes 2097152 | tf_op jit(solution)/shard_map/all_to_all | solution.py:56
  178.9 2.5 copy-start.2
  179.0 4.1 %copy-start = (f32[4,8,8,2048]{3,2,0,1:T(8,128)}, f32[4,8,8,2048]{3,2,0,1:T(8,128)S(1)}, u32[]{:S(2)}) copy-start(f32[4,8,8,2048]{3,2,0,1:T(8,128)S(1)} %copy.13) | copy-start | bytes 6291460
  183.1 13.7 %collective-permute-start = (bf16[64,8192]{1,0:T(8,128)(2,1)}, bf16[64,8192]{1,0:T(8,128)(2,1)S(1)}, u32[]{:S(2)}, u32[]{:S(2)}) collective-permute-start(bf16[64,8192]{1,0:T(8,128)(2,1)} %get-tuple-element.15), channel_id=1, source_target_pairs={{16,0},{17,1},{18,2},{19,3},{20,4},{21,5},{22,6},{23,7},{24,8},{25... | collective-permute-start | bytes 3145736 | tf_op jit(solution)/shard_map/ppermute | solution.py:12
  184.4 12.4 %collective-permute-start.1 = (bf16[64,8192]{1,0:T(8,128)(2,1)}, bf16[64,8192]{1,0:T(8,128)(2,1)}, u32[]{:S(2)}, u32[]{:S(2)}) collective-permute-start(bf16[64,8192]{1,0:T(8,128)(2,1)} %get-tuple-element.16), channel_id=1, source_target_pairs={{16,0},{17,1},{18,2},{19,3},{20,4},{21,5},{22,6},{23,7},{24,8},{25... | collective-permute-start | bytes 3145736 | tf_op jit(solution)/shard_map/ppermute | solution.py:12
Sparse Core Ops, SparseCore 0:
  143.0 173.9 all-reduce.5
where the time goes:
time: 333 us
  waiting for transfers between devices  168 us (50%)
  blocking collectives  76.8 us (23%)
  other arithmetic  23.5 us (7%)
  starting transfers between devices  20.4 us (6%)
  matrix products  18.1 us (5%)
  between operations  14.9 us (4%)
  local copies, waits for them, and re-layouts  10.5 us (3%)
    psum x1, waiting for transfers between devices, local(): weight_total, gain_total = lax.psum((weight_total, gain_total), 'rep')  115 us
    all_gather x2, blocking collectives, local(): grads_all = lax.all_gather(grad_rows, 'fsdp', axis=0, tiled=True)  36 us
    all_to_all x2, waiting for transfers between devices, local(): lax.all_to_all(local_cols, 'fsdp', split_axis=0, concat_axis=1, tiled=True)  29.6 us
    all_to_all x2, waiting for transfers between devices, local(): lax.all_to_all(layer_rows, 'fsdp', split_axis=1, concat_axis=0, tiled=True)  23.5 us
    unnamed x1, blocking collectives  20.7 us
    dot_general x2, matrix products, local(): lax.dot_general(grads_all, weight_shard, (((1,), (1,)), ((), ())), prefer...  11 us
    psum x1, blocking collectives, local(): weight_total, gain_total = lax.psum((weight_total, gain_total), 'rep')  10.5 us
    all_to_all x2, starting transfers between devices, local(): lax.all_to_all(layer_rows, 'fsdp', split_axis=1, concat_axis=0, tiled=True)  9.84 us
  transfers between devices with their start and end apart: 7, of which 4 were waited for; matrix products, arithmetic and copies ran while one was open for 7% of the time, Pallas kernels for 0%

commit v1 on v0

v1 whole, which is shorter than its diff:
```python
import jax
import jax.numpy as jnp
from jax import lax
from jax.sharding import PartitionSpec as P

norm_eps = 1e-05
bf16 = jnp.bfloat16
f32 = jnp.float32


def cyclic(value, axis, steps):
    count = lax.axis_size(axis)
    return lax.ppermute(value, axis, [(i, (i + steps) % count) for i in range(count)])


def flipped(value, axis, bit):
    count = lax.axis_size(axis)
    return lax.ppermute(value, axis, [(i, i ^ (1 << bit)) for i in range(count)])


def line_gather(value, axis):
    count = lax.axis_size(axis)
    me = lax.axis_index(axis)
    right, left = [value], [value]
    for k in range(1, count):
        right.append(lax.ppermute(right[-1], axis, [(i, i + 1) for i in range(k - 1, count - 1)]))
        left.append(lax.ppermute(left[-1], axis, [(i, i - 1) for i in range(1, count - k + 1)]))
    return [value] + [jnp.where(me >= j, right[j], left[count - j]) for j in range(1, count)]


def summed_over_rep(part, order):
    me = lax.axis_index("rep")
    for bit in order:
        half = part.shape[0] // 2
        mine = (me >> bit) & 1
        keep = lax.dynamic_slice_in_dim(part, mine * half, half, 0)
        send = lax.dynamic_slice_in_dim(part, (1 - mine) * half, half, 0)
        part = keep + flipped(send.astype(bf16), "rep", bit).astype(f32)
    part = part.astype(bf16)
    for bit in reversed(order):
        mine = ((me >> bit) & 1) == 1
        other = flipped(part, "rep", bit)
        part = jnp.concatenate([jnp.where(mine, other, part), jnp.where(mine, part, other)], axis=0)
    return part


def local(layer_input, value_grad, value_weight, norm_gain, top_grad):
    groups = lax.axis_size("fsdp")
    reps = lax.axis_size("rep")
    bits = reps.bit_length() - 1
    me = lax.axis_index("fsdp")
    _, micro, rows, width = layer_input.shape
    tokens = micro * rows
    shard = width // groups
    total_rows = tokens * reps * groups
    norm_scale = float(total_rows) ** (-0.5)
    chunks = 2
    chunk = shard // chunks

    weight = value_weight[0]
    gain = norm_gain[0].astype(f32)
    x = layer_input[0].reshape(tokens, width).astype(f32)
    grads = value_grad[0].reshape(tokens, -1)

    grad_slots = line_gather(grads, "fsdp")
    grads_all = jnp.concatenate(grad_slots, axis=0)

    scale = lax.rsqrt(jnp.mean(x * x, axis=1, keepdims=True) + norm_eps)
    hat = (x * scale).astype(bf16)

    sums = []
    for c in range(chunks):
        blocks = []
        for j in range(groups):
            start = ((me + j) % groups) * shard + c * chunk
            block = lax.dynamic_slice_in_dim(hat, start, chunk, 1)
            blocks.append(cyclic(block, "fsdp", j) if j else block)
        columns = jnp.concatenate(blocks, axis=0)
        product = lax.dot_general(columns, grads_all, (((0,), (0,)), ((), ())), preferred_element_type=f32)
        orders = [tuple(range(bits)), tuple(reversed(range(bits)))] if bits > 1 else [tuple(range(bits))]
        piece = chunk // len(orders)
        for p, order in enumerate(orders):
            sums.append(summed_over_rep(product[p * piece : (p + 1) * piece], order))
    raw = jnp.concatenate(sums, axis=0).astype(f32)
    weight_grad = raw * (gain * norm_scale)[:, None]
    gain_grad = jnp.sum(raw * weight.astype(f32), axis=1) * norm_scale

    back = lax.dot_general(grads_all, weight, (((1,), (1,)), ((), ())), preferred_element_type=f32)
    back = (back * gain).astype(bf16).reshape(groups, micro, rows, shard)
    results = []
    for m in range(micro):
        dhat = jnp.zeros((rows, width), bf16)
        for j in range(groups):
            block = back[j, m]
            block = cyclic(block, "fsdp", -j) if j else block
            dhat = lax.dynamic_update_slice(dhat, block, (0, ((me + j) % groups) * shard))
        dhat = dhat.astype(f32)
        own = x[m * rows : (m + 1) * rows] * scale[m * rows : (m + 1) * rows]
        mean = jnp.sum(dhat * own, axis=1, keepdims=True) / width
        piece = (scale[m * rows : (m + 1) * rows] * (dhat - own * mean)).astype(bf16).astype(f32)
        upper = (top_grad[m].astype(f32) + piece).astype(bf16)
        passed = lax.ppermute(upper, "section", [(1, 0)])
        lower = (passed.astype(f32) + piece).astype(bf16)
        results.append(jnp.where(lax.axis_index("section") == 1, upper, lower))
    return (jnp.stack(results)[None], weight_grad[None], gain_grad[None])


def solution(mesh):
    return jax.shard_map(
        local,
        mesh=mesh,
        in_specs=(
            P("section", None, ("rep", "fsdp"), None),
            P("section", None, ("rep", "fsdp"), None),
            P("section", "fsdp", None),
            P("section", "fsdp"),
            P(None, ("rep", "fsdp"), None),
        ),
        out_specs=(
            P("section", None, ("rep", "fsdp"), None),
            P("section", "fsdp", None),
            P("section", "fsdp"),
        ),
        check_vma=False,
    )
```

time: 333 us -> 198 us (0.59)
  blocking collectives: 76.8 us -> 0 us
  waiting for transfers between devices: 168 us -> 104 us
  starting transfers between devices: 20.4 us -> 52.2 us
  between operations: 14.9 us -> 1.34 us
  matrix products: 18.1 us -> 9.16 us
  local copies, waits for them, and re-layouts: 10.5 us -> 7.16 us
    psum x1 -> x0, waiting for transfers between devices: 115 us -> none  [local(): weight_total, gain_total = lax.psum((weight_total, gain_total), 'rep')]
    ppermute x2 -> x36, waiting for transfers between devices: 0.01 us -> 104 us  [the longest x12 42 us: cyclic(): lax.ppermute(value, axis, [(i, (i + steps) % count) for i in range(count)])]
    all_to_all x4 -> x0, waiting for transfers between devices: 53.1 us -> none  [the longest x2 29.6 us: local(): lax.all_to_all(local_cols, 'fsdp', split_axis=0, concat_axis=1, tiled=True)]
    ppermute x2 -> x36, starting transfers between devices: 2.57 us -> 52.2 us  [the longest x16 18.7 us: flipped(): return lax.ppermute(value, axis, [(i, i ^ 1 << bit) for i in range(count)])]
    all_gather x2 -> x0, blocking collectives: 36 us -> none  [local(): grads_all = lax.all_gather(grad_rows, 'fsdp', axis=0, tiled=True)]
    unnamed x1 -> x0, blocking collectives: 20.7 us -> none
    psum x2 -> x0, blocking collectives: 20.2 us -> none  [the longest x1 10.5 us: local(): weight_total, gain_total = lax.psum((weight_total, gain_total), 'rep')]
    all_to_all x4 -> x0, starting transfers between devices: 17.8 us -> none  [the longest x2 9.84 us: local(): lax.all_to_all(layer_rows, 'fsdp', split_axis=1, concat_axis=0, tiled=True)]
  transfers between devices with their start and end apart: 7 -> 36, of which waited for: 4 -> 16; matrix products, arithmetic and copies ran while one was open for 7% -> 15% of each run, Pallas kernels for 0% -> 0%
where the time goes in v1:
time: 198 us
  waiting for transfers between devices  104 us (53%)
  starting transfers between devices  52.2 us (26%)
  other arithmetic  24.1 us (12%)
  matrix products  9.16 us (5%)
  local copies, waits for them, and re-layouts  7.16 us (4%)
    ppermute x12, waiting for transfers between devices, cyclic(): lax.ppermute(value, axis, [(i, (i + steps) % count) for i in range(count)])  42 us
    ppermute x16, waiting for transfers between devices, flipped(): return lax.ppermute(value, axis, [(i, i ^ 1 << bit) for i in range(count)])  35.8 us
    ppermute x3, waiting for transfers between devices, line_gather(): lax.ppermute(left[-1], axis, [(i, i - 1) for i in range(1, count - k + 1)])  25.9 us
    ppermute x16, starting transfers between devices, flipped(): return lax.ppermute(value, axis, [(i, i ^ 1 << bit) for i in range(count)])  18.7 us
    ppermute x12, starting transfers between devices, cyclic(): lax.ppermute(value, axis, [(i, (i + steps) % count) for i in range(count)])  18.4 us
    ppermute x3, starting transfers between devices, line_gather(): lax.ppermute(right[-1], axis, [(i, i + 1) for i in range(k - 1, count - 1)])  8.44 us
    dot_general x1, matrix products, local(): lax.dot_general(grads_all, weight, (((1,), (1,)), ((), ())), preferred_el...  4.59 us
    dot_general x2, matrix products, local(): lax.dot_general(columns, grads_all, (((0,), (0,)), ((), ())), preferred_e...  4.57 us
  transfers between devices with their start and end apart: 36, of which 16 were waited for; matrix products, arithmetic and copies ran while one was open for 15% of the time, Pallas kernels for 0%

profile of v1, /device:TPU:0, one launch (start us, length us, event | category | flops | bytes accessed | tf_op | source)
XLA Modules:
  0.0 197.6 jit_solution(15677284119583183523)
XLA Ops:
  0.6 1.4 collective-permute-start.1
  2.1 6.3 %collective-permute-start = (bf16[128,1024]{1,0:T(8,128)(2,1)}, bf16[128,1024]{1,0:T(8,128)(2,1)}, u32[]{:S(2)}, u32[]{:S(2)}) collective-permute-start(bf16[128,1024]{1,0:T(8,128)(2,1)} %bitcast.96), channel_id=1, source_target_pairs={{0,1},{1,2},{2,3},{4,5},{5,6},{6,7},{8,9},{9,10},{10,11},{12,13},{... | collective-permute-start | bytes 786440 | tf_op jit(solution)/shard_map/ppermute | solution.py:26
  8.3 2.1 %multiply_reduce_fusion.1 = f32[2,64]{1,0:T(2,128)S(1)} fusion(bf16[1,2,64,8192]{3,2,1,0:T(8,128)(2,1)} %param.5), kind=kLoop, calls=%fused_computation.7 | loop fusion | flops 3145600 | bytes 2097664 | tf_op jit(solution)/shard_map/reduce_sum | solution.py:68
  10.5 1.8 fusion
  12.3 2.6 %constant_dynamic-slice_fusion.3 = (bf16[128,1024]{1,0:T(8,128)(2,1)S(1)}, bf16[128,1024]{1,0:T(8,128)(2,1)S(1)}, bf16[128,1024]{1,0:T(8,128)(2,1)S(1)}, bf16[12...) fusion(bf16[128,8192]{1,0:T(8,128)(2,1)} %fusion, ...), kind=kLoop, calls=%fused_computation.120 | loop fusion | bytes 4194336 | tf_op jit(solution)/shard_map/dynamic_slice | solution.py:76
  14.9 1.8 collective-permute-start.27
  16.7 1.2 collective-permute-start.26
  17.9 1.5 collective-permute-start.16
  19.4 1.3 collective-permute-start.2
  20.7 1.4 collective-permute-start.4
  22.1 17.5 %collective-permute-done.2 = bf16[128,1024]{1,0:T(8,128)(2,1)} collective-permute-done((bf16[128,1024]{1,0:T(8,128)(2,1)}, bf16[128,1024]{1,0:T(8,128)(2,1)}, u32[]{:S(2)}, u32[]{:S(2)}) %collective-permute-start.2) | collective-permute-done | bytes 262176 | tf_op jit(solution)/shard_map/ppermute | solution.py:27
  39.6 1.3 collective-permute-start.3
  40.9 2.4 %convert_element_type.147 = f32[1,2,64,8192]{3,2,1,0:T(8,128)} convert(bf16[1,2,64,8192]{3,2,1,0:T(8,128)(2,1)S(1)} %copy-done.1) | non-fusion elementwise | flops 1048576 | bytes 6291456 | tf_op jit(solution)/shard_map/convert_element_type | solution.py:62
  45.2 8.3 %collective-permute-done.3 = bf16[128,1024]{1,0:T(8,128)(2,1)} collective-permute-done((bf16[128,1024]{1,0:T(8,128)(2,1)}, bf16[128,1024]{1,0:T(8,128)(2,1)}, u32[]{:S(2)}, u32[]{:S(2)}) %collective-permute-start.3) | collective-permute-done | bytes 262176 | tf_op jit(solution)/shard_map/ppermute | solution.py:27
  55.6 4.6 %multiply_convert_fusion = bf16[512,2048]{1,0:T(8,128)(2,1)S(1)} fusion(bf16[1,2048,1024]{2,1,0:T(8,128)(2,1)} %param.7, f32[2048]{0:T(1024)S(1)} %bitcast.93, bf16[128,1024]{1,0:T(8,128)(2,1)S(1)} %broadcast_select_fusion.16, bf16[128,1024]{1,0:T(8,128)(2,1)S(1)} %broadcast_select_fusion.17, bf16[128,1024]{1,0:T(8,128)(2,1)S(1)} %broadcast_select_fusion.18, ...), kind=kOutput, calls=%fused_computation.6 | convolution fusion | flops 2153775104 | bytes 7348224 | tf_op jit(solution)/shard_map/dot_general | solution.py:88
  60.6 3.5 %collective-permute-start.25 = (bf16[128,1024]{1,0:T(8,128)(2,1)S(1)}, bf16[128,1024]{1,0:T(8,128)(2,1)S(1)}, u32[]{:S(2)}, u32[]{:S(2)}) collective-permute-start(bf16[128,1024]{1,0:T(8,128)(2,1)S(1)} %get-tuple-element.18), channel_id=1, source_target_pairs={{0,1},{1,2},{2,3},{3,0},{4,5},{5,6},{6,7},{7,4},{8,9},{9,10},{10,1... | collective-permute-start | bytes 786440 | tf_op jit(solution)/shard_map/ppermute | solution.py:13
  64.1 13.3 %collective-permute-done.15 = bf16[128,1024]{1,0:T(8,128)(2,1)S(1)} collective-permute-done((bf16[128,1024]{1,0:T(8,128)(2,1)}, bf16[128,1024]{1,0:T(8,128)(2,1)S(1)}, u32[]{:S(2)}, u32[]{:S(2)}) %collective-permute-start.15) | collective-permute-done | bytes 262176 | tf_op jit(solution)/shard_map/ppermute | solution.py:13
  77.4 2.2 %fusion.21 = f32[1024,1024]{1,0:T(8,128)S(1)} fusion(bf16[128,1024]{1,0:T(8,128)(2,1)} %collective-permute-done.16, bf16[128,1024]{1,0:T(8,128)(2,1)S(1)} %collective-permute-done.15, bf16[128,1024]{1,0:T(8,128)(2,1)S(1)} %collective-permute-done.14, bf16[128,1024]{1,0:T(8,128)(2,1)S(1)} %get-tuple-element.22, ...), kind=kOutput, calls=%fused_computation.36 | convolution fusion | flops 1082130432 | bytes 6291456 | tf_op jit(solution)/shard_map/dot_general | solution.py:79
  80.3 3.9 %collective-permute-start.10 = (bf16[64,2048]{1,0:T(8,128)(2,1)S(1)}, bf16[64,2048]{1,0:T(8,128)(2,1)S(1)}, u32[]{:S(2)}, u32[]{:S(2)}) collective-permute-start(bf16[64,2048]{1,0:T(8,128)(2,1)S(1)} %get-tuple-element.27), channel_id=1, source_target_pairs={{0,3},{1,0},{2,1},{3,2},{4,7},{5,4},{6,5},{7,6},{8,11},{9,8},{10,9... | collective-permute-start | bytes 786440 | tf_op jit(solution)/shard_map/ppermute | solution.py:13
  84.8 1.5 collective-permute-start.7
  86.2 2.3 %fusion.29 = f32[1024,1024]{1,0:T(8,128)S(1)} fusion(bf16[128,1024]{1,0:T(8,128)(2,1)} %collective-permute-done.27, bf16[128,1024]{1,0:T(8,128)(2,1)} %collective-permute-done.26, bf16[128,1024]{1,0:T(8,128)(2,1)S(1)} %collective-permute-done.25, bf16[128,1024]{1,0:T(8,128)(2,1)S(1)} %get-tuple-element.15, ...), kind=kOutput, calls=%fused_computation.44 | convolution fusion | flops 1082130432 | bytes 6291456 | tf_op jit(solution)/shard_map/dot_general | solution.py:79
  89.5 5.9 %collective-permute-done.10 = bf16[64,2048]{1,0:T(8,128)(2,1)S(1)} collective-permute-done((bf16[64,2048]{1,0:T(8,128)(2,1)S(1)}, bf16[64,2048]{1,0:T(8,128)(2,1)S(1)}, u32[]{:S(2)}, u32[]{:S(2)}) %collective-permute-start.10) | collective-permute-done | bytes 262176 | tf_op jit(solution)/shard_map/ppermute | solution.py:13
  95.4 4.3 %collective-permute-start.6 = (bf16[64,2048]{1,0:T(8,128)(2,1)S(1)}, bf16[64,2048]{1,0:T(8,128)(2,1)S(1)}, u32[]{:S(2)}, u32[]{:S(2)}) collective-permute-start(bf16[64,2048]{1,0:T(8,128)(2,1)S(1)} %get-tuple-element.30), channel_id=1, source_target_pairs={{0,3},{1,0},{2,1},{3,2},{4,7},{5,4},{6,5},{7,6},{8,11},{9,8},{10,9... | collective-permute-start | bytes 786440 | tf_op jit(solution)/shard_map/ppermute | solution.py:13
  99.8 1.6 collective-permute-start.17
  101.4 1.6 collective-permute-start.21
  103.0 22.8 %collective-permute-done.6 = bf16[64,2048]{1,0:T(8,128)(2,1)S(1)} collective-permute-done((bf16[64,2048]{1,0:T(8,128)(2,1)S(1)}, bf16[64,2048]{1,0:T(8,128)(2,1)S(1)}, u32[]{:S(2)}, u32[]{:S(2)}) %collective-permute-start.6) | collective-permute-done | bytes 262176 | tf_op jit(solution)/shard_map/ppermute | solution.py:13
  125.7 1.5 collective-permute-start.28
  127.2 1.6 collective-permute-start.32
  130.5 1.4 fusion.8
  131.9 1.3 collective-permute-start.9
  133.2 1.5 collective-permute-start.13
  135.8 3.6 %collective-permute-done.28 = bf16[256,1024]{1,0:T(8,128)(2,1)S(1)} collective-permute-done((bf16[256,1024]{1,0:T(8,128)(2,1)S(1)}, bf16[256,1024]{1,0:T(8,128)(2,1)S(1)}, u32[]{:S(2)}, u32[]{:S(2)}) %collective-permute-start.28) | collective-permute-done | bytes 524320 | tf_op jit(solution)/shard_map/ppermute | solution.py:18
  139.4 1.5 collective-permute-start.22
  142.2 1.5 collective-permute-start.29
  143.9 3.9 %collective-permute-done.18 = bf16[128,1024]{1,0:T(8,128)(2,1)S(1)} collective-permute-done((bf16[128,1024]{1,0:T(8,128)(2,1)S(1)}, bf16[128,1024]{1,0:T(8,128)(2,1)S(1)}, u32[]{:S(2)}, u32[]{:S(2)}) %collective-permute-start.18) | collective-permute-done | bytes 262176 | tf_op jit(solution)/shard_map/ppermute | solution.py:18
  148.4 1.6 collective-permute-start.19
  150.0 3.4 %collective-permute-done.29 = bf16[128,1024]{1,0:T(8,128)(2,1)S(1)} collective-permute-done((bf16[128,1024]{1,0:T(8,128)(2,1)S(1)}, bf16[128,1024]{1,0:T(8,128)(2,1)S(1)}, u32[]{:S(2)}, u32[]{:S(2)}) %collective-permute-start.29) | collective-permute-done | bytes 262176 | tf_op jit(solution)/shard_map/ppermute | solution.py:18
  155.0 1.5 collective-permute-start.30
  156.6 2.4 %collective-permute-done.19 = bf16[128,1024]{1,0:T(8,128)(2,1)S(1)} collective-permute-done((bf16[128,1024]{1,0:T(8,128)(2,1)S(1)}, bf16[128,1024]{1,0:T(8,128)(2,1)S(1)}, u32[]{:S(2)}, u32[]{:S(2)}) %collective-permute-start.19) | collective-permute-done | bytes 262176 | tf_op jit(solution)/shard_map/ppermute | solution.py:18
  161.3 1.9 collective-permute-done.30
  163.2 1.5 collective-permute-start.24
  164.8 3.5 %collective-permute-done.34 = bf16[128,1024]{1,0:T(8,128)(2,1)S(1)} collective-permute-done((bf16[128,1024]{1,0:T(8,128)(2,1)S(1)}, bf16[128,1024]{1,0:T(8,128)(2,1)S(1)}, u32[]{:S(2)}, u32[]{:S(2)}) %collective-permute-start.34) | collective-permute-done | bytes 262176 | tf_op jit(solution)/shard_map/ppermute | solution.py:18
  168.9 1.6 collective-permute-start.35
  171.5 1.5 maximum_bitcast_fusion
  173.0 6.5 %collective-permute-done.20 = bf16[256,1024]{1,0:T(8,128)(2,1)S(1)} collective-permute-done((bf16[256,1024]{1,0:T(8,128)(2,1)S(1)}, bf16[256,1024]{1,0:T(8,128)(2,1)S(1)}, u32[]{:S(2)}, u32[]{:S(2)}) %collective-permute-start.20) | collective-permute-done | bytes 524320 | tf_op jit(solution)/shard_map/ppermute | solution.py:18
  180.3 7.6 %collective-permute-done.31 = bf16[256,1024]{1,0:T(8,128)(2,1)S(1)} collective-permute-done((bf16[256,1024]{1,0:T(8,128)(2,1)S(1)}, bf16[256,1024]{1,0:T(8,128)(2,1)S(1)}, u32[]{:S(2)}, u32[]{:S(2)}) %collective-permute-start.31) | collective-permute-done | bytes 524320 | tf_op jit(solution)/shard_map/ppermute | solution.py:18
  188.7 1.6 copy-done.3
  193.6 4.0 %convert_multiply_fusion = f32[1,2048,1024]{2,1,0:T(8,128)} fusion(bf16[1,2048,1024]{2,1,0:T(8,128)(2,1)S(1)} %bitcast_dynamic-update-slice_fusion, f32[2048]{0:T(1024)S(1)} %bitcast.92), kind=kLoop, calls=%fused_computation.1 | loop fusion | flops 4194304 | bytes 12591104 | tf_op jit(solution)/shard_map/mul | solution.py:85
  (112 shorter events, 21.8 us)
Async XLA Ops:
  0.6 9.9 %copy-start.1 = (bf16[1,2,64,8192]{3,2,1,0:T(8,128)(2,1)S(1)}, bf16[1,2,64,8192]{3,2,1,0:T(8,128)(2,1)}, u32[]{:S(2)}) copy-start(bf16[1,2,64,8192]{3,2,1,0:T(8,128)(2,1)} %param.5) | copy-start | bytes 6291460
  0.6 18.7 %collective-permute-start.1 = (bf16[128,1024]{1,0:T(8,128)(2,1)}, bf16[128,1024]{1,0:T(8,128)(2,1)}, u32[]{:S(2)}, u32[]{:S(2)}) collective-permute-start(bf16[128,1024]{1,0:T(8,128)(2,1)} %bitcast.95), channel_id=1, source_target_pairs={{1,0},{2,1},{3,2},{5,4},{6,5},{7,6},{9,8},{10,9},{11,10},{13,12},{... | collective-permute-start | bytes 786440 | tf_op jit(solution)/shard_map/ppermute | solution.py:27
  2.1 18.6 %collective-permute-start = (bf16[128,1024]{1,0:T(8,128)(2,1)}, bf16[128,1024]{1,0:T(8,128)(2,1)}, u32[]{:S(2)}, u32[]{:S(2)}) collective-permute-start(bf16[128,1024]{1,0:T(8,128)(2,1)} %bitcast.96), channel_id=1, source_target_pairs={{0,1},{1,2},{2,3},{4,5},{5,6},{6,7},{8,9},{9,10},{10,11},{12,13},{... | collective-permute-start | bytes 786440 | tf_op jit(solution)/shard_map/ppermute | solution.py:26
  12.3 9.7 %copy-start.4 = (bf16[1,2048]{1,0:T(2,128)(2,1)S(1)}, bf16[1,2048]{1,0:T(2,128)(2,1)}, u32[]{:S(2)}) copy-start(bf16[1,2048]{1,0:T(2,128)(2,1)} %param.8) | copy-start | bytes 12292
  14.9 65.4 %collective-permute-start.27 = (bf16[128,1024]{1,0:T(8,128)(2,1)S(1)}, bf16[128,1024]{1,0:T(8,128)(2,1)}, u32[]{:S(2)}, u32[]{:S(2)}) collective-permute-start(bf16[128,1024]{1,0:T(8,128)(2,1)S(1)} %get-tuple-element.16), channel_id=1, source_target_pairs={{0,3},{1,0},{2,1},{3,2},{4,7},{5,4},{6,5},{7,6},{8,11},{9,8},{10,9... | collective-permute-start | bytes 786440 | tf_op jit(solution)/shard_map/ppermute | solution.py:13
  16.7 67.4 %collective-permute-start.26 = (bf16[128,1024]{1,0:T(8,128)(2,1)S(1)}, bf16[128,1024]{1,0:T(8,128)(2,1)}, u32[]{:S(2)}, u32[]{:S(2)}) collective-permute-start(bf16[128,1024]{1,0:T(8,128)(2,1)S(1)} %get-tuple-element.17), channel_id=1, source_target_pairs={{0,2},{1,3},{2,0},{3,1},{4,6},{5,7},{6,4},{7,5},{8,10},{9,11},{10,... | collective-permute-start | bytes 786440 | tf_op jit(solution)/shard_map/ppermute | solution.py:13
  17.9 42.7 %collective-permute-start.16 = (bf16[128,1024]{1,0:T(8,128)(2,1)}, bf16[128,1024]{1,0:T(8,128)(2,1)}, u32[]{:S(2)}, u32[]{:S(2)}) collective-permute-start(bf16[128,1024]{1,0:T(8,128)(2,1)} %get-tuple-element.19), channel_id=1, source_target_pairs={{0,3},{1,0},{2,1},{3,2},{4,7},{5,4},{6,5},{7,6},{8,11},{9,8},{10,9... | collective-permute-start | bytes 786440 | tf_op jit(solution)/shard_map/ppermute | solution.py:13
  19.4 20.2 %collective-permute-start.2 = (bf16[128,1024]{1,0:T(8,128)(2,1)}, bf16[128,1024]{1,0:T(8,128)(2,1)}, u32[]{:S(2)}, u32[]{:S(2)}) collective-permute-start(bf16[128,1024]{1,0:T(8,128)(2,1)} %collective-permute-done.1), channel_id=1, source_target_pairs={{1,0},{2,1},{5,4},{6,5},{9,8},{10,9},{13,12},{14,13},{17,16},{18,1... | collective-permute-start | bytes 786440 | tf_op jit(solution)/shard_map/ppermute | solution.py:27
  20.7 22.7 %collective-permute-start.4 = (bf16[128,1024]{1,0:T(8,128)(2,1)}, bf16[128,1024]{1,0:T(8,128)(2,1)}, u32[]{:S(2)}, u32[]{:S(2)}) collective-permute-start(bf16[128,1024]{1,0:T(8,128)(2,1)} %collective-permute-done), channel_id=1, source_target_pairs={{1,2},{2,3},{5,6},{6,7},{9,10},{10,11},{13,14},{14,15},{17,18},{18... | collective-permute-start | bytes 786440 | tf_op jit(solution)/shard_map/ppermute | solution.py:26
  39.6 13.9 %collective-permute-start.3 = (bf16[128,1024]{1,0:T(8,128)(2,1)}, bf16[128,1024]{1,0:T(8,128)(2,1)}, u32[]{:S(2)}, u32[]{:S(2)}) collective-permute-start(bf16[128,1024]{1,0:T(8,128)(2,1)} %collective-permute-done.2), channel_id=1, source_target_pairs={{1,0},{5,4},{9,8},{13,12},{17,16},{21,20},{25,24},{29,28}} | collective-permute-start | bytes 786440 | tf_op jit(solution)/shard_map/ppermute | solution.py:27
  43.4 12.2 %copy-start.5 = (bf16[1,2,64,1024]{3,2,1,0:T(8,128)(2,1)S(1)}, bf16[1,2,64,1024]{3,2,1,0:T(8,128)(2,1)}, u32[]{:S(2)}) copy-start(bf16[1,2,64,1024]{3,2,1,0:T(8,128)(2,1)} %param.6) | copy-start | bytes 786436
  43.4 11.1 %collective-permute-start.5 = (bf16[128,1024]{1,0:T(8,128)(2,1)}, bf16[128,1024]{1,0:T(8,128)(2,1)S(1)}, u32[]{:S(2)}, u32[]{:S(2)}) collective-permute-start(bf16[128,1024]{1,0:T(8,128)(2,1)} %collective-permute-done.4), channel_id=1, source_target_pairs={{2,3},{6,7},{10,11},{14,15},{18,19},{22,23},{26,27},{30,31}} | collective-permute-start | bytes 786440 | tf_op jit(solution)/shard_map/ppermute | solution.py:26
  53.5 23.9 %collective-permute-start.15 = (bf16[128,1024]{1,0:T(8,128)(2,1)}, bf16[128,1024]{1,0:T(8,128)(2,1)S(1)}, u32[]{:S(2)}, u32[]{:S(2)}) collective-permute-start(bf16[128,1024]{1,0:T(8,128)(2,1)} %get-tuple-element.20), channel_id=1, source_target_pairs={{0,2},{1,3},{2,0},{3,1},{4,6},{5,7},{6,4},{7,5},{8,10},{9,11},{10,... | collective-permute-start | bytes 786440 | tf_op jit(solution)/shard_map/ppermute | solution.py:13
  54.5 22.9 %collective-permute-start.14 = (bf16[128,1024]{1,0:T(8,128)(2,1)}, bf16[128,1024]{1,0:T(8,128)(2,1)S(1)}, u32[]{:S(2)}, u32[]{:S(2)}) collective-permute-start(bf16[128,1024]{1,0:T(8,128)(2,1)} %get-tuple-element.21), channel_id=1, source_target_pairs={{0,1},{1,2},{2,3},{3,0},{4,5},{5,6},{6,7},{7,4},{8,9},{9,10},{10,1... | collective-permute-start | bytes 786440 | tf_op jit(solution)/shard_map/ppermute | solution.py:13
  60.6 24.2 %collective-permute-start.25 = (bf16[128,1024]{1,0:T(8,128)(2,1)S(1)}, bf16[128,1024]{1,0:T(8,128)(2,1)S(1)}, u32[]{:S(2)}, u32[]{:S(2)}) collective-permute-start(bf16[128,1024]{1,0:T(8,128)(2,1)S(1)} %get-tuple-element.18), channel_id=1, source_target_pairs={{0,1},{1,2},{2,3},{3,0},{4,5},{5,6},{6,7},{7,4},{8,9},{9,10},{10,1... | collective-permute-start | bytes 786440 | tf_op jit(solution)/shard_map/ppermute | solution.py:13
  77.4 23.9 %collective-permute-start.12 = (bf16[64,2048]{1,0:T(8,128)(2,1)S(1)}, bf16[64,2048]{1,0:T(8,128)(2,1)S(1)}, u32[]{:S(2)}, u32[]{:S(2)}) collective-permute-start(bf16[64,2048]{1,0:T(8,128)(2,1)S(1)} %get-tuple-element.25), channel_id=1, source_target_pairs={{0,1},{1,2},{2,3},{3,0},{4,5},{5,6},{6,7},{7,4},{8,9},{9,10},{10,1... | collective-permute-start | bytes 786440 | tf_op jit(solution)/shard_map/ppermute | solution.py:13
  77.4 22.3 %collective-permute-start.11 = (bf16[64,2048]{1,0:T(8,128)(2,1)S(1)}, bf16[64,2048]{1,0:T(8,128)(2,1)S(1)}, u32[]{:S(2)}, u32[]{:S(2)}) collective-permute-start(bf16[64,2048]{1,0:T(8,128)(2,1)S(1)} %get-tuple-element.26), channel_id=1, source_target_pairs={{0,2},{1,3},{2,0},{3,1},{4,6},{5,7},{6,4},{7,5},{8,10},{9,11},{10,... | collective-permute-start | bytes 786440 | tf_op jit(solution)/shard_map/ppermute | solution.py:13
  80.3 15.1 %collective-permute-start.10 = (bf16[64,2048]{1,0:T(8,128)(2,1)S(1)}, bf16[64,2048]{1,0:T(8,128)(2,1)S(1)}, u32[]{:S(2)}, u32[]{:S(2)}) collective-permute-start(bf16[64,2048]{1,0:T(8,128)(2,1)S(1)} %get-tuple-element.27), channel_id=1, source_target_pairs={{0,3},{1,0},{2,1},{3,2},{4,7},{5,4},{6,5},{7,6},{8,11},{9,8},{10,9... | collective-permute-start | bytes 786440 | tf_op jit(solution)/shard_map/ppermute | solution.py:13
  84.2 44.7 %collective-permute-start.8 = (bf16[64,2048]{1,0:T(8,128)(2,1)S(1)}, bf16[64,2048]{1,0:T(8,128)(2,1)S(1)}, u32[]{:S(2)}, u32[]{:S(2)}) collective-permute-start(bf16[64,2048]{1,0:T(8,128)(2,1)S(1)} %get-tuple-element.28), channel_id=1, source_target_pairs={{0,1},{1,2},{2,3},{3,0},{4,5},{5,6},{6,7},{7,4},{8,9},{9,10},{10,1... | collective-permute-start | bytes 786440 | tf_op jit(solution)/shard_map/ppermute | solution.py:13
  84.8 42.5 %collective-permute-start.7 = (bf16[64,2048]{1,0:T(8,128)(2,1)S(1)}, bf16[64,2048]{1,0:T(8,128)(2,1)S(1)}, u32[]{:S(2)}, u32[]{:S(2)}) collective-permute-start(bf16[64,2048]{1,0:T(8,128)(2,1)S(1)} %get-tuple-element.29), channel_id=1, source_target_pairs={{0,2},{1,3},{2,0},{3,1},{4,6},{5,7},{6,4},{7,5},{8,10},{9,11},{10,... | collective-permute-start | bytes 786440 | tf_op jit(solution)/shard_map/ppermute | solution.py:13
  89.4 39.5 %copy-start = (f32[1,2,64,8192]{3,2,1,0:T(8,128)S(1)}, f32[1,2,64,8192]{3,2,1,0:T(8,128)}, u32[]{:S(2)}) copy-start(f32[1,2,64,8192]{3,2,1,0:T(8,128)} %convert_element_type.147) | copy-start | bytes 12582916
  95.4 30.3 %collective-permute-start.6 = (bf16[64,2048]{1,0:T(8,128)(2,1)S(1)}, bf16[64,2048]{1,0:T(8,128)(2,1)S(1)}, u32[]{:S(2)}, u32[]{:S(2)}) collective-permute-start(bf16[64,2048]{1,0:T(8,128)(2,1)S(1)} %get-tuple-element.30), channel_id=1, source_target_pairs={{0,3},{1,0},{2,1},{3,2},{4,7},{5,4},{6,5},{7,6},{8,11},{9,8},{10,9... | collective-permute-start | bytes 786440 | tf_op jit(solution)/shard_map/ppermute | solution.py:13
  99.8 33.4 %collective-permute-start.17 = (bf16[256,1024]{1,0:T(8,128)(2,1)S(1)}, bf16[256,1024]{1,0:T(8,128)(2,1)S(1)}, u32[]{:S(2)}, u32[]{:S(2)}) collective-permute-start(bf16[256,1024]{1,0:T(8,128)(2,1)S(1)} %dynamic-slice_convert_fusion.3), channel_id=1, source_target_pairs={{0,4},{4,0},{8,12},{12,8},{1,5},{5,1},{9,13},{13,9},{2,6},{6,2},{1... | collective-permute-start | bytes 1572872 | tf_op jit(solution)/shard_map/ppermute | solution.py:18
  101.4 33.6 %collective-permute-start.21 = (bf16[256,1024]{1,0:T(8,128)(2,1)S(1)}, bf16[256,1024]{1,0:T(8,128)(2,1)S(1)}, u32[]{:S(2)}, u32[]{:S(2)}) collective-permute-start(bf16[256,1024]{1,0:T(8,128)(2,1)S(1)} %dynamic-slice_convert_fusion.2), channel_id=1, source_target_pairs={{0,8},{4,12},{8,0},{12,4},{1,9},{5,13},{9,1},{13,5},{2,10},{6,14},... | collective-permute-start | bytes 1572872 | tf_op jit(solution)/shard_map/ppermute | solution.py:18
  125.7 13.7 %collective-permute-start.28 = (bf16[256,1024]{1,0:T(8,128)(2,1)S(1)}, bf16[256,1024]{1,0:T(8,128)(2,1)S(1)}, u32[]{:S(2)}, u32[]{:S(2)}) collective-permute-start(bf16[256,1024]{1,0:T(8,128)(2,1)S(1)} %dynamic-slice_convert_fusion.1), channel_id=1, source_target_pairs={{0,4},{4,0},{8,12},{12,8},{1,5},{5,1},{9,13},{13,9},{2,6},{6,2},{1... | collective-permute-start | bytes 1572872 | tf_op jit(solution)/shard_map/ppermute | solution.py:18
  127.2 14.9 %collective-permute-start.32 = (bf16[256,1024]{1,0:T(8,128)(2,1)S(1)}, bf16[256,1024]{1,0:T(8,128)(2,1)S(1)}, u32[]{:S(2)}, u32[]{:S(2)}) collective-permute-start(bf16[256,1024]{1,0:T(8,128)(2,1)S(1)} %dynamic-slice_convert_fusion), channel_id=1, source_target_pairs={{0,8},{4,12},{8,0},{12,4},{1,9},{5,13},{9,1},{13,5},{2,10},{6,14},... | collective-permute-start | bytes 1572872 | tf_op jit(solution)/shard_map/ppermute | solution.py:18
  128.9 1.6 copy-start.2
  131.9 37.0 %collective-permute-start.9 = (bf16[64,8192]{1,0:T(8,128)(2,1)S(1)}, bf16[64,8192]{1,0:T(8,128)(2,1)S(1)}, u32[]{:S(2)}, u32[]{:S(2)}) collective-permute-start(bf16[64,8192]{1,0:T(8,128)(2,1)S(1)} %get-tuple-element.5), channel_id=1, source_target_pairs={{16,0},{17,1},{18,2},{19,3},{20,4},{21,5},{22,6},{23,7},{24,8},{25... | collective-permute-start | bytes 3145736 | tf_op jit(solution)/shard_map/ppermute | solution.py:102
  133.2 37.3 %collective-permute-start.13 = (bf16[64,8192]{1,0:T(8,128)(2,1)S(1)}, bf16[64,8192]{1,0:T(8,128)(2,1)S(1)}, u32[]{:S(2)}, u32[]{:S(2)}) collective-permute-start(bf16[64,8192]{1,0:T(8,128)(2,1)S(1)} %get-tuple-element.9), channel_id=1, source_target_pairs={{16,0},{17,1},{18,2},{19,3},{20,4},{21,5},{22,6},{23,7},{24,8},{25... | collective-permute-start | bytes 3145736 | tf_op jit(solution)/shard_map/ppermute | solution.py:102
  134.9 12.8 %collective-permute-start.18 = (bf16[128,1024]{1,0:T(8,128)(2,1)S(1)}, bf16[128,1024]{1,0:T(8,128)(2,1)S(1)}, u32[]{:S(2)}, u32[]{:S(2)}) collective-permute-start(bf16[128,1024]{1,0:T(8,128)(2,1)S(1)} %dynamic-slice_convert_fusion.7), channel_id=1, source_target_pairs={{0,8},{4,12},{8,0},{12,4},{1,9},{5,13},{9,1},{13,5},{2,10},{6,14},... | collective-permute-start | bytes 786440 | tf_op jit(solution)/shard_map/ppermute | solution.py:18
  139.4 9.0 %collective-permute-start.22 = (bf16[128,1024]{1,0:T(8,128)(2,1)S(1)}, bf16[128,1024]{1,0:T(8,128)(2,1)S(1)}, u32[]{:S(2)}, u32[]{:S(2)}) collective-permute-start(bf16[128,1024]{1,0:T(8,128)(2,1)S(1)} %dynamic-slice_convert_fusion.6), channel_id=1, source_target_pairs={{0,4},{4,0},{8,12},{12,8},{1,5},{5,1},{9,13},{13,9},{2,6},{6,2},{1... | collective-permute-start | bytes 786440 | tf_op jit(solution)/shard_map/ppermute | solution.py:18
  142.2 11.2 %collective-permute-start.29 = (bf16[128,1024]{1,0:T(8,128)(2,1)S(1)}, bf16[128,1024]{1,0:T(8,128)(2,1)S(1)}, u32[]{:S(2)}, u32[]{:S(2)}) collective-permute-start(bf16[128,1024]{1,0:T(8,128)(2,1)S(1)} %dynamic-slice_convert_fusion.5), channel_id=1, source_target_pairs={{0,8},{4,12},{8,0},{12,4},{1,9},{5,13},{9,1},{13,5},{2,10},{6,14},... | collective-permute-start | bytes 786440 | tf_op jit(solution)/shard_map/ppermute | solution.py:18
  147.8 7.3 %collective-permute-start.33 = (bf16[128,1024]{1,0:T(8,128)(2,1)S(1)}, bf16[128,1024]{1,0:T(8,128)(2,1)S(1)}, u32[]{:S(2)}, u32[]{:S(2)}) collective-permute-start(bf16[128,1024]{1,0:T(8,128)(2,1)S(1)} %dynamic-slice_convert_fusion.4), channel_id=1, source_target_pairs={{0,4},{4,0},{8,12},{12,8},{1,5},{5,1},{9,13},{13,9},{2,6},{6,2},{1... | collective-permute-start | bytes 786440 | tf_op jit(solution)/shard_map/ppermute | solution.py:18
  148.4 10.6 %collective-permute-start.19 = (bf16[128,1024]{1,0:T(8,128)(2,1)S(1)}, bf16[128,1024]{1,0:T(8,128)(2,1)S(1)}, u32[]{:S(2)}, u32[]{:S(2)}) collective-permute-start(bf16[128,1024]{1,0:T(8,128)(2,1)S(1)} %add_convert_fusion.3), channel_id=1, source_target_pairs={{0,8},{4,12},{8,0},{12,4},{1,9},{5,13},{9,1},{13,5},{2,10},{6,14},... | collective-permute-start | bytes 786440 | tf_op jit(solution)/shard_map/ppermute | solution.py:18
  153.4 7.3 %collective-permute-start.23 = (bf16[128,1024]{1,0:T(8,128)(2,1)S(1)}, bf16[128,1024]{1,0:T(8,128)(2,1)S(1)}, u32[]{:S(2)}, u32[]{:S(2)}) collective-permute-start(bf16[128,1024]{1,0:T(8,128)(2,1)S(1)} %add_convert_fusion.2), channel_id=1, source_target_pairs={{0,4},{4,0},{8,12},{12,8},{1,5},{5,1},{9,13},{13,9},{2,6},{6,2},{1... | collective-permute-start | bytes 786440 | tf_op jit(solution)/shard_map/ppermute | solution.py:18
  155.0 8.1 %collective-permute-start.30 = (bf16[128,1024]{1,0:T(8,128)(2,1)S(1)}, bf16[128,1024]{1,0:T(8,128)(2,1)S(1)}, u32[]{:S(2)}, u32[]{:S(2)}) collective-permute-start(bf16[128,1024]{1,0:T(8,128)(2,1)S(1)} %add_convert_fusion.1), channel_id=1, source_target_pairs={{0,8},{4,12},{8,0},{12,4},{1,9},{5,13},{9,1},{13,5},{2,10},{6,14},... | collective-permute-start | bytes 786440 | tf_op jit(solution)/shard_map/ppermute | solution.py:18
  159.0 9.2 %collective-permute-start.34 = (bf16[128,1024]{1,0:T(8,128)(2,1)S(1)}, bf16[128,1024]{1,0:T(8,128)(2,1)S(1)}, u32[]{:S(2)}, u32[]{:S(2)}) collective-permute-start(bf16[128,1024]{1,0:T(8,128)(2,1)S(1)} %add_convert_fusion), channel_id=1, source_target_pairs={{0,4},{4,0},{8,12},{12,8},{1,5},{5,1},{9,13},{13,9},{2,6},{6,2},{1... | collective-permute-start | bytes 786440 | tf_op jit(solution)/shard_map/ppermute | solution.py:18
  160.7 18.8 %collective-permute-start.20 = (bf16[256,1024]{1,0:T(8,128)(2,1)S(1)}, bf16[256,1024]{1,0:T(8,128)(2,1)S(1)}, u32[]{:S(2)}, u32[]{:S(2)}) collective-permute-start(bf16[256,1024]{1,0:T(8,128)(2,1)S(1)} %pad_maximum_fusion.1), channel_id=1, source_target_pairs={{0,4},{4,0},{8,12},{12,8},{1,5},{5,1},{9,13},{13,9},{2,6},{6,2},{1... | collective-permute-start | bytes 1572872 | tf_op jit(solution)/shard_map/ppermute | solution.py:18
  163.2 16.7 %collective-permute-start.24 = (bf16[256,1024]{1,0:T(8,128)(2,1)S(1)}, bf16[256,1024]{1,0:T(8,128)(2,1)S(1)}, u32[]{:S(2)}, u32[]{:S(2)}) collective-permute-start(bf16[256,1024]{1,0:T(8,128)(2,1)S(1)} %pad_maximum_fusion.2), channel_id=1, source_target_pairs={{0,8},{4,12},{8,0},{12,4},{1,9},{5,13},{9,1},{13,5},{2,10},{6,14},... | collective-permute-start | bytes 1572872 | tf_op jit(solution)/shard_map/ppermute | solution.py:18
  168.3 19.6 %collective-permute-start.31 = (bf16[256,1024]{1,0:T(8,128)(2,1)S(1)}, bf16[256,1024]{1,0:T(8,128)(2,1)S(1)}, u32[]{:S(2)}, u32[]{:S(2)}) collective-permute-start(bf16[256,1024]{1,0:T(8,128)(2,1)S(1)} %pad_maximum_fusion.3), channel_id=1, source_target_pairs={{0,4},{4,0},{8,12},{12,8},{1,5},{5,1},{9,13},{13,9},{2,6},{6,2},{1... | collective-permute-start | bytes 1572872 | tf_op jit(solution)/shard_map/ppermute | solution.py:18
  168.9 19.4 %collective-permute-start.35 = (bf16[256,1024]{1,0:T(8,128)(2,1)S(1)}, bf16[256,1024]{1,0:T(8,128)(2,1)S(1)}, u32[]{:S(2)}, u32[]{:S(2)}) collective-permute-start(bf16[256,1024]{1,0:T(8,128)(2,1)S(1)} %pad_maximum_fusion.4), channel_id=1, source_target_pairs={{0,8},{4,12},{8,0},{12,4},{1,9},{5,13},{9,1},{13,5},{2,10},{6,14},... | collective-permute-start | bytes 1572872 | tf_op jit(solution)/shard_map/ppermute | solution.py:18
  188.1 2.2 %copy-start.3 = (bf16[1,2048,1024]{2,1,0:T(8,128)(2,1)S(1)}, bf16[1,2048,1024]{2,1,0:T(8,128)(2,1)}, u32[]{:S(2)}) copy-start(bf16[1,2048,1024]{2,1,0:T(8,128)(2,1)} %param.7) | copy-start | bytes 12582916

commit v2 on v1

v2 whole, which is shorter than its diff:
```python
import jax
import jax.numpy as jnp
from jax import lax
from jax.experimental import pallas as pl
from jax.experimental.pallas import tpu as pltpu
from jax.sharding import PartitionSpec as P

norm_eps = 1e-05
bf16 = jnp.bfloat16
f32 = jnp.float32
MIB = 1 << 20
SMEM_ARG = pl.BlockSpec(memory_space=pltpu.SMEM)
VMEM_ARG = pl.BlockSpec(memory_space=pltpu.VMEM)


def cyclic(value, axis, steps):
    count = lax.axis_size(axis)
    return lax.ppermute(value, axis, [(i, (i + steps) % count) for i in range(count)])


def flipped(value, axis, bit):
    count = lax.axis_size(axis)
    return lax.ppermute(value, axis, [(i, i ^ (1 << bit)) for i in range(count)])


def after(value, *others):
    return lax.optimization_barrier((value, *others))[0]


def params(mib):
    return pltpu.CompilerParams(vmem_limit_bytes=mib * MIB)


def cost(flops, bytes_accessed):
    return pl.CostEstimate(flops=int(flops), bytes_accessed=int(bytes_accessed), transcendentals=0)


def line_gather(value, axis):
    count = lax.axis_size(axis)
    me = lax.axis_index(axis)
    right, left = [value], [value]
    for k in range(1, count):
        right.append(lax.ppermute(right[-1], axis, [(i, i + 1) for i in range(k - 1, count - 1)]))
        left.append(lax.ppermute(left[-1], axis, [(i, i - 1) for i in range(1, count - k + 1)]))
    return [value] + [jnp.where(me >= j, right[j], left[count - j]) for j in range(1, count)]


def mask_of(pos, order):
    bits = len(order)
    return sum(((pos >> (bits - 1 - i)) & 1) << order[i] for i in range(bits))


def scaled_blocks(x, me, groups, chunks):
    tokens, width = x.shape
    chunk = width // groups // chunks
    step = 16

    def kernel(me_ref, x_ref, *out_refs):
        start = me_ref[0]

        @pl.loop(0, tokens, step=step)
        def _(row):
            rows = pl.ds(pl.multiple_of(row, step), step)
            total = jnp.zeros((step, 128), f32)
            span = 1024 if width % 1024 == 0 else 128
            for c in range(0, width, span):
                v = x_ref[rows, c : c + span].astype(f32)
                v = v * v
                for k in range(0, span, 128):
                    total = total + v[:, k : k + 128]
            scale = lax.rsqrt(jnp.sum(total, axis=1, keepdims=True) / width + norm_eps)
            for c in range(chunks):
                for j in range(groups):
                    at = lax.rem(start + j, groups) * (chunk * chunks) + c * chunk
                    v = x_ref[rows, pl.ds(pl.multiple_of(at, chunk), chunk)].astype(f32)
                    out_refs[c * groups + j][rows, :] = (v * scale).astype(bf16)

    outs = pl.pallas_call(
        kernel,
        out_shape=[jax.ShapeDtypeStruct((tokens, chunk), bf16)] * (chunks * groups),
        in_specs=[SMEM_ARG, VMEM_ARG],
        out_specs=[VMEM_ARG] * (chunks * groups),
        compiler_params=params(24),
        cost_estimate=cost(6 * x.size, 4 * x.size),
        name="scaled_blocks",
    )(me, x)
    return [list(outs[c * groups : (c + 1) * groups]) for c in range(chunks)]


def weight_product(blocks, slots, rep, reps, orders):
    groups = len(blocks)
    tokens, chunk = blocks[0].shape
    features = slots[0].shape[1]
    part = chunk // len(orders)
    piece = part // reps
    half = part // 2
    tile = min(part, 256)

    def kernel(rep_ref, *refs):
        block_refs, slot_refs = refs[:groups], refs[groups : 2 * groups]
        out_refs, total = refs[2 * groups : -1], refs[-1]
        values = jnp.concatenate([s[...] for s in slot_refs], axis=0)
        for p, order in enumerate(orders):
            for t in range(0, part, tile):
                at = p * part + t
                columns = jnp.concatenate([b[:, at : at + tile] for b in block_refs], axis=0)
                total[t : t + tile, :] = lax.dot_general(
                    columns, values, (((0,), (0,)), ((), ())), preferred_element_type=f32
                )
            for pos in range(reps):
                owner = rep_ref[0] ^ mask_of(pos, order)
                rows = total[pl.ds(pl.multiple_of(owner * piece, piece), piece), :]
                if pos < reps // 2:
                    out_refs[2 * p][pos * piece : (pos + 1) * piece, :] = rows
                else:
                    at = (pos - reps // 2) * piece
                    out_refs[2 * p + 1][at : at + piece, :] = rows.astype(bf16)

    shapes = []
    for _ in orders:
        shapes += [jax.ShapeDtypeStruct((half, features), f32), jax.ShapeDtypeStruct((half, features), bf16)]
    return pl.pallas_call(
        kernel,
        out_shape=shapes,
        in_specs=[SMEM_ARG] + [VMEM_ARG] * (2 * groups),
        out_specs=[VMEM_ARG] * len(shapes),
        scratch_shapes=[pltpu.VMEM((part, features), f32)],
        compiler_params=params(32),
        cost_estimate=cost(2 * groups * tokens * chunk * features, 2 * groups * tokens * (chunk + features) + 3 * chunk * features),
        name="weight_product",
    )(rep, *blocks, *slots)


def returned_blocks(slots, weight, gain, micro):
    groups = len(slots)
    tokens, features = slots[0].shape
    rows = tokens // micro
    shard = weight.shape[0]
    tile = min(shard, 512)

    def kernel(*refs):
        slot_refs, weight_ref, gain_ref = refs[:groups], refs[groups], refs[groups + 1]
        out_refs = refs[groups + 2 :]
        factor = gain_ref[...].astype(f32)
        pair = 2 if groups % 2 == 0 else 1
        for j in range(0, groups, pair):
            values = jnp.concatenate([slot_refs[j + i][...] for i in range(pair)], axis=0)
            back = lax.dot_general(values, weight_ref[...], (((1,), (1,)), ((), ())), preferred_element_type=f32)
            back = (back * factor).astype(bf16)
            for i in range(pair):
                for m in range(micro):
                    at = i * tokens + m * rows
                    out_refs[(j + i) * micro + m][...] = back[at : at + rows, :]

    outs = pl.pallas_call(
        kernel,
        grid=(shard // tile,),
        out_shape=[jax.ShapeDtypeStruct((rows, shard), bf16)] * (groups * micro),
        in_specs=[pl.BlockSpec((tokens, features), lambda i: (0, 0))] * groups
        + [pl.BlockSpec((tile, features), lambda i: (i, 0)), pl.BlockSpec((1, tile), lambda i: (0, i))],
        out_specs=[pl.BlockSpec((rows, tile), lambda i: (0, i))] * (groups * micro),
        compiler_params=params(32),
        cost_estimate=cost(2 * groups * tokens * shard * features, 2 * groups * tokens * (shard + features) + 2 * shard * features),
        name="returned_blocks",
    )(*slots, weight, gain)
    return [list(outs[j * micro : (j + 1) * micro]) for j in range(groups)]


def row_gradient(x, top, blocks, me, m):
    groups = len(blocks)
    rows, shard = blocks[0].shape
    width = shard * groups
    step = 16

    def kernel(me_ref, x_ref, top_ref, *refs):
        block_refs, upper_ref, piece_ref = refs[:groups], refs[groups], refs[groups + 1]
        squares = jnp.zeros((step, 128), f32)
        dots = jnp.zeros((step, 128), f32)
        starts = [pl.multiple_of(lax.rem(me_ref[0] + j, groups) * shard, shard) for j in range(groups)]
        span = min(shard, 512)
        for j in range(groups):
            for c in range(0, shard, span):
                v = x_ref[0, 0, :, pl.ds(pl.multiple_of(starts[j] + c, span), span)].astype(f32)
                d = block_refs[j][:, c : c + span].astype(f32) * v
                v = v * v
                for k in range(0, span, 128):
                    squares = squares + v[:, k : k + 128]
                    dots = dots + d[:, k : k + 128]
        scale = lax.rsqrt(jnp.sum(squares, axis=1, keepdims=True) / width + norm_eps)
        mean = jnp.sum(dots, axis=1, keepdims=True) * scale / width
        slope = scale * mean
        for j in range(groups):
            for c in range(0, shard, span):
                at = pl.ds(pl.multiple_of(starts[j] + c, span), span)
                v = x_ref[0, 0, :, at].astype(f32)
                piece = (scale * (block_refs[j][:, c : c + span].astype(f32) - v * slope)).astype(bf16)
                piece_ref[:, at] = piece
                upper_ref[:, at] = (top_ref[0, :, at].astype(f32) + piece.astype(f32)).astype(bf16)

    return pl.pallas_call(
        kernel,
        grid=(rows // step,),
        out_shape=[jax.ShapeDtypeStruct((rows, width), bf16)] * 2,
        in_specs=[
            SMEM_ARG,
            pl.BlockSpec((1, 1, step, width), lambda i: (0, m, i, 0)),
            pl.BlockSpec((1, step, width), lambda i: (m, i, 0)),
        ]
        + [pl.BlockSpec((step, shard), lambda i: (i, 0))] * groups,
        out_specs=[pl.BlockSpec((step, width), lambda i: (i, 0))] * 2,
        compiler_params=params(24),
        cost_estimate=cost(12 * rows * width, 10 * rows * width),
        name="row_gradient",
    )(me, x, top, *blocks)


def finished_chunk(parts, orders, rep, reps, weight, factor, c, earlier):
    shard, features = weight.shape
    half_rows = parts[0][0].shape[0]
    piece = half_rows * 2 // reps
    count = len(parts)
    base = c * count * reps
    half = reps // 2
    steps = count * reps

    def owner(i, rep_ref):
        at = i * 0 + base
        for p, order in enumerate(orders):
            bits = len(order)
            pos = i - p * reps
            mask = sum(((pos >> (bits - 1 - b)) & 1) << order[b] for b in range(bits))
            inside = (i >= p * reps) & (i < (p + 1) * reps)
            at = at + jnp.where(inside, p * reps + (rep_ref[0] ^ mask), 0)
        return (at, 0)

    def kernel(rep_ref, *refs):
        part_refs = refs[: 2 * count]
        weight_ref, factor_ref = refs[2 * count], refs[2 * count + 1]
        grad_ref, gain_ref = refs[-2], refs[-1]
        i = pl.program_id(0)
        for k in range(2 * count):

            @pl.when((i >= k * half) & (i < (k + 1) * half))
            def _():
                raw = part_refs[k][...].astype(f32)
                grad_ref[...] = raw * factor_ref[:, 0:1]
                gain_ref[...] = jnp.sum(raw * weight_ref[...].astype(f32), axis=1, keepdims=True) * factor_ref[:, 1:2]

    def held(k):
        return lambda i, rep_ref: (jnp.clip(i - k * half, 0, half - 1), 0)

    operands = [a for pair in parts for a in pair]
    in_specs = [pl.BlockSpec((piece, features), held(k)) for k in range(2 * count)]
    in_specs += [pl.BlockSpec((piece, features), owner), pl.BlockSpec((piece, 2), owner)]
    aliases = {}
    extra = []
    if earlier is not None:
        extra = list(earlier)
        in_specs += [pl.BlockSpec(memory_space=pl.ANY)] * 2
        aliases = {1 + len(operands) + 2: 0, 1 + len(operands) + 3: 1}
    return pl.pallas_call(
        kernel,
        grid_spec=pltpu.PrefetchScalarGridSpec(
            num_scalar_prefetch=1,
            grid=(steps,),
            in_specs=in_specs,
            out_specs=[pl.BlockSpec((piece, features), owner), pl.BlockSpec((piece, 1), owner)],
        ),
        out_shape=[jax.ShapeDtypeStruct((shard, features), f32), jax.ShapeDtypeStruct((shard, 1), f32)],
        input_output_aliases=aliases,
        compiler_params=params(24),
        cost_estimate=cost(4 * piece * steps * features, 8 * piece * steps * features),
        name="finished_chunk",
    )(rep, *operands, weight, factor, *extra)


def local(layer_input, value_grad, value_weight, norm_gain, top_grad):
    groups = lax.axis_size("fsdp")
    reps = lax.axis_size("rep")
    bits = reps.bit_length() - 1
    me = lax.axis_index("fsdp").astype(jnp.int32)[None]
    rep = lax.axis_index("rep").astype(jnp.int32)[None]
    _, micro, rows, width = layer_input.shape
    tokens = micro * rows
    shard = width // groups
    norm_scale = float(tokens * reps * groups) ** (-0.5)
    chunks = 2
    orders = [tuple(range(bits)), tuple(reversed(range(bits)))]

    weight = value_weight[0]
    grads = value_grad[0].reshape(tokens, -1)
    gain = norm_gain[0].astype(f32) * norm_scale
    factor = jnp.stack([gain, jnp.full_like(gain, norm_scale)], axis=1)

    slots = line_gather(grads, "fsdp")
    hats = scaled_blocks(layer_input[0].reshape(tokens, width), me, groups, chunks)
    columns = []
    for c in range(chunks):
        sent = hats[c] if c == 0 else [after(h, *slots[1:]) for h in hats[c]]
        columns.append([sent[j] if j == 0 else cyclic(sent[j], "fsdp", j) for j in range(groups)])

    back = returned_blocks(slots, weight, norm_gain, micro)
    returned = []
    for m in range(micro):
        line = []
        for j in range(groups):
            block = back[j][m]
            if j:
                block = after(block, columns[-1][j] if m == 0 else returned[-1][1])
                block = cyclic(block, "fsdp", -j)
            line.append(block)
        returned.append(line)

    finished = None
    for c in range(chunks):
        product = weight_product(columns[c], slots, rep, reps, orders)
        kept = [product[2 * p] for p in range(len(orders))]
        sent = [product[2 * p + 1] for p in range(len(orders))]
        for b in range(bits):
            for p, order in enumerate(orders):
                other = flipped(sent[p], "rep", order[b])
                total = kept[p] + other.astype(f32)
                if b + 1 < bits:
                    half = total.shape[0] // 2
                    kept[p], sent[p] = total[:half], total[half:].astype(bf16)
                else:
                    kept[p] = total.astype(bf16)
        for b in reversed(range(bits)):
            for p, order in enumerate(orders):
                other = flipped(kept[p], "rep", order[b])
                kept[p] = jnp.concatenate([kept[p], other], axis=0) if b else (kept[p], other)
        finished = finished_chunk(kept, orders, rep, reps, weight, factor, c, finished)
    weight_grad, gain_grad = finished

    results = []
    is_upper = lax.axis_index("section") == 1
    for m in range(micro):
        upper, piece = row_gradient(layer_input, top_grad, returned[m], me, m)
        passed = lax.ppermute(upper, "section", [(1, 0)])
        lower = (passed.astype(f32) + piece.astype(f32)).astype(bf16)
        results.append(jnp.where(is_upper, upper, lower))
    return (jnp.stack(results)[None], weight_grad[None], gain_grad[:, 0][None])


def solution(mesh):
    return jax.shard_map(
        local,
        mesh=mesh,
        in_specs=(
            P("section", None, ("rep", "fsdp"), None),
            P("section", None, ("rep", "fsdp"), None),
            P("section", "fsdp", None),
            P("section", "fsdp"),
            P(None, ("rep", "fsdp"), None),
        ),
        out_specs=(
            P("section", None, ("rep", "fsdp"), None),
            P("section", "fsdp", None),
            P("section", "fsdp"),
        ),
        check_vma=False,
    )
```

time: 198 us -> 185 us (0.934); the launches traced: 198 us -> 182 us
  waiting for transfers between devices: 104 us -> 81.6 us
  Pallas kernels: 0 us -> 22.3 us
  other arithmetic: 24.1 us -> 7.77 us
  matrix products: 9.16 us -> 0 us
  local copies, waits for them, and re-layouts: 7.16 us -> 13.9 us
  starting transfers between devices: 52.2 us -> 55 us
    pallas_call x0 -> x8, Pallas kernels: none -> 22.3 us  [the longest x2 8.8 us: finished_chunk(): pl.pallas_call(kernel, grid_spec=pltpu.PrefetchScalarGridSpec(num_scalar_...]
    ppermute x16, waiting for transfers between devices: 35.8 us -> 20.9 us  [flipped(): return lax.ppermute(value, axis, [(i, i ^ 1 << bit) for i in range(count)])]
    dot_general x3 -> x0, matrix products: 9.16 us -> none  [the longest x1 4.59 us: local(): lax.dot_general(grads_all, weight, (((1,), (1,)), ((), ())), preferred_el...]
    unnamed x12 -> x38, local copies, waits for them, and re-layouts: 2.39 us -> 11.1 us
    ppermute x3, waiting for transfers between devices: 25.9 us -> 19.1 us  [line_gather(): lax.ppermute(left[-1], axis, [(i, i - 1) for i in range(1, count - k + 1)])]
    convert_element_type x7 -> x4, other arithmetic: 5.83 us -> 0.21 us  [local(): kept[p] = total.astype(bf16)]
    ppermute x12, starting transfers between devices: 18.4 us -> 23.4 us  [cyclic(): lax.ppermute(value, axis, [(i, (i + steps) % count) for i in range(count)])]
    ppermute x12, waiting for transfers between devices: 42 us -> 37.1 us  [cyclic(): lax.ppermute(value, axis, [(i, (i + steps) % count) for i in range(count)])]
  transfers between devices with their start and end apart: 36 -> 36, of which waited for: 16 -> 15; matrix products, arithmetic and copies ran while one was open for 15% -> 4% of each run, Pallas kernels for 0% -> 11%
where the time goes in v2:
time: 185 us; the launch traced here: 182 us
  waiting for transfers between devices  81.6 us (44%)
  starting transfers between devices  55 us (30%)
  Pallas kernels  22.3 us (12%)
  local copies, waits for them, and re-layouts  13.9 us (8%)
  other arithmetic  7.77 us (4%)
    ppermute x12, waiting for transfers between devices, cyclic(): lax.ppermute(value, axis, [(i, (i + steps) % count) for i in range(count)])  37.1 us
    ppermute x12, starting transfers between devices, cyclic(): lax.ppermute(value, axis, [(i, (i + steps) % count) for i in range(count)])  23.4 us
    ppermute x16, waiting for transfers between devices, flipped(): return lax.ppermute(value, axis, [(i, i ^ 1 << bit) for i in range(count)])  20.9 us
    ppermute x3, waiting for transfers between devices, line_gather(): lax.ppermute(left[-1], axis, [(i, i - 1) for i in range(1, count - k + 1)])  19.1 us
    ppermute x16, starting transfers between devices, flipped(): return lax.ppermute(value, axis, [(i, i ^ 1 << bit) for i in range(count)])  18.7 us
    unnamed x38, local copies, waits for them, and re-layouts  11.1 us
    pallas_call x2, Pallas kernels, finished_chunk(): pl.pallas_call(kernel, grid_spec=pltpu.PrefetchScalarGridSpec(num_scalar_...  8.8 us
    ppermute x3, starting transfers between devices, line_gather(): lax.ppermute(right[-1], axis, [(i, i + 1) for i in range(k - 1, count - 1)])  6.29 us
  transfers between devices with their start and end apart: 36, of which 15 were waited for; matrix products, arithmetic and copies ran while one was open for 4% of the time, Pallas kernels for 11%

profile of v2, /device:TPU:0, one launch (start us, length us, event | category | flops | bytes accessed | tf_op | source)
XLA Modules:
  0.0 181.8 jit_solution(11151277062554017465)
XLA Ops:
  0.6 4.9 %collective-permute-start = (bf16[128,1024]{1,0:T(8,128)(2,1)}, bf16[128,1024]{1,0:T(8,128)(2,1)S(1)}, u32[]{:S(2)}, u32[]{:S(2)}) collective-permute-start(bf16[128,1024]{1,0:T(8,128)(2,1)} %bitcast.19), channel_id=1, source_target_pairs={{0,1},{1,2},{2,3},{4,5},{5,6},{6,7},{8,9},{9,10},{10,11},{12,13},{... | collective-permute-start | bytes 786440 | tf_op jit(solution)/shard_map/ppermute | solution.py:43
  6.9 4.5 %collective-permute-done = bf16[128,1024]{1,0:T(8,128)(2,1)S(1)} collective-permute-done((bf16[128,1024]{1,0:T(8,128)(2,1)}, bf16[128,1024]{1,0:T(8,128)(2,1)S(1)}, u32[]{:S(2)}, u32[]{:S(2)}) %collective-permute-start) | collective-permute-done | bytes 262176 | tf_op jit(solution)/shard_map/ppermute | solution.py:43
  12.1 3.4 %collective-permute-done.1 = bf16[128,1024]{1,0:T(8,128)(2,1)S(1)} collective-permute-done((bf16[128,1024]{1,0:T(8,128)(2,1)}, bf16[128,1024]{1,0:T(8,128)(2,1)S(1)}, u32[]{:S(2)}, u32[]{:S(2)}) %collective-permute-start.1) | collective-permute-done | bytes 262176 | tf_op jit(solution)/shard_map/ppermute | solution.py:44
  17.5 1.6 copy-done
  19.0 2.5 %scaled_blocks.1 = (bf16[128,1024]{1,0:T(8,128)(2,1)S(1)}, bf16[128,1024]{1,0:T(8,128)(2,1)S(1)}, bf16[128,1024]{1,0:T(8,128)(2,1)S(1)}, bf16[128,1024]{1,0:T(8,...) custom-call(s32[1]{0:T(128)} %bitcast.me_ref, ...), custom_call_target="tpu_custom_call" | custom-call | flops 6291456 | bytes 4194304 | tf_op jit(solution)/shard_map/scaled_blocks/pallas_call | solution.py:78
  22.9 5.2 %collective-permute-start.25 = (bf16[128,1024]{1,0:T(8,128)(2,1)S(1)}, bf16[128,1024]{1,0:T(8,128)(2,1)S(1)}, u32[]{:S(2)}, u32[]{:S(2)}) collective-permute-start(bf16[128,1024]{1,0:T(8,128)(2,1)S(1)} %get-tuple-element.76), channel_id=1, source_target_pairs={{0,1},{1,2},{2,3},{3,0},{4,5},{5,6},{6,7},{7,4},{8,9},{9,10},{10,1... | collective-permute-start | bytes 786440 | tf_op jit(solution)/shard_map/ppermute | solution.py:18
  28.1 4.7 %collective-permute-start.26 = (bf16[128,1024]{1,0:T(8,128)(2,1)S(1)}, bf16[128,1024]{1,0:T(8,128)(2,1)S(1)}, u32[]{:S(2)}, u32[]{:S(2)}) collective-permute-start(bf16[128,1024]{1,0:T(8,128)(2,1)S(1)} %get-tuple-element.77), channel_id=1, source_target_pairs={{0,2},{1,3},{2,0},{3,1},{4,6},{5,7},{6,4},{7,5},{8,10},{9,11},{10,... | collective-permute-start | bytes 786440 | tf_op jit(solution)/shard_map/ppermute | solution.py:18
  32.8 2.9 %collective-permute-start.27 = (bf16[128,1024]{1,0:T(8,128)(2,1)S(1)}, bf16[128,1024]{1,0:T(8,128)(2,1)S(1)}, u32[]{:S(2)}, u32[]{:S(2)}) collective-permute-start(bf16[128,1024]{1,0:T(8,128)(2,1)S(1)} %get-tuple-element.78), channel_id=1, source_target_pairs={{0,3},{1,0},{2,1},{3,2},{4,7},{5,4},{6,5},{7,6},{8,11},{9,8},{10,9... | collective-permute-start | bytes 786440 | tf_op jit(solution)/shard_map/ppermute | solution.py:18
  35.7 1.4 collective-permute-start.3
  37.2 15.7 %collective-permute-done.3 = bf16[128,1024]{1,0:T(8,128)(2,1)S(1)} collective-permute-done((bf16[128,1024]{1,0:T(8,128)(2,1)S(1)}, bf16[128,1024]{1,0:T(8,128)(2,1)S(1)}, u32[]{:S(2)}, u32[]{:S(2)}) %collective-permute-start.3) | collective-permute-done | bytes 262176 | tf_op jit(solution)/shard_map/ppermute | solution.py:44
  59.0 2.3 %weight_product.3 = (f32[256,1024]{1,0:T(8,128)S(1)}, bf16[256,1024]{1,0:T(8,128)(2,1)S(1)}, f32[256,1024]{1,0:T(8,128)S(1)}, bf16[256,1024]{1,0:T(8,128)(2,1)}) custom-call(s32[1]{0:T(128)} %bitcast.7.rep_ref, bf16[128,1024]{1,0:T(8,128)(2,1)S(1)} %copy-done.11, bf16[128,1024]{1,0:T(8,128)(2,1)S(1)} %copy-done.13, bf16[128,1024]{1,0:T(8,128)(2,1)S(1)} %copy-done.15, ...), custom_call_target="tpu_custom_call" | custom-call | flops 1073741824 | bytes 5242880 | tf_op jit(solution)/shard_map/weight_product/pallas_call | solution.py:122
  61.3 1.5 collective-permute-start.32
  62.8 2.8 %collective-permute-start.10 = (bf16[128,1024]{1,0:T(8,128)(2,1)}, bf16[128,1024]{1,0:T(8,128)(2,1)}, u32[]{:S(2)}, u32[]{:S(2)}) collective-permute-start(bf16[128,1024]{1,0:T(8,128)(2,1)} %get-tuple-element.56), channel_id=1, source_target_pairs={{0,3},{1,0},{2,1},{3,2},{4,7},{5,4},{6,5},{7,6},{8,11},{9,8},{10,9... | collective-permute-start | bytes 786440 | tf_op jit(solution)/shard_map/ppermute | solution.py:18
  66.2 1.3 copy.10
  67.5 1.3 stack.16.refs_5_
  68.9 1.6 collective-permute-start.28
  70.4 2.2 %copy-done.2 = bf16[1,2048,1024]{2,1,0:T(8,128)(2,1)S(1)} copy-done((bf16[1,2048,1024]{2,1,0:T(8,128)(2,1)S(1)}, bf16[1,2048,1024]{2,1,0:T(8,128)(2,1)}, u32[]{:S(2)}) %copy-start.2) | copy-done | bytes 4194328
  72.6 3.2 %returned_blocks.1 = (bf16[64,2048]{1,0:T(8,128)(2,1)S(1)}, bf16[64,2048]{1,0:T(8,128)(2,1)S(1)}, bf16[64,2048]{1,0:T(8,128)(2,1)S(1)}, bf16[64,2048]{1,0:T(8,12...) custom-call(bf16[128,1024]{1,0:T(8,128)(2,1)S(1)} %bitcast.22, ...), custom_call_target="tpu_custom_call" | custom-call | flops 2147483648 | bytes 7340032 | tf_op jit(solution)/shard_map/returned_blocks/pallas_call | solution.py:155
  75.8 2.7 %collective-permute-done.6.refs_1_ = bf16[128,1024]{1,0:T(8,128)(2,1)} collective-permute-done((bf16[128,1024]{1,0:T(8,128)(2,1)}, bf16[128,1024]{1,0:T(8,128)(2,1)}, u32[]{:S(2)}, u32[]{:S(2)}) %collective-permute-start.6) | collective-permute-done | bytes 262176 | tf_op jit(solution)/shard_map/ppermute | solution.py:18
  78.5 7.9 %collective-permute-done.8.refs_2_ = bf16[128,1024]{1,0:T(8,128)(2,1)} collective-permute-done((bf16[128,1024]{1,0:T(8,128)(2,1)}, bf16[128,1024]{1,0:T(8,128)(2,1)}, u32[]{:S(2)}, u32[]{:S(2)}) %collective-permute-start.8) | collective-permute-done | bytes 262176 | tf_op jit(solution)/shard_map/ppermute | solution.py:18
  86.5 2.6 %weight_product.2 = (f32[256,1024]{1,0:T(8,128)S(1)}, bf16[256,1024]{1,0:T(8,128)(2,1)S(1)}, f32[256,1024]{1,0:T(8,128)S(1)}, bf16[256,1024]{1,0:T(8,128)(2,1)S(1)}) custom-call(s32[1]{0:T(128)} %bitcast.7.rep_ref, bf16[128,1024]{1,0:T(8,128)(2,1)S(1)} %copy-done.9, bf16[128,1024]{1,0:T(8,128)(2,1)} %collective-permute-done.6.refs_1_, ...), custom_call_target="tpu_custom_call" | custom-call | flops 1073741824 | bytes 5242880 | tf_op jit(solution)/shard_map/weight_product/pallas_call | solution.py:122
  89.7 1.5 collective-permute-start.17
  91.2 2.6 %collective-permute-start.7 = (bf16[64,2048]{1,0:T(8,128)(2,1)S(1)}, bf16[64,2048]{1,0:T(8,128)(2,1)S(1)}, u32[]{:S(2)}, u32[]{:S(2)}) collective-permute-start(bf16[64,2048]{1,0:T(8,128)(2,1)S(1)} %get-tuple-element.49), channel_id=1, source_target_pairs={{0,3},{1,0},{2,1},{3,2},{4,7},{5,4},{6,5},{7,6},{8,11},{9,8},{10,9... | collective-permute-start | bytes 786440 | tf_op jit(solution)/shard_map/ppermute | solution.py:18
  96.0 7.0 %collective-permute-done.7.refs_1_ = bf16[64,2048]{1,0:T(8,128)(2,1)S(1)} collective-permute-done((bf16[64,2048]{1,0:T(8,128)(2,1)S(1)}, bf16[64,2048]{1,0:T(8,128)(2,1)S(1)}, u32[]{:S(2)}, u32[]{:S(2)}) %collective-permute-start.7) | collective-permute-done | bytes 262176 | tf_op jit(solution)/shard_map/ppermute | solution.py:18
  103.6 2.8 %collective-permute-done.11.refs_3_ = bf16[64,2048]{1,0:T(8,128)(2,1)S(1)} collective-permute-done((bf16[64,2048]{1,0:T(8,128)(2,1)S(1)}, bf16[64,2048]{1,0:T(8,128)(2,1)S(1)}, u32[]{:S(2)}, u32[]{:S(2)}) %collective-permute-start.11) | collective-permute-done | bytes 262176 | tf_op jit(solution)/shard_map/ppermute | solution.py:18
  106.4 1.5 collective-permute-start.29
  107.9 5.8 %collective-permute-done.9.refs_2_ = bf16[64,2048]{1,0:T(8,128)(2,1)S(1)} collective-permute-done((bf16[64,2048]{1,0:T(8,128)(2,1)S(1)}, bf16[64,2048]{1,0:T(8,128)(2,1)S(1)}, u32[]{:S(2)}, u32[]{:S(2)}) %collective-permute-start.9) | collective-permute-done | bytes 262176 | tf_op jit(solution)/shard_map/ppermute | solution.py:18
  113.8 1.5 row_gradient.2
  115.4 3.4 %collective-permute-start.14 = (bf16[64,2048]{1,0:T(8,128)(2,1)S(1)}, bf16[64,2048]{1,0:T(8,128)(2,1)S(1)}, u32[]{:S(2)}, u32[]{:S(2)}) collective-permute-start(bf16[64,2048]{1,0:T(8,128)(2,1)S(1)} %get-tuple-element.64), channel_id=1, source_target_pairs={{0,2},{1,3},{2,0},{3,1},{4,6},{5,7},{6,4},{7,5},{8,10},{9,11},{10,... | collective-permute-start | bytes 786440 | tf_op jit(solution)/shard_map/ppermute | solution.py:18
  121.6 3.2 %collective-permute-done.15.refs_3_ = bf16[64,2048]{1,0:T(8,128)(2,1)S(1)} collective-permute-done((bf16[64,2048]{1,0:T(8,128)(2,1)S(1)}, bf16[64,2048]{1,0:T(8,128)(2,1)S(1)}, u32[]{:S(2)}, u32[]{:S(2)}) %collective-permute-start.15) | collective-permute-done | bytes 262176 | tf_op jit(solution)/shard_map/ppermute | solution.py:18
  124.8 1.5 collective-permute-start.18
  126.4 7.6 %collective-permute-done.14.refs_2_ = bf16[64,2048]{1,0:T(8,128)(2,1)S(1)} collective-permute-done((bf16[64,2048]{1,0:T(8,128)(2,1)S(1)}, bf16[64,2048]{1,0:T(8,128)(2,1)S(1)}, u32[]{:S(2)}, u32[]{:S(2)}) %collective-permute-start.14) | collective-permute-done | bytes 262176 | tf_op jit(solution)/shard_map/ppermute | solution.py:18
  134.6 1.5 collective-permute-start.30
  136.1 1.5 row_gradient.3
  139.0 1.6 collective-permute-start.23
  140.6 1.6 collective-permute-done.34
  142.2 1.5 collective-permute-start.19
  144.4 2.7 %collective-permute-done.23 = bf16[128,1024]{1,0:T(8,128)(2,1)S(1)} collective-permute-done((bf16[128,1024]{1,0:T(8,128)(2,1)S(1)}, bf16[128,1024]{1,0:T(8,128)(2,1)S(1)}, u32[]{:S(2)}, u32[]{:S(2)}) %collective-permute-start.23) | collective-permute-done | bytes 262176 | tf_op jit(solution)/shard_map/ppermute | solution.py:23
  147.0 1.5 collective-permute-start.31
  148.6 2.7 %collective-permute-done.19 = bf16[128,1024]{1,0:T(8,128)(2,1)S(1)} collective-permute-done((bf16[128,1024]{1,0:T(8,128)(2,1)S(1)}, bf16[128,1024]{1,0:T(8,128)(2,1)S(1)}, u32[]{:S(2)}, u32[]{:S(2)}) %collective-permute-start.19) | collective-permute-done | bytes 262176 | tf_op jit(solution)/shard_map/ppermute | solution.py:23
  151.3 1.6 collective-permute-start.24
  153.6 1.3 fusion.1
  154.9 7.6 %collective-permute-done.35.refs_3_ = bf16[256,1024]{1,0:T(8,128)(2,1)S(1)} collective-permute-done((bf16[256,1024]{1,0:T(8,128)(2,1)S(1)}, bf16[256,1024]{1,0:T(8,128)(2,1)S(1)}, u32[]{:S(2)}, u32[]{:S(2)}) %collective-permute-start.35) | collective-permute-done | bytes 524320 | tf_op jit(solution)/shard_map/ppermute | solution.py:23
  162.5 4.4 %finished_chunk.2 = (f32[2048,1024]{1,0:T(8,128)}, f32[2048,1]{1,0:T(8,128)S(1)}) custom-call(s32[1]{0:T(128)} %bitcast.7.rep_ref, bf16[256,1024]{1,0:T(8,128)(2,1)S(1)} %pad_maximum_fusion.2.refs_0_, bf16[256,1024]{1,0:T(8,128)(2,1)S(1)} %collective-permute-done.31.refs_1_, bf16[256,1024]{1,0:T(8,128)(2,1)S(1)} %pad_maximum_fusion.3.refs_2_, ...), custom_call_target="tpu_custom_call" | custom-call | flops 4194304 | bytes 8388608 | tf_op jit(solution)/shard_map/finished_chunk/pallas_call | solution.py:261
  166.9 6.3 %collective-permute-done.24.refs_3_ = bf16[256,1024]{1,0:T(8,128)(2,1)S(1)} collective-permute-done((bf16[256,1024]{1,0:T(8,128)(2,1)S(1)}, bf16[256,1024]{1,0:T(8,128)(2,1)S(1)}, u32[]{:S(2)}, u32[]{:S(2)}) %collective-permute-start.24) | collective-permute-done | bytes 524320 | tf_op jit(solution)/shard_map/ppermute | solution.py:23
  173.2 4.4 %finished_chunk.3 = (f32[2048,1024]{1,0:T(8,128)}, f32[2048,1]{1,0:T(8,128)S(1)}) custom-call(s32[1]{0:T(128)} %bitcast.7.rep_ref, bf16[256,1024]{1,0:T(8,128)(2,1)S(1)} %pad_maximum_fusion.refs_0_, bf16[256,1024]{1,0:T(8,128)(2,1)S(1)} %collective-permute-done.20.refs_1_, ...), custom_call_target="tpu_custom_call", output_to_operand_aliasing={{0}: (7, {}), {1}: (8, {})} | custom-call | flops 4194304 | bytes 8388608 | tf_op jit(solution)/shard_map/finished_chunk/pallas_call | solution.py:261
  178.6 1.7 fusion.3
  180.3 1.5 maximum_bitcast_fusion
  (96 shorter events, 22.4 us)
Async XLA Ops:
  0.6 10.8 %collective-permute-start = (bf16[128,1024]{1,0:T(8,128)(2,1)}, bf16[128,1024]{1,0:T(8,128)(2,1)S(1)}, u32[]{:S(2)}, u32[]{:S(2)}) collective-permute-start(bf16[128,1024]{1,0:T(8,128)(2,1)} %bitcast.19), channel_id=1, source_target_pairs={{0,1},{1,2},{2,3},{4,5},{5,6},{6,7},{8,9},{9,10},{10,11},{12,13},{... | collective-permute-start | bytes 786440 | tf_op jit(solution)/shard_map/ppermute | solution.py:43
  5.6 9.9 %collective-permute-start.1 = (bf16[128,1024]{1,0:T(8,128)(2,1)}, bf16[128,1024]{1,0:T(8,128)(2,1)S(1)}, u32[]{:S(2)}, u32[]{:S(2)}) collective-permute-start(bf16[128,1024]{1,0:T(8,128)(2,1)} %bitcast.20), channel_id=1, source_target_pairs={{1,0},{2,1},{3,2},{5,4},{6,5},{7,6},{9,8},{10,9},{11,10},{13,12},{... | collective-permute-start | bytes 786440 | tf_op jit(solution)/shard_map/ppermute | solution.py:44
  11.4 5.3 %collective-permute-start.4 = (bf16[128,1024]{1,0:T(8,128)(2,1)S(1)}, bf16[128,1024]{1,0:T(8,128)(2,1)S(1)}, u32[]{:S(2)}, u32[]{:S(2)}) collective-permute-start(bf16[128,1024]{1,0:T(8,128)(2,1)S(1)} %collective-permute-done), channel_id=1, source_target_pairs={{1,2},{2,3},{5,6},{6,7},{9,10},{10,11},{13,14},{14,15},{17,18},{18... | collective-permute-start | bytes 786440 | tf_op jit(solution)/shard_map/ppermute | solution.py:43
  15.5 20.3 %collective-permute-start.2 = (bf16[128,1024]{1,0:T(8,128)(2,1)S(1)}, bf16[128,1024]{1,0:T(8,128)(2,1)S(1)}, u32[]{:S(2)}, u32[]{:S(2)}) collective-permute-start(bf16[128,1024]{1,0:T(8,128)(2,1)S(1)} %collective-permute-done.1), channel_id=1, source_target_pairs={{1,0},{2,1},{5,4},{6,5},{9,8},{10,9},{13,12},{14,13},{17,16},{18,1... | collective-permute-start | bytes 786440 | tf_op jit(solution)/shard_map/ppermute | solution.py:44
  16.8 20.4 %collective-permute-start.5 = (bf16[128,1024]{1,0:T(8,128)(2,1)S(1)}, bf16[128,1024]{1,0:T(8,128)(2,1)S(1)}, u32[]{:S(2)}, u32[]{:S(2)}) collective-permute-start(bf16[128,1024]{1,0:T(8,128)(2,1)S(1)} %collective-permute-done.4), channel_id=1, source_target_pairs={{2,3},{6,7},{10,11},{14,15},{18,19},{22,23},{26,27},{30,31}} | collective-permute-start | bytes 786440 | tf_op jit(solution)/shard_map/ppermute | solution.py:43
  17.4 1.6 copy-start
  22.9 30.2 %collective-permute-start.25 = (bf16[128,1024]{1,0:T(8,128)(2,1)S(1)}, bf16[128,1024]{1,0:T(8,128)(2,1)S(1)}, u32[]{:S(2)}, u32[]{:S(2)}) collective-permute-start(bf16[128,1024]{1,0:T(8,128)(2,1)S(1)} %get-tuple-element.76), channel_id=1, source_target_pairs={{0,1},{1,2},{2,3},{3,0},{4,5},{5,6},{6,7},{7,4},{8,9},{9,10},{10,1... | collective-permute-start | bytes 786440 | tf_op jit(solution)/shard_map/ppermute | solution.py:18
  28.1 25.7 %collective-permute-start.26 = (bf16[128,1024]{1,0:T(8,128)(2,1)S(1)}, bf16[128,1024]{1,0:T(8,128)(2,1)S(1)}, u32[]{:S(2)}, u32[]{:S(2)}) collective-permute-start(bf16[128,1024]{1,0:T(8,128)(2,1)S(1)} %get-tuple-element.77), channel_id=1, source_target_pairs={{0,2},{1,3},{2,0},{3,1},{4,6},{5,7},{6,4},{7,5},{8,10},{9,11},{10,... | collective-permute-start | bytes 786440 | tf_op jit(solution)/shard_map/ppermute | solution.py:18
  32.8 21.7 %collective-permute-start.27 = (bf16[128,1024]{1,0:T(8,128)(2,1)S(1)}, bf16[128,1024]{1,0:T(8,128)(2,1)S(1)}, u32[]{:S(2)}, u32[]{:S(2)}) collective-permute-start(bf16[128,1024]{1,0:T(8,128)(2,1)S(1)} %get-tuple-element.78), channel_id=1, source_target_pairs={{0,3},{1,0},{2,1},{3,2},{4,7},{5,4},{6,5},{7,6},{8,11},{9,8},{10,9... | collective-permute-start | bytes 786440 | tf_op jit(solution)/shard_map/ppermute | solution.py:18
  35.7 19.5 %copy-start.11 = (bf16[128,1024]{1,0:T(8,128)(2,1)S(1)}, bf16[128,1024]{1,0:T(8,128)(2,1)}, u32[]{:S(2)}) copy-start(bf16[128,1024]{1,0:T(8,128)(2,1)} %copy-done.10) | copy-start | bytes 786436
  35.7 17.2 %collective-permute-start.3 = (bf16[128,1024]{1,0:T(8,128)(2,1)S(1)}, bf16[128,1024]{1,0:T(8,128)(2,1)S(1)}, u32[]{:S(2)}, u32[]{:S(2)}) collective-permute-start(bf16[128,1024]{1,0:T(8,128)(2,1)S(1)} %collective-permute-done.2), channel_id=1, source_target_pairs={{1,0},{5,4},{9,8},{13,12},{17,16},{21,20},{25,24},{29,28}} | collective-permute-start | bytes 786440 | tf_op jit(solution)/shard_map/ppermute | solution.py:44
  53.0 13.1 %copy-start.5 = (bf16[1,2048]{1,0:T(2,128)(2,1)S(1)}, bf16[1,2048]{1,0:T(2,128)(2,1)}, u32[]{:S(2)}) copy-start(bf16[1,2048]{1,0:T(2,128)(2,1)} %refs_5_.1) | copy-start | bytes 12292
  55.2 1.0 copy-start.6
  56.1 0.9 copy-start.13
  61.3 32.5 %collective-permute-start.32 = (bf16[256,1024]{1,0:T(8,128)(2,1)}, bf16[256,1024]{1,0:T(8,128)(2,1)}, u32[]{:S(2)}, u32[]{:S(2)}) collective-permute-start(bf16[256,1024]{1,0:T(8,128)(2,1)} %get-tuple-element.82), channel_id=1, source_target_pairs={{0,8},{4,12},{8,0},{12,4},{1,9},{5,13},{9,1},{13,5},{2,10},{6,14},... | collective-permute-start | bytes 1572872 | tf_op jit(solution)/shard_map/ppermute | solution.py:23
  62.8 13.0 %collective-permute-start.10 = (bf16[128,1024]{1,0:T(8,128)(2,1)}, bf16[128,1024]{1,0:T(8,128)(2,1)}, u32[]{:S(2)}, u32[]{:S(2)}) collective-permute-start(bf16[128,1024]{1,0:T(8,128)(2,1)} %get-tuple-element.56), channel_id=1, source_target_pairs={{0,3},{1,0},{2,1},{3,2},{4,7},{5,4},{6,5},{7,6},{8,11},{9,8},{10,9... | collective-permute-start | bytes 786440 | tf_op jit(solution)/shard_map/ppermute | solution.py:18
  65.6 12.9 %collective-permute-start.6 = (bf16[128,1024]{1,0:T(8,128)(2,1)}, bf16[128,1024]{1,0:T(8,128)(2,1)}, u32[]{:S(2)}, u32[]{:S(2)}) collective-permute-start(bf16[128,1024]{1,0:T(8,128)(2,1)} %get-tuple-element.48), channel_id=1, source_target_pairs={{0,1},{1,2},{2,3},{3,0},{4,5},{5,6},{6,7},{7,4},{8,9},{9,10},{10,1... | collective-permute-start | bytes 786440 | tf_op jit(solution)/shard_map/ppermute | solution.py:18
  65.6 20.9 %collective-permute-start.8 = (bf16[128,1024]{1,0:T(8,128)(2,1)}, bf16[128,1024]{1,0:T(8,128)(2,1)}, u32[]{:S(2)}, u32[]{:S(2)}) collective-permute-start(bf16[128,1024]{1,0:T(8,128)(2,1)} %get-tuple-element.52), channel_id=1, source_target_pairs={{0,2},{1,3},{2,0},{3,1},{4,6},{5,7},{6,4},{7,5},{8,10},{9,11},{10,... | collective-permute-start | bytes 786440 | tf_op jit(solution)/shard_map/ppermute | solution.py:18
  67.5 2.9 %copy-start.7 = (bf16[1,2,64,1024]{3,2,1,0:T(8,128)(2,1)S(1)}, bf16[1,2,64,1024]{3,2,1,0:T(8,128)(2,1)}, u32[]{:S(2)}) copy-start(bf16[1,2,64,1024]{3,2,1,0:T(8,128)(2,1)} %param.6) | copy-start | bytes 786436
  68.9 26.3 %collective-permute-start.28 = (bf16[256,1024]{1,0:T(8,128)(2,1)S(1)}, bf16[256,1024]{1,0:T(8,128)(2,1)S(1)}, u32[]{:S(2)}, u32[]{:S(2)}) collective-permute-start(bf16[256,1024]{1,0:T(8,128)(2,1)S(1)} %get-tuple-element.80), channel_id=1, source_target_pairs={{0,4},{4,0},{8,12},{12,8},{1,5},{5,1},{9,13},{13,9},{2,6},{6,2},{1... | collective-permute-start | bytes 1572872 | tf_op jit(solution)/shard_map/ppermute | solution.py:23
  70.4 2.2 %copy-start.2 = (bf16[1,2048,1024]{2,1,0:T(8,128)(2,1)S(1)}, bf16[1,2048,1024]{2,1,0:T(8,128)(2,1)}, u32[]{:S(2)}) copy-start(bf16[1,2048,1024]{2,1,0:T(8,128)(2,1)} %param.7) | copy-start | bytes 12582916
  72.6 13.9 %copy-start.9 = (bf16[128,1024]{1,0:T(8,128)(2,1)S(1)}, bf16[128,1024]{1,0:T(8,128)(2,1)}, u32[]{:S(2)}) copy-start(bf16[128,1024]{1,0:T(8,128)(2,1)} %copy-done.8) | copy-start | bytes 786436
  89.1 26.2 %collective-permute-start.21 = (bf16[256,1024]{1,0:T(8,128)(2,1)S(1)}, bf16[256,1024]{1,0:T(8,128)(2,1)S(1)}, u32[]{:S(2)}, u32[]{:S(2)}) collective-permute-start(bf16[256,1024]{1,0:T(8,128)(2,1)S(1)} %get-tuple-element.74), channel_id=1, source_target_pairs={{0,8},{4,12},{8,0},{12,4},{1,9},{5,13},{9,1},{13,5},{2,10},{6,14},... | collective-permute-start | bytes 1572872 | tf_op jit(solution)/shard_map/ppermute | solution.py:23
  89.7 29.3 %collective-permute-start.17 = (bf16[256,1024]{1,0:T(8,128)(2,1)S(1)}, bf16[256,1024]{1,0:T(8,128)(2,1)S(1)}, u32[]{:S(2)}, u32[]{:S(2)}) collective-permute-start(bf16[256,1024]{1,0:T(8,128)(2,1)S(1)} %get-tuple-element.72), channel_id=1, source_target_pairs={{0,4},{4,0},{8,12},{12,8},{1,5},{5,1},{9,13},{13,9},{2,6},{6,2},{1... | collective-permute-start | bytes 1572872 | tf_op jit(solution)/shard_map/ppermute | solution.py:23
  91.2 11.8 %collective-permute-start.7 = (bf16[64,2048]{1,0:T(8,128)(2,1)S(1)}, bf16[64,2048]{1,0:T(8,128)(2,1)S(1)}, u32[]{:S(2)}, u32[]{:S(2)}) collective-permute-start(bf16[64,2048]{1,0:T(8,128)(2,1)S(1)} %get-tuple-element.49), channel_id=1, source_target_pairs={{0,3},{1,0},{2,1},{3,2},{4,7},{5,4},{6,5},{7,6},{8,11},{9,8},{10,9... | collective-permute-start | bytes 786440 | tf_op jit(solution)/shard_map/ppermute | solution.py:18
  93.8 12.6 %collective-permute-start.11 = (bf16[64,2048]{1,0:T(8,128)(2,1)S(1)}, bf16[64,2048]{1,0:T(8,128)(2,1)S(1)}, u32[]{:S(2)}, u32[]{:S(2)}) collective-permute-start(bf16[64,2048]{1,0:T(8,128)(2,1)S(1)} %get-tuple-element.57), channel_id=1, source_target_pairs={{0,1},{1,2},{2,3},{3,0},{4,5},{5,6},{6,7},{7,4},{8,9},{9,10},{10,1... | collective-permute-start | bytes 786440 | tf_op jit(solution)/shard_map/ppermute | solution.py:18
  93.8 20.0 %copy-start.4 = (bf16[2,64,8192]{2,1,0:T(8,128)(2,1)S(1)}, bf16[2,64,8192]{2,1,0:T(8,128)(2,1)}, u32[]{:S(2)}) copy-start(bf16[2,64,8192]{2,1,0:T(8,128)(2,1)} %top_ref.3) | copy-start | bytes 6291460
  95.2 18.7 %copy-start.1 = (bf16[1,2,64,8192]{3,2,1,0:T(8,128)(2,1)S(1)}, bf16[1,2,64,8192]{3,2,1,0:T(8,128)(2,1)}, u32[]{:S(2)}) copy-start(bf16[1,2,64,8192]{3,2,1,0:T(8,128)(2,1)} %x_ref.3) | copy-start | bytes 6291460
  95.2 18.5 %collective-permute-start.9 = (bf16[64,2048]{1,0:T(8,128)(2,1)S(1)}, bf16[64,2048]{1,0:T(8,128)(2,1)S(1)}, u32[]{:S(2)}, u32[]{:S(2)}) collective-permute-start(bf16[64,2048]{1,0:T(8,128)(2,1)S(1)} %get-tuple-element.53), channel_id=1, source_target_pairs={{0,2},{1,3},{2,0},{3,1},{4,6},{5,7},{6,4},{7,5},{8,10},{9,11},{10,... | collective-permute-start | bytes 786440 | tf_op jit(solution)/shard_map/ppermute | solution.py:18
  103.0 16.6 %collective-permute-start.33 = (bf16[128,1024]{1,0:T(8,128)(2,1)S(1)}, bf16[128,1024]{1,0:T(8,128)(2,1)S(1)}, u32[]{:S(2)}, u32[]{:S(2)}) collective-permute-start(bf16[128,1024]{1,0:T(8,128)(2,1)S(1)} %slice.60), channel_id=1, source_target_pairs={{0,4},{4,0},{8,12},{12,8},{1,5},{5,1},{9,13},{13,9},{2,6},{6,2},{1... | collective-permute-start | bytes 786440 | tf_op jit(solution)/shard_map/ppermute | solution.py:23
  106.4 13.9 %collective-permute-start.29 = (bf16[128,1024]{1,0:T(8,128)(2,1)S(1)}, bf16[128,1024]{1,0:T(8,128)(2,1)S(1)}, u32[]{:S(2)}, u32[]{:S(2)}) collective-permute-start(bf16[128,1024]{1,0:T(8,128)(2,1)S(1)} %slice.61), channel_id=1, source_target_pairs={{0,8},{4,12},{8,0},{12,4},{1,9},{5,13},{9,1},{13,5},{2,10},{6,14},... | collective-permute-start | bytes 786440 | tf_op jit(solution)/shard_map/ppermute | solution.py:23
  113.7 11.2 %collective-permute-start.15 = (bf16[64,2048]{1,0:T(8,128)(2,1)S(1)}, bf16[64,2048]{1,0:T(8,128)(2,1)S(1)}, u32[]{:S(2)}, u32[]{:S(2)}) collective-permute-start(bf16[64,2048]{1,0:T(8,128)(2,1)S(1)} %get-tuple-element.66), channel_id=1, source_target_pairs={{0,1},{1,2},{2,3},{3,0},{4,5},{5,6},{6,7},{7,4},{8,9},{9,10},{10,1... | collective-permute-start | bytes 786440 | tf_op jit(solution)/shard_map/ppermute | solution.py:18
  115.4 18.7 %collective-permute-start.14 = (bf16[64,2048]{1,0:T(8,128)(2,1)S(1)}, bf16[64,2048]{1,0:T(8,128)(2,1)S(1)}, u32[]{:S(2)}, u32[]{:S(2)}) collective-permute-start(bf16[64,2048]{1,0:T(8,128)(2,1)S(1)} %get-tuple-element.64), channel_id=1, source_target_pairs={{0,2},{1,3},{2,0},{3,1},{4,6},{5,7},{6,4},{7,5},{8,10},{9,11},{10,... | collective-permute-start | bytes 786440 | tf_op jit(solution)/shard_map/ppermute | solution.py:18
  119.0 15.6 %collective-permute-start.13 = (bf16[64,2048]{1,0:T(8,128)(2,1)S(1)}, bf16[64,2048]{1,0:T(8,128)(2,1)S(1)}, u32[]{:S(2)}, u32[]{:S(2)}) collective-permute-start(bf16[64,2048]{1,0:T(8,128)(2,1)S(1)} %get-tuple-element.62), channel_id=1, source_target_pairs={{0,3},{1,0},{2,1},{3,2},{4,7},{5,4},{6,5},{7,6},{8,11},{9,8},{10,9... | collective-permute-start | bytes 786440 | tf_op jit(solution)/shard_map/ppermute | solution.py:18
  119.6 18.0 %collective-permute-start.22 = (bf16[128,1024]{1,0:T(8,128)(2,1)S(1)}, bf16[128,1024]{1,0:T(8,128)(2,1)S(1)}, u32[]{:S(2)}, u32[]{:S(2)}) collective-permute-start(bf16[128,1024]{1,0:T(8,128)(2,1)S(1)} %slice.62), channel_id=1, source_target_pairs={{0,4},{4,0},{8,12},{12,8},{1,5},{5,1},{9,13},{13,9},{2,6},{6,2},{1... | collective-permute-start | bytes 786440 | tf_op jit(solution)/shard_map/ppermute | solution.py:23
  120.3 32.7 %collective-permute-start.12 = (bf16[64,8192]{1,0:T(8,128)(2,1)S(1)}, bf16[64,8192]{1,0:T(8,128)(2,1)S(1)}, u32[]{:S(2)}, u32[]{:S(2)}) collective-permute-start(bf16[64,8192]{1,0:T(8,128)(2,1)S(1)} %get-tuple-element.58), channel_id=1, source_target_pairs={{16,0},{17,1},{18,2},{19,3},{20,4},{21,5},{22,6},{23,7},{24,8},{25... | collective-permute-start | bytes 3145736 | tf_op jit(solution)/shard_map/ppermute | solution.py:339
  124.8 14.1 %collective-permute-start.18 = (bf16[128,1024]{1,0:T(8,128)(2,1)S(1)}, bf16[128,1024]{1,0:T(8,128)(2,1)S(1)}, u32[]{:S(2)}, u32[]{:S(2)}) collective-permute-start(bf16[128,1024]{1,0:T(8,128)(2,1)S(1)} %slice.63), channel_id=1, source_target_pairs={{0,8},{4,12},{8,0},{12,4},{1,9},{5,13},{9,1},{13,5},{2,10},{6,14},... | collective-permute-start | bytes 786440 | tf_op jit(solution)/shard_map/ppermute | solution.py:23
  134.0 8.1 %collective-permute-start.34 = (bf16[128,1024]{1,0:T(8,128)(2,1)S(1)}, bf16[128,1024]{1,0:T(8,128)(2,1)S(1)}, u32[]{:S(2)}, u32[]{:S(2)}) collective-permute-start(bf16[128,1024]{1,0:T(8,128)(2,1)S(1)} %fusion.4), channel_id=1, source_target_pairs={{0,4},{4,0},{8,12},{12,8},{1,5},{5,1},{9,13},{13,9},{2,6},{6,2},{1... | collective-permute-start | bytes 786440 | tf_op jit(solution)/shard_map/ppermute | solution.py:23
  134.6 9.2 %collective-permute-start.30 = (bf16[128,1024]{1,0:T(8,128)(2,1)S(1)}, bf16[128,1024]{1,0:T(8,128)(2,1)S(1)}, u32[]{:S(2)}, u32[]{:S(2)}) collective-permute-start(bf16[128,1024]{1,0:T(8,128)(2,1)S(1)} %fusion.5), channel_id=1, source_target_pairs={{0,8},{4,12},{8,0},{12,4},{1,9},{5,13},{9,1},{13,5},{2,10},{6,14},... | collective-permute-start | bytes 786440 | tf_op jit(solution)/shard_map/ppermute | solution.py:23
  137.6 41.0 %collective-permute-start.16 = (bf16[64,8192]{1,0:T(8,128)(2,1)S(1)}, bf16[64,8192]{1,0:T(8,128)(2,1)}, u32[]{:S(2)}, u32[]{:S(2)}) collective-permute-start(bf16[64,8192]{1,0:T(8,128)(2,1)S(1)} %get-tuple-element.67), channel_id=1, source_target_pairs={{16,0},{17,1},{18,2},{19,3},{20,4},{21,5},{22,6},{23,7},{24,8},{25... | collective-permute-start | bytes 3145736 | tf_op jit(solution)/shard_map/ppermute | solution.py:339
  139.0 8.1 %collective-permute-start.23 = (bf16[128,1024]{1,0:T(8,128)(2,1)S(1)}, bf16[128,1024]{1,0:T(8,128)(2,1)S(1)}, u32[]{:S(2)}, u32[]{:S(2)}) collective-permute-start(bf16[128,1024]{1,0:T(8,128)(2,1)S(1)} %fusion.6), channel_id=1, source_target_pairs={{0,4},{4,0},{8,12},{12,8},{1,5},{5,1},{9,13},{13,9},{2,6},{6,2},{1... | collective-permute-start | bytes 786440 | tf_op jit(solution)/shard_map/ppermute | solution.py:23
  142.2 9.1 %collective-permute-start.19 = (bf16[128,1024]{1,0:T(8,128)(2,1)S(1)}, bf16[128,1024]{1,0:T(8,128)(2,1)S(1)}, u32[]{:S(2)}, u32[]{:S(2)}) collective-permute-start(bf16[128,1024]{1,0:T(8,128)(2,1)S(1)} %fusion.7), channel_id=1, source_target_pairs={{0,8},{4,12},{8,0},{12,4},{1,9},{5,13},{9,1},{13,5},{2,10},{6,14},... | collective-permute-start | bytes 786440 | tf_op jit(solution)/shard_map/ppermute | solution.py:23
  143.7 18.8 %collective-permute-start.35 = (bf16[256,1024]{1,0:T(8,128)(2,1)S(1)}, bf16[256,1024]{1,0:T(8,128)(2,1)S(1)}, u32[]{:S(2)}, u32[]{:S(2)}) collective-permute-start(bf16[256,1024]{1,0:T(8,128)(2,1)S(1)} %pad_maximum_fusion.3.refs_2_), channel_id=1, source_target_pairs={{0,8},{4,12},{8,0},{12,4},{1,9},{5,13},{9,1},{13,5},{2,10},{6,14},... | collective-permute-start | bytes 1572872 | tf_op jit(solution)/shard_map/ppermute | solution.py:23
  147.0 15.5 %collective-permute-start.31 = (bf16[256,1024]{1,0:T(8,128)(2,1)S(1)}, bf16[256,1024]{1,0:T(8,128)(2,1)S(1)}, u32[]{:S(2)}, u32[]{:S(2)}) collective-permute-start(bf16[256,1024]{1,0:T(8,128)(2,1)S(1)} %pad_maximum_fusion.2.refs_0_), channel_id=1, source_target_pairs={{0,4},{4,0},{8,12},{12,8},{1,5},{5,1},{9,13},{13,9},{2,6},{6,2},{1... | collective-permute-start | bytes 1572872 | tf_op jit(solution)/shard_map/ppermute | solution.py:23
  151.3 21.9 %collective-permute-start.24 = (bf16[256,1024]{1,0:T(8,128)(2,1)S(1)}, bf16[256,1024]{1,0:T(8,128)(2,1)S(1)}, u32[]{:S(2)}, u32[]{:S(2)}) collective-permute-start(bf16[256,1024]{1,0:T(8,128)(2,1)S(1)} %pad_maximum_fusion.1.refs_2_), channel_id=1, source_target_pairs={{0,8},{4,12},{8,0},{12,4},{1,9},{5,13},{9,1},{13,5},{2,10},{6,14},... | collective-permute-start | bytes 1572872 | tf_op jit(solution)/shard_map/ppermute | solution.py:23
  153.0 20.2 %collective-permute-start.20 = (bf16[256,1024]{1,0:T(8,128)(2,1)S(1)}, bf16[256,1024]{1,0:T(8,128)(2,1)S(1)}, u32[]{:S(2)}, u32[]{:S(2)}) collective-permute-start(bf16[256,1024]{1,0:T(8,128)(2,1)S(1)} %pad_maximum_fusion.refs_0_), channel_id=1, source_target_pairs={{0,4},{4,0},{8,12},{12,8},{1,5},{5,1},{9,13},{13,9},{2,6},{6,2},{1... | collective-permute-start | bytes 1572872 | tf_op jit(solution)/shard_map/ppermute | solution.py:23
  153.6 9.0 %copy-start.3 = (bf16[1,2048,1024]{2,1,0:T(8,128)(2,1)S(1)}, bf16[1,2048,1024]{2,1,0:T(8,128)(2,1)}, u32[]{:S(2)}) copy-start(bf16[1,2048,1024]{2,1,0:T(8,128)(2,1)} %param.7) | copy-start | bytes 12582916
  178.6 1.7 copy-start.18
  (7 other events, 5.4 us)

commit v3 on v0

v3 whole, which is shorter than its diff:
```python
import jax
import jax.numpy as jnp
from jax import lax
from jax.experimental import pallas as pl
from jax.experimental.pallas import tpu as pltpu
from jax.sharding import PartitionSpec as P

norm_eps = 1e-05
bf16 = jnp.bfloat16
f32 = jnp.float32
MIB = 1 << 20
SMEM_ARG = pl.BlockSpec(memory_space=pltpu.SMEM)
VMEM_ARG = pl.BlockSpec(memory_space=pltpu.VMEM)


def cyclic(value, axis, steps):
    count = lax.axis_size(axis)
    return lax.ppermute(value, axis, [(i, (i + steps) % count) for i in range(count)])


def flipped(value, axis, mask):
    count = lax.axis_size(axis)
    return lax.ppermute(value, axis, [(i, i ^ mask) for i in range(count)])


def after(value, *others):
    return lax.optimization_barrier((value, *others))[0]


def params(mib):
    return pltpu.CompilerParams(vmem_limit_bytes=mib * MIB)


def cost(flops, bytes_accessed):
    return pl.CostEstimate(flops=int(flops), bytes_accessed=int(bytes_accessed), transcendentals=0)


def scaled_blocks(x, me, rep, groups, reps, chunks):
    tokens, width = x.shape
    shard = width // groups
    piece = shard // reps
    chunk = piece // chunks
    if chunk % 128:
        x = x.astype(f32)
        hat = (x * lax.rsqrt(jnp.mean(x * x, axis=1, keepdims=True) + norm_eps)).astype(bf16)
        hat = jnp.roll(hat.reshape(tokens, groups, reps, chunks, chunk), -me[0], axis=1)
        take = lambda e, c: lax.dynamic_index_in_dim(hat, rep[0] ^ e, 2, False)[:, :, c].reshape(tokens, groups * chunk)
        return [[take(e, c) for e in range(reps)] for c in range(chunks)]
    step = 16
    block = min(tokens, 32)

    def kernel(me_ref, rep_ref, x_ref, *out_refs):
        span = min(shard, 512)
        for row in range(0, block, step):
            rows = slice(row, row + step)
            total = jnp.zeros((step, 128), f32)
            for c in range(0, width, span):
                v = x_ref[rows, c : c + span].astype(f32)
                v = v * v
                for k in range(0, span, 128):
                    total = total + v[:, k : k + 128]
            scale = lax.rsqrt(jnp.sum(total, axis=1, keepdims=True) / width + norm_eps)
            for c in range(chunks):
                for e in range(reps):
                    for j in range(groups):
                        at = lax.rem(me_ref[0] + j, groups) * shard + (rep_ref[0] ^ e) * piece + c * chunk
                        v = x_ref[rows, pl.ds(pl.multiple_of(at, chunk), chunk)].astype(f32)
                        out_refs[c * reps + e][rows, j * chunk : (j + 1) * chunk] = (v * scale).astype(bf16)

    outs = pl.pallas_call(
        kernel,
        grid=(tokens // block,),
        out_shape=[jax.ShapeDtypeStruct((tokens, groups * chunk), bf16)] * (chunks * reps),
        in_specs=[SMEM_ARG, SMEM_ARG, pl.BlockSpec((block, width), lambda i: (i, 0))],
        out_specs=[pl.BlockSpec((block, groups * chunk), lambda i: (i, 0))] * (chunks * reps),
        compiler_params=params(8),
        cost_estimate=cost(6 * x.size, 4 * x.size),
        name="scaled_blocks",
    )(me, rep, x)
    return [list(outs[c * reps : (c + 1) * reps]) for c in range(chunks)]


def regrouped(blocks, groups):
    tokens, width = blocks[0].shape
    chunk = width // groups
    reps = len(blocks)
    if chunk % 128:
        return [jnp.concatenate([b[:, j * chunk : (j + 1) * chunk] for b in blocks], axis=0) for j in range(groups)]

    def kernel(*refs):
        for e in range(reps):
            for j in range(groups):
                refs[reps + j][e * tokens : (e + 1) * tokens, :] = refs[e][:, j * chunk : (j + 1) * chunk]

    return list(
        pl.pallas_call(
            kernel,
            out_shape=[jax.ShapeDtypeStruct((reps * tokens, chunk), bf16)] * groups,
            in_specs=[VMEM_ARG] * reps,
            out_specs=[VMEM_ARG] * groups,
            compiler_params=params(8),
            cost_estimate=cost(0, 4 * reps * tokens * width),
            name="regrouped",
        )(*blocks)
    )


def weight_product(chunks, grads, me, rep, groups, reps):
    rows, chunk = chunks[0][0].shape
    features = grads.shape[1]
    tokens = rows // reps
    count = len(chunks)

    def place(me, rep, j, e):
        return ((rep ^ e) * groups + lax.rem(me - j + groups, groups)) * tokens

    if chunk % 128:
        order = [lax.dynamic_slice_in_dim(grads, place(me[0], rep[0], j, e), tokens, 0) for j in range(groups) for e in range(reps)]
        values = jnp.concatenate(order, axis=0)
        contract = (((0,), (0,)), ((), ()))
        return [
            lax.dot_general(jnp.concatenate(c, axis=0), values, contract, preferred_element_type=f32).astype(bf16)
            for c in chunks
        ]

    def kernel(me_ref, rep_ref, *refs):
        block_refs, grads_ref = refs[: count * groups], refs[count * groups]
        out_refs, total = refs[count * groups + 1 : -1], refs[-1]
        for j in range(groups):
            values = []
            for e in range(reps):
                at = place(me_ref[0], rep_ref[0], j, e)
                values.append(grads_ref[pl.ds(pl.multiple_of(at, tokens), tokens), :])
            values = jnp.concatenate(values, axis=0)
            for c in range(count):
                product = lax.dot_general(
                    block_refs[c * groups + j][...], values, (((0,), (0,)), ((), ())), preferred_element_type=f32
                )
                if j == 0:
                    total[c] = product
                elif j + 1 < groups:
                    total[c] += product
                else:
                    out_refs[c][...] = (total[c] + product).astype(bf16)

    return pl.pallas_call(
        kernel,
        out_shape=[jax.ShapeDtypeStruct((chunk, features), bf16)] * count,
        in_specs=[SMEM_ARG] * 2 + [VMEM_ARG] * (count * groups + 1),
        out_specs=[VMEM_ARG] * count,
        scratch_shapes=[pltpu.VMEM((count, chunk, features), f32)],
        compiler_params=params(20),
        cost_estimate=cost(
            2 * groups * rows * chunk * count * features, 2 * groups * rows * (chunk * count + features) + 2 * chunk * count * features
        ),
        name="weight_product",
    )(me, rep, *[b for c in chunks for b in c], grads)


def returned_blocks(grads, weight, gain, me, groups, micro):
    features = grads.shape[1]
    tokens = grads.shape[0] // groups
    rows = tokens // micro
    shard = weight.shape[0]
    tile = min(shard, 512)

    def kernel(me_ref, grads_ref, weight_ref, gain_ref, *out_refs):
        factor = gain_ref[...].astype(f32)
        pair = 2 if groups % 2 == 0 else 1
        for j in range(0, groups, pair):
            values = []
            for i in range(pair):
                at = lax.rem(me_ref[0] - j - i + groups, groups) * tokens
                values.append(grads_ref[pl.ds(pl.multiple_of(at, tokens), tokens), :])
            values = jnp.concatenate(values, axis=0)
            back = lax.dot_general(values, weight_ref[...], (((1,), (1,)), ((), ())), preferred_element_type=f32)
            back = (back * factor).astype(bf16)
            for i in range(pair):
                for m in range(micro):
                    at = i * tokens + m * rows
                    out_refs[(j + i) * micro + m][...] = back[at : at + rows, :]

    outs = pl.pallas_call(
        kernel,
        grid=(shard // tile,),
        out_shape=[jax.ShapeDtypeStruct((rows, shard), bf16)] * (groups * micro),
        in_specs=[
            SMEM_ARG,
            pl.BlockSpec((groups * tokens, features), lambda i: (0, 0)),
            pl.BlockSpec((tile, features), lambda i: (i, 0)),
            pl.BlockSpec((1, tile), lambda i: (0, i)),
        ],
        out_specs=[pl.BlockSpec((rows, tile), lambda i: (0, i))] * (groups * micro),
        compiler_params=params(14),
        cost_estimate=cost(2 * groups * tokens * shard * features, 2 * groups * tokens * (shard + features) + 2 * shard * features),
        name="returned_blocks",
    )(me, grads, weight, gain)
    return [list(outs[j * micro : (j + 1) * micro]) for j in range(groups)]


def row_gradient(x, top, blocks, me, m):
    groups = len(blocks)
    rows, shard = blocks[0].shape
    width = shard * groups
    step = 16

    def kernel(me_ref, x_ref, top_ref, *refs):
        block_refs, upper_ref, piece_ref = refs[:groups], refs[groups], refs[groups + 1]
        squares = jnp.zeros((step, 128), f32)
        dots = jnp.zeros((step, 128), f32)
        starts = [pl.multiple_of(lax.rem(me_ref[0] + j, groups) * shard, shard) for j in range(groups)]
        span = min(shard, 512)
        for j in range(groups):
            for c in range(0, shard, span):
                v = x_ref[0, 0, :, pl.ds(pl.multiple_of(starts[j] + c, span), span)].astype(f32)
                d = block_refs[j][:, c : c + span].astype(f32) * v
                v = v * v
                for k in range(0, span, 128):
                    squares = squares + v[:, k : k + 128]
                    dots = dots + d[:, k : k + 128]
        scale = lax.rsqrt(jnp.sum(squares, axis=1, keepdims=True) / width + norm_eps)
        mean = jnp.sum(dots, axis=1, keepdims=True) * scale / width
        slope = scale * mean
        for j in range(groups):
            for c in range(0, shard, span):
                at = pl.ds(pl.multiple_of(starts[j] + c, span), span)
                v = x_ref[0, 0, :, at].astype(f32)
                piece = (scale * (block_refs[j][:, c : c + span].astype(f32) - v * slope)).astype(bf16)
                piece_ref[:, at] = piece
                upper_ref[:, at] = (top_ref[0, :, at].astype(f32) + piece.astype(f32)).astype(bf16)

    return pl.pallas_call(
        kernel,
        grid=(rows // step,),
        out_shape=[jax.ShapeDtypeStruct((rows, width), bf16)] * 2,
        in_specs=[
            SMEM_ARG,
            pl.BlockSpec((1, 1, step, width), lambda i: (0, m, i, 0)),
            pl.BlockSpec((1, step, width), lambda i: (m, i, 0)),
        ]
        + [pl.BlockSpec((step, shard), lambda i: (i, 0))] * groups,
        out_specs=[pl.BlockSpec((step, width), lambda i: (i, 0))] * 2,
        compiler_params=params(8),
        cost_estimate=cost(12 * rows * width, 10 * rows * width),
        name="row_gradient",
    )(me, x, top, *blocks)


def input_gradient(upper, piece, passed, is_upper, shape, m, earlier):
    rows, width = upper.shape
    step = min(rows, 32)

    def kernel(is_upper_ref, upper_ref, piece_ref, passed_ref, *refs):
        lower = (passed_ref[...].astype(f32) + piece_ref[...].astype(f32)).astype(bf16)
        refs[-1][0, 0] = jnp.where(is_upper_ref[0] == 1, upper_ref[...], lower)

    spec = pl.BlockSpec((step, width), lambda i: (i, 0))
    return pl.pallas_call(
        kernel,
        grid=(rows // step,),
        out_shape=jax.ShapeDtypeStruct(shape, bf16),
        in_specs=[SMEM_ARG, spec, spec, spec] + [pl.BlockSpec(memory_space=pl.ANY)] * len(earlier),
        out_specs=pl.BlockSpec((1, 1, step, width), lambda i: (0, m, i, 0)),
        input_output_aliases={4: 0} if earlier else {},
        compiler_params=params(8),
        cost_estimate=cost(4 * rows * width, 8 * rows * width),
        name="input_gradient",
    )(is_upper, upper, piece, passed, *earlier)


def finished_chunk(sums, weight, factor, c, chunks, earlier):
    reps, rows, features = sums.shape
    shard = weight.shape[0]

    def kernel(sum_ref, weight_ref, factor_ref, *refs):
        raw = sum_ref[0].astype(f32)
        refs[-2][...] = raw * factor_ref[:, 0:1]
        refs[-1][...] = jnp.sum(raw * weight_ref[...].astype(f32), axis=1, keepdims=True) * factor_ref[:, 1:2]

    place = lambda i: (i * chunks + c, 0)
    return pl.pallas_call(
        kernel,
        grid=(reps,),
        out_shape=[jax.ShapeDtypeStruct((shard, features), f32), jax.ShapeDtypeStruct((shard, 1), f32)],
        in_specs=[
            pl.BlockSpec((1, rows, features), lambda i: (i, 0, 0)),
            pl.BlockSpec((rows, features), place),
            pl.BlockSpec((rows, 2), place),
        ]
        + [pl.BlockSpec(memory_space=pl.ANY)] * len(earlier),
        out_specs=[pl.BlockSpec((rows, features), place), pl.BlockSpec((rows, 1), place)],
        input_output_aliases={3: 0, 4: 1} if earlier else {},
        compiler_params=params(8),
        cost_estimate=cost(4 * reps * rows * features, 8 * reps * rows * features),
        name="finished_chunk",
    )(sums, weight, factor, *earlier)


def local(layer_input, value_grad, value_weight, norm_gain, top_grad):
    groups = lax.axis_size("fsdp")
    reps = lax.axis_size("rep")
    me = lax.axis_index("fsdp").astype(jnp.int32)[None]
    rep = lax.axis_index("rep").astype(jnp.int32)[None]
    _, micro, rows, width = layer_input.shape
    tokens = micro * rows
    norm_scale = float(tokens * reps * groups) ** (-0.5)
    chunks = 2

    weight = value_weight[0]
    gain = norm_gain[0].astype(f32) * norm_scale
    factor = jnp.stack([gain, jnp.full_like(gain, norm_scale)], axis=1)

    grads = lax.all_gather(value_grad[0].reshape(tokens, -1), "fsdp", axis=0, tiled=True)
    grads_all = lax.all_gather(grads, "rep", axis=0, tiled=True)

    hats = scaled_blocks(layer_input[0].reshape(tokens, width), me, rep, groups, reps, chunks)
    columns = []
    for c in range(chunks):
        plane = [hats[c][e] if e == 0 else flipped(hats[c][e], "rep", e) for e in range(reps)]
        sent = regrouped(plane, groups)
        columns.append([sent[j] if j == 0 else cyclic(sent[j], "fsdp", j) for j in range(groups)])

    sums = weight_product(columns, grads_all, me, rep, groups, reps)
    finished = ()
    for c in range(chunks):
        gathered = lax.all_gather(sums[c], "rep", axis=0)
        finished = finished_chunk(gathered, weight, factor, c, chunks, finished)
    weight_grad, gain_grad = finished

    back = returned_blocks(grads, weight, norm_gain, me, groups, micro)
    ties = [columns[0][1:], columns[1][1:2]]
    result = ()
    is_upper = lax.axis_index("section").astype(jnp.int32)[None]
    for m in range(micro):
        line = [back[j][m] for j in range(groups)]
        for j in range(1, groups):
            line[j] = cyclic(after(line[j], *ties[min(j - 1, 1)]), "fsdp", -j)
        ties = [line[1:2], line[2:3]]
        upper, piece = row_gradient(layer_input, top_grad, line, me, m)
        passed = lax.ppermute(upper, "section", [(1, 0)])
        result = (input_gradient(upper, piece, passed, is_upper, layer_input.shape, m, result),)
    return (result[0], weight_grad[None], gain_grad[:, 0][None])


def solution(mesh):
    return jax.shard_map(
        local,
        mesh=mesh,
        in_specs=(
            P("section", None, ("rep", "fsdp"), None),
            P("section", None, ("rep", "fsdp"), None),
            P("section", "fsdp", None),
            P("section", "fsdp"),
            P(None, ("rep", "fsdp"), None),
        ),
        out_specs=(
            P("section", None, ("rep", "fsdp"), None),
            P("section", "fsdp", None),
            P("section", "fsdp"),
        ),
        check_vma=False,
    )
```

time: 333 us -> 204 us (0.61)
  blocking collectives: 76.8 us -> 0 us
  waiting for transfers between devices: 168 us -> 119 us
  other arithmetic: 23.5 us -> 0.96 us
  Pallas kernels: 0 us -> 21.8 us
  matrix products: 18.1 us -> 0 us
  starting transfers between devices: 20.4 us -> 29.4 us
  local copies, waits for them, and re-layouts: 10.5 us -> 17.2 us
    psum x1 -> x0, waiting for transfers between devices: 115 us -> none  [local(): weight_total, gain_total = lax.psum((weight_total, gain_total), 'rep')]
    ppermute x2 -> x20, waiting for transfers between devices: 0.01 us -> 79.6 us  [the longest x12 54.5 us: cyclic(): lax.ppermute(value, axis, [(i, (i + steps) % count) for i in range(count)])]
    all_to_all x4 -> x0, waiting for transfers between devices: 53.1 us -> none  [the longest x2 29.6 us: local(): lax.all_to_all(local_cols, 'fsdp', split_axis=0, concat_axis=1, tiled=True)]
    all_gather x0 -> x4, waiting for transfers between devices: none -> 38 us  [the longest x1 32.3 us: local(): lax.all_gather(value_grad[0].reshape(tokens, -1), 'fsdp', axis=0, tiled=T...]
    all_gather x2 -> x0, blocking collectives: 36 us -> none  [local(): grads_all = lax.all_gather(grad_rows, 'fsdp', axis=0, tiled=True)]
    ppermute x2 -> x20, starting transfers between devices: 2.57 us -> 29.2 us  [the longest x12 17 us: cyclic(): lax.ppermute(value, axis, [(i, (i + steps) % count) for i in range(count)])]
    pallas_call x0 -> x11, Pallas kernels: none -> 21.8 us  [the longest x2 5.4 us: finished_chunk(): pl.pallas_call(kernel, grid=(reps,), out_shape=[jax.ShapeDtypeStruct((sha...]
    unnamed x1 -> x0, blocking collectives: 20.7 us -> none
  transfers between devices with their start and end apart: 7 -> 24, of which waited for: 4 -> 13; matrix products, arithmetic and copies ran while one was open for 7% -> 1% of each run, Pallas kernels for 0% -> 8%
where the time goes in v3:
time: 204 us; the launch traced here: 202 us
  waiting for transfers between devices  119 us (58%)
  starting transfers between devices  29.4 us (14%)
  Pallas kernels  21.8 us (11%)
  local copies, waits for them, and re-layouts  17.2 us (8%)
  between operations  13.9 us (7%)
    ppermute x12, waiting for transfers between devices, cyclic(): lax.ppermute(value, axis, [(i, (i + steps) % count) for i in range(count)])  54.5 us
    all_gather x1, waiting for transfers between devices, local(): lax.all_gather(value_grad[0].reshape(tokens, -1), 'fsdp', axis=0, tiled=T...  32.3 us
    ppermute x6, waiting for transfers between devices, flipped(): return lax.ppermute(value, axis, [(i, i ^ mask) for i in range(count)])  25.1 us
    ppermute x12, starting transfers between devices, cyclic(): lax.ppermute(value, axis, [(i, (i + steps) % count) for i in range(count)])  17 us
    unnamed x26, local copies, waits for them, and re-layouts  14.5 us
    ppermute x6, starting transfers between devices, flipped(): return lax.ppermute(value, axis, [(i, i ^ mask) for i in range(count)])  9.65 us
    all_gather x1, waiting for transfers between devices, local(): grads_all = lax.all_gather(grads, 'rep', axis=0, tiled=True)  5.71 us
    pallas_call x2, Pallas kernels, finished_chunk(): pl.pallas_call(kernel, grid=(reps,), out_shape=[jax.ShapeDtypeStruct((sha...  5.4 us
  transfers between devices with their start and end apart: 24, of which 13 were waited for; matrix products, arithmetic and copies ran while one was open for 1% of the time, Pallas kernels for 8%

profile of v3, /device:TPU:0, one launch (start us, length us, event | category | flops | bytes accessed | tf_op | source)
XLA Modules:
  0.0 202.1 jit_solution(12142265048812435490)
XLA Ops:
  7.9 32.3 %all-gather.7.cloned.1.call-done.grads_ref = bf16[512,1024]{1,0:T(8,128)(2,1)} async-done(((bf16[128,1024]{1,0:T(8,128)(2,1)}), bf16[512,1024]{1,0:T(8,128)(2,1)}) %all-gather.7.cloned.1.call-update) | async-done | bytes 1048592 | tf_op jit(solution)/shard_map/all_gather | solution.py:313
  40.3 1.6 copy-done
  41.9 1.2 scaled_blocks.1
  43.1 1.5 collective-permute-start
  44.6 1.5 collective-permute-start.1
  46.6 1.5 collective-permute-start.8
  48.1 1.5 collective-permute-start.9
  49.6 3.1 %collective-permute-done.refs_1_ = bf16[128,1024]{1,0:T(8,128)(2,1)S(1)} collective-permute-done((bf16[128,1024]{1,0:T(8,128)(2,1)S(1)}, bf16[128,1024]{1,0:T(8,128)(2,1)S(1)}, u32[]{:S(2)}, u32[]{:S(2)}) %collective-permute-start) | collective-permute-done | bytes 262176 | tf_op jit(solution)/shard_map/ppermute | solution.py:23
  52.6 3.1 %collective-permute-start.10 = (bf16[128,1024]{1,0:T(8,128)(2,1)S(1)}, bf16[128,1024]{1,0:T(8,128)(2,1)S(1)}, u32[]{:S(2)}, u32[]{:S(2)}) collective-permute-start(bf16[128,1024]{1,0:T(8,128)(2,1)S(1)} %get-tuple-element.60), channel_id=1, source_target_pairs={{0,12},{4,8},{8,4},{12,0},{1,13},{5,9},{9,5},{13,1},{2,14},{6,10},... | collective-permute-start | bytes 786440 | tf_op jit(solution)/shard_map/ppermute | solution.py:23
  55.8 4.7 %collective-permute-done.1.refs_2_ = bf16[128,1024]{1,0:T(8,128)(2,1)S(1)} collective-permute-done((bf16[128,1024]{1,0:T(8,128)(2,1)S(1)}, bf16[128,1024]{1,0:T(8,128)(2,1)S(1)}, u32[]{:S(2)}, u32[]{:S(2)}) %collective-permute-start.1) | collective-permute-done | bytes 262176 | tf_op jit(solution)/shard_map/ppermute | solution.py:23
  60.5 4.1 %collective-permute-done.2.refs_3_ = bf16[128,1024]{1,0:T(8,128)(2,1)S(1)} collective-permute-done((bf16[128,1024]{1,0:T(8,128)(2,1)S(1)}, bf16[128,1024]{1,0:T(8,128)(2,1)S(1)}, u32[]{:S(2)}, u32[]{:S(2)}) %collective-permute-start.2) | collective-permute-done | bytes 262176 | tf_op jit(solution)/shard_map/ppermute | solution.py:23
  64.7 1.5 collective-permute-start.3
  66.2 8.6 %collective-permute-done.8.refs_1_ = bf16[128,1024]{1,0:T(8,128)(2,1)S(1)} collective-permute-done((bf16[128,1024]{1,0:T(8,128)(2,1)S(1)}, bf16[128,1024]{1,0:T(8,128)(2,1)S(1)}, u32[]{:S(2)}, u32[]{:S(2)}) %collective-permute-start.8) | collective-permute-done | bytes 262176 | tf_op jit(solution)/shard_map/ppermute | solution.py:23
  75.5 4.6 %collective-permute-done.10.refs_3_ = bf16[128,1024]{1,0:T(8,128)(2,1)S(1)} collective-permute-done((bf16[128,1024]{1,0:T(8,128)(2,1)S(1)}, bf16[128,1024]{1,0:T(8,128)(2,1)S(1)}, u32[]{:S(2)}, u32[]{:S(2)}) %collective-permute-start.10) | collective-permute-done | bytes 262176 | tf_op jit(solution)/shard_map/ppermute | solution.py:23
  80.2 1.4 collective-permute-start.11
  81.7 1.4 collective-permute-start.18
  83.0 2.2 %collective-permute-start.19 = (bf16[512,256]{1,0:T(8,128)(2,1)S(1)}, bf16[512,256]{1,0:T(8,128)(2,1)S(1)}, u32[]{:S(2)}, u32[]{:S(2)}) collective-permute-start(bf16[512,256]{1,0:T(8,128)(2,1)S(1)} %get-tuple-element.76), channel_id=1, source_target_pairs={{0,3},{1,0},{2,1},{3,2},{4,7},{5,4},{6,5},{7,6},{8,11},{9,8},{10,9... | collective-permute-start | bytes 786440 | tf_op jit(solution)/shard_map/ppermute | solution.py:18
  85.2 1.8 collective-permute-done.5.refs_3_
  87.0 4.3 %collective-permute-done.11.refs_5_ = bf16[512,256]{1,0:T(8,128)(2,1)S(1)} collective-permute-done((bf16[512,256]{1,0:T(8,128)(2,1)S(1)}, bf16[512,256]{1,0:T(8,128)(2,1)S(1)}, u32[]{:S(2)}, u32[]{:S(2)}) %collective-permute-start.11) | collective-permute-done | bytes 262176 | tf_op jit(solution)/shard_map/ppermute | solution.py:18
  91.4 12.6 %collective-permute-done.18.refs_6_ = bf16[512,256]{1,0:T(8,128)(2,1)S(1)} collective-permute-done((bf16[512,256]{1,0:T(8,128)(2,1)S(1)}, bf16[512,256]{1,0:T(8,128)(2,1)S(1)}, u32[]{:S(2)}, u32[]{:S(2)}) %collective-permute-start.18) | collective-permute-done | bytes 262176 | tf_op jit(solution)/shard_map/ppermute | solution.py:18
  103.9 5.7 %all-gather.9.cloned.1.call-done.refs_8_ = bf16[2048,1024]{1,0:T(8,128)(2,1)} async-done(((bf16[512,1024]{1,0:T(8,128)(2,1)}), bf16[2048,1024]{1,0:T(8,128)(2,1)}) %all-gather.9.cloned.1.call-update) | async-done | bytes 4194320 | tf_op jit(solution)/shard_map/all_gather | solution.py:314
  109.6 2.2 %copy-done.12 = bf16[2048,1024]{1,0:T(8,128)(2,1)S(1)} copy-done((bf16[2048,1024]{1,0:T(8,128)(2,1)S(1)}, bf16[2048,1024]{1,0:T(8,128)(2,1)}, u32[]{:S(2)}) %copy-start.12) | copy-done | bytes 4194328
  111.8 3.2 %weight_product.1 = (bf16[256,1024]{1,0:T(8,128)(2,1)}, bf16[256,1024]{1,0:T(8,128)(2,1)}) custom-call(s32[1]{0:T(128)} %bitcast.1.me_ref, s32[1]{0:T(128)} %bitcast.4.rep_ref, bf16[512,256]{1,0:T(8,128)(2,1)S(1)} %get-tuple-element.73.refs_0_, bf16[512,256]{1,0:T(8,128)(2,1)S(1)} %collective-permute-done.3.refs_1_, ...), custom_call_target="tpu_custom_call" | custom-call | flops 2147483648 | bytes 7340032 | tf_op jit(solution)/shard_map/weight_product/pallas_call | solution.py:146
  115.7 2.2 %copy-done.2 = bf16[1,2048,1024]{2,1,0:T(8,128)(2,1)S(1)} copy-done((bf16[1,2048,1024]{2,1,0:T(8,128)(2,1)S(1)}, bf16[1,2048,1024]{2,1,0:T(8,128)(2,1)}, u32[]{:S(2)}) %copy-start.2) | copy-done | bytes 4194328
  117.9 3.2 %returned_blocks.1 = (bf16[64,2048]{1,0:T(8,128)(2,1)S(1)}, bf16[64,2048]{1,0:T(8,128)(2,1)S(1)}, bf16[64,2048]{1,0:T(8,128)(2,1)S(1)}, bf16[64,2048]{1,0:T(8,12...) custom-call(s32[1]{0:T(128)} %bitcast.1.me_ref, ...), custom_call_target="tpu_custom_call" | custom-call | flops 2147483648 | bytes 7340032 | tf_op jit(solution)/shard_map/returned_blocks/pallas_call | solution.py:183
  121.0 3.4 %collective-permute-start.6 = (bf16[64,2048]{1,0:T(8,128)(2,1)S(1)}, bf16[64,2048]{1,0:T(8,128)(2,1)S(1)}, u32[]{:S(2)}, u32[]{:S(2)}) collective-permute-start(bf16[64,2048]{1,0:T(8,128)(2,1)S(1)} %get-tuple-element.53), channel_id=1, source_target_pairs={{0,3},{1,0},{2,1},{3,2},{4,7},{5,4},{6,5},{7,6},{8,11},{9,8},{10,9... | collective-permute-start | bytes 786440 | tf_op jit(solution)/shard_map/ppermute | solution.py:18
  124.4 1.1 collective-permute-start.16
  125.5 5.7 %collective-permute-done.6.refs_1_ = bf16[64,2048]{1,0:T(8,128)(2,1)S(1)} collective-permute-done((bf16[64,2048]{1,0:T(8,128)(2,1)S(1)}, bf16[64,2048]{1,0:T(8,128)(2,1)S(1)}, u32[]{:S(2)}, u32[]{:S(2)}) %collective-permute-start.6) | collective-permute-done | bytes 262176 | tf_op jit(solution)/shard_map/ppermute | solution.py:18
  131.2 4.3 %collective-permute-start.7 = (bf16[64,2048]{1,0:T(8,128)(2,1)S(1)}, bf16[64,2048]{1,0:T(8,128)(2,1)S(1)}, u32[]{:S(2)}, u32[]{:S(2)}) collective-permute-start(bf16[64,2048]{1,0:T(8,128)(2,1)S(1)} %get-tuple-element.54), channel_id=1, source_target_pairs={{0,3},{1,0},{2,1},{3,2},{4,7},{5,4},{6,5},{7,6},{8,11},{9,8},{10,9... | collective-permute-start | bytes 786440 | tf_op jit(solution)/shard_map/ppermute | solution.py:18
  135.5 18.2 %collective-permute-done.12.refs_2_ = bf16[64,2048]{1,0:T(8,128)(2,1)S(1)} collective-permute-done((bf16[64,2048]{1,0:T(8,128)(2,1)S(1)}, bf16[64,2048]{1,0:T(8,128)(2,1)S(1)}, u32[]{:S(2)}, u32[]{:S(2)}) %collective-permute-start.12) | collective-permute-done | bytes 262176 | tf_op jit(solution)/shard_map/ppermute | solution.py:18
  153.7 1.0 collective-permute-start.14
  154.7 1.5 row_gradient.3
  156.2 1.3 collective-permute-start.17
  157.5 11.9 %collective-permute-done.13.refs_2_ = bf16[64,2048]{1,0:T(8,128)(2,1)S(1)} collective-permute-done((bf16[64,2048]{1,0:T(8,128)(2,1)S(1)}, bf16[64,2048]{1,0:T(8,128)(2,1)S(1)}, u32[]{:S(2)}, u32[]{:S(2)}) %collective-permute-start.13) | collective-permute-done | bytes 262176 | tf_op jit(solution)/shard_map/ppermute | solution.py:18
  169.4 2.5 %row_gradient.2 = (bf16[64,8192]{1,0:T(8,128)(2,1)}, bf16[64,8192]{1,0:T(8,128)(2,1)S(1)}) custom-call(s32[1]{0:T(128)} %bitcast.1.me_ref, bf16[1,2,64,8192]{3,2,1,0:T(8,128)(2,1)S(1)} %copy-done.1, bf16[2,64,8192]{2,1,0:T(8,128)(2,1)S(1)} %copy-done.5, bf16[64,2048]{1,0:T(8,128)(2,1)S(1)} %get-tuple-element.43.refs_0_, ...), custom_call_target="tpu_custom_call" | custom-call | flops 6291456 | bytes 5242880 | tf_op jit(solution)/shard_map/row_gradient/pallas_call | solution.py:232
  171.9 1.0 copy-done.9
  172.9 1.3 collective-permute-start.15
  174.2 1.3 copy.11
  175.6 1.3 stack.4.factor_ref
  176.9 2.2 %input_gradient.2.refs_0_ = bf16[1,2,64,8192]{3,2,1,0:T(8,128)(2,1)} custom-call(s32[1]{0:T(128)} %bitcast.is_upper_ref, bf16[64,8192]{1,0:T(8,128)(2,1)S(1)} %get-tuple-element.71.upper_ref, bf16[64,8192]{1,0:T(8,128)(2,1)S(1)} %get-tuple-element.72.piece_ref, bf16[64,8192]{1,0:T(8,128)(2,1)} %collective-permute-done.17.passed_ref), custom_call_target="tpu_custom_call" | custom-call | flops 2097152 | bytes 4194304 | tf_op jit(solution)/shard_map/input_gradient/pallas_call | solution.py:258
  179.2 2.5 %input_gradient.3 = bf16[1,2,64,8192]{3,2,1,0:T(8,128)(2,1)} custom-call(s32[1]{0:T(128)} %bitcast.is_upper_ref, bf16[64,8192]{1,0:T(8,128)(2,1)} %get-tuple-element.66.upper_ref, bf16[64,8192]{1,0:T(8,128)(2,1)S(1)} %copy-done.10, bf16[64,8192]{1,0:T(8,128)(2,1)} %collective-permute-done.15.passed_ref, ...), custom_call_target="tpu_custom_call", output_to_operand_aliasing={{}: (4, {})} | custom-call | flops 2097152 | bytes 4194304 | tf_op jit(solution)/shard_map/input_gradient/pallas_call | solution.py:258
  181.6 2.2 %copy-done.3 = bf16[1,2048,1024]{2,1,0:T(8,128)(2,1)S(1)} copy-done((bf16[1,2048,1024]{2,1,0:T(8,128)(2,1)S(1)}, bf16[1,2048,1024]{2,1,0:T(8,128)(2,1)}, u32[]{:S(2)}) %copy-start.3) | copy-done | bytes 4194328
  183.8 1.6 copy-done.6
  185.4 2.7 %finished_chunk.2 = (f32[2048,1024]{1,0:T(8,128)}, f32[2048,1]{1,0:T(8,128)S(1)}) custom-call(bf16[4,256,1024]{2,1,0:T(8,128)(2,1)S(1)} %bitcast.16, bf16[2048,1024]{1,0:T(8,128)(2,1)S(1)} %bitcast.14, f32[2048,2]{1,0:T(8,128)S(1)} %stack.4.factor_ref), custom_call_target="tpu_custom_call" | custom-call | flops 4194304 | bytes 8388608 | tf_op jit(solution)/shard_map/finished_chunk/pallas_call | solution.py:281
  188.1 2.2 %copy-done.4 = bf16[1,2048,1024]{2,1,0:T(8,128)(2,1)S(1)} copy-done((bf16[1,2048,1024]{2,1,0:T(8,128)(2,1)S(1)}, bf16[1,2048,1024]{2,1,0:T(8,128)(2,1)}, u32[]{:S(2)}) %copy-start.4) | copy-done | bytes 4194328
  190.3 1.6 copy-done.7
  191.9 2.7 %finished_chunk.3 = (f32[2048,1024]{1,0:T(8,128)}, f32[2048,1]{1,0:T(8,128)S(1)}) custom-call(bf16[4,256,1024]{2,1,0:T(8,128)(2,1)S(1)} %bitcast.17, bf16[2048,1024]{1,0:T(8,128)(2,1)S(1)} %bitcast.15, f32[2048,2]{1,0:T(8,128)S(1)} %stack.4.factor_ref, f32[2048,1024]{1,0:T(8,128)} %get-tuple-element.79.refs_0_, ...), custom_call_target="tpu_custom_call", output_to_operand_aliasing={{0}: (3, {}), {1}: (4, {})} | custom-call | flops 4194304 | bytes 8388608 | tf_op jit(solution)/shard_map/finished_chunk/pallas_call | solution.py:281
  194.6 0.9 reduce
  (45 shorter events, 2.9 us)
Async XLA Ops:
  7.2 33.1 %all-gather.7.cloned.1.call-start = ((), (), s32[]{:S(2)}) async-start(), calls=%async_computation | async-start | bytes 1310720 | tf_op jit(solution)/shard_map/all_gather | solution.py:313
  7.9 101.7 %all-gather.9.cloned.1.call-start = ((), (), s32[]{:S(2)}) async-start(), calls=%async_computation.1 | async-start | bytes 5242880 | tf_op jit(solution)/shard_map/all_gather | solution.py:314
  40.3 141.4 %all-gather.13.cloned.1.call-start = ((), (), s32[]{:S(2)}) async-start(), calls=%async_computation.3 | async-start | bytes 2621440 | tf_op jit(solution)/shard_map/all_gather | solution.py:326
  40.3 1.6 copy-start
  43.1 9.6 %collective-permute-start = (bf16[128,1024]{1,0:T(8,128)(2,1)S(1)}, bf16[128,1024]{1,0:T(8,128)(2,1)S(1)}, u32[]{:S(2)}, u32[]{:S(2)}) collective-permute-start(bf16[128,1024]{1,0:T(8,128)(2,1)S(1)} %get-tuple-element.47), channel_id=1, source_target_pairs={{0,4},{4,0},{8,12},{12,8},{1,5},{5,1},{9,13},{13,9},{2,6},{6,2},{1... | collective-permute-start | bytes 786440 | tf_op jit(solution)/shard_map/ppermute | solution.py:23
  44.6 15.9 %collective-permute-start.1 = (bf16[128,1024]{1,0:T(8,128)(2,1)S(1)}, bf16[128,1024]{1,0:T(8,128)(2,1)S(1)}, u32[]{:S(2)}, u32[]{:S(2)}) collective-permute-start(bf16[128,1024]{1,0:T(8,128)(2,1)S(1)} %get-tuple-element.48), channel_id=1, source_target_pairs={{0,8},{4,12},{8,0},{12,4},{1,9},{5,13},{9,1},{13,5},{2,10},{6,14},... | collective-permute-start | bytes 786440 | tf_op jit(solution)/shard_map/ppermute | solution.py:23
  46.1 18.6 %collective-permute-start.2 = (bf16[128,1024]{1,0:T(8,128)(2,1)S(1)}, bf16[128,1024]{1,0:T(8,128)(2,1)S(1)}, u32[]{:S(2)}, u32[]{:S(2)}) collective-permute-start(bf16[128,1024]{1,0:T(8,128)(2,1)S(1)} %get-tuple-element.49), channel_id=1, source_target_pairs={{0,12},{4,8},{8,4},{12,0},{1,13},{5,9},{9,5},{13,1},{2,14},{6,10},... | collective-permute-start | bytes 786440 | tf_op jit(solution)/shard_map/ppermute | solution.py:23
  46.6 28.2 %collective-permute-start.8 = (bf16[128,1024]{1,0:T(8,128)(2,1)S(1)}, bf16[128,1024]{1,0:T(8,128)(2,1)S(1)}, u32[]{:S(2)}, u32[]{:S(2)}) collective-permute-start(bf16[128,1024]{1,0:T(8,128)(2,1)S(1)} %get-tuple-element.58), channel_id=1, source_target_pairs={{0,4},{4,0},{8,12},{12,8},{1,5},{5,1},{9,13},{13,9},{2,6},{6,2},{1... | collective-permute-start | bytes 786440 | tf_op jit(solution)/shard_map/ppermute | solution.py:23
  48.1 27.4 %collective-permute-start.9 = (bf16[128,1024]{1,0:T(8,128)(2,1)S(1)}, bf16[128,1024]{1,0:T(8,128)(2,1)S(1)}, u32[]{:S(2)}, u32[]{:S(2)}) collective-permute-start(bf16[128,1024]{1,0:T(8,128)(2,1)S(1)} %get-tuple-element.59), channel_id=1, source_target_pairs={{0,8},{4,12},{8,0},{12,4},{1,9},{5,13},{9,1},{13,5},{2,10},{6,14},... | collective-permute-start | bytes 786440 | tf_op jit(solution)/shard_map/ppermute | solution.py:23
  52.6 27.5 %collective-permute-start.10 = (bf16[128,1024]{1,0:T(8,128)(2,1)S(1)}, bf16[128,1024]{1,0:T(8,128)(2,1)S(1)}, u32[]{:S(2)}, u32[]{:S(2)}) collective-permute-start(bf16[128,1024]{1,0:T(8,128)(2,1)S(1)} %get-tuple-element.60), channel_id=1, source_target_pairs={{0,12},{4,8},{8,4},{12,0},{1,13},{5,9},{9,5},{13,1},{2,14},{6,10},... | collective-permute-start | bytes 786440 | tf_op jit(solution)/shard_map/ppermute | solution.py:23
  64.7 18.3 %collective-permute-start.3 = (bf16[512,256]{1,0:T(8,128)(2,1)S(1)}, bf16[512,256]{1,0:T(8,128)(2,1)S(1)}, u32[]{:S(2)}, u32[]{:S(2)}) collective-permute-start(bf16[512,256]{1,0:T(8,128)(2,1)S(1)} %get-tuple-element.50), channel_id=1, source_target_pairs={{0,1},{1,2},{2,3},{3,0},{4,5},{5,6},{6,7},{7,4},{8,9},{9,10},{10,1... | collective-permute-start | bytes 786440 | tf_op jit(solution)/shard_map/ppermute | solution.py:18
  66.2 19.0 %collective-permute-start.4 = (bf16[512,256]{1,0:T(8,128)(2,1)S(1)}, bf16[512,256]{1,0:T(8,128)(2,1)S(1)}, u32[]{:S(2)}, u32[]{:S(2)}) collective-permute-start(bf16[512,256]{1,0:T(8,128)(2,1)S(1)} %get-tuple-element.51), channel_id=1, source_target_pairs={{0,2},{1,3},{2,0},{3,1},{4,6},{5,7},{6,4},{7,5},{8,10},{9,11},{10,... | collective-permute-start | bytes 786440 | tf_op jit(solution)/shard_map/ppermute | solution.py:18
  74.8 12.2 %collective-permute-start.5 = (bf16[512,256]{1,0:T(8,128)(2,1)S(1)}, bf16[512,256]{1,0:T(8,128)(2,1)S(1)}, u32[]{:S(2)}, u32[]{:S(2)}) collective-permute-start(bf16[512,256]{1,0:T(8,128)(2,1)S(1)} %get-tuple-element.52), channel_id=1, source_target_pairs={{0,3},{1,0},{2,1},{3,2},{4,7},{5,4},{6,5},{7,6},{8,11},{9,8},{10,9... | collective-permute-start | bytes 786440 | tf_op jit(solution)/shard_map/ppermute | solution.py:18
  80.2 11.1 %collective-permute-start.11 = (bf16[512,256]{1,0:T(8,128)(2,1)S(1)}, bf16[512,256]{1,0:T(8,128)(2,1)S(1)}, u32[]{:S(2)}, u32[]{:S(2)}) collective-permute-start(bf16[512,256]{1,0:T(8,128)(2,1)S(1)} %get-tuple-element.61), channel_id=1, source_target_pairs={{0,1},{1,2},{2,3},{3,0},{4,5},{5,6},{6,7},{7,4},{8,9},{9,10},{10,1... | collective-permute-start | bytes 786440 | tf_op jit(solution)/shard_map/ppermute | solution.py:18
  81.7 22.3 %collective-permute-start.18 = (bf16[512,256]{1,0:T(8,128)(2,1)S(1)}, bf16[512,256]{1,0:T(8,128)(2,1)S(1)}, u32[]{:S(2)}, u32[]{:S(2)}) collective-permute-start(bf16[512,256]{1,0:T(8,128)(2,1)S(1)} %get-tuple-element.75), channel_id=1, source_target_pairs={{0,2},{1,3},{2,0},{3,1},{4,6},{5,7},{6,4},{7,5},{8,10},{9,11},{10,... | collective-permute-start | bytes 786440 | tf_op jit(solution)/shard_map/ppermute | solution.py:18
  83.0 20.9 %collective-permute-start.19 = (bf16[512,256]{1,0:T(8,128)(2,1)S(1)}, bf16[512,256]{1,0:T(8,128)(2,1)S(1)}, u32[]{:S(2)}, u32[]{:S(2)}) collective-permute-start(bf16[512,256]{1,0:T(8,128)(2,1)S(1)} %get-tuple-element.76), channel_id=1, source_target_pairs={{0,3},{1,0},{2,1},{3,2},{4,7},{5,4},{6,5},{7,6},{8,11},{9,8},{10,9... | collective-permute-start | bytes 786440 | tf_op jit(solution)/shard_map/ppermute | solution.py:18
  109.6 2.2 %copy-start.12 = (bf16[2048,1024]{1,0:T(8,128)(2,1)S(1)}, bf16[2048,1024]{1,0:T(8,128)(2,1)}, u32[]{:S(2)}) copy-start(bf16[2048,1024]{1,0:T(8,128)(2,1)} %all-gather.9.cloned.1.call-done.refs_8_) | copy-start | bytes 12582916
  111.8 3.8 %copy-start.8 = (bf16[512,1024]{1,0:T(8,128)(2,1)S(1)}, bf16[512,1024]{1,0:T(8,128)(2,1)}, u32[]{:S(2)}) copy-start(bf16[512,1024]{1,0:T(8,128)(2,1)} %all-gather.7.cloned.1.call-done.grads_ref) | copy-start | bytes 3145732
  111.8 3.8 %copy-start.11 = (bf16[1,2048]{1,0:T(2,128)(2,1)S(1)}, bf16[1,2048]{1,0:T(2,128)(2,1)}, u32[]{:S(2)}) copy-start(bf16[1,2048]{1,0:T(2,128)(2,1)} %gain_ref.1) | copy-start | bytes 12292
  115.1 73.0 %all-gather.11.cloned.1.call-start = ((), (), s32[]{:S(2)}) async-start(), calls=%async_computation.2 | async-start | bytes 2621440 | tf_op jit(solution)/shard_map/all_gather | solution.py:326
  115.7 2.2 %copy-start.2 = (bf16[1,2048,1024]{2,1,0:T(8,128)(2,1)S(1)}, bf16[1,2048,1024]{2,1,0:T(8,128)(2,1)}, u32[]{:S(2)}) copy-start(bf16[1,2048,1024]{2,1,0:T(8,128)(2,1)} %param.7) | copy-start | bytes 12582916
  117.9 36.8 %copy-start.1 = (bf16[1,2,64,8192]{3,2,1,0:T(8,128)(2,1)S(1)}, bf16[1,2,64,8192]{3,2,1,0:T(8,128)(2,1)}, u32[]{:S(2)}) copy-start(bf16[1,2,64,8192]{3,2,1,0:T(8,128)(2,1)} %x_ref.3) | copy-start | bytes 6291460
  117.9 36.8 %copy-start.5 = (bf16[2,64,8192]{2,1,0:T(8,128)(2,1)S(1)}, bf16[2,64,8192]{2,1,0:T(8,128)(2,1)}, u32[]{:S(2)}) copy-start(bf16[2,64,8192]{2,1,0:T(8,128)(2,1)} %top_ref.3) | copy-start | bytes 6291460
  121.0 10.1 %collective-permute-start.6 = (bf16[64,2048]{1,0:T(8,128)(2,1)S(1)}, bf16[64,2048]{1,0:T(8,128)(2,1)S(1)}, u32[]{:S(2)}, u32[]{:S(2)}) collective-permute-start(bf16[64,2048]{1,0:T(8,128)(2,1)S(1)} %get-tuple-element.53), channel_id=1, source_target_pairs={{0,3},{1,0},{2,1},{3,2},{4,7},{5,4},{6,5},{7,6},{8,11},{9,8},{10,9... | collective-permute-start | bytes 786440 | tf_op jit(solution)/shard_map/ppermute | solution.py:18
  124.4 29.3 %collective-permute-start.12 = (bf16[64,2048]{1,0:T(8,128)(2,1)S(1)}, bf16[64,2048]{1,0:T(8,128)(2,1)S(1)}, u32[]{:S(2)}, u32[]{:S(2)}) collective-permute-start(bf16[64,2048]{1,0:T(8,128)(2,1)S(1)} %get-tuple-element.62), channel_id=1, source_target_pairs={{0,2},{1,3},{2,0},{3,1},{4,6},{5,7},{6,4},{7,5},{8,10},{9,11},{10,... | collective-permute-start | bytes 786440 | tf_op jit(solution)/shard_map/ppermute | solution.py:18
  124.4 30.3 %collective-permute-start.16 = (bf16[64,2048]{1,0:T(8,128)(2,1)S(1)}, bf16[64,2048]{1,0:T(8,128)(2,1)S(1)}, u32[]{:S(2)}, u32[]{:S(2)}) collective-permute-start(bf16[64,2048]{1,0:T(8,128)(2,1)S(1)} %get-tuple-element.70), channel_id=1, source_target_pairs={{0,1},{1,2},{2,3},{3,0},{4,5},{5,6},{6,7},{7,4},{8,9},{9,10},{10,1... | collective-permute-start | bytes 786440 | tf_op jit(solution)/shard_map/ppermute | solution.py:18
  131.2 26.4 %collective-permute-start.7 = (bf16[64,2048]{1,0:T(8,128)(2,1)S(1)}, bf16[64,2048]{1,0:T(8,128)(2,1)S(1)}, u32[]{:S(2)}, u32[]{:S(2)}) collective-permute-start(bf16[64,2048]{1,0:T(8,128)(2,1)S(1)} %get-tuple-element.54), channel_id=1, source_target_pairs={{0,3},{1,0},{2,1},{3,2},{4,7},{5,4},{6,5},{7,6},{8,11},{9,8},{10,9... | collective-permute-start | bytes 786440 | tf_op jit(solution)/shard_map/ppermute | solution.py:18
  153.7 15.7 %collective-permute-start.13 = (bf16[64,2048]{1,0:T(8,128)(2,1)S(1)}, bf16[64,2048]{1,0:T(8,128)(2,1)S(1)}, u32[]{:S(2)}, u32[]{:S(2)}) collective-permute-start(bf16[64,2048]{1,0:T(8,128)(2,1)S(1)} %get-tuple-element.63), channel_id=1, source_target_pairs={{0,2},{1,3},{2,0},{3,1},{4,6},{5,7},{6,4},{7,5},{8,10},{9,11},{10,... | collective-permute-start | bytes 786440 | tf_op jit(solution)/shard_map/ppermute | solution.py:18
  153.7 15.7 %collective-permute-start.14 = (bf16[64,2048]{1,0:T(8,128)(2,1)S(1)}, bf16[64,2048]{1,0:T(8,128)(2,1)S(1)}, u32[]{:S(2)}, u32[]{:S(2)}) collective-permute-start(bf16[64,2048]{1,0:T(8,128)(2,1)S(1)} %get-tuple-element.65), channel_id=1, source_target_pairs={{0,1},{1,2},{2,3},{3,0},{4,5},{5,6},{6,7},{7,4},{8,9},{9,10},{10,1... | collective-permute-start | bytes 786440 | tf_op jit(solution)/shard_map/ppermute | solution.py:18
  156.2 20.7 %collective-permute-start.17 = (bf16[64,8192]{1,0:T(8,128)(2,1)S(1)}, bf16[64,8192]{1,0:T(8,128)(2,1)}, u32[]{:S(2)}, u32[]{:S(2)}) collective-permute-start(bf16[64,8192]{1,0:T(8,128)(2,1)S(1)} %get-tuple-element.71.upper_ref), channel_id=1, source_target_pairs={{16,0},{17,1},{18,2},{19,3},{20,4},{21,5},{22,6},{23,7},{24,8},{25... | collective-permute-start | bytes 3145736 | tf_op jit(solution)/shard_map/ppermute | solution.py:340
  171.9 1.0 copy-start.9
  172.9 6.2 %collective-permute-start.15 = (bf16[64,8192]{1,0:T(8,128)(2,1)}, bf16[64,8192]{1,0:T(8,128)(2,1)}, u32[]{:S(2)}, u32[]{:S(2)}) collective-permute-start(bf16[64,8192]{1,0:T(8,128)(2,1)} %get-tuple-element.66.upper_ref), channel_id=1, source_target_pairs={{16,0},{17,1},{18,2},{19,3},{20,4},{21,5},{22,6},{23,7},{24,8},{25... | collective-permute-start | bytes 3145736 | tf_op jit(solution)/shard_map/ppermute | solution.py:340
  176.9 2.3 %copy-start.10 = (bf16[64,8192]{1,0:T(8,128)(2,1)S(1)}, bf16[64,8192]{1,0:T(8,128)(2,1)}, u32[]{:S(2)}) copy-start(bf16[64,8192]{1,0:T(8,128)(2,1)} %copy-done.9) | copy-start | bytes 3145732
  181.6 2.2 %copy-start.3 = (bf16[1,2048,1024]{2,1,0:T(8,128)(2,1)S(1)}, bf16[1,2048,1024]{2,1,0:T(8,128)(2,1)}, u32[]{:S(2)}) copy-start(bf16[1,2048,1024]{2,1,0:T(8,128)(2,1)} %param.7) | copy-start | bytes 12582916
  183.8 1.6 copy-start.6
  188.1 2.2 %copy-start.4 = (bf16[1,2048,1024]{2,1,0:T(8,128)(2,1)S(1)}, bf16[1,2048,1024]{2,1,0:T(8,128)(2,1)}, u32[]{:S(2)}) copy-start(bf16[1,2048,1024]{2,1,0:T(8,128)(2,1)} %param.7) | copy-start | bytes 12582916
  190.3 1.6 copy-start.7
Sparse Core Ops, SparseCore 0:
  9.6 30.6 all-gather.6
  42.1 67.5 all-gather.8
  115.2 35.3 all-gather.12
  152.2 35.3 all-gather.10

commit v4 on v3

--- a/solution.py
+++ b/solution.py
@@ -10,7 +10,7 @@
 f32 = jnp.float32
 MIB = 1 << 20
 SMEM_ARG = pl.BlockSpec(memory_space=pltpu.SMEM)
-VMEM_ARG = pl.BlockSpec(memory_space=pltpu.VMEM)
+ANY_ARG = pl.BlockSpec(memory_space=pl.ANY)
 
 
 def cyclic(value, axis, steps):
@@ -80,6 +80,16 @@
     return [list(outs[c * reps : (c + 1) * reps]) for c in range(chunks)]
 
 
+def doubled(value, order):
+    for bit in order[:-1]:
+        value = jnp.concatenate([value, flipped(value, "rep", 1 << bit)], axis=0)
+    return value, flipped(value, "rep", 1 << order[-1])
+
+
+def mask_of(pos, order):
+    return sum(((pos >> i) & 1) << bit for i, bit in enumerate(order))
+
+
 def regrouped(blocks, groups):
     tokens, width = blocks[0].shape
     chunk = width // groups
@@ -88,16 +98,23 @@
         return [jnp.concatenate([b[:, j * chunk : (j + 1) * chunk] for b in blocks], axis=0) for j in range(groups)]
 
     def kernel(*refs):
+        copies = []
         for e in range(reps):
             for j in range(groups):
-                refs[reps + j][e * tokens : (e + 1) * tokens, :] = refs[e][:, j * chunk : (j + 1) * chunk]
+                source = refs[e].at[:, j * chunk : (j + 1) * chunk]
+                target = refs[reps + j].at[e * tokens : (e + 1) * tokens, :]
+                copies.append(pltpu.make_async_copy(source, target, refs[-1].at[e * groups + j]))
+                copies[-1].start()
+        for copy in copies:
+            copy.wait()
 
     return list(
         pl.pallas_call(
             kernel,
             out_shape=[jax.ShapeDtypeStruct((reps * tokens, chunk), bf16)] * groups,
-            in_specs=[VMEM_ARG] * reps,
-            out_specs=[VMEM_ARG] * groups,
+            in_specs=[ANY_ARG] * reps,
+            out_specs=[ANY_ARG] * groups,
+            scratch_shapes=[pltpu.SemaphoreType.DMA((reps * groups,))],
             compiler_params=params(8),
             cost_estimate=cost(0, 4 * reps * tokens * width),
             name="regrouped",
@@ -105,74 +122,108 @@
     )
 
 
-def weight_product(chunks, grads, me, rep, groups, reps):
-    rows, chunk = chunks[0][0].shape
-    features = grads.shape[1]
+def weight_product(columns, values, weight, gain, groups, count, norm_scale):
+    rows, width = columns[0].shape
+    reps = len(values)
     tokens = rows // reps
-    count = len(chunks)
-
-    def place(me, rep, j, e):
-        return ((rep ^ e) * groups + lax.rem(me - j + groups, groups)) * tokens
+    features = values[0].shape[1]
+    chunk = width // count
+    contract = (((0,), (0,)), ((), ()))
+
+    def thirds(row):
+        first = row.astype(bf16)
+        rest = row - first.astype(f32)
+        second = rest.astype(bf16)
+        return first, second, (rest - second.astype(f32)).astype(bf16)
 
     if chunk % 128:
-        order = [lax.dynamic_slice_in_dim(grads, place(me[0], rep[0], j, e), tokens, 0) for j in range(groups) for e in range(reps)]
-        values = jnp.concatenate(order, axis=0)
-        contract = (((0,), (0,)), ((), ()))
-        return [
-            lax.dot_general(jnp.concatenate(c, axis=0), values, contract, preferred_element_type=f32).astype(bf16)
-            for c in chunks
-        ]
-
-    def kernel(me_ref, rep_ref, *refs):
-        block_refs, grads_ref = refs[: count * groups], refs[count * groups]
-        out_refs, total = refs[count * groups + 1 : -1], refs[-1]
+        order = jnp.stack([v.reshape(groups, tokens, features) for v in values], axis=1)
+        raw = lax.dot_general(
+            jnp.concatenate(columns, axis=0), order.reshape(-1, features), contract, preferred_element_type=f32
+        )
+        dots = jnp.sum(raw * weight.astype(f32), axis=1) * norm_scale
+        raw = (raw * gain).astype(bf16)
+        outs = []
+        for c in range(count):
+            at = slice(c * chunk, (c + 1) * chunk)
+            under = jnp.stack(thirds(dots[at]) + (jnp.zeros((chunk,), bf16),) * 13)
+            outs.append(jnp.concatenate([raw[at], jnp.pad(under, ((0, 0), (0, features - chunk)))], axis=0))
+        return outs
+
+    def kernel(*refs):
+        column_refs, value_refs = refs[:groups], refs[groups : groups + reps]
+        weight_ref, gain_ref = refs[groups + reps], refs[groups + reps + 1]
+        out_refs = refs[groups + reps + 2 : -5]
+        left, right, own, total, sems = refs[-5:]
+        copies = []
         for j in range(groups):
-            values = []
+            line = [pltpu.make_async_copy(column_refs[j], left.at[j], sems.at[j, reps])]
             for e in range(reps):
-                at = place(me_ref[0], rep_ref[0], j, e)
-                values.append(grads_ref[pl.ds(pl.multiple_of(at, tokens), tokens), :])
-            values = jnp.concatenate(values, axis=0)
+                source = value_refs[e].at[j * tokens : (j + 1) * tokens, :]
+                target = right.at[j, e * tokens : (e + 1) * tokens, :]
+                line.append(pltpu.make_async_copy(source, target, sems.at[j, e]))
+            for copy in line:
+                copy.start()
+            copies.append(line)
+        copy = pltpu.make_async_copy(weight_ref, own, sems.at[groups, 0])
+        copy.start()
+        for j in range(groups):
+            for c in copies[j]:
+                c.wait()
             for c in range(count):
-                product = lax.dot_general(
-                    block_refs[c * groups + j][...], values, (((0,), (0,)), ((), ())), preferred_element_type=f32
-                )
+                block = left[j, :, c * chunk : (c + 1) * chunk]
+                product = lax.dot_general(block, right[j], contract, preferred_element_type=f32)
                 if j == 0:
                     total[c] = product
-                elif j + 1 < groups:
+                else:
                     total[c] += product
-                else:
-                    out_refs[c][...] = (total[c] + product).astype(bf16)
+        copy.wait()
+        for c in range(count):
+            at = slice(c * chunk, (c + 1) * chunk)
+            raw = total[c]
+            out_refs[c][:chunk, :] = (raw * gain_ref[at, :]).astype(bf16)
+            dots = lax.dot_general(
+                jnp.full((8, features), norm_scale, f32),
+                raw * own[at, :].astype(f32),
+                (((1,), (1,)), ((), ())),
+                precision=lax.Precision.HIGHEST,
+                preferred_element_type=f32,
+            )
+            under = jnp.concatenate([row[0:1, :].astype(f32) for row in thirds(dots)] + [jnp.zeros((13, chunk), f32)], axis=0)
+            out_refs[c][chunk:, :chunk] = under.astype(bf16)
+            out_refs[c][chunk:, chunk:] = jnp.zeros((16, features - chunk), bf16)
 
     return pl.pallas_call(
         kernel,
-        out_shape=[jax.ShapeDtypeStruct((chunk, features), bf16)] * count,
-        in_specs=[SMEM_ARG] * 2 + [VMEM_ARG] * (count * groups + 1),
-        out_specs=[VMEM_ARG] * count,
-        scratch_shapes=[pltpu.VMEM((count, chunk, features), f32)],
-        compiler_params=params(20),
-        cost_estimate=cost(
-            2 * groups * rows * chunk * count * features, 2 * groups * rows * (chunk * count + features) + 2 * chunk * count * features
-        ),
+        out_shape=[jax.ShapeDtypeStruct((chunk + 16, features), bf16)] * count,
+        in_specs=[ANY_ARG] * (groups + reps + 1) + [pl.BlockSpec(memory_space=pltpu.VMEM)],
+        scratch_shapes=[
+            pltpu.VMEM((groups, rows, width), bf16),
+            pltpu.VMEM((groups, rows, features), bf16),
+            pltpu.VMEM((width, features), bf16),
+            pltpu.VMEM((count, chunk, features), f32),
+            pltpu.SemaphoreType.DMA((groups + 1, reps + 1)),
+        ],
+        compiler_params=params(24),
+        cost_estimate=cost(2 * groups * rows * width * features, 2 * groups * rows * (width + features) + 4 * width * features),
         name="weight_product",
-    )(me, rep, *[b for c in chunks for b in c], grads)
-
-
-def returned_blocks(grads, weight, gain, me, groups, micro):
-    features = grads.shape[1]
-    tokens = grads.shape[0] // groups
+    )(*columns, *values, weight, gain)
+
+
+def returned_blocks(slots, weight, gain, micro):
+    groups = len(slots)
+    tokens, features = slots[0].shape
     rows = tokens // micro
     shard = weight.shape[0]
     tile = min(shard, 512)
 
-    def kernel(me_ref, grads_ref, weight_ref, gain_ref, *out_refs):
+    def kernel(*refs):
+        slot_refs, weight_ref, gain_ref = refs[:groups], refs[groups], refs[groups + 1]
+        out_refs = refs[groups + 2 :]
         factor = gain_ref[...].astype(f32)
         pair = 2 if groups % 2 == 0 else 1
         for j in range(0, groups, pair):
-            values = []
-            for i in range(pair):
-                at = lax.rem(me_ref[0] - j - i + groups, groups) * tokens
-                values.append(grads_ref[pl.ds(pl.multiple_of(at, tokens), tokens), :])
-            values = jnp.concatenate(values, axis=0)
+            values = jnp.concatenate([slot_refs[j + i][...] for i in range(pair)], axis=0)
             back = lax.dot_general(values, weight_ref[...], (((1,), (1,)), ((), ())), preferred_element_type=f32)
             back = (back * factor).astype(bf16)
             for i in range(pair):
@@ -184,17 +235,13 @@
         kernel,
         grid=(shard // tile,),
         out_shape=[jax.ShapeDtypeStruct((rows, shard), bf16)] * (groups * micro),
-        in_specs=[
-            SMEM_ARG,
-            pl.BlockSpec((groups * tokens, features), lambda i: (0, 0)),
-            pl.BlockSpec((tile, features), lambda i: (i, 0)),
-            pl.BlockSpec((1, tile), lambda i: (0, i)),
-        ],
+        in_specs=[pl.BlockSpec((tokens, features), lambda i: (0, 0))] * groups
+        + [pl.BlockSpec((tile, features), lambda i: (i, 0)), pl.BlockSpec((1, tile), lambda i: (0, i))],
         out_specs=[pl.BlockSpec((rows, tile), lambda i: (0, i))] * (groups * micro),
-        compiler_params=params(14),
+        compiler_params=params(8),
         cost_estimate=cost(2 * groups * tokens * shard * features, 2 * groups * tokens * (shard + features) + 2 * shard * features),
         name="returned_blocks",
-    )(me, grads, weight, gain)
+    )(*slots, weight, gain)
     return [list(outs[j * micro : (j + 1) * micro]) for j in range(groups)]
 
 
@@ -259,7 +306,7 @@
         kernel,
         grid=(rows // step,),
         out_shape=jax.ShapeDtypeStruct(shape, bf16),
-        in_specs=[SMEM_ARG, spec, spec, spec] + [pl.BlockSpec(memory_space=pl.ANY)] * len(earlier),
+        in_specs=[SMEM_ARG, spec, spec, spec] + [ANY_ARG] * len(earlier),
         out_specs=pl.BlockSpec((1, 1, step, width), lambda i: (0, m, i, 0)),
         input_output_aliases={4: 0} if earlier else {},
         compiler_params=params(8),
@@ -268,78 +315,111 @@
     )(is_upper, upper, piece, passed, *earlier)
 
 
-def finished_chunk(sums, weight, factor, c, chunks, earlier):
-    reps, rows, features = sums.shape
-    shard = weight.shape[0]
-
-    def kernel(sum_ref, weight_ref, factor_ref, *refs):
-        raw = sum_ref[0].astype(f32)
-        refs[-2][...] = raw * factor_ref[:, 0:1]
-        refs[-1][...] = jnp.sum(raw * weight_ref[...].astype(f32), axis=1, keepdims=True) * factor_ref[:, 1:2]
-
-    place = lambda i: (i * chunks + c, 0)
+def finished_half(sums, rep, order, half, c, chunks, earlier):
+    pieces = (1 << len(order)) // 2
+    rows = sums.shape[0] // pieces - 16
+    features = sums.shape[1]
+    shard = rows * chunks * pieces * 2
+
+    def place(i, rep_ref):
+        return (rep_ref[0] ^ mask_of(i + half * pieces, order)) * chunks + c
+
+    def total(under):
+        return under[0:1, :rows] + under[1:2, :rows] + under[2:3, :rows]
+
+    if rows % 128:
+        earlier = earlier or (jnp.zeros((shard, features), f32), jnp.zeros((1, shard), f32))
+        for i in range(pieces):
+            piece = sums[i * (rows + 16) : (i + 1) * (rows + 16)].astype(f32)
+            at = place(i, rep) * rows
+            earlier = (
+                lax.dynamic_update_slice(earlier[0], piece[:rows], (at, 0)),
+                lax.dynamic_update_slice(earlier[1], total(piece[rows:]), (0, at)),
+            )
+        return earlier
+
+    def kernel(rep_ref, sum_ref, *refs):
+        refs[-2][...] = sum_ref[:rows, :].astype(f32)
+        refs[-1][...] = total(sum_ref[rows:, :].astype(f32))
+
     return pl.pallas_call(
         kernel,
-        grid=(reps,),
-        out_shape=[jax.ShapeDtypeStruct((shard, features), f32), jax.ShapeDtypeStruct((shard, 1), f32)],
-        in_specs=[
-            pl.BlockSpec((1, rows, features), lambda i: (i, 0, 0)),
-            pl.BlockSpec((rows, features), place),
-            pl.BlockSpec((rows, 2), place),
-        ]
-        + [pl.BlockSpec(memory_space=pl.ANY)] * len(earlier),
-        out_specs=[pl.BlockSpec((rows, features), place), pl.BlockSpec((rows, 1), place)],
-        input_output_aliases={3: 0, 4: 1} if earlier else {},
+        grid_spec=pltpu.PrefetchScalarGridSpec(
+            num_scalar_prefetch=1,
+            grid=(pieces,),
+            in_specs=[pl.BlockSpec((rows + 16, features), lambda i, rep_ref: (i, 0))] + [ANY_ARG] * len(earlier),
+            out_specs=[
+                pl.BlockSpec((rows, features), lambda i, rep_ref: (place(i, rep_ref), 0)),
+                pl.BlockSpec((1, rows), lambda i, rep_ref: (0, place(i, rep_ref))),
+            ],
+        ),
+        out_shape=[jax.ShapeDtypeStruct((shard, features), f32), jax.ShapeDtypeStruct((1, shard), f32)],
+        input_output_aliases={2: 0, 3: 1} if earlier else {},
         compiler_params=params(8),
-        cost_estimate=cost(4 * reps * rows * features, 8 * reps * rows * features),
-        name="finished_chunk",
-    )(sums, weight, factor, *earlier)
+        cost_estimate=cost(sums.size, 6 * sums.size),
+        name="finished_half",
+    )(rep, sums, *earlier)
 
 
 def local(layer_input, value_grad, value_weight, norm_gain, top_grad):
     groups = lax.axis_size("fsdp")
     reps = lax.axis_size("rep")
+    bits = reps.bit_length() - 1
     me = lax.axis_index("fsdp").astype(jnp.int32)[None]
     rep = lax.axis_index("rep").astype(jnp.int32)[None]
     _, micro, rows, width = layer_input.shape
     tokens = micro * rows
     norm_scale = float(tokens * reps * groups) ** (-0.5)
     chunks = 2
+    orders = [tuple(range(bits)), tuple(reversed(range(bits)))]
 
     weight = value_weight[0]
-    gain = norm_gain[0].astype(f32) * norm_scale
-    factor = jnp.stack([gain, jnp.full_like(gain, norm_scale)], axis=1)
-
-    grads = lax.all_gather(value_grad[0].reshape(tokens, -1), "fsdp", axis=0, tiled=True)
-    grads_all = lax.all_gather(grads, "rep", axis=0, tiled=True)
-
-    hats = scaled_blocks(layer_input[0].reshape(tokens, width), me, rep, groups, reps, chunks)
-    columns = []
-    for c in range(chunks):
-        plane = [hats[c][e] if e == 0 else flipped(hats[c][e], "rep", e) for e in range(reps)]
-        sent = regrouped(plane, groups)
-        columns.append([sent[j] if j == 0 else cyclic(sent[j], "fsdp", j) for j in range(groups)])
-
-    sums = weight_product(columns, grads_all, me, rep, groups, reps)
-    finished = ()
-    for c in range(chunks):
-        gathered = lax.all_gather(sums[c], "rep", axis=0)
-        finished = finished_chunk(gathered, weight, factor, c, chunks, finished)
-    weight_grad, gain_grad = finished
-
-    back = returned_blocks(grads, weight, norm_gain, me, groups, micro)
-    ties = [columns[0][1:], columns[1][1:2]]
-    result = ()
-    is_upper = lax.axis_index("section").astype(jnp.int32)[None]
+    piece = weight.shape[0] // reps
+    own_weight = lax.dynamic_slice_in_dim(weight, rep[0] * piece, piece, 0)
+    own_gain = lax.dynamic_slice_in_dim(norm_gain[0], rep[0] * piece, piece, 0).astype(f32)[:, None] * norm_scale
+
+    hats = scaled_blocks(layer_input[0].reshape(tokens, width), me, rep, groups, reps, 1)[0]
+    plane = list(hats)
+    for e in range(1, reps):
+        plane[e] = flipped(hats[e], "rep", e)
+    grads = after(value_grad[0].reshape(tokens, -1), hats[0])
+    slots = [grads] + [cyclic(grads, "fsdp", j) for j in range(1, groups)]
+
+    sent = regrouped(plane, groups)
+    back = returned_blocks(slots, weight, norm_gain, micro)
+    columns = list(sent)
+    for j in range(1, groups):
+        columns[j] = cyclic(after(sent[j], back[0][0]) if j == groups - 1 else sent[j], "fsdp", j)
+    held = after(jnp.concatenate(slots, axis=0), sent[0])
+    values = [held if e == 0 else flipped(held, "rep", e) for e in range(reps)]
+
+    lines = []
+    ties = [columns[1:2], columns[2:]]
     for m in range(micro):
         line = [back[j][m] for j in range(groups)]
         for j in range(1, groups):
             line[j] = cyclic(after(line[j], *ties[min(j - 1, 1)]), "fsdp", -j)
         ties = [line[1:2], line[2:3]]
-        upper, piece = row_gradient(layer_input, top_grad, line, me, m)
+        lines.append(line)
+    own = (after(own_weight, back[0][0]), after(own_gain, back[0][0]))
+    sums = weight_product(columns, values, *own, groups, chunks, norm_scale)
+    gathered = [doubled(sums[c], orders[c]) for c in range(chunks)]
+    finished = ()
+    for half in (0, 1):
+        for c in range(chunks):
+            finished = finished_half(gathered[c][half], rep, orders[c], half, c, chunks, finished)
+        if half == 0:
+            early = finished
+    weight_grad, gain_grad = finished
+
+    result = ()
+    is_upper = lax.axis_index("section").astype(jnp.int32)[None]
+    for m in range(micro):
+        lines[m][0] = after(lines[m][0], *([g[0] for g in gathered] if m == 0 else early))
+        upper, piece = row_gradient(layer_input, top_grad, lines[m], me, m)
         passed = lax.ppermute(upper, "section", [(1, 0)])
         result = (input_gradient(upper, piece, passed, is_upper, layer_input.shape, m, result),)
-    return (result[0], weight_grad[None], gain_grad[:, 0][None])
+    return (result[0], weight_grad[None], gain_grad)
 
 
 def solution(mesh):

time: 204 us -> 155 us (0.76)
  waiting for transfers between devices: 119 us -> 73.3 us
  between operations: 13.9 us -> 0.89 us
  Pallas kernels: 21.8 us -> 27.9 us
  starting transfers between devices: 29.4 us -> 34.1 us
    all_gather x4 -> x0, waiting for transfers between devices: 38 us -> none  [the longest x1 32.3 us: local(): lax.all_gather(value_grad[0].reshape(tokens, -1), 'fsdp', axis=0, tiled=T...]
    ppermute x6 -> x10, waiting for transfers between devices: 25.1 us -> 11.7 us  [flipped(): return lax.ppermute(value, axis, [(i, i ^ mask) for i in range(count)])]
    ppermute x12, waiting for transfers between devices: 54.5 us -> 61.5 us  [cyclic(): lax.ppermute(value, axis, [(i, (i + steps) % count) for i in range(count)])]
    ppermute x12, starting transfers between devices: 17 us -> 22 us  [cyclic(): lax.ppermute(value, axis, [(i, (i + steps) % count) for i in range(count)])]
    pallas_call x3 -> x5, Pallas kernels: 8.61 us -> 12.5 us  [the longest x4 6.73 us: finished_half(): pl.pallas_call(kernel, grid_spec=pltpu.PrefetchScalarGridSpec(num_scalar_...]
    unnamed x26 -> x62, local copies, waits for them, and re-layouts: 14.5 us -> 15 us
    ppermute x6 -> x10, starting transfers between devices: 9.65 us -> 9.6 us  [flipped(): return lax.ppermute(value, axis, [(i, i ^ mask) for i in range(count)])]
  transfers between devices with their start and end apart: 24 -> 24, of which waited for: 13 -> 9; matrix products, arithmetic and copies ran while one was open for 1% -> 1% of each run, Pallas kernels for 8% -> 12%
where the time goes in v4:
time: 155 us; the launch traced here: 153 us
  waiting for transfers between devices  73.3 us (47%)
  starting transfers between devices  34.1 us (22%)
  Pallas kernels  27.9 us (18%)
  local copies, waits for them, and re-layouts  16.5 us (11%)
    ppermute x12, waiting for transfers between devices, cyclic(): lax.ppermute(value, axis, [(i, (i + steps) % count) for i in range(count)])  61.5 us
    ppermute x12, starting transfers between devices, cyclic(): lax.ppermute(value, axis, [(i, (i + steps) % count) for i in range(count)])  22 us
    unnamed x62, local copies, waits for them, and re-layouts  15 us
    ppermute x10, waiting for transfers between devices, flipped(): return lax.ppermute(value, axis, [(i, i ^ mask) for i in range(count)])  11.7 us
    ppermute x10, starting transfers between devices, flipped(): return lax.ppermute(value, axis, [(i, i ^ mask) for i in range(count)])  9.6 us
    pallas_call x4, Pallas kernels, finished_half(): pl.pallas_call(kernel, grid_spec=pltpu.PrefetchScalarGridSpec(num_scalar_...  6.73 us
    pallas_call x1, Pallas kernels, weight_product(): pl.pallas_call(kernel, out_shape=[jax.ShapeDtypeStruct((chunk + 16, featu...  5.78 us
    pallas_call x2, Pallas kernels, row_gradient(): pl.pallas_call(kernel, grid=(rows // step,), out_shape=[jax.ShapeDtypeStr...  5.05 us
  transfers between devices with their start and end apart: 24, of which 9 were waited for; matrix products, arithmetic and copies ran while one was open for 1% of the time, Pallas kernels for 12%

profile of v4, /device:TPU:0, one launch (start us, length us, event | category | flops | bytes accessed | tf_op | source)
XLA Modules:
  0.0 152.8 jit_solution(8757496072991335629)
XLA Ops:
  0.6 1.6 %copy-done = bf16[1,2,64,8192]{3,2,1,0:T(8,128)(2,1)S(1)} copy-done((bf16[1,2,64,8192]{3,2,1,0:T(8,128)(2,1)S(1)}, bf16[1,2,64,8192]{3,2,1,0:T(8,128)(2,1)}, u32[]{:S(2)}) %copy-start) | copy-done | bytes 2097176
  2.2 1.1 scaled_blocks.1
  3.3 3.1 %collective-permute-start = (bf16[128,1024]{1,0:T(8,128)(2,1)S(1)}, bf16[128,1024]{1,0:T(8,128)(2,1)S(1)}, u32[]{:S(2)}, u32[]{:S(2)}) collective-permute-start(bf16[128,1024]{1,0:T(8,128)(2,1)S(1)} %bitcast.13), channel_id=1, source_target_pairs={{0,1},{1,2},{2,3},{3,0},{4,5},{5,6},{6,7},{7,4},{8,9},{9,10},{10,1... | collective-permute-start | bytes 786440 | tf_op jit(solution)/shard_map/ppermute | solution.py:18
  6.4 1.5 collective-permute-start.3
  7.9 1.5 collective-permute-start.4
  9.9 2.6 %collective-permute-start.1 = (bf16[128,1024]{1,0:T(8,128)(2,1)S(1)}, bf16[128,1024]{1,0:T(8,128)(2,1)S(1)}, u32[]{:S(2)}, u32[]{:S(2)}) collective-permute-start(bf16[128,1024]{1,0:T(8,128)(2,1)S(1)} %bitcast.14), channel_id=1, source_target_pairs={{0,2},{1,3},{2,0},{3,1},{4,6},{5,7},{6,4},{7,5},{8,10},{9,11},{10,... | collective-permute-start | bytes 786440 | tf_op jit(solution)/shard_map/ppermute | solution.py:18
  12.5 3.2 %collective-permute-done.refs_1_ = bf16[128,1024]{1,0:T(8,128)(2,1)S(1)} collective-permute-done((bf16[128,1024]{1,0:T(8,128)(2,1)S(1)}, bf16[128,1024]{1,0:T(8,128)(2,1)S(1)}, u32[]{:S(2)}, u32[]{:S(2)}) %collective-permute-start) | collective-permute-done | bytes 262176 | tf_op jit(solution)/shard_map/ppermute | solution.py:18
  15.6 1.4 collective-permute-start.2
  17.0 9.0 %collective-permute-done.1.refs_2_ = bf16[128,1024]{1,0:T(8,128)(2,1)S(1)} collective-permute-done((bf16[128,1024]{1,0:T(8,128)(2,1)S(1)}, bf16[128,1024]{1,0:T(8,128)(2,1)S(1)}, u32[]{:S(2)}, u32[]{:S(2)}) %collective-permute-start.1) | collective-permute-done | bytes 262176 | tf_op jit(solution)/shard_map/ppermute | solution.py:18
  26.0 4.2 %collective-permute-done.2.refs_3_ = bf16[128,1024]{1,0:T(8,128)(2,1)S(1)} collective-permute-done((bf16[128,1024]{1,0:T(8,128)(2,1)S(1)}, bf16[128,1024]{1,0:T(8,128)(2,1)S(1)}, u32[]{:S(2)}, u32[]{:S(2)}) %collective-permute-start.2) | collective-permute-done | bytes 262176 | tf_op jit(solution)/shard_map/ppermute | solution.py:18
  30.3 1.9 %collective-permute-done.4.refs_2_ = bf16[128,2048]{1,0:T(8,128)(2,1)S(1)} collective-permute-done((bf16[128,2048]{1,0:T(8,128)(2,1)S(1)}, bf16[128,2048]{1,0:T(8,128)(2,1)S(1)}, u32[]{:S(2)}, u32[]{:S(2)}) %collective-permute-start.4) | collective-permute-done | bytes 524320 | tf_op jit(solution)/shard_map/ppermute | solution.py:23
  32.2 1.1 regrouped.1
  33.4 1.6 %collective-permute-start.6 = (bf16[512,512]{1,0:T(8,128)(2,1)S(1)}, bf16[512,512]{1,0:T(8,128)(2,1)S(1)}, u32[]{:S(2)}, u32[]{:S(2)}) collective-permute-start(bf16[512,512]{1,0:T(8,128)(2,1)S(1)} %get-tuple-element.53), channel_id=1, source_target_pairs={{0,1},{1,2},{2,3},{3,0},{4,5},{5,6},{6,7},{7,4},{8,9},{9,10},{10,1... | collective-permute-start | bytes 1572872 | tf_op jit(solution)/shard_map/ppermute | solution.py:18
  35.0 1.2 collective-permute-start.9
  36.2 0.8 collective-permute-start.10
  37.1 1.4 collective-permute-start.11
  38.5 3.2 %returned_blocks.1 = (bf16[64,2048]{1,0:T(8,128)(2,1)S(1)}, bf16[64,2048]{1,0:T(8,128)(2,1)S(1)}, bf16[64,2048]{1,0:T(8,128)(2,1)S(1)}, bf16[64,2048]{1,0:T(8,12...) custom-call(bf16[128,1024]{1,0:T(8,128)(2,1)S(1)} %bitcast.17, ...), custom_call_target="tpu_custom_call" | custom-call | flops 2147483648 | bytes 7340032 | tf_op jit(solution)/shard_map/returned_blocks/pallas_call | solution.py:234
  42.4 0.7 copy-done.11
  47.4 1.4 collective-permute-start.7
  48.7 0.8 copy-done.16
  49.5 2.6 %collective-permute-start.8 = (bf16[512,512]{1,0:T(8,128)(2,1)}, bf16[512,512]{1,0:T(8,128)(2,1)}, u32[]{:S(2)}, u32[]{:S(2)}) collective-permute-start(bf16[512,512]{1,0:T(8,128)(2,1)} %get-tuple-element.57), channel_id=1, source_target_pairs={{0,3},{1,0},{2,1},{3,2},{4,7},{5,4},{6,5},{7,6},{8,11},{9,8},{10,9... | collective-permute-start | bytes 1572872 | tf_op jit(solution)/shard_map/ppermute | solution.py:18
  52.1 1.3 dynamic-slice_bitcast_fusion.refs_8_
  53.6 18.5 %collective-permute-done.7.refs_2_ = bf16[512,512]{1,0:T(8,128)(2,1)} collective-permute-done((bf16[512,512]{1,0:T(8,128)(2,1)}, bf16[512,512]{1,0:T(8,128)(2,1)}, u32[]{:S(2)}, u32[]{:S(2)}) %collective-permute-start.7) | collective-permute-done | bytes 524320 | tf_op jit(solution)/shard_map/ppermute | solution.py:18
  72.1 9.8 %collective-permute-done.10.refs_6_ = bf16[512,1024]{1,0:T(8,128)(2,1)} collective-permute-done((bf16[512,1024]{1,0:T(8,128)(2,1)S(1)}, bf16[512,1024]{1,0:T(8,128)(2,1)}, u32[]{:S(2)}, u32[]{:S(2)}) %collective-permute-start.10) | collective-permute-done | bytes 1048608 | tf_op jit(solution)/shard_map/ppermute | solution.py:23
  82.0 1.0 copy-done.15
  83.0 1.0 copy-done.17
  84.1 5.8 %weight_product.1 = (bf16[272,1024]{1,0:T(8,128)(2,1)S(1)}, bf16[272,1024]{1,0:T(8,128)(2,1)S(1)}) custom-call(bf16[512,512]{1,0:T(8,128)(2,1)S(1)} %copy-done.15, bf16[512,512]{1,0:T(8,128)(2,1)S(1)} %copy-done.17, bf16[512,512]{1,0:T(8,128)(2,1)} %collective-permute-done.7.refs_2_, bf16[512,512]{1,0:T(8,128)(2,1)} %collective-permute-done.8.refs_3_, ...), custom_call_target="tpu_custom_call" | custom-call | flops 2147483648 | bytes 8388608 | tf_op jit(solution)/shard_map/weight_product/pallas_call | solution.py:196
  90.5 3.4 %collective-permute-start.14 = (bf16[64,2048]{1,0:T(8,128)(2,1)S(1)}, bf16[64,2048]{1,0:T(8,128)(2,1)S(1)}, u32[]{:S(2)}, u32[]{:S(2)}) collective-permute-start(bf16[64,2048]{1,0:T(8,128)(2,1)S(1)} %copy-done.29), channel_id=1, source_target_pairs={{0,3},{1,0},{2,1},{3,2},{4,7},{5,4},{6,5},{7,6},{8,11},{9,8},{10,9... | collective-permute-start | bytes 786440 | tf_op jit(solution)/shard_map/ppermute | solution.py:18
  93.9 0.8 collective-permute-start.12
  95.2 5.4 %collective-permute-done.14.refs_1_ = bf16[64,2048]{1,0:T(8,128)(2,1)S(1)} collective-permute-done((bf16[64,2048]{1,0:T(8,128)(2,1)S(1)}, bf16[64,2048]{1,0:T(8,128)(2,1)S(1)}, u32[]{:S(2)}, u32[]{:S(2)}) %collective-permute-start.14) | collective-permute-done | bytes 262176 | tf_op jit(solution)/shard_map/ppermute | solution.py:18
  100.7 4.3 %collective-permute-start.15 = (bf16[64,2048]{1,0:T(8,128)(2,1)S(1)}, bf16[64,2048]{1,0:T(8,128)(2,1)S(1)}, u32[]{:S(2)}, u32[]{:S(2)}) collective-permute-start(bf16[64,2048]{1,0:T(8,128)(2,1)S(1)} %copy-done.23), channel_id=1, source_target_pairs={{0,3},{1,0},{2,1},{3,2},{4,7},{5,4},{6,5},{7,6},{8,11},{9,8},{10,9... | collective-permute-start | bytes 786440 | tf_op jit(solution)/shard_map/ppermute | solution.py:18
  105.0 17.7 %collective-permute-done.16.refs_2_ = bf16[64,2048]{1,0:T(8,128)(2,1)S(1)} collective-permute-done((bf16[64,2048]{1,0:T(8,128)(2,1)S(1)}, bf16[64,2048]{1,0:T(8,128)(2,1)S(1)}, u32[]{:S(2)}, u32[]{:S(2)}) %collective-permute-start.16) | collective-permute-done | bytes 262176 | tf_op jit(solution)/shard_map/ppermute | solution.py:18
  122.9 1.2 collective-permute-start.18
  125.3 1.4 finished_half.4
  126.7 1.4 finished_half.5
  128.1 0.9 copy-done.1
  129.6 2.5 %row_gradient.3 = (bf16[64,8192]{1,0:T(8,128)(2,1)}, bf16[64,8192]{1,0:T(8,128)(2,1)S(1)}) custom-call(s32[1]{0:T(128)} %bitcast.1.me_ref, bf16[1,2,64,8192]{3,2,1,0:T(8,128)(2,1)S(1)} %copy-done.1, bf16[2,64,8192]{2,1,0:T(8,128)(2,1)S(1)} %copy-done.2, bf16[64,2048]{1,0:T(8,128)(2,1)S(1)} %copy-done.12, ...), custom_call_target="tpu_custom_call" | custom-call | flops 6291456 | bytes 5242880 | tf_op jit(solution)/shard_map/row_gradient/pallas_call | solution.py:279
  132.1 1.0 copy-done.3
  133.1 1.3 collective-permute-start.21
  134.4 3.4 %collective-permute-done.17.refs_2_ = bf16[64,2048]{1,0:T(8,128)(2,1)S(1)} collective-permute-done((bf16[64,2048]{1,0:T(8,128)(2,1)S(1)}, bf16[64,2048]{1,0:T(8,128)(2,1)S(1)}, u32[]{:S(2)}, u32[]{:S(2)}) %collective-permute-start.17) | collective-permute-done | bytes 262176 | tf_op jit(solution)/shard_map/ppermute | solution.py:18
  137.8 2.6 %row_gradient.2 = (bf16[64,8192]{1,0:T(8,128)(2,1)}, bf16[64,8192]{1,0:T(8,128)(2,1)S(1)}) custom-call(s32[1]{0:T(128)} %bitcast.1.me_ref, bf16[1,2,64,8192]{3,2,1,0:T(8,128)(2,1)S(1)} %copy-done.1, bf16[2,64,8192]{2,1,0:T(8,128)(2,1)S(1)} %copy-done.2, bf16[64,2048]{1,0:T(8,128)(2,1)S(1)} %copy-done.10, ...), custom_call_target="tpu_custom_call" | custom-call | flops 6291456 | bytes 5242880 | tf_op jit(solution)/shard_map/row_gradient/pallas_call | solution.py:279
  140.4 1.0 copy-done.5
  141.4 1.3 collective-permute-start.19
  142.7 1.2 copy-done.4
  143.9 2.5 %input_gradient.2.refs_0_ = bf16[1,2,64,8192]{3,2,1,0:T(8,128)(2,1)} custom-call(s32[1]{0:T(128)} %bitcast.is_upper_ref, bf16[64,8192]{1,0:T(8,128)(2,1)} %get-tuple-element.83.upper_ref, bf16[64,8192]{1,0:T(8,128)(2,1)S(1)} %copy-done.4, bf16[64,8192]{1,0:T(8,128)(2,1)} %collective-permute-done.21.passed_ref), custom_call_target="tpu_custom_call" | custom-call | flops 2097152 | bytes 4194304 | tf_op jit(solution)/shard_map/input_gradient/pallas_call | solution.py:305
  146.4 2.5 %input_gradient.3 = bf16[1,2,64,8192]{3,2,1,0:T(8,128)(2,1)} custom-call(s32[1]{0:T(128)} %bitcast.is_upper_ref, bf16[64,8192]{1,0:T(8,128)(2,1)} %get-tuple-element.78.upper_ref, bf16[64,8192]{1,0:T(8,128)(2,1)S(1)} %copy-done.6, bf16[64,8192]{1,0:T(8,128)(2,1)} %collective-permute-done.19.passed_ref, ...), custom_call_target="tpu_custom_call", output_to_operand_aliasing={{}: (4, {})} | custom-call | flops 2097152 | bytes 4194304 | tf_op jit(solution)/shard_map/input_gradient/pallas_call | solution.py:305
  148.9 2.5 %finished_half.6 = (f32[2048,1024]{1,0:T(8,128)}, f32[1,2048]{1,0:T(1,128)}) custom-call(s32[1]{0:T(128)} %bitcast.3.rep_ref, bf16[544,1024]{1,0:T(8,128)(2,1)} %collective-permute-done.23.sum_ref, f32[2048,1024]{1,0:T(8,128)} %get-tuple-element.65.refs_0_, f32[1,2048]{1,0:T(1,128)} %get-tuple-element.66.refs_1_), custom_call_target="tpu_custom_call", output_to_operand_aliasing={{0}: (2, {}), {1}: (3, {})} | custom-call | flops 557056 | bytes 3342336 | tf_op jit(solution)/shard_map/finished_half/pallas_call | solution.py:345
  151.4 1.4 finished_half.7
  (80 shorter events, 8.8 us)
Async XLA Ops:
  0.6 1.6 %copy-start = (bf16[1,2,64,8192]{3,2,1,0:T(8,128)(2,1)S(1)}, bf16[1,2,64,8192]{3,2,1,0:T(8,128)(2,1)}, u32[]{:S(2)}) copy-start(bf16[1,2,64,8192]{3,2,1,0:T(8,128)(2,1)} %x_ref.3) | copy-start | bytes 6291460
  2.2 1.1 copy-start.8
  3.3 12.3 %collective-permute-start = (bf16[128,1024]{1,0:T(8,128)(2,1)S(1)}, bf16[128,1024]{1,0:T(8,128)(2,1)S(1)}, u32[]{:S(2)}, u32[]{:S(2)}) collective-permute-start(bf16[128,1024]{1,0:T(8,128)(2,1)S(1)} %bitcast.13), channel_id=1, source_target_pairs={{0,1},{1,2},{2,3},{3,0},{4,5},{5,6},{6,7},{7,4},{8,9},{9,10},{10,1... | collective-permute-start | bytes 786440 | tf_op jit(solution)/shard_map/ppermute | solution.py:18
  6.4 23.9 %collective-permute-start.3 = (bf16[128,2048]{1,0:T(8,128)(2,1)S(1)}, bf16[128,2048]{1,0:T(8,128)(2,1)S(1)}, u32[]{:S(2)}, u32[]{:S(2)}) collective-permute-start(bf16[128,2048]{1,0:T(8,128)(2,1)S(1)} %get-tuple-element.49), channel_id=1, source_target_pairs={{0,4},{4,0},{8,12},{12,8},{1,5},{5,1},{9,13},{13,9},{2,6},{6,2},{1... | collective-permute-start | bytes 1572872 | tf_op jit(solution)/shard_map/ppermute | solution.py:23
  7.9 30.6 %copy-start.13 = (bf16[1,2048]{1,0:T(2,128)(2,1)S(1)}, bf16[1,2048]{1,0:T(2,128)(2,1)}, u32[]{:S(2)}) copy-start(bf16[1,2048]{1,0:T(2,128)(2,1)} %refs_5_.1) | copy-start | bytes 12292
  7.9 24.3 %collective-permute-start.4 = (bf16[128,2048]{1,0:T(8,128)(2,1)S(1)}, bf16[128,2048]{1,0:T(8,128)(2,1)S(1)}, u32[]{:S(2)}, u32[]{:S(2)}) collective-permute-start(bf16[128,2048]{1,0:T(8,128)(2,1)S(1)} %get-tuple-element.50), channel_id=1, source_target_pairs={{0,8},{4,12},{8,0},{12,4},{1,9},{5,13},{9,1},{13,5},{2,10},{6,14},... | collective-permute-start | bytes 1572872 | tf_op jit(solution)/shard_map/ppermute | solution.py:23
  9.4 29.1 %copy-start.7 = (bf16[1,2048,1024]{2,1,0:T(8,128)(2,1)S(1)}, bf16[1,2048,1024]{2,1,0:T(8,128)(2,1)}, u32[]{:S(2)}) copy-start(bf16[1,2048,1024]{2,1,0:T(8,128)(2,1)} %param.7) | copy-start | bytes 12582916
  9.4 22.8 %collective-permute-start.5 = (bf16[128,2048]{1,0:T(8,128)(2,1)S(1)}, bf16[128,2048]{1,0:T(8,128)(2,1)S(1)}, u32[]{:S(2)}, u32[]{:S(2)}) collective-permute-start(bf16[128,2048]{1,0:T(8,128)(2,1)S(1)} %get-tuple-element.51), channel_id=1, source_target_pairs={{0,12},{4,8},{8,4},{12,0},{1,13},{5,9},{9,5},{13,1},{2,14},{6,10},... | collective-permute-start | bytes 1572872 | tf_op jit(solution)/shard_map/ppermute | solution.py:23
  9.9 16.2 %collective-permute-start.1 = (bf16[128,1024]{1,0:T(8,128)(2,1)S(1)}, bf16[128,1024]{1,0:T(8,128)(2,1)S(1)}, u32[]{:S(2)}, u32[]{:S(2)}) collective-permute-start(bf16[128,1024]{1,0:T(8,128)(2,1)S(1)} %bitcast.14), channel_id=1, source_target_pairs={{0,2},{1,3},{2,0},{3,1},{4,6},{5,7},{6,4},{7,5},{8,10},{9,11},{10,... | collective-permute-start | bytes 786440 | tf_op jit(solution)/shard_map/ppermute | solution.py:18
  15.6 14.6 %collective-permute-start.2 = (bf16[128,1024]{1,0:T(8,128)(2,1)S(1)}, bf16[128,1024]{1,0:T(8,128)(2,1)S(1)}, u32[]{:S(2)}, u32[]{:S(2)}) collective-permute-start(bf16[128,1024]{1,0:T(8,128)(2,1)S(1)} %bitcast.15), channel_id=1, source_target_pairs={{0,3},{1,0},{2,1},{3,2},{4,7},{5,4},{6,5},{7,6},{8,11},{9,8},{10,9... | collective-permute-start | bytes 786440 | tf_op jit(solution)/shard_map/ppermute | solution.py:18
  33.4 8.3 %copy-start.14 = (bf16[512,512]{1,0:T(8,128)(2,1)}, bf16[512,512]{1,0:T(8,128)(2,1)S(1)}, u32[]{:S(2)}) copy-start(bf16[512,512]{1,0:T(8,128)(2,1)S(1)} %get-tuple-element.52.refs_0_) | copy-start | bytes 1572868
  33.4 15.4 %collective-permute-start.6 = (bf16[512,512]{1,0:T(8,128)(2,1)S(1)}, bf16[512,512]{1,0:T(8,128)(2,1)S(1)}, u32[]{:S(2)}, u32[]{:S(2)}) collective-permute-start(bf16[512,512]{1,0:T(8,128)(2,1)S(1)} %get-tuple-element.53), channel_id=1, source_target_pairs={{0,1},{1,2},{2,3},{3,0},{4,5},{5,6},{6,7},{7,4},{8,9},{9,10},{10,1... | collective-permute-start | bytes 1572872 | tf_op jit(solution)/shard_map/ppermute | solution.py:18
  35.0 37.1 %collective-permute-start.9 = (bf16[512,1024]{1,0:T(8,128)(2,1)S(1)}, bf16[512,1024]{1,0:T(8,128)(2,1)S(1)}, u32[]{:S(2)}, u32[]{:S(2)}) collective-permute-start(bf16[512,1024]{1,0:T(8,128)(2,1)S(1)} %pad_maximum_fusion.refs_4_), channel_id=1, source_target_pairs={{0,4},{4,0},{8,12},{12,8},{1,5},{5,1},{9,13},{13,9},{2,6},{6,2},{1... | collective-permute-start | bytes 3145736 | tf_op jit(solution)/shard_map/ppermute | solution.py:23
  36.2 45.7 %collective-permute-start.10 = (bf16[512,1024]{1,0:T(8,128)(2,1)S(1)}, bf16[512,1024]{1,0:T(8,128)(2,1)}, u32[]{:S(2)}, u32[]{:S(2)}) collective-permute-start(bf16[512,1024]{1,0:T(8,128)(2,1)S(1)} %pad_maximum_fusion.refs_4_), channel_id=1, source_target_pairs={{0,8},{4,12},{8,0},{12,4},{1,9},{5,13},{9,1},{13,5},{2,10},{6,14},... | collective-permute-start | bytes 3145736 | tf_op jit(solution)/shard_map/ppermute | solution.py:23
  37.1 44.9 %collective-permute-start.11 = (bf16[512,1024]{1,0:T(8,128)(2,1)S(1)}, bf16[512,1024]{1,0:T(8,128)(2,1)}, u32[]{:S(2)}, u32[]{:S(2)}) collective-permute-start(bf16[512,1024]{1,0:T(8,128)(2,1)S(1)} %pad_maximum_fusion.refs_4_), channel_id=1, source_target_pairs={{0,12},{4,8},{8,4},{12,0},{1,13},{5,9},{9,5},{13,1},{2,14},{6,10},... | collective-permute-start | bytes 3145736 | tf_op jit(solution)/shard_map/ppermute | solution.py:23
  42.4 0.7 copy-start.11
  46.6 0.7 copy-start.28
  47.4 24.8 %collective-permute-start.7 = (bf16[512,512]{1,0:T(8,128)(2,1)}, bf16[512,512]{1,0:T(8,128)(2,1)}, u32[]{:S(2)}, u32[]{:S(2)}) collective-permute-start(bf16[512,512]{1,0:T(8,128)(2,1)} %get-tuple-element.54), channel_id=1, source_target_pairs={{0,2},{1,3},{2,0},{3,1},{4,6},{5,7},{6,4},{7,5},{8,10},{9,11},{10,... | collective-permute-start | bytes 1572872 | tf_op jit(solution)/shard_map/ppermute | solution.py:18
  48.7 0.8 copy-start.16
  49.5 22.6 %collective-permute-start.8 = (bf16[512,512]{1,0:T(8,128)(2,1)}, bf16[512,512]{1,0:T(8,128)(2,1)}, u32[]{:S(2)}, u32[]{:S(2)}) collective-permute-start(bf16[512,512]{1,0:T(8,128)(2,1)} %get-tuple-element.57), channel_id=1, source_target_pairs={{0,3},{1,0},{2,1},{3,2},{4,7},{5,4},{6,5},{7,6},{8,11},{9,8},{10,9... | collective-permute-start | bytes 1572872 | tf_op jit(solution)/shard_map/ppermute | solution.py:18
  82.0 1.0 copy-start.15
  83.0 1.0 copy-start.17
  84.0 6.5 %copy-start.29 = (bf16[64,2048]{1,0:T(8,128)(2,1)S(1)}, bf16[64,2048]{1,0:T(8,128)(2,1)}, u32[]{:S(2)}) copy-start(bf16[64,2048]{1,0:T(8,128)(2,1)} %copy-done.28) | copy-start | bytes 786436
  84.0 9.8 %copy-start.27 = (bf16[64,2048]{1,0:T(8,128)(2,1)S(1)}, bf16[64,2048]{1,0:T(8,128)(2,1)}, u32[]{:S(2)}) copy-start(bf16[64,2048]{1,0:T(8,128)(2,1)} %copy-done.26) | copy-start | bytes 786436
  84.0 10.7 %copy-start.25 = (bf16[64,2048]{1,0:T(8,128)(2,1)S(1)}, bf16[64,2048]{1,0:T(8,128)(2,1)}, u32[]{:S(2)}) copy-start(bf16[64,2048]{1,0:T(8,128)(2,1)} %copy-done.24) | copy-start | bytes 786436
  84.1 16.6 %copy-start.23 = (bf16[64,2048]{1,0:T(8,128)(2,1)S(1)}, bf16[64,2048]{1,0:T(8,128)(2,1)}, u32[]{:S(2)}) copy-start(bf16[64,2048]{1,0:T(8,128)(2,1)} %copy-done.22) | copy-start | bytes 786436
  84.1 38.7 %copy-start.21 = (bf16[64,2048]{1,0:T(8,128)(2,1)S(1)}, bf16[64,2048]{1,0:T(8,128)(2,1)}, u32[]{:S(2)}) copy-start(bf16[64,2048]{1,0:T(8,128)(2,1)} %copy-done.20) | copy-start | bytes 786436
  89.9 33.0 %copy-start.19 = (bf16[64,2048]{1,0:T(8,128)(2,1)S(1)}, bf16[64,2048]{1,0:T(8,128)(2,1)}, u32[]{:S(2)}) copy-start(bf16[64,2048]{1,0:T(8,128)(2,1)} %copy-done.18) | copy-start | bytes 786436
  89.9 33.0 %collective-permute-start.13 = (bf16[272,1024]{1,0:T(8,128)(2,1)S(1)}, bf16[272,1024]{1,0:T(8,128)(2,1)S(1)}, u32[]{:S(2)}, u32[]{:S(2)}) collective-permute-start(bf16[272,1024]{1,0:T(8,128)(2,1)S(1)} %get-tuple-element.62), channel_id=1, source_target_pairs={{0,4},{4,0},{8,12},{12,8},{1,5},{5,1},{9,13},{13,9},{2,6},{6,2},{1... | collective-permute-start | bytes 1671176 | tf_op jit(solution)/shard_map/ppermute | solution.py:23
  90.5 10.1 %collective-permute-start.14 = (bf16[64,2048]{1,0:T(8,128)(2,1)S(1)}, bf16[64,2048]{1,0:T(8,128)(2,1)S(1)}, u32[]{:S(2)}, u32[]{:S(2)}) collective-permute-start(bf16[64,2048]{1,0:T(8,128)(2,1)S(1)} %copy-done.29), channel_id=1, source_target_pairs={{0,3},{1,0},{2,1},{3,2},{4,7},{5,4},{6,5},{7,6},{8,11},{9,8},{10,9... | collective-permute-start | bytes 786440 | tf_op jit(solution)/shard_map/ppermute | solution.py:18
  93.9 28.9 %collective-permute-start.16 = (bf16[64,2048]{1,0:T(8,128)(2,1)S(1)}, bf16[64,2048]{1,0:T(8,128)(2,1)S(1)}, u32[]{:S(2)}, u32[]{:S(2)}) collective-permute-start(bf16[64,2048]{1,0:T(8,128)(2,1)S(1)} %copy-done.27), channel_id=1, source_target_pairs={{0,2},{1,3},{2,0},{3,1},{4,6},{5,7},{6,4},{7,5},{8,10},{9,11},{10,... | collective-permute-start | bytes 786440 | tf_op jit(solution)/shard_map/ppermute | solution.py:18
  93.9 30.2 %collective-permute-start.12 = (bf16[272,1024]{1,0:T(8,128)(2,1)S(1)}, bf16[272,1024]{1,0:T(8,128)(2,1)S(1)}, u32[]{:S(2)}, u32[]{:S(2)}) collective-permute-start(bf16[272,1024]{1,0:T(8,128)(2,1)S(1)} %get-tuple-element.61), channel_id=1, source_target_pairs={{0,8},{4,12},{8,0},{12,4},{1,9},{5,13},{9,1},{13,5},{2,10},{6,14},... | collective-permute-start | bytes 1671176 | tf_op jit(solution)/shard_map/ppermute | solution.py:23
  94.7 29.9 %collective-permute-start.20 = (bf16[64,2048]{1,0:T(8,128)(2,1)S(1)}, bf16[64,2048]{1,0:T(8,128)(2,1)S(1)}, u32[]{:S(2)}, u32[]{:S(2)}) collective-permute-start(bf16[64,2048]{1,0:T(8,128)(2,1)S(1)} %copy-done.25), channel_id=1, source_target_pairs={{0,1},{1,2},{2,3},{3,0},{4,5},{5,6},{6,7},{7,4},{8,9},{9,10},{10,1... | collective-permute-start | bytes 786440 | tf_op jit(solution)/shard_map/ppermute | solution.py:18
  100.7 32.4 %collective-permute-start.15 = (bf16[64,2048]{1,0:T(8,128)(2,1)S(1)}, bf16[64,2048]{1,0:T(8,128)(2,1)S(1)}, u32[]{:S(2)}, u32[]{:S(2)}) collective-permute-start(bf16[64,2048]{1,0:T(8,128)(2,1)S(1)} %copy-done.23), channel_id=1, source_target_pairs={{0,3},{1,0},{2,1},{3,2},{4,7},{5,4},{6,5},{7,6},{8,11},{9,8},{10,9... | collective-permute-start | bytes 786440 | tf_op jit(solution)/shard_map/ppermute | solution.py:18
  122.7 15.1 %collective-permute-start.17 = (bf16[64,2048]{1,0:T(8,128)(2,1)S(1)}, bf16[64,2048]{1,0:T(8,128)(2,1)S(1)}, u32[]{:S(2)}, u32[]{:S(2)}) collective-permute-start(bf16[64,2048]{1,0:T(8,128)(2,1)S(1)} %copy-done.21), channel_id=1, source_target_pairs={{0,2},{1,3},{2,0},{3,1},{4,6},{5,7},{6,4},{7,5},{8,10},{9,11},{10,... | collective-permute-start | bytes 786440 | tf_op jit(solution)/shard_map/ppermute | solution.py:18
  122.9 15.0 %collective-permute-start.18 = (bf16[64,2048]{1,0:T(8,128)(2,1)S(1)}, bf16[64,2048]{1,0:T(8,128)(2,1)S(1)}, u32[]{:S(2)}, u32[]{:S(2)}) collective-permute-start(bf16[64,2048]{1,0:T(8,128)(2,1)S(1)} %copy-done.19), channel_id=1, source_target_pairs={{0,1},{1,2},{2,3},{3,0},{4,5},{5,6},{6,7},{7,4},{8,9},{9,10},{10,1... | collective-permute-start | bytes 786440 | tf_op jit(solution)/shard_map/ppermute | solution.py:18
  124.1 24.9 %collective-permute-start.23 = (bf16[544,1024]{1,0:T(8,128)(2,1)S(1)}, bf16[544,1024]{1,0:T(8,128)(2,1)}, u32[]{:S(2)}, u32[]{:S(2)}) collective-permute-start(bf16[544,1024]{1,0:T(8,128)(2,1)S(1)} %constant_dynamic-update-slice_fusion.2.sum_ref), channel_id=1, source_target_pairs={{0,8},{4,12},{8,0},{12,4},{1,9},{5,13},{9,1},{13,5},{2,10},{6,14},... | collective-permute-start | bytes 3342344 | tf_op jit(solution)/shard_map/ppermute | solution.py:23
  124.6 26.8 %collective-permute-start.22 = (bf16[544,1024]{1,0:T(8,128)(2,1)S(1)}, bf16[544,1024]{1,0:T(8,128)(2,1)S(1)}, u32[]{:S(2)}, u32[]{:S(2)}) collective-permute-start(bf16[544,1024]{1,0:T(8,128)(2,1)S(1)} %constant_dynamic-update-slice_fusion.sum_ref), channel_id=1, source_target_pairs={{0,4},{4,0},{8,12},{12,8},{1,5},{5,1},{9,13},{13,9},{2,6},{6,2},{1... | collective-permute-start | bytes 3342344 | tf_op jit(solution)/shard_map/ppermute | solution.py:23
  126.7 2.3 %copy-start.1 = (bf16[1,2,64,8192]{3,2,1,0:T(8,128)(2,1)S(1)}, bf16[1,2,64,8192]{3,2,1,0:T(8,128)(2,1)}, u32[]{:S(2)}) copy-start(bf16[1,2,64,8192]{3,2,1,0:T(8,128)(2,1)} %x_ref.3) | copy-start | bytes 6291460
  126.7 3.0 %copy-start.2 = (bf16[2,64,8192]{2,1,0:T(8,128)(2,1)S(1)}, bf16[2,64,8192]{2,1,0:T(8,128)(2,1)}, u32[]{:S(2)}) copy-start(bf16[2,64,8192]{2,1,0:T(8,128)(2,1)} %top_ref.3) | copy-start | bytes 6291460
  126.7 3.0 %copy-start.12 = (bf16[64,2048]{1,0:T(8,128)(2,1)S(1)}, bf16[64,2048]{1,0:T(8,128)(2,1)}, u32[]{:S(2)}) copy-start(bf16[64,2048]{1,0:T(8,128)(2,1)} %copy-done.11) | copy-start | bytes 786436
  129.6 8.2 %copy-start.10 = (bf16[64,2048]{1,0:T(8,128)(2,1)S(1)}, bf16[64,2048]{1,0:T(8,128)(2,1)}, u32[]{:S(2)}) copy-start(bf16[64,2048]{1,0:T(8,128)(2,1)} %copy-done.9) | copy-start | bytes 786436
  132.1 1.0 copy-start.3
  133.1 9.6 %collective-permute-start.21 = (bf16[64,8192]{1,0:T(8,128)(2,1)}, bf16[64,8192]{1,0:T(8,128)(2,1)}, u32[]{:S(2)}, u32[]{:S(2)}) collective-permute-start(bf16[64,8192]{1,0:T(8,128)(2,1)} %get-tuple-element.83.upper_ref), channel_id=1, source_target_pairs={{16,0},{17,1},{18,2},{19,3},{20,4},{21,5},{22,6},{23,7},{24,8},{25... | collective-permute-start | bytes 3145736 | tf_op jit(solution)/shard_map/ppermute | solution.py:420
  140.4 1.0 copy-start.5
  141.4 5.1 %collective-permute-start.19 = (bf16[64,8192]{1,0:T(8,128)(2,1)}, bf16[64,8192]{1,0:T(8,128)(2,1)}, u32[]{:S(2)}, u32[]{:S(2)}) collective-permute-start(bf16[64,8192]{1,0:T(8,128)(2,1)} %get-tuple-element.78.upper_ref), channel_id=1, source_target_pairs={{16,0},{17,1},{18,2},{19,3},{20,4},{21,5},{22,6},{23,7},{24,8},{25... | collective-permute-start | bytes 3145736 | tf_op jit(solution)/shard_map/ppermute | solution.py:420
  142.7 1.2 copy-start.4
  143.9 2.5 %copy-start.6 = (bf16[64,8192]{1,0:T(8,128)(2,1)S(1)}, bf16[64,8192]{1,0:T(8,128)(2,1)}, u32[]{:S(2)}) copy-start(bf16[64,8192]{1,0:T(8,128)(2,1)} %copy-done.5) | copy-start | bytes 3145732
  (6 other events, 4.2 us)

commit v5 on v4

--- a/solution.py
+++ b/solution.py
@@ -80,9 +80,35 @@
     return [list(outs[c * reps : (c + 1) * reps]) for c in range(chunks)]
 
 
+def joined(arrays):
+    rows, width = arrays[0].shape
+    if rows % 16 or width % 128:
+        return jnp.concatenate(arrays, axis=0)
+
+    def kernel(*refs):
+        copies = []
+        for k in range(len(arrays)):
+            target = refs[-2].at[k * rows : (k + 1) * rows, :]
+            copies.append(pltpu.make_async_copy(refs[k], target, refs[-1].at[k]))
+            copies[-1].start()
+        for copy in copies:
+            copy.wait()
+
+    return pl.pallas_call(
+        kernel,
+        out_shape=jax.ShapeDtypeStruct((len(arrays) * rows, width), bf16),
+        in_specs=[ANY_ARG] * len(arrays),
+        out_specs=ANY_ARG,
+        scratch_shapes=[pltpu.SemaphoreType.DMA((len(arrays),))],
+        compiler_params=params(4),
+        cost_estimate=cost(0, 4 * len(arrays) * rows * width),
+        name="joined",
+    )(*arrays)
+
+
 def doubled(value, order):
     for bit in order[:-1]:
-        value = jnp.concatenate([value, flipped(value, "rep", 1 << bit)], axis=0)
+        value = joined([value, flipped(value, "rep", 1 << bit)])
     return value, flipped(value, "rep", 1 << order[-1])
 
 
@@ -122,7 +148,7 @@
     )
 
 
-def weight_product(columns, values, weight, gain, groups, count, norm_scale):
+def weight_product(columns, values, weight, gain, rep, groups, count, norm_scale):
     rows, width = columns[0].shape
     reps = len(values)
     tokens = rows // reps
@@ -141,8 +167,10 @@
         raw = lax.dot_general(
             jnp.concatenate(columns, axis=0), order.reshape(-1, features), contract, preferred_element_type=f32
         )
-        dots = jnp.sum(raw * weight.astype(f32), axis=1) * norm_scale
-        raw = (raw * gain).astype(bf16)
+        own = lax.dynamic_slice_in_dim(weight, rep[0] * width, width, 0).astype(f32)
+        dots = jnp.sum(raw * own, axis=1) * norm_scale
+        factor = lax.dynamic_slice_in_dim(gain[0], rep[0] * width, width, 0).astype(f32) * norm_scale
+        raw = (raw * factor[:, None]).astype(bf16)
         outs = []
         for c in range(count):
             at = slice(c * chunk, (c + 1) * chunk)
@@ -150,9 +178,10 @@
             outs.append(jnp.concatenate([raw[at], jnp.pad(under, ((0, 0), (0, features - chunk)))], axis=0))
         return outs
 
-    def kernel(*refs):
+    def kernel(rep_ref, *refs):
         column_refs, value_refs = refs[:groups], refs[groups : groups + reps]
         weight_ref, gain_ref = refs[groups + reps], refs[groups + reps + 1]
+        start = pl.multiple_of(rep_ref[0] * width, width)
         out_refs = refs[groups + reps + 2 : -5]
         left, right, own, total, sems = refs[-5:]
         copies = []
@@ -165,7 +194,7 @@
             for copy in line:
                 copy.start()
             copies.append(line)
-        copy = pltpu.make_async_copy(weight_ref, own, sems.at[groups, 0])
+        copy = pltpu.make_async_copy(weight_ref.at[pl.ds(start, width), :], own, sems.at[groups, 0])
         copy.start()
         for j in range(groups):
             for c in copies[j]:
@@ -181,7 +210,9 @@
         for c in range(count):
             at = slice(c * chunk, (c + 1) * chunk)
             raw = total[c]
-            out_refs[c][:chunk, :] = (raw * gain_ref[at, :]).astype(bf16)
+            factor = gain_ref[:, pl.ds(pl.multiple_of(start + c * chunk, chunk), chunk)].astype(f32) * norm_scale
+            factor = jnp.transpose(jnp.broadcast_to(factor, (128, chunk)))[:, 0:1]
+            out_refs[c][:chunk, :] = (raw * factor).astype(bf16)
             dots = lax.dot_general(
                 jnp.full((8, features), norm_scale, f32),
                 raw * own[at, :].astype(f32),
@@ -196,7 +227,7 @@
     return pl.pallas_call(
         kernel,
         out_shape=[jax.ShapeDtypeStruct((chunk + 16, features), bf16)] * count,
-        in_specs=[ANY_ARG] * (groups + reps + 1) + [pl.BlockSpec(memory_space=pltpu.VMEM)],
+        in_specs=[SMEM_ARG] + [ANY_ARG] * (groups + reps + 1) + [pl.BlockSpec(memory_space=pltpu.VMEM)],
         scratch_shapes=[
             pltpu.VMEM((groups, rows, width), bf16),
             pltpu.VMEM((groups, rows, features), bf16),
@@ -204,10 +235,10 @@
             pltpu.VMEM((count, chunk, features), f32),
             pltpu.SemaphoreType.DMA((groups + 1, reps + 1)),
         ],
-        compiler_params=params(24),
+        compiler_params=params(16),
         cost_estimate=cost(2 * groups * rows * width * features, 2 * groups * rows * (width + features) + 4 * width * features),
         name="weight_product",
-    )(*columns, *values, weight, gain)
+    )(rep, *columns, *values, weight, gain)
 
 
 def returned_blocks(slots, weight, gain, micro):
@@ -374,35 +405,35 @@
     orders = [tuple(range(bits)), tuple(reversed(range(bits)))]
 
     weight = value_weight[0]
-    piece = weight.shape[0] // reps
-    own_weight = lax.dynamic_slice_in_dim(weight, rep[0] * piece, piece, 0)
-    own_gain = lax.dynamic_slice_in_dim(norm_gain[0], rep[0] * piece, piece, 0).astype(f32)[:, None] * norm_scale
-
-    hats = scaled_blocks(layer_input[0].reshape(tokens, width), me, rep, groups, reps, 1)[0]
+    is_upper = lax.axis_index("section").astype(jnp.int32)[None]
+    inputs = after(layer_input[0].reshape(tokens, width), me, rep, is_upper)
+
+    hats = scaled_blocks(inputs, me, rep, groups, reps, 1)[0]
     plane = list(hats)
     for e in range(1, reps):
         plane[e] = flipped(hats[e], "rep", e)
     grads = after(value_grad[0].reshape(tokens, -1), hats[0])
     slots = [grads] + [cyclic(grads, "fsdp", j) for j in range(1, groups)]
 
+    plane[0] = after(plane[0], *slots[1:])
     sent = regrouped(plane, groups)
     back = returned_blocks(slots, weight, norm_gain, micro)
     columns = list(sent)
     for j in range(1, groups):
         columns[j] = cyclic(after(sent[j], back[0][0]) if j == groups - 1 else sent[j], "fsdp", j)
-    held = after(jnp.concatenate(slots, axis=0), sent[0])
+    held = after(joined(slots), sent[0])
     values = [held if e == 0 else flipped(held, "rep", e) for e in range(reps)]
 
-    lines = []
-    ties = [columns[1:2], columns[2:]]
-    for m in range(micro):
-        line = [back[j][m] for j in range(groups)]
-        for j in range(1, groups):
-            line[j] = cyclic(after(line[j], *ties[min(j - 1, 1)]), "fsdp", -j)
-        ties = [line[1:2], line[2:3]]
-        lines.append(line)
-    own = (after(own_weight, back[0][0]), after(own_gain, back[0][0]))
-    sums = weight_product(columns, values, *own, groups, chunks, norm_scale)
+    lines = [[back[j][m] for j in range(groups)] for m in range(micro)]
+    far = groups // 2
+    near = [(m, j) for m in range(micro) for j in range(1, groups) if j != far]
+    for chain in (near, [(m, far) for m in range(micro)]):
+        ties = [columns[1]]
+        for m, j in chain:
+            lines[m][j] = cyclic(after(lines[m][j], *ties), "fsdp", -j)
+            ties = [lines[m][j]]
+    columns[0] = after(columns[0], lines[0][1])
+    sums = weight_product(columns, values, weight, norm_gain, rep, groups, chunks, norm_scale)
     gathered = [doubled(sums[c], orders[c]) for c in range(chunks)]
     finished = ()
     for half in (0, 1):
@@ -413,9 +444,9 @@
     weight_grad, gain_grad = finished
 
     result = ()
-    is_upper = lax.axis_index("section").astype(jnp.int32)[None]
     for m in range(micro):
-        lines[m][0] = after(lines[m][0], *([g[0] for g in gathered] if m == 0 else early))
+        ties = [lines[-1][1], *[g[0] for g in gathered]] if m == 0 else [*finished, *result]
+        lines[m][0] = after(lines[m][0], *ties)
         upper, piece = row_gradient(layer_input, top_grad, lines[m], me, m)
         passed = lax.ppermute(upper, "section", [(1, 0)])
         result = (input_gradient(upper, piece, passed, is_upper, layer_input.shape, m, result),)

time: 155 us -> 150 us (0.968); the launches traced: 153 us -> 150 us
  waiting for transfers between devices: 73.3 us -> 94.8 us
  local copies, waits for them, and re-layouts: 16.5 us -> 1.6 us
  Pallas kernels: 27.9 us -> 21.2 us
  starting transfers between devices: 34.1 us -> 31.6 us
    ppermute x12, waiting for transfers between devices: 61.5 us -> 89.6 us  [cyclic(): lax.ppermute(value, axis, [(i, (i + steps) % count) for i in range(count)])]
    unnamed x62 -> x12, local copies, waits for them, and re-layouts: 15 us -> 1.6 us
    ppermute x10, waiting for transfers between devices: 11.7 us -> 1.98 us  [flipped(): return lax.ppermute(value, axis, [(i, i ^ mask) for i in range(count)])]
    ppermute x12, starting transfers between devices: 22 us -> 17.7 us  [cyclic(): lax.ppermute(value, axis, [(i, (i + steps) % count) for i in range(count)])]
    ppermute x2, waiting for transfers between devices: 0.01 us -> 3.26 us  [local(): passed = lax.ppermute(upper, 'section', [(1, 0)])]
    pallas_call x2, Pallas kernels: 5.01 us -> 2.21 us  [input_gradient(): pl.pallas_call(kernel, grid=(rows // step,), out_shape=jax.ShapeDtypeStru...]
    pallas_call x2, Pallas kernels: 5.05 us -> 3 us  [row_gradient(): pl.pallas_call(kernel, grid=(rows // step,), out_shape=[jax.ShapeDtypeStr...]
    ppermute x10, starting transfers between devices: 9.6 us -> 11.3 us  [flipped(): return lax.ppermute(value, axis, [(i, i ^ mask) for i in range(count)])]
  transfers between devices with their start and end apart: 24 -> 24, of which waited for: 9 -> 13; matrix products, arithmetic and copies ran while one was open for 1% -> 0% of each run, Pallas kernels for 12% -> 8%
where the time goes in v5:
time: 150 us
  waiting for transfers between devices  94.8 us (63%)
  starting transfers between devices  31.6 us (21%)
  Pallas kernels  21.2 us (14%)
  local copies, waits for them, and re-layouts  1.6 us (1%)
    ppermute x12, waiting for transfers between devices, cyclic(): lax.ppermute(value, axis, [(i, (i + steps) % count) for i in range(count)])  89.6 us
    ppermute x12, starting transfers between devices, cyclic(): lax.ppermute(value, axis, [(i, (i + steps) % count) for i in range(count)])  17.7 us
    ppermute x10, starting transfers between devices, flipped(): return lax.ppermute(value, axis, [(i, i ^ mask) for i in range(count)])  11.3 us
    pallas_call x4, Pallas kernels, finished_half(): pl.pallas_call(kernel, grid_spec=pltpu.PrefetchScalarGridSpec(num_scalar_...  5.61 us
    pallas_call x1, Pallas kernels, weight_product(): pl.pallas_call(kernel, out_shape=[jax.ShapeDtypeStruct((chunk + 16, featu...  5.12 us
    ppermute x2, waiting for transfers between devices, local(): passed = lax.ppermute(upper, 'section', [(1, 0)])  3.26 us
    pallas_call x1, Pallas kernels, returned_blocks(): pl.pallas_call(kernel, grid=(shard // tile,), out_shape=[jax.ShapeDtypeSt...  3.25 us
  transfers between devices with their start and end apart: 24, of which 13 were waited for; matrix products, arithmetic and copies ran while one was open for 0% of the time, Pallas kernels for 8%

profile of v5, /device:TPU:0, one launch (start us, length us, event | category | flops | bytes accessed | tf_op | source)
XLA Modules:
  0.0 150.0 jit_solution(12736556289496486215)
XLA Ops:
  0.6 1.6 %copy-done = bf16[1,2,64,8192]{3,2,1,0:T(8,128)(2,1)S(1)} copy-done((bf16[1,2,64,8192]{3,2,1,0:T(8,128)(2,1)S(1)}, bf16[1,2,64,8192]{3,2,1,0:T(8,128)(2,1)}, u32[]{:S(2)}) %copy-start) | copy-done | bytes 2097176
  2.2 1.1 scaled_blocks.1
  3.3 3.1 %collective-permute-start = (bf16[128,1024]{1,0:T(8,128)(2,1)S(1)}, bf16[128,1024]{1,0:T(8,128)(2,1)S(1)}, u32[]{:S(2)}, u32[]{:S(2)}) collective-permute-start(bf16[128,1024]{1,0:T(8,128)(2,1)S(1)} %bitcast.10), channel_id=1, source_target_pairs={{0,1},{1,2},{2,3},{3,0},{4,5},{5,6},{6,7},{7,4},{8,9},{9,10},{10,1... | collective-permute-start | bytes 786440 | tf_op jit(solution)/shard_map/ppermute | solution.py:18
  6.4 1.5 collective-permute-start.3
  7.9 1.5 %collective-permute-start.4 = (bf16[128,2048]{1,0:T(8,128)(2,1)S(1)}, bf16[128,2048]{1,0:T(8,128)(2,1)S(1)}, u32[]{:S(2)}, u32[]{:S(2)}) collective-permute-start(bf16[128,2048]{1,0:T(8,128)(2,1)S(1)} %get-tuple-element.53), channel_id=1, source_target_pairs={{0,8},{4,12},{8,0},{12,4},{1,9},{5,13},{9,1},{13,5},{2,10},{6,14},... | collective-permute-start | bytes 1572872 | tf_op jit(solution)/shard_map/ppermute | solution.py:23
  9.4 0.5 collective-permute-start.5
  9.9 2.6 %collective-permute-start.1 = (bf16[128,1024]{1,0:T(8,128)(2,1)S(1)}, bf16[128,1024]{1,0:T(8,128)(2,1)S(1)}, u32[]{:S(2)}, u32[]{:S(2)}) collective-permute-start(bf16[128,1024]{1,0:T(8,128)(2,1)S(1)} %bitcast.11), channel_id=1, source_target_pairs={{0,2},{1,3},{2,0},{3,1},{4,6},{5,7},{6,4},{7,5},{8,10},{9,11},{10,... | collective-permute-start | bytes 786440 | tf_op jit(solution)/shard_map/ppermute | solution.py:18
  12.5 3.2 %collective-permute-done.refs_1_ = bf16[128,1024]{1,0:T(8,128)(2,1)S(1)} collective-permute-done((bf16[128,1024]{1,0:T(8,128)(2,1)S(1)}, bf16[128,1024]{1,0:T(8,128)(2,1)S(1)}, u32[]{:S(2)}, u32[]{:S(2)}) %collective-permute-start) | collective-permute-done | bytes 262176 | tf_op jit(solution)/shard_map/ppermute | solution.py:18
  15.6 1.4 collective-permute-start.2
  17.0 9.0 %collective-permute-done.1.refs_2_ = bf16[128,1024]{1,0:T(8,128)(2,1)S(1)} collective-permute-done((bf16[128,1024]{1,0:T(8,128)(2,1)S(1)}, bf16[128,1024]{1,0:T(8,128)(2,1)S(1)}, u32[]{:S(2)}, u32[]{:S(2)}) %collective-permute-start.1) | collective-permute-done | bytes 262176 | tf_op jit(solution)/shard_map/ppermute | solution.py:18
  26.0 4.2 %collective-permute-done.2.refs_3_ = bf16[128,1024]{1,0:T(8,128)(2,1)S(1)} collective-permute-done((bf16[128,1024]{1,0:T(8,128)(2,1)S(1)}, bf16[128,1024]{1,0:T(8,128)(2,1)S(1)}, u32[]{:S(2)}, u32[]{:S(2)}) %collective-permute-start.2) | collective-permute-done | bytes 262176 | tf_op jit(solution)/shard_map/ppermute | solution.py:18
  30.3 2.0 %collective-permute-done.4.refs_2_ = bf16[128,2048]{1,0:T(8,128)(2,1)S(1)} collective-permute-done((bf16[128,2048]{1,0:T(8,128)(2,1)S(1)}, bf16[128,2048]{1,0:T(8,128)(2,1)S(1)}, u32[]{:S(2)}, u32[]{:S(2)}) %collective-permute-start.4) | collective-permute-done | bytes 524320 | tf_op jit(solution)/shard_map/ppermute | solution.py:23
  32.2 0.5 regrouped.1
  32.7 1.6 %collective-permute-start.6 = (bf16[512,512]{1,0:T(8,128)(2,1)S(1)}, bf16[512,512]{1,0:T(8,128)(2,1)S(1)}, u32[]{:S(2)}, u32[]{:S(2)}) collective-permute-start(bf16[512,512]{1,0:T(8,128)(2,1)S(1)} %get-tuple-element.57), channel_id=1, source_target_pairs={{0,1},{1,2},{2,3},{3,0},{4,5},{5,6},{6,7},{7,4},{8,9},{9,10},{10,1... | collective-permute-start | bytes 1572872 | tf_op jit(solution)/shard_map/ppermute | solution.py:18
  34.4 1.3 collective-permute-start.10
  35.7 0.8 collective-permute-start.11
  36.6 1.4 collective-permute-start.12
  38.0 3.2 %returned_blocks.1 = (bf16[64,2048]{1,0:T(8,128)(2,1)S(1)}, bf16[64,2048]{1,0:T(8,128)(2,1)S(1)}, bf16[64,2048]{1,0:T(8,128)(2,1)S(1)}, bf16[64,2048]{1,0:T(8,12...) custom-call(bf16[128,1024]{1,0:T(8,128)(2,1)S(1)} %bitcast.14, ...), custom_call_target="tpu_custom_call" | custom-call | flops 2147483648 | bytes 7340032 | tf_op jit(solution)/shard_map/returned_blocks/pallas_call | solution.py:265
  41.3 5.6 %collective-permute-done.6.refs_1_ = bf16[512,512]{1,0:T(8,128)(2,1)S(1)} collective-permute-done((bf16[512,512]{1,0:T(8,128)(2,1)S(1)}, bf16[512,512]{1,0:T(8,128)(2,1)S(1)}, u32[]{:S(2)}, u32[]{:S(2)}) %collective-permute-start.6) | collective-permute-done | bytes 524320 | tf_op jit(solution)/shard_map/ppermute | solution.py:18
  46.9 0.7 collective-permute-start.7
  47.5 1.5 %collective-permute-start.9 = (bf16[512,512]{1,0:T(8,128)(2,1)S(1)}, bf16[512,512]{1,0:T(8,128)(2,1)S(1)}, u32[]{:S(2)}, u32[]{:S(2)}) collective-permute-start(bf16[512,512]{1,0:T(8,128)(2,1)S(1)} %get-tuple-element.63), channel_id=1, source_target_pairs={{0,3},{1,0},{2,1},{3,2},{4,7},{5,4},{6,5},{7,6},{8,11},{9,8},{10,9... | collective-permute-start | bytes 1572872 | tf_op jit(solution)/shard_map/ppermute | solution.py:18
  49.1 7.1 %collective-permute-done.7.refs_1_ = bf16[64,2048]{1,0:T(8,128)(2,1)S(1)} collective-permute-done((bf16[64,2048]{1,0:T(8,128)(2,1)S(1)}, bf16[64,2048]{1,0:T(8,128)(2,1)S(1)}, u32[]{:S(2)}, u32[]{:S(2)}) %collective-permute-start.7) | collective-permute-done | bytes 262176 | tf_op jit(solution)/shard_map/ppermute | solution.py:18
  56.1 0.7 collective-permute-start.8
  56.8 8.7 %collective-permute-done.9.refs_3_ = bf16[512,512]{1,0:T(8,128)(2,1)S(1)} collective-permute-done((bf16[512,512]{1,0:T(8,128)(2,1)S(1)}, bf16[512,512]{1,0:T(8,128)(2,1)S(1)}, u32[]{:S(2)}, u32[]{:S(2)}) %collective-permute-start.9) | collective-permute-done | bytes 524320 | tf_op jit(solution)/shard_map/ppermute | solution.py:18
  65.6 20.5 %collective-permute-done.8.refs_2_ = bf16[512,512]{1,0:T(8,128)(2,1)S(1)} collective-permute-done((bf16[512,512]{1,0:T(8,128)(2,1)S(1)}, bf16[512,512]{1,0:T(8,128)(2,1)S(1)}, u32[]{:S(2)}, u32[]{:S(2)}) %collective-permute-start.8) | collective-permute-done | bytes 524320 | tf_op jit(solution)/shard_map/ppermute | solution.py:18
  86.1 5.1 %weight_product.1 = (bf16[272,1024]{1,0:T(8,128)(2,1)S(1)}, bf16[272,1024]{1,0:T(8,128)(2,1)S(1)}) custom-call(s32[1]{0:T(128)} %bitcast.3.rep_ref, bf16[512,512]{1,0:T(8,128)(2,1)S(1)} %get-tuple-element.59.refs_0_, bf16[512,512]{1,0:T(8,128)(2,1)S(1)} %collective-permute-done.6.refs_1_, bf16[512,512]{1,0:T(8,128)(2,1)S(1)} %collective-permute-done.8.refs_2_, ...), custom_call_target="tpu_custom_call" | custom-call | flops 2147483648 | bytes 8388608 | tf_op jit(solution)/shard_map/weight_product/pallas_call | solution.py:227
  91.3 1.5 %collective-permute-start.15 = (bf16[272,1024]{1,0:T(8,128)(2,1)S(1)}, bf16[272,1024]{1,0:T(8,128)(2,1)S(1)}, u32[]{:S(2)}, u32[]{:S(2)}) collective-permute-start(bf16[272,1024]{1,0:T(8,128)(2,1)S(1)} %get-tuple-element.66.refs_0_), channel_id=1, source_target_pairs={{0,4},{4,0},{8,12},{12,8},{1,5},{5,1},{9,13},{13,9},{2,6},{6,2},{1... | collective-permute-start | bytes 1671176 | tf_op jit(solution)/shard_map/ppermute | solution.py:23
  92.8 0.6 collective-permute-start.13
  93.3 8.7 %collective-permute-done.17.refs_3_ = bf16[64,2048]{1,0:T(8,128)(2,1)S(1)} collective-permute-done((bf16[64,2048]{1,0:T(8,128)(2,1)S(1)}, bf16[64,2048]{1,0:T(8,128)(2,1)S(1)}, u32[]{:S(2)}, u32[]{:S(2)}) %collective-permute-start.17) | collective-permute-done | bytes 262176 | tf_op jit(solution)/shard_map/ppermute | solution.py:18
  102.1 1.7 %collective-permute-start.18 = (bf16[64,2048]{1,0:T(8,128)(2,1)S(1)}, bf16[64,2048]{1,0:T(8,128)(2,1)S(1)}, u32[]{:S(2)}, u32[]{:S(2)}) collective-permute-start(bf16[64,2048]{1,0:T(8,128)(2,1)S(1)} %get-tuple-element.78), channel_id=1, source_target_pairs={{0,3},{1,0},{2,1},{3,2},{4,7},{5,4},{6,5},{7,6},{8,11},{9,8},{10,9... | collective-permute-start | bytes 786440 | tf_op jit(solution)/shard_map/ppermute | solution.py:18
  103.8 0.2 joined.5.sum_ref
  103.9 1.8 %collective-permute-start.16 = (bf16[544,1024]{1,0:T(8,128)(2,1)S(1)}, bf16[544,1024]{1,0:T(8,128)(2,1)S(1)}, u32[]{:S(2)}, u32[]{:S(2)}) collective-permute-start(bf16[544,1024]{1,0:T(8,128)(2,1)S(1)} %joined.5.sum_ref), channel_id=1, source_target_pairs={{0,8},{4,12},{8,0},{12,4},{1,9},{5,13},{9,1},{13,5},{2,10},{6,14},... | collective-permute-start | bytes 3342344 | tf_op jit(solution)/shard_map/ppermute | solution.py:23
  105.9 0.4 collective-permute-start.14
  106.3 4.2 %collective-permute-done.18.refs_1_ = bf16[64,2048]{1,0:T(8,128)(2,1)S(1)} collective-permute-done((bf16[64,2048]{1,0:T(8,128)(2,1)S(1)}, bf16[64,2048]{1,0:T(8,128)(2,1)S(1)}, u32[]{:S(2)}, u32[]{:S(2)}) %collective-permute-start.18) | collective-permute-done | bytes 262176 | tf_op jit(solution)/shard_map/ppermute | solution.py:18
  110.5 8.3 %collective-permute-done.19.refs_2_ = bf16[64,2048]{1,0:T(8,128)(2,1)S(1)} collective-permute-done((bf16[64,2048]{1,0:T(8,128)(2,1)S(1)}, bf16[64,2048]{1,0:T(8,128)(2,1)S(1)}, u32[]{:S(2)}, u32[]{:S(2)}) %collective-permute-start.19) | collective-permute-done | bytes 262176 | tf_op jit(solution)/shard_map/ppermute | solution.py:18
  118.9 1.5 row_gradient.2
  120.4 1.3 collective-permute-start.20
  121.8 4.4 %collective-permute-start.22 = (bf16[64,2048]{1,0:T(8,128)(2,1)S(1)}, bf16[64,2048]{1,0:T(8,128)(2,1)S(1)}, u32[]{:S(2)}, u32[]{:S(2)}) collective-permute-start(bf16[64,2048]{1,0:T(8,128)(2,1)S(1)} %get-tuple-element.88), channel_id=1, source_target_pairs={{0,1},{1,2},{2,3},{3,0},{4,5},{5,6},{6,7},{7,4},{8,9},{9,10},{10,1... | collective-permute-start | bytes 786440 | tf_op jit(solution)/shard_map/ppermute | solution.py:18
  126.1 1.4 finished_half.4
  127.5 1.4 finished_half.5
  128.9 1.1 input_gradient.2.refs_0_
  130.0 1.4 finished_half.6
  131.4 1.4 finished_half.7
  132.9 10.0 %collective-permute-done.21.refs_2_ = bf16[64,2048]{1,0:T(8,128)(2,1)S(1)} collective-permute-done((bf16[64,2048]{1,0:T(8,128)(2,1)S(1)}, bf16[64,2048]{1,0:T(8,128)(2,1)S(1)}, u32[]{:S(2)}, u32[]{:S(2)}) %collective-permute-start.21) | collective-permute-done | bytes 262176 | tf_op jit(solution)/shard_map/ppermute | solution.py:18
  142.8 1.5 %row_gradient.3 = (bf16[64,8192]{1,0:T(8,128)(2,1)S(1)}, bf16[64,8192]{1,0:T(8,128)(2,1)S(1)}) custom-call(s32[1]{0:T(128)} %bitcast.1.me_ref, bf16[1,2,64,8192]{3,2,1,0:T(8,128)(2,1)S(1)} %copy-done.1, bf16[2,64,8192]{2,1,0:T(8,128)(2,1)S(1)} %copy-done.2, bf16[64,2048]{1,0:T(8,128)(2,1)S(1)} %get-tuple-element.84.refs_0_, ...), custom_call_target="tpu_custom_call" | custom-call | flops 6291456 | bytes 5242880 | tf_op jit(solution)/shard_map/row_gradient/pallas_call | solution.py:310
  144.3 1.3 collective-permute-start.23
  145.6 3.3 %collective-permute-done.23.passed_ref = bf16[64,8192]{1,0:T(8,128)(2,1)S(1)} collective-permute-done((bf16[64,8192]{1,0:T(8,128)(2,1)S(1)}, bf16[64,8192]{1,0:T(8,128)(2,1)S(1)}, u32[]{:S(2)}, u32[]{:S(2)}) %collective-permute-start.23) | collective-permute-done | bytes 1048608 | tf_op jit(solution)/shard_map/ppermute | solution.py:451
  148.9 1.1 input_gradient.3
  (27 shorter events, 0.4 us)
Async XLA Ops:
  0.6 1.6 %copy-start = (bf16[1,2,64,8192]{3,2,1,0:T(8,128)(2,1)S(1)}, bf16[1,2,64,8192]{3,2,1,0:T(8,128)(2,1)}, u32[]{:S(2)}) copy-start(bf16[1,2,64,8192]{3,2,1,0:T(8,128)(2,1)} %x_ref.3) | copy-start | bytes 6291460
  2.2 1.1 copy-start.4
  3.3 12.3 %collective-permute-start = (bf16[128,1024]{1,0:T(8,128)(2,1)S(1)}, bf16[128,1024]{1,0:T(8,128)(2,1)S(1)}, u32[]{:S(2)}, u32[]{:S(2)}) collective-permute-start(bf16[128,1024]{1,0:T(8,128)(2,1)S(1)} %bitcast.10), channel_id=1, source_target_pairs={{0,1},{1,2},{2,3},{3,0},{4,5},{5,6},{6,7},{7,4},{8,9},{9,10},{10,1... | collective-permute-start | bytes 786440 | tf_op jit(solution)/shard_map/ppermute | solution.py:18
  6.4 23.9 %collective-permute-start.3 = (bf16[128,2048]{1,0:T(8,128)(2,1)S(1)}, bf16[128,2048]{1,0:T(8,128)(2,1)S(1)}, u32[]{:S(2)}, u32[]{:S(2)}) collective-permute-start(bf16[128,2048]{1,0:T(8,128)(2,1)S(1)} %get-tuple-element.52), channel_id=1, source_target_pairs={{0,4},{4,0},{8,12},{12,8},{1,5},{5,1},{9,13},{13,9},{2,6},{6,2},{1... | collective-permute-start | bytes 1572872 | tf_op jit(solution)/shard_map/ppermute | solution.py:23
  7.9 30.1 %copy-start.5 = (bf16[1,2048]{1,0:T(2,128)(2,1)S(1)}, bf16[1,2048]{1,0:T(2,128)(2,1)}, u32[]{:S(2)}) copy-start(bf16[1,2048]{1,0:T(2,128)(2,1)} %refs_9_.1) | copy-start | bytes 12292
  7.9 24.3 %collective-permute-start.4 = (bf16[128,2048]{1,0:T(8,128)(2,1)S(1)}, bf16[128,2048]{1,0:T(8,128)(2,1)S(1)}, u32[]{:S(2)}, u32[]{:S(2)}) collective-permute-start(bf16[128,2048]{1,0:T(8,128)(2,1)S(1)} %get-tuple-element.53), channel_id=1, source_target_pairs={{0,8},{4,12},{8,0},{12,4},{1,9},{5,13},{9,1},{13,5},{2,10},{6,14},... | collective-permute-start | bytes 1572872 | tf_op jit(solution)/shard_map/ppermute | solution.py:23
  9.4 28.6 %copy-start.3 = (bf16[1,2048,1024]{2,1,0:T(8,128)(2,1)S(1)}, bf16[1,2048,1024]{2,1,0:T(8,128)(2,1)}, u32[]{:S(2)}) copy-start(bf16[1,2048,1024]{2,1,0:T(8,128)(2,1)} %param.7) | copy-start | bytes 12582916
  9.4 22.8 %collective-permute-start.5 = (bf16[128,2048]{1,0:T(8,128)(2,1)S(1)}, bf16[128,2048]{1,0:T(8,128)(2,1)S(1)}, u32[]{:S(2)}, u32[]{:S(2)}) collective-permute-start(bf16[128,2048]{1,0:T(8,128)(2,1)S(1)} %get-tuple-element.54), channel_id=1, source_target_pairs={{0,12},{4,8},{8,4},{12,0},{1,13},{5,9},{9,5},{13,1},{2,14},{6,10},... | collective-permute-start | bytes 1572872 | tf_op jit(solution)/shard_map/ppermute | solution.py:23
  9.9 16.2 %collective-permute-start.1 = (bf16[128,1024]{1,0:T(8,128)(2,1)S(1)}, bf16[128,1024]{1,0:T(8,128)(2,1)S(1)}, u32[]{:S(2)}, u32[]{:S(2)}) collective-permute-start(bf16[128,1024]{1,0:T(8,128)(2,1)S(1)} %bitcast.11), channel_id=1, source_target_pairs={{0,2},{1,3},{2,0},{3,1},{4,6},{5,7},{6,4},{7,5},{8,10},{9,11},{10,... | collective-permute-start | bytes 786440 | tf_op jit(solution)/shard_map/ppermute | solution.py:18
  15.6 14.6 %collective-permute-start.2 = (bf16[128,1024]{1,0:T(8,128)(2,1)S(1)}, bf16[128,1024]{1,0:T(8,128)(2,1)S(1)}, u32[]{:S(2)}, u32[]{:S(2)}) collective-permute-start(bf16[128,1024]{1,0:T(8,128)(2,1)S(1)} %bitcast.12), channel_id=1, source_target_pairs={{0,3},{1,0},{2,1},{3,2},{4,7},{5,4},{6,5},{7,6},{8,11},{9,8},{10,9... | collective-permute-start | bytes 786440 | tf_op jit(solution)/shard_map/ppermute | solution.py:18
  32.7 14.2 %collective-permute-start.6 = (bf16[512,512]{1,0:T(8,128)(2,1)S(1)}, bf16[512,512]{1,0:T(8,128)(2,1)S(1)}, u32[]{:S(2)}, u32[]{:S(2)}) collective-permute-start(bf16[512,512]{1,0:T(8,128)(2,1)S(1)} %get-tuple-element.57), channel_id=1, source_target_pairs={{0,1},{1,2},{2,3},{3,0},{4,5},{5,6},{6,7},{7,4},{8,9},{9,10},{10,1... | collective-permute-start | bytes 1572872 | tf_op jit(solution)/shard_map/ppermute | solution.py:18
  34.4 51.7 %collective-permute-start.10 = (bf16[512,1024]{1,0:T(8,128)(2,1)S(1)}, bf16[512,1024]{1,0:T(8,128)(2,1)S(1)}, u32[]{:S(2)}, u32[]{:S(2)}) collective-permute-start(bf16[512,1024]{1,0:T(8,128)(2,1)S(1)} %joined.3.refs_4_), channel_id=1, source_target_pairs={{0,4},{4,0},{8,12},{12,8},{1,5},{5,1},{9,13},{13,9},{2,6},{6,2},{1... | collective-permute-start | bytes 3145736 | tf_op jit(solution)/shard_map/ppermute | solution.py:23
  35.7 50.4 %collective-permute-start.11 = (bf16[512,1024]{1,0:T(8,128)(2,1)S(1)}, bf16[512,1024]{1,0:T(8,128)(2,1)S(1)}, u32[]{:S(2)}, u32[]{:S(2)}) collective-permute-start(bf16[512,1024]{1,0:T(8,128)(2,1)S(1)} %joined.3.refs_4_), channel_id=1, source_target_pairs={{0,8},{4,12},{8,0},{12,4},{1,9},{5,13},{9,1},{13,5},{2,10},{6,14},... | collective-permute-start | bytes 3145736 | tf_op jit(solution)/shard_map/ppermute | solution.py:23
  36.6 49.6 %collective-permute-start.12 = (bf16[512,1024]{1,0:T(8,128)(2,1)S(1)}, bf16[512,1024]{1,0:T(8,128)(2,1)S(1)}, u32[]{:S(2)}, u32[]{:S(2)}) collective-permute-start(bf16[512,1024]{1,0:T(8,128)(2,1)S(1)} %joined.3.refs_4_), channel_id=1, source_target_pairs={{0,12},{4,8},{8,4},{12,0},{1,13},{5,9},{9,5},{13,1},{2,14},{6,10},... | collective-permute-start | bytes 3145736 | tf_op jit(solution)/shard_map/ppermute | solution.py:23
  46.9 9.2 %collective-permute-start.7 = (bf16[64,2048]{1,0:T(8,128)(2,1)S(1)}, bf16[64,2048]{1,0:T(8,128)(2,1)S(1)}, u32[]{:S(2)}, u32[]{:S(2)}) collective-permute-start(bf16[64,2048]{1,0:T(8,128)(2,1)S(1)} %get-tuple-element.58), channel_id=1, source_target_pairs={{0,3},{1,0},{2,1},{3,2},{4,7},{5,4},{6,5},{7,6},{8,11},{9,8},{10,9... | collective-permute-start | bytes 786440 | tf_op jit(solution)/shard_map/ppermute | solution.py:18
  47.5 18.0 %collective-permute-start.9 = (bf16[512,512]{1,0:T(8,128)(2,1)S(1)}, bf16[512,512]{1,0:T(8,128)(2,1)S(1)}, u32[]{:S(2)}, u32[]{:S(2)}) collective-permute-start(bf16[512,512]{1,0:T(8,128)(2,1)S(1)} %get-tuple-element.63), channel_id=1, source_target_pairs={{0,3},{1,0},{2,1},{3,2},{4,7},{5,4},{6,5},{7,6},{8,11},{9,8},{10,9... | collective-permute-start | bytes 1572872 | tf_op jit(solution)/shard_map/ppermute | solution.py:18
  56.1 30.0 %collective-permute-start.8 = (bf16[512,512]{1,0:T(8,128)(2,1)S(1)}, bf16[512,512]{1,0:T(8,128)(2,1)S(1)}, u32[]{:S(2)}, u32[]{:S(2)}) collective-permute-start(bf16[512,512]{1,0:T(8,128)(2,1)S(1)} %get-tuple-element.60), channel_id=1, source_target_pairs={{0,2},{1,3},{2,0},{3,1},{4,6},{5,7},{6,4},{7,5},{8,10},{9,11},{10,... | collective-permute-start | bytes 1572872 | tf_op jit(solution)/shard_map/ppermute | solution.py:18
  91.3 12.5 %collective-permute-start.15 = (bf16[272,1024]{1,0:T(8,128)(2,1)S(1)}, bf16[272,1024]{1,0:T(8,128)(2,1)S(1)}, u32[]{:S(2)}, u32[]{:S(2)}) collective-permute-start(bf16[272,1024]{1,0:T(8,128)(2,1)S(1)} %get-tuple-element.66.refs_0_), channel_id=1, source_target_pairs={{0,4},{4,0},{8,12},{12,8},{1,5},{5,1},{9,13},{13,9},{2,6},{6,2},{1... | collective-permute-start | bytes 1671176 | tf_op jit(solution)/shard_map/ppermute | solution.py:23
  92.8 13.0 %collective-permute-start.13 = (bf16[272,1024]{1,0:T(8,128)(2,1)S(1)}, bf16[272,1024]{1,0:T(8,128)(2,1)S(1)}, u32[]{:S(2)}, u32[]{:S(2)}) collective-permute-start(bf16[272,1024]{1,0:T(8,128)(2,1)S(1)} %get-tuple-element.65.refs_0_), channel_id=1, source_target_pairs={{0,8},{4,12},{8,0},{12,4},{1,9},{5,13},{9,1},{13,5},{2,10},{6,14},... | collective-permute-start | bytes 1671176 | tf_op jit(solution)/shard_map/ppermute | solution.py:23
  93.3 8.7 %collective-permute-start.17 = (bf16[64,2048]{1,0:T(8,128)(2,1)S(1)}, bf16[64,2048]{1,0:T(8,128)(2,1)S(1)}, u32[]{:S(2)}, u32[]{:S(2)}) collective-permute-start(bf16[64,2048]{1,0:T(8,128)(2,1)S(1)} %get-tuple-element.77), channel_id=1, source_target_pairs={{0,1},{1,2},{2,3},{3,0},{4,5},{5,6},{6,7},{7,4},{8,9},{9,10},{10,1... | collective-permute-start | bytes 786440 | tf_op jit(solution)/shard_map/ppermute | solution.py:18
  102.1 16.8 %copy-start.1 = (bf16[1,2,64,8192]{3,2,1,0:T(8,128)(2,1)S(1)}, bf16[1,2,64,8192]{3,2,1,0:T(8,128)(2,1)}, u32[]{:S(2)}) copy-start(bf16[1,2,64,8192]{3,2,1,0:T(8,128)(2,1)} %x_ref.3) | copy-start | bytes 6291460
  102.1 16.8 %copy-start.2 = (bf16[2,64,8192]{2,1,0:T(8,128)(2,1)S(1)}, bf16[2,64,8192]{2,1,0:T(8,128)(2,1)}, u32[]{:S(2)}) copy-start(bf16[2,64,8192]{2,1,0:T(8,128)(2,1)} %top_ref.3) | copy-start | bytes 6291460
  102.1 8.4 %collective-permute-start.18 = (bf16[64,2048]{1,0:T(8,128)(2,1)S(1)}, bf16[64,2048]{1,0:T(8,128)(2,1)S(1)}, u32[]{:S(2)}, u32[]{:S(2)}) collective-permute-start(bf16[64,2048]{1,0:T(8,128)(2,1)S(1)} %get-tuple-element.78), channel_id=1, source_target_pairs={{0,3},{1,0},{2,1},{3,2},{4,7},{5,4},{6,5},{7,6},{8,11},{9,8},{10,9... | collective-permute-start | bytes 786440 | tf_op jit(solution)/shard_map/ppermute | solution.py:18
  103.8 15.1 %collective-permute-start.19 = (bf16[64,2048]{1,0:T(8,128)(2,1)S(1)}, bf16[64,2048]{1,0:T(8,128)(2,1)S(1)}, u32[]{:S(2)}, u32[]{:S(2)}) collective-permute-start(bf16[64,2048]{1,0:T(8,128)(2,1)S(1)} %get-tuple-element.81), channel_id=1, source_target_pairs={{0,2},{1,3},{2,0},{3,1},{4,6},{5,7},{6,4},{7,5},{8,10},{9,11},{10,... | collective-permute-start | bytes 786440 | tf_op jit(solution)/shard_map/ppermute | solution.py:18
  103.9 26.1 %collective-permute-start.16 = (bf16[544,1024]{1,0:T(8,128)(2,1)S(1)}, bf16[544,1024]{1,0:T(8,128)(2,1)S(1)}, u32[]{:S(2)}, u32[]{:S(2)}) collective-permute-start(bf16[544,1024]{1,0:T(8,128)(2,1)S(1)} %joined.5.sum_ref), channel_id=1, source_target_pairs={{0,8},{4,12},{8,0},{12,4},{1,9},{5,13},{9,1},{13,5},{2,10},{6,14},... | collective-permute-start | bytes 3342344 | tf_op jit(solution)/shard_map/ppermute | solution.py:23
  105.9 25.5 %collective-permute-start.14 = (bf16[544,1024]{1,0:T(8,128)(2,1)S(1)}, bf16[544,1024]{1,0:T(8,128)(2,1)S(1)}, u32[]{:S(2)}, u32[]{:S(2)}) collective-permute-start(bf16[544,1024]{1,0:T(8,128)(2,1)S(1)} %joined.4.sum_ref), channel_id=1, source_target_pairs={{0,4},{4,0},{8,12},{12,8},{1,5},{5,1},{9,13},{13,9},{2,6},{6,2},{1... | collective-permute-start | bytes 3342344 | tf_op jit(solution)/shard_map/ppermute | solution.py:23
  120.4 8.6 %collective-permute-start.20 = (bf16[64,8192]{1,0:T(8,128)(2,1)S(1)}, bf16[64,8192]{1,0:T(8,128)(2,1)S(1)}, u32[]{:S(2)}, u32[]{:S(2)}) collective-permute-start(bf16[64,8192]{1,0:T(8,128)(2,1)S(1)} %get-tuple-element.82.upper_ref), channel_id=1, source_target_pairs={{16,0},{17,1},{18,2},{19,3},{20,4},{21,5},{22,6},{23,7},{24,8},{25... | collective-permute-start | bytes 3145736 | tf_op jit(solution)/shard_map/ppermute | solution.py:451
  121.7 21.2 %collective-permute-start.21 = (bf16[64,2048]{1,0:T(8,128)(2,1)S(1)}, bf16[64,2048]{1,0:T(8,128)(2,1)S(1)}, u32[]{:S(2)}, u32[]{:S(2)}) collective-permute-start(bf16[64,2048]{1,0:T(8,128)(2,1)S(1)} %get-tuple-element.86), channel_id=1, source_target_pairs={{0,2},{1,3},{2,0},{3,1},{4,6},{5,7},{6,4},{7,5},{8,10},{9,11},{10,... | collective-permute-start | bytes 786440 | tf_op jit(solution)/shard_map/ppermute | solution.py:18
  121.8 21.1 %collective-permute-start.22 = (bf16[64,2048]{1,0:T(8,128)(2,1)S(1)}, bf16[64,2048]{1,0:T(8,128)(2,1)S(1)}, u32[]{:S(2)}, u32[]{:S(2)}) collective-permute-start(bf16[64,2048]{1,0:T(8,128)(2,1)S(1)} %get-tuple-element.88), channel_id=1, source_target_pairs={{0,1},{1,2},{2,3},{3,0},{4,5},{5,6},{6,7},{7,4},{8,9},{9,10},{10,1... | collective-permute-start | bytes 786440 | tf_op jit(solution)/shard_map/ppermute | solution.py:18
  144.3 4.6 %collective-permute-start.23 = (bf16[64,8192]{1,0:T(8,128)(2,1)S(1)}, bf16[64,8192]{1,0:T(8,128)(2,1)S(1)}, u32[]{:S(2)}, u32[]{:S(2)}) collective-permute-start(bf16[64,8192]{1,0:T(8,128)(2,1)S(1)} %get-tuple-element.89.upper_ref), channel_id=1, source_target_pairs={{16,0},{17,1},{18,2},{19,3},{20,4},{21,5},{22,6},{23,7},{24,8},{25... | collective-permute-start | bytes 3145736 | tf_op jit(solution)/shard_map/ppermute | solution.py:451

commit v6 on v5

--- a/solution.py
+++ b/solution.py
@@ -181,41 +181,28 @@
     def kernel(rep_ref, *refs):
         column_refs, value_refs = refs[:groups], refs[groups : groups + reps]
         weight_ref, gain_ref = refs[groups + reps], refs[groups + reps + 1]
+        out_refs, total = refs[groups + reps + 2 : -1], refs[-1]
         start = pl.multiple_of(rep_ref[0] * width, width)
-        out_refs = refs[groups + reps + 2 : -5]
-        left, right, own, total, sems = refs[-5:]
-        copies = []
         for j in range(groups):
-            line = [pltpu.make_async_copy(column_refs[j], left.at[j], sems.at[j, reps])]
-            for e in range(reps):
-                source = value_refs[e].at[j * tokens : (j + 1) * tokens, :]
-                target = right.at[j, e * tokens : (e + 1) * tokens, :]
-                line.append(pltpu.make_async_copy(source, target, sems.at[j, e]))
-            for copy in line:
-                copy.start()
-            copies.append(line)
-        copy = pltpu.make_async_copy(weight_ref.at[pl.ds(start, width), :], own, sems.at[groups, 0])
-        copy.start()
-        for j in range(groups):
-            for c in copies[j]:
-                c.wait()
+            right = jnp.concatenate([v[j * tokens : (j + 1) * tokens, :] for v in value_refs], axis=0)
             for c in range(count):
-                block = left[j, :, c * chunk : (c + 1) * chunk]
-                product = lax.dot_general(block, right[j], contract, preferred_element_type=f32)
+                block = column_refs[j][:, c * chunk : (c + 1) * chunk]
+                product = lax.dot_general(block, right, contract, preferred_element_type=f32)
                 if j == 0:
                     total[c] = product
                 else:
                     total[c] += product
-        copy.wait()
         for c in range(count):
-            at = slice(c * chunk, (c + 1) * chunk)
+            at = pl.ds(pl.multiple_of(start + c * chunk, chunk), chunk)
             raw = total[c]
-            factor = gain_ref[:, pl.ds(pl.multiple_of(start + c * chunk, chunk), chunk)].astype(f32) * norm_scale
+            factor = gain_ref[:, at].astype(f32) * norm_scale
             factor = jnp.transpose(jnp.broadcast_to(factor, (128, chunk)))[:, 0:1]
             out_refs[c][:chunk, :] = (raw * factor).astype(bf16)
+            terms = raw * weight_ref[at, :].astype(f32)
+            terms = sum(terms[:, k : k + 128] for k in range(0, features, 128))
             dots = lax.dot_general(
-                jnp.full((8, features), norm_scale, f32),
-                raw * own[at, :].astype(f32),
+                jnp.full((8, 128), norm_scale, f32),
+                terms,
                 (((1,), (1,)), ((), ())),
                 precision=lax.Precision.HIGHEST,
                 preferred_element_type=f32,
@@ -224,18 +211,14 @@
             out_refs[c][chunk:, :chunk] = under.astype(bf16)
             out_refs[c][chunk:, chunk:] = jnp.zeros((16, features - chunk), bf16)
 
+    vmem = pl.BlockSpec(memory_space=pltpu.VMEM)
     return pl.pallas_call(
         kernel,
         out_shape=[jax.ShapeDtypeStruct((chunk + 16, features), bf16)] * count,
-        in_specs=[SMEM_ARG] + [ANY_ARG] * (groups + reps + 1) + [pl.BlockSpec(memory_space=pltpu.VMEM)],
-        scratch_shapes=[
-            pltpu.VMEM((groups, rows, width), bf16),
-            pltpu.VMEM((groups, rows, features), bf16),
-            pltpu.VMEM((width, features), bf16),
-            pltpu.VMEM((count, chunk, features), f32),
-            pltpu.SemaphoreType.DMA((groups + 1, reps + 1)),
-        ],
-        compiler_params=params(16),
+        in_specs=[SMEM_ARG] + [vmem] * (groups + reps + 2),
+        out_specs=[vmem] * count,
+        scratch_shapes=[pltpu.VMEM((count, chunk, features), f32)],
+        compiler_params=params(24),
         cost_estimate=cost(2 * groups * rows * width * features, 2 * groups * rows * (width + features) + 4 * width * features),
         name="weight_product",
     )(rep, *columns, *values, weight, gain)
@@ -418,21 +401,26 @@
     plane[0] = after(plane[0], *slots[1:])
     sent = regrouped(plane, groups)
     back = returned_blocks(slots, weight, norm_gain, micro)
+    lines = [[back[j][m] for j in range(groups)] for m in range(micro)]
+    far = groups // 2
+    near = [j for j in range(1, groups) if j != far]
     columns = list(sent)
-    for j in range(1, groups):
-        columns[j] = cyclic(after(sent[j], back[0][0]) if j == groups - 1 else sent[j], "fsdp", j)
+    columns[far] = cyclic(sent[far], "fsdp", far)
+    columns[near[0]] = cyclic(sent[near[0]], "fsdp", near[0])
+    for j in near[1:]:
+        columns[j] = cyclic(after(sent[j], back[0][0], columns[near[0]]), "fsdp", j)
     held = after(joined(slots), sent[0])
     values = [held if e == 0 else flipped(held, "rep", e) for e in range(reps)]
 
-    lines = [[back[j][m] for j in range(groups)] for m in range(micro)]
-    far = groups // 2
-    near = [(m, j) for m in range(micro) for j in range(1, groups) if j != far]
-    for chain in (near, [(m, far) for m in range(micro)]):
-        ties = [columns[1]]
-        for m, j in chain:
-            lines[m][j] = cyclic(after(lines[m][j], *ties), "fsdp", -j)
-            ties = [lines[m][j]]
-    columns[0] = after(columns[0], lines[0][1])
+    def send_back(m, j, *ties):
+        lines[m][j] = cyclic(after(lines[m][j], *ties), "fsdp", -j)
+
+    send_back(0, near[0], columns[far])
+    for m, j in [(0, far), *((0, j) for j in near[1:]), (1, near[0])]:
+        send_back(m, j, columns[near[-1]])
+    for j in [far, *near[1:]]:
+        send_back(1, j, *lines[0][1:], lines[1][near[0]])
+    columns[0] = after(columns[0], lines[0][near[0]])
     sums = weight_product(columns, values, weight, norm_gain, rep, groups, chunks, norm_scale)
     gathered = [doubled(sums[c], orders[c]) for c in range(chunks)]
     finished = ()
@@ -445,7 +433,7 @@
 
     result = ()
     for m in range(micro):
-        ties = [lines[-1][1], *[g[0] for g in gathered]] if m == 0 else [*finished, *result]
+        ties = [lines[-1][near[0]], *[g[0] for g in gathered]] if m == 0 else [*finished, *result]
         lines[m][0] = after(lines[m][0], *ties)
         upper, piece = row_gradient(layer_input, top_grad, lines[m], me, m)
         passed = lax.ppermute(upper, "section", [(1, 0)])

time: 150 us -> 146 us (0.973)
  waiting for transfers between devices: 94.8 us -> 82.1 us
  starting transfers between devices: 31.6 us -> 42.6 us
  Pallas kernels: 21.2 us -> 18.8 us
    ppermute x12, waiting for transfers between devices: 89.6 us -> 66.9 us  [cyclic(): lax.ppermute(value, axis, [(i, (i + steps) % count) for i in range(count)])]
    ppermute x12, starting transfers between devices: 17.7 us -> 30.5 us  [cyclic(): lax.ppermute(value, axis, [(i, (i + steps) % count) for i in range(count)])]
    ppermute x10, waiting for transfers between devices: 1.98 us -> 12 us  [flipped(): return lax.ppermute(value, axis, [(i, i ^ mask) for i in range(count)])]
    pallas_call x1, Pallas kernels: 5.12 us -> 2.73 us  [weight_product(): pl.pallas_call(kernel, out_shape=[jax.ShapeDtypeStruct((chunk + 16, featu...]
    ppermute x10, starting transfers between devices: 11.3 us -> 9.48 us  [flipped(): return lax.ppermute(value, axis, [(i, i ^ mask) for i in range(count)])]
where the time goes in v6:
time: 146 us
  waiting for transfers between devices  82.1 us (56%)
  starting transfers between devices  42.6 us (29%)
  Pallas kernels  18.8 us (13%)
  local copies, waits for them, and re-layouts  1.6 us (1%)
    ppermute x12, waiting for transfers between devices, cyclic(): lax.ppermute(value, axis, [(i, (i + steps) % count) for i in range(count)])  66.9 us
    ppermute x12, starting transfers between devices, cyclic(): lax.ppermute(value, axis, [(i, (i + steps) % count) for i in range(count)])  30.5 us
    ppermute x10, waiting for transfers between devices, flipped(): return lax.ppermute(value, axis, [(i, i ^ mask) for i in range(count)])  12 us
    ppermute x10, starting transfers between devices, flipped(): return lax.ppermute(value, axis, [(i, i ^ mask) for i in range(count)])  9.48 us
    pallas_call x4, Pallas kernels, finished_half(): pl.pallas_call(kernel, grid_spec=pltpu.PrefetchScalarGridSpec(num_scalar_...  5.61 us
    ppermute x2, waiting for transfers between devices, local(): passed = lax.ppermute(upper, 'section', [(1, 0)])  3.26 us
    pallas_call x1, Pallas kernels, returned_blocks(): pl.pallas_call(kernel, grid=(shard // tile,), out_shape=[jax.ShapeDtypeSt...  3.22 us
    pallas_call x2, Pallas kernels, row_gradient(): pl.pallas_call(kernel, grid=(rows // step,), out_shape=[jax.ShapeDtypeStr...  3.02 us
  transfers between devices with their start and end apart: 24, of which 13 were waited for; matrix products, arithmetic and copies ran while one was open for 0% of the time, Pallas kernels for 8%

profile of v6, /device:TPU:0, one launch (start us, length us, event | category | flops | bytes accessed | tf_op | source)
XLA Modules:
  0.0 145.9 jit_solution(17779924032257616495)
XLA Ops:
  0.6 1.6 %copy-done = bf16[1,2,64,8192]{3,2,1,0:T(8,128)(2,1)S(1)} copy-done((bf16[1,2,64,8192]{3,2,1,0:T(8,128)(2,1)S(1)}, bf16[1,2,64,8192]{3,2,1,0:T(8,128)(2,1)}, u32[]{:S(2)}) %copy-start) | copy-done | bytes 2097176
  2.2 1.1 scaled_blocks.1
  3.3 3.1 %collective-permute-start = (bf16[128,1024]{1,0:T(8,128)(2,1)S(1)}, bf16[128,1024]{1,0:T(8,128)(2,1)S(1)}, u32[]{:S(2)}, u32[]{:S(2)}) collective-permute-start(bf16[128,1024]{1,0:T(8,128)(2,1)S(1)} %bitcast.10), channel_id=1, source_target_pairs={{0,1},{1,2},{2,3},{3,0},{4,5},{5,6},{6,7},{7,4},{8,9},{9,10},{10,1... | collective-permute-start | bytes 786440 | tf_op jit(solution)/shard_map/ppermute | solution.py:18
  6.4 1.5 %collective-permute-start.3 = (bf16[128,2048]{1,0:T(8,128)(2,1)S(1)}, bf16[128,2048]{1,0:T(8,128)(2,1)S(1)}, u32[]{:S(2)}, u32[]{:S(2)}) collective-permute-start(bf16[128,2048]{1,0:T(8,128)(2,1)S(1)} %get-tuple-element.52), channel_id=1, source_target_pairs={{0,4},{4,0},{8,12},{12,8},{1,5},{5,1},{9,13},{13,9},{2,6},{6,2},{1... | collective-permute-start | bytes 1572872 | tf_op jit(solution)/shard_map/ppermute | solution.py:23
  7.9 1.5 %collective-permute-start.4 = (bf16[128,2048]{1,0:T(8,128)(2,1)S(1)}, bf16[128,2048]{1,0:T(8,128)(2,1)S(1)}, u32[]{:S(2)}, u32[]{:S(2)}) collective-permute-start(bf16[128,2048]{1,0:T(8,128)(2,1)S(1)} %get-tuple-element.53), channel_id=1, source_target_pairs={{0,8},{4,12},{8,0},{12,4},{1,9},{5,13},{9,1},{13,5},{2,10},{6,14},... | collective-permute-start | bytes 1572872 | tf_op jit(solution)/shard_map/ppermute | solution.py:23
  9.4 0.5 collective-permute-start.5
  9.9 2.6 %collective-permute-start.1 = (bf16[128,1024]{1,0:T(8,128)(2,1)S(1)}, bf16[128,1024]{1,0:T(8,128)(2,1)S(1)}, u32[]{:S(2)}, u32[]{:S(2)}) collective-permute-start(bf16[128,1024]{1,0:T(8,128)(2,1)S(1)} %bitcast.11), channel_id=1, source_target_pairs={{0,2},{1,3},{2,0},{3,1},{4,6},{5,7},{6,4},{7,5},{8,10},{9,11},{10,... | collective-permute-start | bytes 786440 | tf_op jit(solution)/shard_map/ppermute | solution.py:18
  12.5 3.2 %collective-permute-done.refs_1_ = bf16[128,1024]{1,0:T(8,128)(2,1)S(1)} collective-permute-done((bf16[128,1024]{1,0:T(8,128)(2,1)S(1)}, bf16[128,1024]{1,0:T(8,128)(2,1)S(1)}, u32[]{:S(2)}, u32[]{:S(2)}) %collective-permute-start) | collective-permute-done | bytes 262176 | tf_op jit(solution)/shard_map/ppermute | solution.py:18
  15.6 1.4 collective-permute-start.2
  17.0 9.0 %collective-permute-done.1.refs_2_ = bf16[128,1024]{1,0:T(8,128)(2,1)S(1)} collective-permute-done((bf16[128,1024]{1,0:T(8,128)(2,1)S(1)}, bf16[128,1024]{1,0:T(8,128)(2,1)S(1)}, u32[]{:S(2)}, u32[]{:S(2)}) %collective-permute-start.1) | collective-permute-done | bytes 262176 | tf_op jit(solution)/shard_map/ppermute | solution.py:18
  26.0 4.2 %collective-permute-done.2.refs_3_ = bf16[128,1024]{1,0:T(8,128)(2,1)S(1)} collective-permute-done((bf16[128,1024]{1,0:T(8,128)(2,1)S(1)}, bf16[128,1024]{1,0:T(8,128)(2,1)S(1)}, u32[]{:S(2)}, u32[]{:S(2)}) %collective-permute-start.2) | collective-permute-done | bytes 262176 | tf_op jit(solution)/shard_map/ppermute | solution.py:18
  30.3 2.0 %collective-permute-done.4.refs_2_ = bf16[128,2048]{1,0:T(8,128)(2,1)S(1)} collective-permute-done((bf16[128,2048]{1,0:T(8,128)(2,1)S(1)}, bf16[128,2048]{1,0:T(8,128)(2,1)S(1)}, u32[]{:S(2)}, u32[]{:S(2)}) %collective-permute-start.4) | collective-permute-done | bytes 524320 | tf_op jit(solution)/shard_map/ppermute | solution.py:23
  32.2 0.5 regrouped.1
  32.7 1.6 %collective-permute-start.8 = (bf16[512,512]{1,0:T(8,128)(2,1)S(1)}, bf16[512,512]{1,0:T(8,128)(2,1)S(1)}, u32[]{:S(2)}, u32[]{:S(2)}) collective-permute-start(bf16[512,512]{1,0:T(8,128)(2,1)S(1)} %get-tuple-element.60), channel_id=1, source_target_pairs={{0,1},{1,2},{2,3},{3,0},{4,5},{5,6},{6,7},{7,4},{8,9},{9,10},{10,1... | collective-permute-start | bytes 1572872 | tf_op jit(solution)/shard_map/ppermute | solution.py:18
  34.4 1.3 collective-permute-start.10
  35.7 0.8 collective-permute-start.11
  36.6 1.4 collective-permute-start.12
  38.0 1.4 collective-permute-start.6
  39.4 3.2 %returned_blocks.1 = (bf16[64,2048]{1,0:T(8,128)(2,1)S(1)}, bf16[64,2048]{1,0:T(8,128)(2,1)S(1)}, bf16[64,2048]{1,0:T(8,128)(2,1)S(1)}, bf16[64,2048]{1,0:T(8,12...) custom-call(bf16[128,1024]{1,0:T(8,128)(2,1)S(1)} %bitcast.14, ...), custom_call_target="tpu_custom_call" | custom-call | flops 2147483648 | bytes 7340032 | tf_op jit(solution)/shard_map/returned_blocks/pallas_call | solution.py:248
  42.6 6.9 %collective-permute-done.8.refs_1_ = bf16[512,512]{1,0:T(8,128)(2,1)S(1)} collective-permute-done((bf16[512,512]{1,0:T(8,128)(2,1)S(1)}, bf16[512,512]{1,0:T(8,128)(2,1)S(1)}, u32[]{:S(2)}, u32[]{:S(2)}) %collective-permute-start.8) | collective-permute-done | bytes 524320 | tf_op jit(solution)/shard_map/ppermute | solution.py:18
  49.5 19.9 %collective-permute-done.6.refs_2_ = bf16[512,512]{1,0:T(8,128)(2,1)S(1)} collective-permute-done((bf16[512,512]{1,0:T(8,128)(2,1)S(1)}, bf16[512,512]{1,0:T(8,128)(2,1)S(1)}, u32[]{:S(2)}, u32[]{:S(2)}) %collective-permute-start.6) | collective-permute-done | bytes 524320 | tf_op jit(solution)/shard_map/ppermute | solution.py:18
  69.4 12.8 %collective-permute-start.7 = (bf16[64,2048]{1,0:T(8,128)(2,1)S(1)}, bf16[64,2048]{1,0:T(8,128)(2,1)S(1)}, u32[]{:S(2)}, u32[]{:S(2)}) collective-permute-start(bf16[64,2048]{1,0:T(8,128)(2,1)S(1)} %get-tuple-element.58), channel_id=1, source_target_pairs={{0,3},{1,0},{2,1},{3,2},{4,7},{5,4},{6,5},{7,6},{8,11},{9,8},{10,9... | collective-permute-start | bytes 786440 | tf_op jit(solution)/shard_map/ppermute | solution.py:18
  82.2 3.9 %collective-permute-done.7.refs_1_ = bf16[64,2048]{1,0:T(8,128)(2,1)S(1)} collective-permute-done((bf16[64,2048]{1,0:T(8,128)(2,1)S(1)}, bf16[64,2048]{1,0:T(8,128)(2,1)S(1)}, u32[]{:S(2)}, u32[]{:S(2)}) %collective-permute-start.7) | collective-permute-done | bytes 262176 | tf_op jit(solution)/shard_map/ppermute | solution.py:18
  86.1 2.7 %weight_product.1 = (bf16[272,1024]{1,0:T(8,128)(2,1)S(1)}, bf16[272,1024]{1,0:T(8,128)(2,1)S(1)}) custom-call(s32[1]{0:T(128)} %bitcast.3.rep_ref, bf16[512,512]{1,0:T(8,128)(2,1)S(1)} %get-tuple-element.59.refs_0_, bf16[512,512]{1,0:T(8,128)(2,1)S(1)} %collective-permute-done.8.refs_1_, bf16[512,512]{1,0:T(8,128)(2,1)S(1)} %collective-permute-done.6.refs_2_, ...), custom_call_target="tpu_custom_call" | custom-call | flops 2147483648 | bytes 8388608 | tf_op jit(solution)/shard_map/weight_product/pallas_call | solution.py:215
  88.9 1.5 %collective-permute-start.15 = (bf16[272,1024]{1,0:T(8,128)(2,1)S(1)}, bf16[272,1024]{1,0:T(8,128)(2,1)S(1)}, u32[]{:S(2)}, u32[]{:S(2)}) collective-permute-start(bf16[272,1024]{1,0:T(8,128)(2,1)S(1)} %get-tuple-element.66.refs_0_), channel_id=1, source_target_pairs={{0,4},{4,0},{8,12},{12,8},{1,5},{5,1},{9,13},{13,9},{2,6},{6,2},{1... | collective-permute-start | bytes 1671176 | tf_op jit(solution)/shard_map/ppermute | solution.py:23
  90.4 0.6 collective-permute-start.13
  90.9 4.3 %collective-permute-start.17 = (bf16[64,2048]{1,0:T(8,128)(2,1)S(1)}, bf16[64,2048]{1,0:T(8,128)(2,1)S(1)}, u32[]{:S(2)}, u32[]{:S(2)}) collective-permute-start(bf16[64,2048]{1,0:T(8,128)(2,1)S(1)} %get-tuple-element.76), channel_id=1, source_target_pairs={{0,3},{1,0},{2,1},{3,2},{4,7},{5,4},{6,5},{7,6},{8,11},{9,8},{10,9... | collective-permute-start | bytes 786440 | tf_op jit(solution)/shard_map/ppermute | solution.py:18
  95.2 0.6 collective-permute-start.19
  95.8 4.4 %collective-permute-done.15.refs_1_ = bf16[272,1024]{1,0:T(8,128)(2,1)S(1)} collective-permute-done((bf16[272,1024]{1,0:T(8,128)(2,1)S(1)}, bf16[272,1024]{1,0:T(8,128)(2,1)S(1)}, u32[]{:S(2)}, u32[]{:S(2)}) %collective-permute-start.15) | collective-permute-done | bytes 557088 | tf_op jit(solution)/shard_map/ppermute | solution.py:23
  100.2 0.2 joined.5.sum_ref
  100.3 0.3 collective-permute-start.16
  100.6 3.6 %collective-permute-done.13.refs_1_ = bf16[272,1024]{1,0:T(8,128)(2,1)S(1)} collective-permute-done((bf16[272,1024]{1,0:T(8,128)(2,1)S(1)}, bf16[272,1024]{1,0:T(8,128)(2,1)S(1)}, u32[]{:S(2)}, u32[]{:S(2)}) %collective-permute-start.13) | collective-permute-done | bytes 557088 | tf_op jit(solution)/shard_map/ppermute | solution.py:23
  104.5 9.3 %collective-permute-done.18.refs_2_ = bf16[64,2048]{1,0:T(8,128)(2,1)S(1)} collective-permute-done((bf16[64,2048]{1,0:T(8,128)(2,1)S(1)}, bf16[64,2048]{1,0:T(8,128)(2,1)S(1)}, u32[]{:S(2)}, u32[]{:S(2)}) %collective-permute-start.18) | collective-permute-done | bytes 262176 | tf_op jit(solution)/shard_map/ppermute | solution.py:18
  113.8 1.5 %row_gradient.2 = (bf16[64,8192]{1,0:T(8,128)(2,1)S(1)}, bf16[64,8192]{1,0:T(8,128)(2,1)S(1)}) custom-call(s32[1]{0:T(128)} %bitcast.1.me_ref, bf16[1,2,64,8192]{3,2,1,0:T(8,128)(2,1)S(1)} %copy-done.1, bf16[2,64,8192]{2,1,0:T(8,128)(2,1)S(1)} %copy-done.2, bf16[64,2048]{1,0:T(8,128)(2,1)S(1)} %get-tuple-element.77.refs_0_, ...), custom_call_target="tpu_custom_call" | custom-call | flops 6291456 | bytes 5242880 | tf_op jit(solution)/shard_map/row_gradient/pallas_call | solution.py:293
  115.4 1.3 collective-permute-start.20
  116.7 0.8 collective-permute-start.22
  117.5 2.0 %collective-permute-start.21 = (bf16[64,2048]{1,0:T(8,128)(2,1)S(1)}, bf16[64,2048]{1,0:T(8,128)(2,1)S(1)}, u32[]{:S(2)}, u32[]{:S(2)}) collective-permute-start(bf16[64,2048]{1,0:T(8,128)(2,1)S(1)} %get-tuple-element.86), channel_id=1, source_target_pairs={{0,2},{1,3},{2,0},{3,1},{4,6},{5,7},{6,4},{7,5},{8,10},{9,11},{10,... | collective-permute-start | bytes 786440 | tf_op jit(solution)/shard_map/ppermute | solution.py:18
  119.5 1.4 finished_half.4
  120.8 1.4 finished_half.5
  122.2 1.1 input_gradient.2.refs_0_
  123.3 2.0 %collective-permute-done.16.sum_ref = bf16[544,1024]{1,0:T(8,128)(2,1)S(1)} collective-permute-done((bf16[544,1024]{1,0:T(8,128)(2,1)S(1)}, bf16[544,1024]{1,0:T(8,128)(2,1)S(1)}, u32[]{:S(2)}, u32[]{:S(2)}) %collective-permute-start.16) | collective-permute-done | bytes 1114144 | tf_op jit(solution)/shard_map/ppermute | solution.py:23
  125.4 1.4 finished_half.6
  126.8 1.4 finished_half.7
  128.2 10.5 %collective-permute-done.21.refs_2_ = bf16[64,2048]{1,0:T(8,128)(2,1)S(1)} collective-permute-done((bf16[64,2048]{1,0:T(8,128)(2,1)S(1)}, bf16[64,2048]{1,0:T(8,128)(2,1)S(1)}, u32[]{:S(2)}, u32[]{:S(2)}) %collective-permute-start.21) | collective-permute-done | bytes 262176 | tf_op jit(solution)/shard_map/ppermute | solution.py:18
  138.7 1.5 %row_gradient.3 = (bf16[64,8192]{1,0:T(8,128)(2,1)S(1)}, bf16[64,8192]{1,0:T(8,128)(2,1)S(1)}) custom-call(s32[1]{0:T(128)} %bitcast.1.me_ref, bf16[1,2,64,8192]{3,2,1,0:T(8,128)(2,1)S(1)} %copy-done.1, bf16[2,64,8192]{2,1,0:T(8,128)(2,1)S(1)} %copy-done.2, bf16[64,2048]{1,0:T(8,128)(2,1)S(1)} %get-tuple-element.84.refs_0_, ...), custom_call_target="tpu_custom_call" | custom-call | flops 6291456 | bytes 5242880 | tf_op jit(solution)/shard_map/row_gradient/pallas_call | solution.py:293
  140.2 1.3 collective-permute-start.23
  141.5 3.3 %collective-permute-done.23.passed_ref = bf16[64,8192]{1,0:T(8,128)(2,1)S(1)} collective-permute-done((bf16[64,8192]{1,0:T(8,128)(2,1)S(1)}, bf16[64,8192]{1,0:T(8,128)(2,1)S(1)}, u32[]{:S(2)}, u32[]{:S(2)}) %collective-permute-start.23) | collective-permute-done | bytes 1048608 | tf_op jit(solution)/shard_map/ppermute | solution.py:439
  144.8 1.1 input_gradient.3
  (27 shorter events, 0.4 us)
Async XLA Ops:
  0.6 1.6 %copy-start = (bf16[1,2,64,8192]{3,2,1,0:T(8,128)(2,1)S(1)}, bf16[1,2,64,8192]{3,2,1,0:T(8,128)(2,1)}, u32[]{:S(2)}) copy-start(bf16[1,2,64,8192]{3,2,1,0:T(8,128)(2,1)} %x_ref.3) | copy-start | bytes 6291460
  2.2 1.1 copy-start.4
  3.3 12.3 %collective-permute-start = (bf16[128,1024]{1,0:T(8,128)(2,1)S(1)}, bf16[128,1024]{1,0:T(8,128)(2,1)S(1)}, u32[]{:S(2)}, u32[]{:S(2)}) collective-permute-start(bf16[128,1024]{1,0:T(8,128)(2,1)S(1)} %bitcast.10), channel_id=1, source_target_pairs={{0,1},{1,2},{2,3},{3,0},{4,5},{5,6},{6,7},{7,4},{8,9},{9,10},{10,1... | collective-permute-start | bytes 786440 | tf_op jit(solution)/shard_map/ppermute | solution.py:18
  6.4 23.9 %collective-permute-start.3 = (bf16[128,2048]{1,0:T(8,128)(2,1)S(1)}, bf16[128,2048]{1,0:T(8,128)(2,1)S(1)}, u32[]{:S(2)}, u32[]{:S(2)}) collective-permute-start(bf16[128,2048]{1,0:T(8,128)(2,1)S(1)} %get-tuple-element.52), channel_id=1, source_target_pairs={{0,4},{4,0},{8,12},{12,8},{1,5},{5,1},{9,13},{13,9},{2,6},{6,2},{1... | collective-permute-start | bytes 1572872 | tf_op jit(solution)/shard_map/ppermute | solution.py:23
  7.9 24.3 %collective-permute-start.4 = (bf16[128,2048]{1,0:T(8,128)(2,1)S(1)}, bf16[128,2048]{1,0:T(8,128)(2,1)S(1)}, u32[]{:S(2)}, u32[]{:S(2)}) collective-permute-start(bf16[128,2048]{1,0:T(8,128)(2,1)S(1)} %get-tuple-element.53), channel_id=1, source_target_pairs={{0,8},{4,12},{8,0},{12,4},{1,9},{5,13},{9,1},{13,5},{2,10},{6,14},... | collective-permute-start | bytes 1572872 | tf_op jit(solution)/shard_map/ppermute | solution.py:23
  9.4 30.0 %copy-start.5 = (bf16[1,2048]{1,0:T(2,128)(2,1)S(1)}, bf16[1,2048]{1,0:T(2,128)(2,1)}, u32[]{:S(2)}) copy-start(bf16[1,2048]{1,0:T(2,128)(2,1)} %refs_9_.1) | copy-start | bytes 12292
  9.4 30.0 %copy-start.3 = (bf16[1,2048,1024]{2,1,0:T(8,128)(2,1)S(1)}, bf16[1,2048,1024]{2,1,0:T(8,128)(2,1)}, u32[]{:S(2)}) copy-start(bf16[1,2048,1024]{2,1,0:T(8,128)(2,1)} %param.7) | copy-start | bytes 12582916
  9.4 22.8 %collective-permute-start.5 = (bf16[128,2048]{1,0:T(8,128)(2,1)S(1)}, bf16[128,2048]{1,0:T(8,128)(2,1)S(1)}, u32[]{:S(2)}, u32[]{:S(2)}) collective-permute-start(bf16[128,2048]{1,0:T(8,128)(2,1)S(1)} %get-tuple-element.54), channel_id=1, source_target_pairs={{0,12},{4,8},{8,4},{12,0},{1,13},{5,9},{9,5},{13,1},{2,14},{6,10},... | collective-permute-start | bytes 1572872 | tf_op jit(solution)/shard_map/ppermute | solution.py:23
  9.9 16.2 %collective-permute-start.1 = (bf16[128,1024]{1,0:T(8,128)(2,1)S(1)}, bf16[128,1024]{1,0:T(8,128)(2,1)S(1)}, u32[]{:S(2)}, u32[]{:S(2)}) collective-permute-start(bf16[128,1024]{1,0:T(8,128)(2,1)S(1)} %bitcast.11), channel_id=1, source_target_pairs={{0,2},{1,3},{2,0},{3,1},{4,6},{5,7},{6,4},{7,5},{8,10},{9,11},{10,... | collective-permute-start | bytes 786440 | tf_op jit(solution)/shard_map/ppermute | solution.py:18
  15.6 14.6 %collective-permute-start.2 = (bf16[128,1024]{1,0:T(8,128)(2,1)S(1)}, bf16[128,1024]{1,0:T(8,128)(2,1)S(1)}, u32[]{:S(2)}, u32[]{:S(2)}) collective-permute-start(bf16[128,1024]{1,0:T(8,128)(2,1)S(1)} %bitcast.12), channel_id=1, source_target_pairs={{0,3},{1,0},{2,1},{3,2},{4,7},{5,4},{6,5},{7,6},{8,11},{9,8},{10,9... | collective-permute-start | bytes 786440 | tf_op jit(solution)/shard_map/ppermute | solution.py:18
  32.7 16.8 %collective-permute-start.8 = (bf16[512,512]{1,0:T(8,128)(2,1)S(1)}, bf16[512,512]{1,0:T(8,128)(2,1)S(1)}, u32[]{:S(2)}, u32[]{:S(2)}) collective-permute-start(bf16[512,512]{1,0:T(8,128)(2,1)S(1)} %get-tuple-element.60), channel_id=1, source_target_pairs={{0,1},{1,2},{2,3},{3,0},{4,5},{5,6},{6,7},{7,4},{8,9},{9,10},{10,1... | collective-permute-start | bytes 1572872 | tf_op jit(solution)/shard_map/ppermute | solution.py:18
  34.4 51.7 %collective-permute-start.10 = (bf16[512,1024]{1,0:T(8,128)(2,1)S(1)}, bf16[512,1024]{1,0:T(8,128)(2,1)S(1)}, u32[]{:S(2)}, u32[]{:S(2)}) collective-permute-start(bf16[512,1024]{1,0:T(8,128)(2,1)S(1)} %joined.3.refs_4_), channel_id=1, source_target_pairs={{0,4},{4,0},{8,12},{12,8},{1,5},{5,1},{9,13},{13,9},{2,6},{6,2},{1... | collective-permute-start | bytes 3145736 | tf_op jit(solution)/shard_map/ppermute | solution.py:23
  35.7 50.4 %collective-permute-start.11 = (bf16[512,1024]{1,0:T(8,128)(2,1)S(1)}, bf16[512,1024]{1,0:T(8,128)(2,1)S(1)}, u32[]{:S(2)}, u32[]{:S(2)}) collective-permute-start(bf16[512,1024]{1,0:T(8,128)(2,1)S(1)} %joined.3.refs_4_), channel_id=1, source_target_pairs={{0,8},{4,12},{8,0},{12,4},{1,9},{5,13},{9,1},{13,5},{2,10},{6,14},... | collective-permute-start | bytes 3145736 | tf_op jit(solution)/shard_map/ppermute | solution.py:23
  36.6 49.5 %collective-permute-start.12 = (bf16[512,1024]{1,0:T(8,128)(2,1)S(1)}, bf16[512,1024]{1,0:T(8,128)(2,1)S(1)}, u32[]{:S(2)}, u32[]{:S(2)}) collective-permute-start(bf16[512,1024]{1,0:T(8,128)(2,1)S(1)} %joined.3.refs_4_), channel_id=1, source_target_pairs={{0,12},{4,8},{8,4},{12,0},{1,13},{5,9},{9,5},{13,1},{2,14},{6,10},... | collective-permute-start | bytes 3145736 | tf_op jit(solution)/shard_map/ppermute | solution.py:23
  38.0 31.4 %collective-permute-start.6 = (bf16[512,512]{1,0:T(8,128)(2,1)S(1)}, bf16[512,512]{1,0:T(8,128)(2,1)S(1)}, u32[]{:S(2)}, u32[]{:S(2)}) collective-permute-start(bf16[512,512]{1,0:T(8,128)(2,1)S(1)} %get-tuple-element.57), channel_id=1, source_target_pairs={{0,2},{1,3},{2,0},{3,1},{4,6},{5,7},{6,4},{7,5},{8,10},{9,11},{10,... | collective-permute-start | bytes 1572872 | tf_op jit(solution)/shard_map/ppermute | solution.py:18
  49.5 36.6 %collective-permute-start.9 = (bf16[512,512]{1,0:T(8,128)(2,1)S(1)}, bf16[512,512]{1,0:T(8,128)(2,1)S(1)}, u32[]{:S(2)}, u32[]{:S(2)}) collective-permute-start(bf16[512,512]{1,0:T(8,128)(2,1)S(1)} %get-tuple-element.63), channel_id=1, source_target_pairs={{0,3},{1,0},{2,1},{3,2},{4,7},{5,4},{6,5},{7,6},{8,11},{9,8},{10,9... | collective-permute-start | bytes 1572872 | tf_op jit(solution)/shard_map/ppermute | solution.py:18
  69.4 16.7 %collective-permute-start.7 = (bf16[64,2048]{1,0:T(8,128)(2,1)S(1)}, bf16[64,2048]{1,0:T(8,128)(2,1)S(1)}, u32[]{:S(2)}, u32[]{:S(2)}) collective-permute-start(bf16[64,2048]{1,0:T(8,128)(2,1)S(1)} %get-tuple-element.58), channel_id=1, source_target_pairs={{0,3},{1,0},{2,1},{3,2},{4,7},{5,4},{6,5},{7,6},{8,11},{9,8},{10,9... | collective-permute-start | bytes 786440 | tf_op jit(solution)/shard_map/ppermute | solution.py:18
  88.9 11.3 %collective-permute-start.15 = (bf16[272,1024]{1,0:T(8,128)(2,1)S(1)}, bf16[272,1024]{1,0:T(8,128)(2,1)S(1)}, u32[]{:S(2)}, u32[]{:S(2)}) collective-permute-start(bf16[272,1024]{1,0:T(8,128)(2,1)S(1)} %get-tuple-element.66.refs_0_), channel_id=1, source_target_pairs={{0,4},{4,0},{8,12},{12,8},{1,5},{5,1},{9,13},{13,9},{2,6},{6,2},{1... | collective-permute-start | bytes 1671176 | tf_op jit(solution)/shard_map/ppermute | solution.py:23
  90.4 13.9 %collective-permute-start.13 = (bf16[272,1024]{1,0:T(8,128)(2,1)S(1)}, bf16[272,1024]{1,0:T(8,128)(2,1)S(1)}, u32[]{:S(2)}, u32[]{:S(2)}) collective-permute-start(bf16[272,1024]{1,0:T(8,128)(2,1)S(1)} %get-tuple-element.65.refs_0_), channel_id=1, source_target_pairs={{0,8},{4,12},{8,0},{12,4},{1,9},{5,13},{9,1},{13,5},{2,10},{6,14},... | collective-permute-start | bytes 1671176 | tf_op jit(solution)/shard_map/ppermute | solution.py:23
  90.9 13.6 %collective-permute-start.17 = (bf16[64,2048]{1,0:T(8,128)(2,1)S(1)}, bf16[64,2048]{1,0:T(8,128)(2,1)S(1)}, u32[]{:S(2)}, u32[]{:S(2)}) collective-permute-start(bf16[64,2048]{1,0:T(8,128)(2,1)S(1)} %get-tuple-element.76), channel_id=1, source_target_pairs={{0,3},{1,0},{2,1},{3,2},{4,7},{5,4},{6,5},{7,6},{8,11},{9,8},{10,9... | collective-permute-start | bytes 786440 | tf_op jit(solution)/shard_map/ppermute | solution.py:18
  95.2 18.6 %collective-permute-start.18 = (bf16[64,2048]{1,0:T(8,128)(2,1)S(1)}, bf16[64,2048]{1,0:T(8,128)(2,1)S(1)}, u32[]{:S(2)}, u32[]{:S(2)}) collective-permute-start(bf16[64,2048]{1,0:T(8,128)(2,1)S(1)} %get-tuple-element.79), channel_id=1, source_target_pairs={{0,2},{1,3},{2,0},{3,1},{4,6},{5,7},{6,4},{7,5},{8,10},{9,11},{10,... | collective-permute-start | bytes 786440 | tf_op jit(solution)/shard_map/ppermute | solution.py:18
  95.2 18.6 %copy-start.1 = (bf16[1,2,64,8192]{3,2,1,0:T(8,128)(2,1)S(1)}, bf16[1,2,64,8192]{3,2,1,0:T(8,128)(2,1)}, u32[]{:S(2)}) copy-start(bf16[1,2,64,8192]{3,2,1,0:T(8,128)(2,1)} %x_ref.3) | copy-start | bytes 6291460
  95.2 18.6 %copy-start.2 = (bf16[2,64,8192]{2,1,0:T(8,128)(2,1)S(1)}, bf16[2,64,8192]{2,1,0:T(8,128)(2,1)}, u32[]{:S(2)}) copy-start(bf16[2,64,8192]{2,1,0:T(8,128)(2,1)} %top_ref.3) | copy-start | bytes 6291460
  95.2 18.6 %collective-permute-start.19 = (bf16[64,2048]{1,0:T(8,128)(2,1)S(1)}, bf16[64,2048]{1,0:T(8,128)(2,1)S(1)}, u32[]{:S(2)}, u32[]{:S(2)}) collective-permute-start(bf16[64,2048]{1,0:T(8,128)(2,1)S(1)} %get-tuple-element.81), channel_id=1, source_target_pairs={{0,1},{1,2},{2,3},{3,0},{4,5},{5,6},{6,7},{7,4},{8,9},{9,10},{10,1... | collective-permute-start | bytes 786440 | tf_op jit(solution)/shard_map/ppermute | solution.py:18
  100.3 25.0 %collective-permute-start.16 = (bf16[544,1024]{1,0:T(8,128)(2,1)S(1)}, bf16[544,1024]{1,0:T(8,128)(2,1)S(1)}, u32[]{:S(2)}, u32[]{:S(2)}) collective-permute-start(bf16[544,1024]{1,0:T(8,128)(2,1)S(1)} %joined.5.sum_ref), channel_id=1, source_target_pairs={{0,8},{4,12},{8,0},{12,4},{1,9},{5,13},{9,1},{13,5},{2,10},{6,14},... | collective-permute-start | bytes 3342344 | tf_op jit(solution)/shard_map/ppermute | solution.py:23
  104.4 22.4 %collective-permute-start.14 = (bf16[544,1024]{1,0:T(8,128)(2,1)S(1)}, bf16[544,1024]{1,0:T(8,128)(2,1)S(1)}, u32[]{:S(2)}, u32[]{:S(2)}) collective-permute-start(bf16[544,1024]{1,0:T(8,128)(2,1)S(1)} %joined.4.sum_ref), channel_id=1, source_target_pairs={{0,4},{4,0},{8,12},{12,8},{1,5},{5,1},{9,13},{13,9},{2,6},{6,2},{1... | collective-permute-start | bytes 3342344 | tf_op jit(solution)/shard_map/ppermute | solution.py:23
  115.4 6.9 %collective-permute-start.20 = (bf16[64,8192]{1,0:T(8,128)(2,1)S(1)}, bf16[64,8192]{1,0:T(8,128)(2,1)S(1)}, u32[]{:S(2)}, u32[]{:S(2)}) collective-permute-start(bf16[64,8192]{1,0:T(8,128)(2,1)S(1)} %get-tuple-element.82.upper_ref), channel_id=1, source_target_pairs={{16,0},{17,1},{18,2},{19,3},{20,4},{21,5},{22,6},{23,7},{24,8},{25... | collective-permute-start | bytes 3145736 | tf_op jit(solution)/shard_map/ppermute | solution.py:439
  116.7 11.5 %collective-permute-start.22 = (bf16[64,2048]{1,0:T(8,128)(2,1)S(1)}, bf16[64,2048]{1,0:T(8,128)(2,1)S(1)}, u32[]{:S(2)}, u32[]{:S(2)}) collective-permute-start(bf16[64,2048]{1,0:T(8,128)(2,1)S(1)} %get-tuple-element.88), channel_id=1, source_target_pairs={{0,1},{1,2},{2,3},{3,0},{4,5},{5,6},{6,7},{7,4},{8,9},{9,10},{10,1... | collective-permute-start | bytes 786440 | tf_op jit(solution)/shard_map/ppermute | solution.py:18
  117.5 21.3 %collective-permute-start.21 = (bf16[64,2048]{1,0:T(8,128)(2,1)S(1)}, bf16[64,2048]{1,0:T(8,128)(2,1)S(1)}, u32[]{:S(2)}, u32[]{:S(2)}) collective-permute-start(bf16[64,2048]{1,0:T(8,128)(2,1)S(1)} %get-tuple-element.86), channel_id=1, source_target_pairs={{0,2},{1,3},{2,0},{3,1},{4,6},{5,7},{6,4},{7,5},{8,10},{9,11},{10,... | collective-permute-start | bytes 786440 | tf_op jit(solution)/shard_map/ppermute | solution.py:18
  140.2 4.6 %collective-permute-start.23 = (bf16[64,8192]{1,0:T(8,128)(2,1)S(1)}, bf16[64,8192]{1,0:T(8,128)(2,1)S(1)}, u32[]{:S(2)}, u32[]{:S(2)}) collective-permute-start(bf16[64,8192]{1,0:T(8,128)(2,1)S(1)} %get-tuple-element.89.upper_ref), channel_id=1, source_target_pairs={{16,0},{17,1},{18,2},{19,3},{20,4},{21,5},{22,6},{23,7},{24,8},{25... | collective-permute-start | bytes 3145736 | tf_op jit(solution)/shard_map/ppermute | solution.py:439

commit v7 on v6

--- a/solution.py
+++ b/solution.py
@@ -415,12 +415,13 @@
     def send_back(m, j, *ties):
         lines[m][j] = cyclic(after(lines[m][j], *ties), "fsdp", -j)
 
-    send_back(0, near[0], columns[far])
-    for m, j in [(0, far), *((0, j) for j in near[1:]), (1, near[0])]:
-        send_back(m, j, columns[near[-1]])
-    for j in [far, *near[1:]]:
-        send_back(1, j, *lines[0][1:], lines[1][near[0]])
-    columns[0] = after(columns[0], lines[0][near[0]])
+    send_back(0, far, columns[far])
+    for j in near:
+        send_back(0, j, columns[far])
+    send_back(1, near[0], lines[0][far])
+    for j in near[1:]:
+        send_back(1, j, lines[1][near[0]])
+    send_back(1, far, *[lines[0][j] for j in near])
     sums = weight_product(columns, values, weight, norm_gain, rep, groups, chunks, norm_scale)
     gathered = [doubled(sums[c], orders[c]) for c in range(chunks)]
     finished = ()
@@ -433,7 +434,7 @@
 
     result = ()
     for m in range(micro):
-        ties = [lines[-1][near[0]], *[g[0] for g in gathered]] if m == 0 else [*finished, *result]
+        ties = [*finished, *result] if m else [lines[1][near[-1]], *[g[0] for g in gathered]]
         lines[m][0] = after(lines[m][0], *ties)
         upper, piece = row_gradient(layer_input, top_grad, lines[m], me, m)
         passed = lax.ppermute(upper, "section", [(1, 0)])

time: 146 us -> 143 us (0.979); the launches traced: 146 us -> 140 us
  waiting for transfers between devices: 82.1 us -> 73.4 us
  starting transfers between devices: 42.6 us -> 45.8 us
    ppermute x12, waiting for transfers between devices: 66.9 us -> 58.5 us  [cyclic(): lax.ppermute(value, axis, [(i, (i + steps) % count) for i in range(count)])]
    ppermute x10, starting transfers between devices: 9.48 us -> 17.4 us  [flipped(): return lax.ppermute(value, axis, [(i, i ^ mask) for i in range(count)])]
    ppermute x12, starting transfers between devices: 30.5 us -> 25.8 us  [cyclic(): lax.ppermute(value, axis, [(i, (i + steps) % count) for i in range(count)])]
  transfers between devices with their start and end apart: 24 -> 24, of which waited for: 13 -> 15; matrix products, arithmetic and copies ran while one was open for 0% -> 0% of each run, Pallas kernels for 8% -> 10%
where the time goes in v7:
time: 143 us; the launch traced here: 140 us
  waiting for transfers between devices  73.4 us (51%)
  starting transfers between devices  45.8 us (32%)
  Pallas kernels  18.7 us (13%)
  local copies, waits for them, and re-layouts  1.6 us (1%)
    ppermute x12, waiting for transfers between devices, cyclic(): lax.ppermute(value, axis, [(i, (i + steps) % count) for i in range(count)])  58.5 us
    ppermute x12, starting transfers between devices, cyclic(): lax.ppermute(value, axis, [(i, (i + steps) % count) for i in range(count)])  25.8 us
    ppermute x10, starting transfers between devices, flipped(): return lax.ppermute(value, axis, [(i, i ^ mask) for i in range(count)])  17.4 us
    ppermute x10, waiting for transfers between devices, flipped(): return lax.ppermute(value, axis, [(i, i ^ mask) for i in range(count)])  11.6 us
    pallas_call x4, Pallas kernels, finished_half(): pl.pallas_call(kernel, grid_spec=pltpu.PrefetchScalarGridSpec(num_scalar_...  5.57 us
    ppermute x2, waiting for transfers between devices, local(): passed = lax.ppermute(upper, 'section', [(1, 0)])  3.26 us
    pallas_call x1, Pallas kernels, returned_blocks(): pl.pallas_call(kernel, grid=(shard // tile,), out_shape=[jax.ShapeDtypeSt...  3.19 us
    pallas_call x2, Pallas kernels, row_gradient(): pl.pallas_call(kernel, grid=(rows // step,), out_shape=[jax.ShapeDtypeStr...  2.99 us
  transfers between devices with their start and end apart: 24, of which 15 were waited for; matrix products, arithmetic and copies ran while one was open for 0% of the time, Pallas kernels for 10%

profile of v7, /device:TPU:0, one launch (start us, length us, event | category | flops | bytes accessed | tf_op | source)
XLA Modules:
  0.0 140.3 jit_solution(6508823687984350411)
XLA Ops:
  0.6 1.6 %copy-done = bf16[1,2,64,8192]{3,2,1,0:T(8,128)(2,1)S(1)} copy-done((bf16[1,2,64,8192]{3,2,1,0:T(8,128)(2,1)S(1)}, bf16[1,2,64,8192]{3,2,1,0:T(8,128)(2,1)}, u32[]{:S(2)}) %copy-start) | copy-done | bytes 2097176
  2.2 1.1 scaled_blocks.1
  3.3 3.1 %collective-permute-start = (bf16[128,1024]{1,0:T(8,128)(2,1)S(1)}, bf16[128,1024]{1,0:T(8,128)(2,1)S(1)}, u32[]{:S(2)}, u32[]{:S(2)}) collective-permute-start(bf16[128,1024]{1,0:T(8,128)(2,1)S(1)} %bitcast.10), channel_id=1, source_target_pairs={{0,1},{1,2},{2,3},{3,0},{4,5},{5,6},{6,7},{7,4},{8,9},{9,10},{10,1... | collective-permute-start | bytes 786440 | tf_op jit(solution)/shard_map/ppermute | solution.py:18
  6.4 1.5 %collective-permute-start.3 = (bf16[128,2048]{1,0:T(8,128)(2,1)S(1)}, bf16[128,2048]{1,0:T(8,128)(2,1)S(1)}, u32[]{:S(2)}, u32[]{:S(2)}) collective-permute-start(bf16[128,2048]{1,0:T(8,128)(2,1)S(1)} %get-tuple-element.51), channel_id=1, source_target_pairs={{0,4},{4,0},{8,12},{12,8},{1,5},{5,1},{9,13},{13,9},{2,6},{6,2},{1... | collective-permute-start | bytes 1572872 | tf_op jit(solution)/shard_map/ppermute | solution.py:23
  7.9 1.5 %collective-permute-start.4 = (bf16[128,2048]{1,0:T(8,128)(2,1)S(1)}, bf16[128,2048]{1,0:T(8,128)(2,1)S(1)}, u32[]{:S(2)}, u32[]{:S(2)}) collective-permute-start(bf16[128,2048]{1,0:T(8,128)(2,1)S(1)} %get-tuple-element.52), channel_id=1, source_target_pairs={{0,8},{4,12},{8,0},{12,4},{1,9},{5,13},{9,1},{13,5},{2,10},{6,14},... | collective-permute-start | bytes 1572872 | tf_op jit(solution)/shard_map/ppermute | solution.py:23
  9.4 0.5 collective-permute-start.5
  9.9 2.6 %collective-permute-start.1 = (bf16[128,1024]{1,0:T(8,128)(2,1)S(1)}, bf16[128,1024]{1,0:T(8,128)(2,1)S(1)}, u32[]{:S(2)}, u32[]{:S(2)}) collective-permute-start(bf16[128,1024]{1,0:T(8,128)(2,1)S(1)} %bitcast.11), channel_id=1, source_target_pairs={{0,2},{1,3},{2,0},{3,1},{4,6},{5,7},{6,4},{7,5},{8,10},{9,11},{10,... | collective-permute-start | bytes 786440 | tf_op jit(solution)/shard_map/ppermute | solution.py:18
  12.5 3.2 %collective-permute-done.refs_1_ = bf16[128,1024]{1,0:T(8,128)(2,1)S(1)} collective-permute-done((bf16[128,1024]{1,0:T(8,128)(2,1)S(1)}, bf16[128,1024]{1,0:T(8,128)(2,1)S(1)}, u32[]{:S(2)}, u32[]{:S(2)}) %collective-permute-start) | collective-permute-done | bytes 262176 | tf_op jit(solution)/shard_map/ppermute | solution.py:18
  15.6 1.4 collective-permute-start.2
  17.0 9.0 %collective-permute-done.1.refs_2_ = bf16[128,1024]{1,0:T(8,128)(2,1)S(1)} collective-permute-done((bf16[128,1024]{1,0:T(8,128)(2,1)S(1)}, bf16[128,1024]{1,0:T(8,128)(2,1)S(1)}, u32[]{:S(2)}, u32[]{:S(2)}) %collective-permute-start.1) | collective-permute-done | bytes 262176 | tf_op jit(solution)/shard_map/ppermute | solution.py:18
  26.0 4.2 %collective-permute-done.2.refs_3_ = bf16[128,1024]{1,0:T(8,128)(2,1)S(1)} collective-permute-done((bf16[128,1024]{1,0:T(8,128)(2,1)S(1)}, bf16[128,1024]{1,0:T(8,128)(2,1)S(1)}, u32[]{:S(2)}, u32[]{:S(2)}) %collective-permute-start.2) | collective-permute-done | bytes 262176 | tf_op jit(solution)/shard_map/ppermute | solution.py:18
  30.4 1.8 %collective-permute-done.4.refs_2_ = bf16[128,2048]{1,0:T(8,128)(2,1)S(1)} collective-permute-done((bf16[128,2048]{1,0:T(8,128)(2,1)S(1)}, bf16[128,2048]{1,0:T(8,128)(2,1)S(1)}, u32[]{:S(2)}, u32[]{:S(2)}) %collective-permute-start.4) | collective-permute-done | bytes 524320 | tf_op jit(solution)/shard_map/ppermute | solution.py:23
  32.2 0.5 regrouped.1
  32.7 1.6 %collective-permute-start.6 = (bf16[512,512]{1,0:T(8,128)(2,1)S(1)}, bf16[512,512]{1,0:T(8,128)(2,1)S(1)}, u32[]{:S(2)}, u32[]{:S(2)}) collective-permute-start(bf16[512,512]{1,0:T(8,128)(2,1)S(1)} %get-tuple-element.55), channel_id=1, source_target_pairs={{0,1},{1,2},{2,3},{3,0},{4,5},{5,6},{6,7},{7,4},{8,9},{9,10},{10,1... | collective-permute-start | bytes 1572872 | tf_op jit(solution)/shard_map/ppermute | solution.py:18
  34.3 1.5 %collective-permute-start.10 = (bf16[512,1024]{1,0:T(8,128)(2,1)S(1)}, bf16[512,1024]{1,0:T(8,128)(2,1)S(1)}, u32[]{:S(2)}, u32[]{:S(2)}) collective-permute-start(bf16[512,1024]{1,0:T(8,128)(2,1)S(1)} %joined.3.refs_4_), channel_id=1, source_target_pairs={{0,8},{4,12},{8,0},{12,4},{1,9},{5,13},{9,1},{13,5},{2,10},{6,14},... | collective-permute-start | bytes 3145736 | tf_op jit(solution)/shard_map/ppermute | solution.py:23
  35.8 1.2 collective-permute-start.11
  37.0 0.8 collective-permute-start.9
  37.8 1.4 collective-permute-start.7
  39.2 3.2 %returned_blocks.1 = (bf16[64,2048]{1,0:T(8,128)(2,1)S(1)}, bf16[64,2048]{1,0:T(8,128)(2,1)S(1)}, bf16[64,2048]{1,0:T(8,128)(2,1)S(1)}, bf16[64,2048]{1,0:T(8,12...) custom-call(bf16[128,1024]{1,0:T(8,128)(2,1)S(1)} %bitcast.14, ...), custom_call_target="tpu_custom_call" | custom-call | flops 2147483648 | bytes 7340032 | tf_op jit(solution)/shard_map/returned_blocks/pallas_call | solution.py:248
  42.4 7.1 %collective-permute-done.6.refs_1_ = bf16[512,512]{1,0:T(8,128)(2,1)S(1)} collective-permute-done((bf16[512,512]{1,0:T(8,128)(2,1)S(1)}, bf16[512,512]{1,0:T(8,128)(2,1)S(1)}, u32[]{:S(2)}, u32[]{:S(2)}) %collective-permute-start.6) | collective-permute-done | bytes 524320 | tf_op jit(solution)/shard_map/ppermute | solution.py:18
  49.5 19.9 %collective-permute-done.7.refs_2_ = bf16[512,512]{1,0:T(8,128)(2,1)S(1)} collective-permute-done((bf16[512,512]{1,0:T(8,128)(2,1)S(1)}, bf16[512,512]{1,0:T(8,128)(2,1)S(1)}, u32[]{:S(2)}, u32[]{:S(2)}) %collective-permute-start.7) | collective-permute-done | bytes 524320 | tf_op jit(solution)/shard_map/ppermute | solution.py:18
  69.4 3.3 %collective-permute-start.16 = (bf16[64,2048]{1,0:T(8,128)(2,1)S(1)}, bf16[64,2048]{1,0:T(8,128)(2,1)S(1)}, u32[]{:S(2)}, u32[]{:S(2)}) collective-permute-start(bf16[64,2048]{1,0:T(8,128)(2,1)S(1)} %get-tuple-element.74), channel_id=1, source_target_pairs={{0,2},{1,3},{2,0},{3,1},{4,6},{5,7},{6,4},{7,5},{8,10},{9,11},{10,... | collective-permute-start | bytes 786440 | tf_op jit(solution)/shard_map/ppermute | solution.py:18
  72.7 7.3 %collective-permute-done.10.refs_6_ = bf16[512,1024]{1,0:T(8,128)(2,1)S(1)} collective-permute-done((bf16[512,1024]{1,0:T(8,128)(2,1)S(1)}, bf16[512,1024]{1,0:T(8,128)(2,1)S(1)}, u32[]{:S(2)}, u32[]{:S(2)}) %collective-permute-start.10) | collective-permute-done | bytes 1048608 | tf_op jit(solution)/shard_map/ppermute | solution.py:23
  80.0 1.2 collective-permute-done.9.refs_5_
  81.2 2.7 %weight_product.1 = (bf16[272,1024]{1,0:T(8,128)(2,1)S(1)}, bf16[272,1024]{1,0:T(8,128)(2,1)S(1)}) custom-call(s32[1]{0:T(128)} %bitcast.3.rep_ref, bf16[512,512]{1,0:T(8,128)(2,1)S(1)} %get-tuple-element.54.refs_0_, bf16[512,512]{1,0:T(8,128)(2,1)S(1)} %collective-permute-done.6.refs_1_, bf16[512,512]{1,0:T(8,128)(2,1)S(1)} %collective-permute-done.7.refs_2_, ...), custom_call_target="tpu_custom_call" | custom-call | flops 2147483648 | bytes 8388608 | tf_op jit(solution)/shard_map/weight_product/pallas_call | solution.py:215
  84.0 1.5 %collective-permute-start.14 = (bf16[272,1024]{1,0:T(8,128)(2,1)S(1)}, bf16[272,1024]{1,0:T(8,128)(2,1)S(1)}, u32[]{:S(2)}, u32[]{:S(2)}) collective-permute-start(bf16[272,1024]{1,0:T(8,128)(2,1)S(1)} %get-tuple-element.62.refs_0_), channel_id=1, source_target_pairs={{0,4},{4,0},{8,12},{12,8},{1,5},{5,1},{9,13},{13,9},{2,6},{6,2},{1... | collective-permute-start | bytes 1671176 | tf_op jit(solution)/shard_map/ppermute | solution.py:23
  85.5 1.2 collective-permute-start.12
  86.7 8.4 %collective-permute-start.17 = (bf16[64,2048]{1,0:T(8,128)(2,1)S(1)}, bf16[64,2048]{1,0:T(8,128)(2,1)S(1)}, u32[]{:S(2)}, u32[]{:S(2)}) collective-permute-start(bf16[64,2048]{1,0:T(8,128)(2,1)S(1)} %get-tuple-element.75), channel_id=1, source_target_pairs={{0,3},{1,0},{2,1},{3,2},{4,7},{5,4},{6,5},{7,6},{8,11},{9,8},{10,9... | collective-permute-start | bytes 786440 | tf_op jit(solution)/shard_map/ppermute | solution.py:18
  95.1 6.8 %collective-permute-done.17.refs_1_ = bf16[64,2048]{1,0:T(8,128)(2,1)S(1)} collective-permute-done((bf16[64,2048]{1,0:T(8,128)(2,1)S(1)}, bf16[64,2048]{1,0:T(8,128)(2,1)S(1)}, u32[]{:S(2)}, u32[]{:S(2)}) %collective-permute-start.17) | collective-permute-done | bytes 262176 | tf_op jit(solution)/shard_map/ppermute | solution.py:18
  101.9 0.5 collective-permute-start.18
  102.4 0.8 collective-permute-start.20
  103.4 7.7 %collective-permute-start.15 = (bf16[544,1024]{1,0:T(8,128)(2,1)S(1)}, bf16[544,1024]{1,0:T(8,128)(2,1)S(1)}, u32[]{:S(2)}, u32[]{:S(2)}) collective-permute-start(bf16[544,1024]{1,0:T(8,128)(2,1)S(1)} %joined.5.sum_ref), channel_id=1, source_target_pairs={{0,8},{4,12},{8,0},{12,4},{1,9},{5,13},{9,1},{13,5},{2,10},{6,14},... | collective-permute-start | bytes 3342344 | tf_op jit(solution)/shard_map/ppermute | solution.py:23
  111.3 0.7 collective-permute-done.18.refs_3_
  112.0 2.8 %collective-permute-done.20.refs_3_ = bf16[64,2048]{1,0:T(8,128)(2,1)S(1)} collective-permute-done((bf16[64,2048]{1,0:T(8,128)(2,1)S(1)}, bf16[64,2048]{1,0:T(8,128)(2,1)S(1)}, u32[]{:S(2)}, u32[]{:S(2)}) %collective-permute-start.20) | collective-permute-done | bytes 262176 | tf_op jit(solution)/shard_map/ppermute | solution.py:18
  114.8 1.5 %row_gradient.2 = (bf16[64,8192]{1,0:T(8,128)(2,1)S(1)}, bf16[64,8192]{1,0:T(8,128)(2,1)S(1)}) custom-call(s32[1]{0:T(128)} %bitcast.1.me_ref, bf16[1,2,64,8192]{3,2,1,0:T(8,128)(2,1)S(1)} %copy-done.1, bf16[2,64,8192]{2,1,0:T(8,128)(2,1)S(1)} %copy-done.2, bf16[64,2048]{1,0:T(8,128)(2,1)S(1)} %get-tuple-element.77.refs_0_, ...), custom_call_target="tpu_custom_call" | custom-call | flops 6291456 | bytes 5242880 | tf_op jit(solution)/shard_map/row_gradient/pallas_call | solution.py:293
  116.3 1.3 collective-permute-start.21
  117.6 2.7 %collective-permute-start.22 = (bf16[64,2048]{1,0:T(8,128)(2,1)S(1)}, bf16[64,2048]{1,0:T(8,128)(2,1)S(1)}, u32[]{:S(2)}, u32[]{:S(2)}) collective-permute-start(bf16[64,2048]{1,0:T(8,128)(2,1)S(1)} %get-tuple-element.86), channel_id=1, source_target_pairs={{0,2},{1,3},{2,0},{3,1},{4,6},{5,7},{6,4},{7,5},{8,10},{9,11},{10,... | collective-permute-start | bytes 786440 | tf_op jit(solution)/shard_map/ppermute | solution.py:18
  120.3 1.4 finished_half.4
  121.7 1.4 finished_half.5
  123.1 1.1 input_gradient.2.refs_0_
  124.5 1.4 finished_half.6
  125.9 0.9 collective-permute-done.13.sum_ref
  126.8 1.4 finished_half.7
  128.2 4.9 %collective-permute-done.22.refs_2_ = bf16[64,2048]{1,0:T(8,128)(2,1)S(1)} collective-permute-done((bf16[64,2048]{1,0:T(8,128)(2,1)S(1)}, bf16[64,2048]{1,0:T(8,128)(2,1)S(1)}, u32[]{:S(2)}, u32[]{:S(2)}) %collective-permute-start.22) | collective-permute-done | bytes 262176 | tf_op jit(solution)/shard_map/ppermute | solution.py:18
  133.1 1.5 %row_gradient.3 = (bf16[64,8192]{1,0:T(8,128)(2,1)S(1)}, bf16[64,8192]{1,0:T(8,128)(2,1)S(1)}) custom-call(s32[1]{0:T(128)} %bitcast.1.me_ref, bf16[1,2,64,8192]{3,2,1,0:T(8,128)(2,1)S(1)} %copy-done.1, bf16[2,64,8192]{2,1,0:T(8,128)(2,1)S(1)} %copy-done.2, bf16[64,2048]{1,0:T(8,128)(2,1)S(1)} %get-tuple-element.84.refs_0_, ...), custom_call_target="tpu_custom_call" | custom-call | flops 6291456 | bytes 5242880 | tf_op jit(solution)/shard_map/row_gradient/pallas_call | solution.py:293
  134.6 1.3 collective-permute-start.23
  135.9 3.3 %collective-permute-done.23.passed_ref = bf16[64,8192]{1,0:T(8,128)(2,1)S(1)} collective-permute-done((bf16[64,8192]{1,0:T(8,128)(2,1)S(1)}, bf16[64,8192]{1,0:T(8,128)(2,1)S(1)}, u32[]{:S(2)}, u32[]{:S(2)}) %collective-permute-start.23) | collective-permute-done | bytes 1048608 | tf_op jit(solution)/shard_map/ppermute | solution.py:440
  139.2 1.1 input_gradient.3
  (27 shorter events, 1.0 us)
Async XLA Ops:
  0.6 1.6 %copy-start = (bf16[1,2,64,8192]{3,2,1,0:T(8,128)(2,1)S(1)}, bf16[1,2,64,8192]{3,2,1,0:T(8,128)(2,1)}, u32[]{:S(2)}) copy-start(bf16[1,2,64,8192]{3,2,1,0:T(8,128)(2,1)} %x_ref.3) | copy-start | bytes 6291460
  2.2 1.1 copy-start.4
  3.3 12.3 %collective-permute-start = (bf16[128,1024]{1,0:T(8,128)(2,1)S(1)}, bf16[128,1024]{1,0:T(8,128)(2,1)S(1)}, u32[]{:S(2)}, u32[]{:S(2)}) collective-permute-start(bf16[128,1024]{1,0:T(8,128)(2,1)S(1)} %bitcast.10), channel_id=1, source_target_pairs={{0,1},{1,2},{2,3},{3,0},{4,5},{5,6},{6,7},{7,4},{8,9},{9,10},{10,1... | collective-permute-start | bytes 786440 | tf_op jit(solution)/shard_map/ppermute | solution.py:18
  6.4 24.0 %collective-permute-start.3 = (bf16[128,2048]{1,0:T(8,128)(2,1)S(1)}, bf16[128,2048]{1,0:T(8,128)(2,1)S(1)}, u32[]{:S(2)}, u32[]{:S(2)}) collective-permute-start(bf16[128,2048]{1,0:T(8,128)(2,1)S(1)} %get-tuple-element.51), channel_id=1, source_target_pairs={{0,4},{4,0},{8,12},{12,8},{1,5},{5,1},{9,13},{13,9},{2,6},{6,2},{1... | collective-permute-start | bytes 1572872 | tf_op jit(solution)/shard_map/ppermute | solution.py:23
  7.9 24.3 %collective-permute-start.4 = (bf16[128,2048]{1,0:T(8,128)(2,1)S(1)}, bf16[128,2048]{1,0:T(8,128)(2,1)S(1)}, u32[]{:S(2)}, u32[]{:S(2)}) collective-permute-start(bf16[128,2048]{1,0:T(8,128)(2,1)S(1)} %get-tuple-element.52), channel_id=1, source_target_pairs={{0,8},{4,12},{8,0},{12,4},{1,9},{5,13},{9,1},{13,5},{2,10},{6,14},... | collective-permute-start | bytes 1572872 | tf_op jit(solution)/shard_map/ppermute | solution.py:23
  9.4 29.8 %copy-start.5 = (bf16[1,2048]{1,0:T(2,128)(2,1)S(1)}, bf16[1,2048]{1,0:T(2,128)(2,1)}, u32[]{:S(2)}) copy-start(bf16[1,2048]{1,0:T(2,128)(2,1)} %refs_9_.1) | copy-start | bytes 12292
  9.4 29.8 %copy-start.3 = (bf16[1,2048,1024]{2,1,0:T(8,128)(2,1)S(1)}, bf16[1,2048,1024]{2,1,0:T(8,128)(2,1)}, u32[]{:S(2)}) copy-start(bf16[1,2048,1024]{2,1,0:T(8,128)(2,1)} %param.7) | copy-start | bytes 12582916
  9.4 22.8 %collective-permute-start.5 = (bf16[128,2048]{1,0:T(8,128)(2,1)S(1)}, bf16[128,2048]{1,0:T(8,128)(2,1)S(1)}, u32[]{:S(2)}, u32[]{:S(2)}) collective-permute-start(bf16[128,2048]{1,0:T(8,128)(2,1)S(1)} %get-tuple-element.53), channel_id=1, source_target_pairs={{0,12},{4,8},{8,4},{12,0},{1,13},{5,9},{9,5},{13,1},{2,14},{6,10},... | collective-permute-start | bytes 1572872 | tf_op jit(solution)/shard_map/ppermute | solution.py:23
  9.9 16.2 %collective-permute-start.1 = (bf16[128,1024]{1,0:T(8,128)(2,1)S(1)}, bf16[128,1024]{1,0:T(8,128)(2,1)S(1)}, u32[]{:S(2)}, u32[]{:S(2)}) collective-permute-start(bf16[128,1024]{1,0:T(8,128)(2,1)S(1)} %bitcast.11), channel_id=1, source_target_pairs={{0,2},{1,3},{2,0},{3,1},{4,6},{5,7},{6,4},{7,5},{8,10},{9,11},{10,... | collective-permute-start | bytes 786440 | tf_op jit(solution)/shard_map/ppermute | solution.py:18
  15.6 14.6 %collective-permute-start.2 = (bf16[128,1024]{1,0:T(8,128)(2,1)S(1)}, bf16[128,1024]{1,0:T(8,128)(2,1)S(1)}, u32[]{:S(2)}, u32[]{:S(2)}) collective-permute-start(bf16[128,1024]{1,0:T(8,128)(2,1)S(1)} %bitcast.12), channel_id=1, source_target_pairs={{0,3},{1,0},{2,1},{3,2},{4,7},{5,4},{6,5},{7,6},{8,11},{9,8},{10,9... | collective-permute-start | bytes 786440 | tf_op jit(solution)/shard_map/ppermute | solution.py:18
  32.7 16.8 %collective-permute-start.6 = (bf16[512,512]{1,0:T(8,128)(2,1)S(1)}, bf16[512,512]{1,0:T(8,128)(2,1)S(1)}, u32[]{:S(2)}, u32[]{:S(2)}) collective-permute-start(bf16[512,512]{1,0:T(8,128)(2,1)S(1)} %get-tuple-element.55), channel_id=1, source_target_pairs={{0,1},{1,2},{2,3},{3,0},{4,5},{5,6},{6,7},{7,4},{8,9},{9,10},{10,1... | collective-permute-start | bytes 1572872 | tf_op jit(solution)/shard_map/ppermute | solution.py:18
  34.3 45.7 %collective-permute-start.10 = (bf16[512,1024]{1,0:T(8,128)(2,1)S(1)}, bf16[512,1024]{1,0:T(8,128)(2,1)S(1)}, u32[]{:S(2)}, u32[]{:S(2)}) collective-permute-start(bf16[512,1024]{1,0:T(8,128)(2,1)S(1)} %joined.3.refs_4_), channel_id=1, source_target_pairs={{0,8},{4,12},{8,0},{12,4},{1,9},{5,13},{9,1},{13,5},{2,10},{6,14},... | collective-permute-start | bytes 3145736 | tf_op jit(solution)/shard_map/ppermute | solution.py:23
  35.8 44.2 %collective-permute-start.11 = (bf16[512,1024]{1,0:T(8,128)(2,1)S(1)}, bf16[512,1024]{1,0:T(8,128)(2,1)S(1)}, u32[]{:S(2)}, u32[]{:S(2)}) collective-permute-start(bf16[512,1024]{1,0:T(8,128)(2,1)S(1)} %joined.3.refs_4_), channel_id=1, source_target_pairs={{0,12},{4,8},{8,4},{12,0},{1,13},{5,9},{9,5},{13,1},{2,14},{6,10},... | collective-permute-start | bytes 3145736 | tf_op jit(solution)/shard_map/ppermute | solution.py:23
  37.0 44.2 %collective-permute-start.9 = (bf16[512,1024]{1,0:T(8,128)(2,1)S(1)}, bf16[512,1024]{1,0:T(8,128)(2,1)S(1)}, u32[]{:S(2)}, u32[]{:S(2)}) collective-permute-start(bf16[512,1024]{1,0:T(8,128)(2,1)S(1)} %joined.3.refs_4_), channel_id=1, source_target_pairs={{0,4},{4,0},{8,12},{12,8},{1,5},{5,1},{9,13},{13,9},{2,6},{6,2},{1... | collective-permute-start | bytes 3145736 | tf_op jit(solution)/shard_map/ppermute | solution.py:23
  37.8 31.6 %collective-permute-start.7 = (bf16[512,512]{1,0:T(8,128)(2,1)S(1)}, bf16[512,512]{1,0:T(8,128)(2,1)S(1)}, u32[]{:S(2)}, u32[]{:S(2)}) collective-permute-start(bf16[512,512]{1,0:T(8,128)(2,1)S(1)} %get-tuple-element.56), channel_id=1, source_target_pairs={{0,2},{1,3},{2,0},{3,1},{4,6},{5,7},{6,4},{7,5},{8,10},{9,11},{10,... | collective-permute-start | bytes 1572872 | tf_op jit(solution)/shard_map/ppermute | solution.py:18
  49.5 31.7 %collective-permute-start.8 = (bf16[512,512]{1,0:T(8,128)(2,1)S(1)}, bf16[512,512]{1,0:T(8,128)(2,1)S(1)}, u32[]{:S(2)}, u32[]{:S(2)}) collective-permute-start(bf16[512,512]{1,0:T(8,128)(2,1)S(1)} %get-tuple-element.59), channel_id=1, source_target_pairs={{0,3},{1,0},{2,1},{3,2},{4,7},{5,4},{6,5},{7,6},{8,11},{9,8},{10,9... | collective-permute-start | bytes 1572872 | tf_op jit(solution)/shard_map/ppermute | solution.py:18
  69.4 17.3 %collective-permute-start.16 = (bf16[64,2048]{1,0:T(8,128)(2,1)S(1)}, bf16[64,2048]{1,0:T(8,128)(2,1)S(1)}, u32[]{:S(2)}, u32[]{:S(2)}) collective-permute-start(bf16[64,2048]{1,0:T(8,128)(2,1)S(1)} %get-tuple-element.74), channel_id=1, source_target_pairs={{0,2},{1,3},{2,0},{3,1},{4,6},{5,7},{6,4},{7,5},{8,10},{9,11},{10,... | collective-permute-start | bytes 786440 | tf_op jit(solution)/shard_map/ppermute | solution.py:18
  84.0 19.2 %collective-permute-start.14 = (bf16[272,1024]{1,0:T(8,128)(2,1)S(1)}, bf16[272,1024]{1,0:T(8,128)(2,1)S(1)}, u32[]{:S(2)}, u32[]{:S(2)}) collective-permute-start(bf16[272,1024]{1,0:T(8,128)(2,1)S(1)} %get-tuple-element.62.refs_0_), channel_id=1, source_target_pairs={{0,4},{4,0},{8,12},{12,8},{1,5},{5,1},{9,13},{13,9},{2,6},{6,2},{1... | collective-permute-start | bytes 1671176 | tf_op jit(solution)/shard_map/ppermute | solution.py:23
  85.5 25.6 %collective-permute-start.12 = (bf16[272,1024]{1,0:T(8,128)(2,1)S(1)}, bf16[272,1024]{1,0:T(8,128)(2,1)S(1)}, u32[]{:S(2)}, u32[]{:S(2)}) collective-permute-start(bf16[272,1024]{1,0:T(8,128)(2,1)S(1)} %get-tuple-element.61.refs_0_), channel_id=1, source_target_pairs={{0,8},{4,12},{8,0},{12,4},{1,9},{5,13},{9,1},{13,5},{2,10},{6,14},... | collective-permute-start | bytes 1671176 | tf_op jit(solution)/shard_map/ppermute | solution.py:23
  86.7 15.2 %collective-permute-start.17 = (bf16[64,2048]{1,0:T(8,128)(2,1)S(1)}, bf16[64,2048]{1,0:T(8,128)(2,1)S(1)}, u32[]{:S(2)}, u32[]{:S(2)}) collective-permute-start(bf16[64,2048]{1,0:T(8,128)(2,1)S(1)} %get-tuple-element.75), channel_id=1, source_target_pairs={{0,3},{1,0},{2,1},{3,2},{4,7},{5,4},{6,5},{7,6},{8,11},{9,8},{10,9... | collective-permute-start | bytes 786440 | tf_op jit(solution)/shard_map/ppermute | solution.py:18
  95.1 16.9 %collective-permute-start.19 = (bf16[64,2048]{1,0:T(8,128)(2,1)S(1)}, bf16[64,2048]{1,0:T(8,128)(2,1)S(1)}, u32[]{:S(2)}, u32[]{:S(2)}) collective-permute-start(bf16[64,2048]{1,0:T(8,128)(2,1)S(1)} %get-tuple-element.79), channel_id=1, source_target_pairs={{0,3},{1,0},{2,1},{3,2},{4,7},{5,4},{6,5},{7,6},{8,11},{9,8},{10,9... | collective-permute-start | bytes 786440 | tf_op jit(solution)/shard_map/ppermute | solution.py:18
  101.9 10.1 %collective-permute-start.18 = (bf16[64,2048]{1,0:T(8,128)(2,1)S(1)}, bf16[64,2048]{1,0:T(8,128)(2,1)S(1)}, u32[]{:S(2)}, u32[]{:S(2)}) collective-permute-start(bf16[64,2048]{1,0:T(8,128)(2,1)S(1)} %get-tuple-element.76), channel_id=1, source_target_pairs={{0,1},{1,2},{2,3},{3,0},{4,5},{5,6},{6,7},{7,4},{8,9},{9,10},{10,1... | collective-permute-start | bytes 786440 | tf_op jit(solution)/shard_map/ppermute | solution.py:18
  102.4 12.4 %copy-start.1 = (bf16[1,2,64,8192]{3,2,1,0:T(8,128)(2,1)S(1)}, bf16[1,2,64,8192]{3,2,1,0:T(8,128)(2,1)}, u32[]{:S(2)}) copy-start(bf16[1,2,64,8192]{3,2,1,0:T(8,128)(2,1)} %x_ref.3) | copy-start | bytes 6291460
  102.4 12.4 %copy-start.2 = (bf16[2,64,8192]{2,1,0:T(8,128)(2,1)S(1)}, bf16[2,64,8192]{2,1,0:T(8,128)(2,1)}, u32[]{:S(2)}) copy-start(bf16[2,64,8192]{2,1,0:T(8,128)(2,1)} %top_ref.3) | copy-start | bytes 6291460
  102.4 12.4 %collective-permute-start.20 = (bf16[64,2048]{1,0:T(8,128)(2,1)S(1)}, bf16[64,2048]{1,0:T(8,128)(2,1)S(1)}, u32[]{:S(2)}, u32[]{:S(2)}) collective-permute-start(bf16[64,2048]{1,0:T(8,128)(2,1)S(1)} %get-tuple-element.81), channel_id=1, source_target_pairs={{0,1},{1,2},{2,3},{3,0},{4,5},{5,6},{6,7},{7,4},{8,9},{9,10},{10,1... | collective-permute-start | bytes 786440 | tf_op jit(solution)/shard_map/ppermute | solution.py:18
  103.4 21.1 %collective-permute-start.15 = (bf16[544,1024]{1,0:T(8,128)(2,1)S(1)}, bf16[544,1024]{1,0:T(8,128)(2,1)S(1)}, u32[]{:S(2)}, u32[]{:S(2)}) collective-permute-start(bf16[544,1024]{1,0:T(8,128)(2,1)S(1)} %joined.5.sum_ref), channel_id=1, source_target_pairs={{0,8},{4,12},{8,0},{12,4},{1,9},{5,13},{9,1},{13,5},{2,10},{6,14},... | collective-permute-start | bytes 3342344 | tf_op jit(solution)/shard_map/ppermute | solution.py:23
  111.2 15.6 %collective-permute-start.13 = (bf16[544,1024]{1,0:T(8,128)(2,1)S(1)}, bf16[544,1024]{1,0:T(8,128)(2,1)S(1)}, u32[]{:S(2)}, u32[]{:S(2)}) collective-permute-start(bf16[544,1024]{1,0:T(8,128)(2,1)S(1)} %joined.4.sum_ref), channel_id=1, source_target_pairs={{0,4},{4,0},{8,12},{12,8},{1,5},{5,1},{9,13},{13,9},{2,6},{6,2},{1... | collective-permute-start | bytes 3342344 | tf_op jit(solution)/shard_map/ppermute | solution.py:23
  116.3 6.8 %collective-permute-start.21 = (bf16[64,8192]{1,0:T(8,128)(2,1)S(1)}, bf16[64,8192]{1,0:T(8,128)(2,1)S(1)}, u32[]{:S(2)}, u32[]{:S(2)}) collective-permute-start(bf16[64,8192]{1,0:T(8,128)(2,1)S(1)} %get-tuple-element.82.upper_ref), channel_id=1, source_target_pairs={{16,0},{17,1},{18,2},{19,3},{20,4},{21,5},{22,6},{23,7},{24,8},{25... | collective-permute-start | bytes 3145736 | tf_op jit(solution)/shard_map/ppermute | solution.py:440
  117.6 15.5 %collective-permute-start.22 = (bf16[64,2048]{1,0:T(8,128)(2,1)S(1)}, bf16[64,2048]{1,0:T(8,128)(2,1)S(1)}, u32[]{:S(2)}, u32[]{:S(2)}) collective-permute-start(bf16[64,2048]{1,0:T(8,128)(2,1)S(1)} %get-tuple-element.86), channel_id=1, source_target_pairs={{0,2},{1,3},{2,0},{3,1},{4,6},{5,7},{6,4},{7,5},{8,10},{9,11},{10,... | collective-permute-start | bytes 786440 | tf_op jit(solution)/shard_map/ppermute | solution.py:18
  134.6 4.6 %collective-permute-start.23 = (bf16[64,8192]{1,0:T(8,128)(2,1)S(1)}, bf16[64,8192]{1,0:T(8,128)(2,1)S(1)}, u32[]{:S(2)}, u32[]{:S(2)}) collective-permute-start(bf16[64,8192]{1,0:T(8,128)(2,1)S(1)} %get-tuple-element.87.upper_ref), channel_id=1, source_target_pairs={{16,0},{17,1},{18,2},{19,3},{20,4},{21,5},{22,6},{23,7},{24,8},{25... | collective-permute-start | bytes 3145736 | tf_op jit(solution)/shard_map/ppermute | solution.py:440

commit v8 on v7

--- a/solution.py
+++ b/solution.py
@@ -116,40 +116,40 @@
     return sum(((pos >> i) & 1) << bit for i, bit in enumerate(order))
 
 
-def regrouped(blocks, groups):
+def regrouped(blocks, me, groups):
     tokens, width = blocks[0].shape
-    chunk = width // groups
+    piece = width // groups
     reps = len(blocks)
-    if chunk % 128:
-        return [jnp.concatenate([b[:, j * chunk : (j + 1) * chunk] for b in blocks], axis=0) for j in range(groups)]
-
-    def kernel(*refs):
+    rows = reps * tokens
+    if piece % 128:
+        parts = jnp.stack([jnp.concatenate([b[:, j * piece : (j + 1) * piece] for b in blocks], axis=0) for j in range(groups)])
+        return jnp.roll(parts, me[0], axis=0).reshape(groups * rows, piece)
+
+    def kernel(me_ref, *refs):
         copies = []
         for e in range(reps):
             for j in range(groups):
-                source = refs[e].at[:, j * chunk : (j + 1) * chunk]
-                target = refs[reps + j].at[e * tokens : (e + 1) * tokens, :]
-                copies.append(pltpu.make_async_copy(source, target, refs[-1].at[e * groups + j]))
+                source = refs[e].at[:, j * piece : (j + 1) * piece]
+                at = pl.multiple_of(lax.rem(me_ref[0] + j, groups) * rows + e * tokens, tokens)
+                copies.append(pltpu.make_async_copy(source, refs[reps].at[pl.ds(at, tokens), :], refs[-1].at[e * groups + j]))
                 copies[-1].start()
         for copy in copies:
             copy.wait()
 
-    return list(
-        pl.pallas_call(
-            kernel,
-            out_shape=[jax.ShapeDtypeStruct((reps * tokens, chunk), bf16)] * groups,
-            in_specs=[ANY_ARG] * reps,
-            out_specs=[ANY_ARG] * groups,
-            scratch_shapes=[pltpu.SemaphoreType.DMA((reps * groups,))],
-            compiler_params=params(8),
-            cost_estimate=cost(0, 4 * reps * tokens * width),
-            name="regrouped",
-        )(*blocks)
-    )
-
-
-def weight_product(columns, values, weight, gain, rep, groups, count, norm_scale):
-    rows, width = columns[0].shape
+    return pl.pallas_call(
+        kernel,
+        out_shape=jax.ShapeDtypeStruct((groups * rows, piece), bf16),
+        in_specs=[SMEM_ARG] + [ANY_ARG] * reps,
+        out_specs=ANY_ARG,
+        scratch_shapes=[pltpu.SemaphoreType.DMA((reps * groups,))],
+        compiler_params=params(8),
+        cost_estimate=cost(0, 4 * rows * width),
+        name="regrouped",
+    )(me, *blocks)
+
+
+def weight_product(columns, values, weight, gain, me, rep, groups, count, norm_scale):
+    rows, width = columns.shape[0] // groups, columns.shape[1]
     reps = len(values)
     tokens = rows // reps
     features = values[0].shape[1]
@@ -164,9 +164,8 @@
 
     if chunk % 128:
         order = jnp.stack([v.reshape(groups, tokens, features) for v in values], axis=1)
-        raw = lax.dot_general(
-            jnp.concatenate(columns, axis=0), order.reshape(-1, features), contract, preferred_element_type=f32
-        )
+        order = jnp.roll(jnp.flip(order, axis=0), me[0] + 1, axis=0)
+        raw = lax.dot_general(columns, order.reshape(-1, features), contract, preferred_element_type=f32)
         own = lax.dynamic_slice_in_dim(weight, rep[0] * width, width, 0).astype(f32)
         dots = jnp.sum(raw * own, axis=1) * norm_scale
         factor = lax.dynamic_slice_in_dim(gain[0], rep[0] * width, width, 0).astype(f32) * norm_scale
@@ -178,15 +177,15 @@
             outs.append(jnp.concatenate([raw[at], jnp.pad(under, ((0, 0), (0, features - chunk)))], axis=0))
         return outs
 
-    def kernel(rep_ref, *refs):
-        column_refs, value_refs = refs[:groups], refs[groups : groups + reps]
-        weight_ref, gain_ref = refs[groups + reps], refs[groups + reps + 1]
-        out_refs, total = refs[groups + reps + 2 : -1], refs[-1]
+    def kernel(me_ref, rep_ref, column_ref, *refs):
+        value_refs, weight_ref, gain_ref = refs[:reps], refs[reps], refs[reps + 1]
+        out_refs, total = refs[reps + 2 : -1], refs[-1]
         start = pl.multiple_of(rep_ref[0] * width, width)
         for j in range(groups):
             right = jnp.concatenate([v[j * tokens : (j + 1) * tokens, :] for v in value_refs], axis=0)
+            at = pl.multiple_of(lax.rem(me_ref[0] - j + groups, groups) * rows, rows)
             for c in range(count):
-                block = column_refs[j][:, c * chunk : (c + 1) * chunk]
+                block = column_ref[pl.ds(at, rows), c * chunk : (c + 1) * chunk]
                 product = lax.dot_general(block, right, contract, preferred_element_type=f32)
                 if j == 0:
                     total[c] = product
@@ -215,13 +214,13 @@
     return pl.pallas_call(
         kernel,
         out_shape=[jax.ShapeDtypeStruct((chunk + 16, features), bf16)] * count,
-        in_specs=[SMEM_ARG] + [vmem] * (groups + reps + 2),
+        in_specs=[SMEM_ARG] * 2 + [vmem] * (reps + 3),
         out_specs=[vmem] * count,
         scratch_shapes=[pltpu.VMEM((count, chunk, features), f32)],
         compiler_params=params(24),
         cost_estimate=cost(2 * groups * rows * width * features, 2 * groups * rows * (width + features) + 4 * width * features),
         name="weight_product",
-    )(rep, *columns, *values, weight, gain)
+    )(me, rep, columns, *values, weight, gain)
 
 
 def returned_blocks(slots, weight, gain, micro):
@@ -399,30 +398,26 @@
     slots = [grads] + [cyclic(grads, "fsdp", j) for j in range(1, groups)]
 
     plane[0] = after(plane[0], *slots[1:])
-    sent = regrouped(plane, groups)
-    back = returned_blocks(slots, weight, norm_gain, micro)
+    sent = regrouped(plane, me, groups)
+    columns = lax.all_to_all(sent, "fsdp", split_axis=0, concat_axis=0, tiled=True)
+    back = returned_blocks([after(slots[0], sent), *slots[1:]], weight, norm_gain, micro)
     lines = [[back[j][m] for j in range(groups)] for m in range(micro)]
     far = groups // 2
     near = [j for j in range(1, groups) if j != far]
-    columns = list(sent)
-    columns[far] = cyclic(sent[far], "fsdp", far)
-    columns[near[0]] = cyclic(sent[near[0]], "fsdp", near[0])
-    for j in near[1:]:
-        columns[j] = cyclic(after(sent[j], back[0][0], columns[near[0]]), "fsdp", j)
-    held = after(joined(slots), sent[0])
+    held = after(joined(slots), sent)
     values = [held if e == 0 else flipped(held, "rep", e) for e in range(reps)]
 
     def send_back(m, j, *ties):
         lines[m][j] = cyclic(after(lines[m][j], *ties), "fsdp", -j)
 
-    send_back(0, far, columns[far])
-    for j in near:
-        send_back(0, j, columns[far])
+    for j in [far, *near]:
+        send_back(0, j, columns)
     send_back(1, near[0], lines[0][far])
     for j in near[1:]:
         send_back(1, j, lines[1][near[0]])
     send_back(1, far, *[lines[0][j] for j in near])
-    sums = weight_product(columns, values, weight, norm_gain, rep, groups, chunks, norm_scale)
+    columns = after(columns, back[0][0])
+    sums = weight_product(columns, values, weight, norm_gain, me, rep, groups, chunks, norm_scale)
     gathered = [doubled(sums[c], orders[c]) for c in range(chunks)]
     finished = ()
     for half in (0, 1):

time: 143 us -> 146 us (1.021); the launches traced: 140 us -> 145 us
  local copies, waits for them, and re-layouts: 1.6 us -> 15.3 us
  starting transfers between devices: 45.8 us -> 32.8 us
  Pallas kernels: 18.7 us -> 21.6 us
    all_to_all x0 -> x1, waiting for transfers between devices: none -> 31.9 us  [local(): lax.all_to_all(sent, 'fsdp', split_axis=0, concat_axis=0, tiled=True)]
    ppermute x12 -> x9, waiting for transfers between devices: 58.5 us -> 35.4 us  [cyclic(): lax.ppermute(value, axis, [(i, (i + steps) % count) for i in range(count)])]
    unnamed x12 -> x62, local copies, waits for them, and re-layouts: 1.6 us -> 15.3 us
    ppermute x12 -> x9, starting transfers between devices: 25.8 us -> 15.7 us  [cyclic(): lax.ppermute(value, axis, [(i, (i + steps) % count) for i in range(count)])]
    ppermute x10, waiting for transfers between devices: 11.6 us -> 4.16 us  [flipped(): return lax.ppermute(value, axis, [(i, i ^ mask) for i in range(count)])]
    ppermute x10, starting transfers between devices: 17.4 us -> 10.6 us  [flipped(): return lax.ppermute(value, axis, [(i, i ^ mask) for i in range(count)])]
    all_to_all x0 -> x1, starting transfers between devices: none -> 3.99 us  [local(): lax.all_to_all(sent, 'fsdp', split_axis=0, concat_axis=0, tiled=True)]
    pallas_call x1, Pallas kernels: 2.73 us -> 4.64 us  [weight_product(): pl.pallas_call(kernel, out_shape=[jax.ShapeDtypeStruct((chunk + 16, featu...]
  transfers between devices with their start and end apart: 24 -> 22, of which waited for: 15 -> 12; matrix products, arithmetic and copies ran while one was open for 0% -> 0% of each run, Pallas kernels for 10% -> 11%
where the time goes in v8:
time: 146 us; the launch traced here: 145 us
  waiting for transfers between devices  74.7 us (51%)
  starting transfers between devices  32.8 us (22%)
  Pallas kernels  21.6 us (15%)
  local copies, waits for them, and re-layouts  15.3 us (10%)
    ppermute x9, waiting for transfers between devices, cyclic(): lax.ppermute(value, axis, [(i, (i + steps) % count) for i in range(count)])  35.4 us
    all_to_all x1, waiting for transfers between devices, local(): lax.all_to_all(sent, 'fsdp', split_axis=0, concat_axis=0, tiled=True)  31.9 us
    ppermute x9, starting transfers between devices, cyclic(): lax.ppermute(value, axis, [(i, (i + steps) % count) for i in range(count)])  15.7 us
    unnamed x62, local copies, waits for them, and re-layouts  15.3 us
    ppermute x10, starting transfers between devices, flipped(): return lax.ppermute(value, axis, [(i, i ^ mask) for i in range(count)])  10.6 us
    pallas_call x4, Pallas kernels, finished_half(): pl.pallas_call(kernel, grid_spec=pltpu.PrefetchScalarGridSpec(num_scalar_...  5.61 us
    pallas_call x1, Pallas kernels, weight_product(): pl.pallas_call(kernel, out_shape=[jax.ShapeDtypeStruct((chunk + 16, featu...  4.64 us
    ppermute x10, waiting for transfers between devices, flipped(): return lax.ppermute(value, axis, [(i, i ^ mask) for i in range(count)])  4.16 us
  transfers between devices with their start and end apart: 22, of which 12 were waited for; matrix products, arithmetic and copies ran while one was open for 0% of the time, Pallas kernels for 11%

profile of v8, /device:TPU:0, one launch (start us, length us, event | category | flops | bytes accessed | tf_op | source)
XLA Modules:
  0.0 145.3 jit_solution(9205891583138237166)
XLA Ops:
  0.6 1.6 %copy-done = bf16[1,2,64,8192]{3,2,1,0:T(8,128)(2,1)S(1)} copy-done((bf16[1,2,64,8192]{3,2,1,0:T(8,128)(2,1)S(1)}, bf16[1,2,64,8192]{3,2,1,0:T(8,128)(2,1)}, u32[]{:S(2)}) %copy-start) | copy-done | bytes 2097176
  2.2 1.1 scaled_blocks.1
  3.3 3.1 %collective-permute-start = (bf16[128,1024]{1,0:T(8,128)(2,1)S(1)}, bf16[128,1024]{1,0:T(8,128)(2,1)S(1)}, u32[]{:S(2)}, u32[]{:S(2)}) collective-permute-start(bf16[128,1024]{1,0:T(8,128)(2,1)S(1)} %bitcast.13), channel_id=1, source_target_pairs={{0,1},{1,2},{2,3},{3,0},{4,5},{5,6},{6,7},{7,4},{8,9},{9,10},{10,1... | collective-permute-start | bytes 786440 | tf_op jit(solution)/shard_map/ppermute | solution.py:18
  6.4 1.5 %collective-permute-start.3 = (bf16[128,2048]{1,0:T(8,128)(2,1)S(1)}, bf16[128,2048]{1,0:T(8,128)(2,1)S(1)}, u32[]{:S(2)}, u32[]{:S(2)}) collective-permute-start(bf16[128,2048]{1,0:T(8,128)(2,1)S(1)} %get-tuple-element.47), channel_id=1, source_target_pairs={{0,4},{4,0},{8,12},{12,8},{1,5},{5,1},{9,13},{13,9},{2,6},{6,2},{1... | collective-permute-start | bytes 1572872 | tf_op jit(solution)/shard_map/ppermute | solution.py:23
  7.9 1.5 %collective-permute-start.4 = (bf16[128,2048]{1,0:T(8,128)(2,1)S(1)}, bf16[128,2048]{1,0:T(8,128)(2,1)S(1)}, u32[]{:S(2)}, u32[]{:S(2)}) collective-permute-start(bf16[128,2048]{1,0:T(8,128)(2,1)S(1)} %get-tuple-element.48), channel_id=1, source_target_pairs={{0,8},{4,12},{8,0},{12,4},{1,9},{5,13},{9,1},{13,5},{2,10},{6,14},... | collective-permute-start | bytes 1572872 | tf_op jit(solution)/shard_map/ppermute | solution.py:23
  9.9 2.6 %collective-permute-start.1 = (bf16[128,1024]{1,0:T(8,128)(2,1)S(1)}, bf16[128,1024]{1,0:T(8,128)(2,1)S(1)}, u32[]{:S(2)}, u32[]{:S(2)}) collective-permute-start(bf16[128,1024]{1,0:T(8,128)(2,1)S(1)} %bitcast.14), channel_id=1, source_target_pairs={{0,2},{1,3},{2,0},{3,1},{4,6},{5,7},{6,4},{7,5},{8,10},{9,11},{10,... | collective-permute-start | bytes 786440 | tf_op jit(solution)/shard_map/ppermute | solution.py:18
  12.5 3.2 %collective-permute-done.refs_1_ = bf16[128,1024]{1,0:T(8,128)(2,1)S(1)} collective-permute-done((bf16[128,1024]{1,0:T(8,128)(2,1)S(1)}, bf16[128,1024]{1,0:T(8,128)(2,1)S(1)}, u32[]{:S(2)}, u32[]{:S(2)}) %collective-permute-start) | collective-permute-done | bytes 262176 | tf_op jit(solution)/shard_map/ppermute | solution.py:18
  15.6 1.4 collective-permute-start.2
  17.0 9.0 %collective-permute-done.1.refs_2_ = bf16[128,1024]{1,0:T(8,128)(2,1)S(1)} collective-permute-done((bf16[128,1024]{1,0:T(8,128)(2,1)S(1)}, bf16[128,1024]{1,0:T(8,128)(2,1)S(1)}, u32[]{:S(2)}, u32[]{:S(2)}) %collective-permute-start.1) | collective-permute-done | bytes 262176 | tf_op jit(solution)/shard_map/ppermute | solution.py:18
  26.0 4.2 %collective-permute-done.2.refs_3_ = bf16[128,1024]{1,0:T(8,128)(2,1)S(1)} collective-permute-done((bf16[128,1024]{1,0:T(8,128)(2,1)S(1)}, bf16[128,1024]{1,0:T(8,128)(2,1)S(1)}, u32[]{:S(2)}, u32[]{:S(2)}) %collective-permute-start.2) | collective-permute-done | bytes 262176 | tf_op jit(solution)/shard_map/ppermute | solution.py:18
  31.0 1.2 collective-permute-done.4.refs_2_
  32.2 1.4 regrouped.1
  33.7 4.0 %all-to-all-start = ((bf16[4,512,512]{2,1,0:T(8,128)(2,1)}), bf16[4,512,512]{2,1,0:T(8,128)(2,1)S(1)}, u32[]{:S(2)}, u32[]{:S(2)}) async-start(bf16[4,512,512]{2,1,0:T(8,128)(2,1)} %bitcast.6), calls=%async_computation | async-start | bytes 4194304 | tf_op jit(solution)/shard_map/all_to_all | solution.py:402
  37.7 0.9 copy-done.7
  38.6 0.9 copy-done.10
  39.6 0.9 copy-done.13
  40.7 1.6 %collective-permute-start.6 = (bf16[512,1024]{1,0:T(8,128)(2,1)S(1)}, bf16[512,1024]{1,0:T(8,128)(2,1)}, u32[]{:S(2)}, u32[]{:S(2)}) collective-permute-start(bf16[512,1024]{1,0:T(8,128)(2,1)S(1)} %joined.3.refs_0_), channel_id=1, source_target_pairs={{0,4},{4,0},{8,12},{12,8},{1,5},{5,1},{9,13},{13,9},{2,6},{6,2},{1... | collective-permute-start | bytes 3145736 | tf_op jit(solution)/shard_map/ppermute | solution.py:23
  42.2 1.5 %collective-permute-start.7 = (bf16[512,1024]{1,0:T(8,128)(2,1)S(1)}, bf16[512,1024]{1,0:T(8,128)(2,1)}, u32[]{:S(2)}, u32[]{:S(2)}) collective-permute-start(bf16[512,1024]{1,0:T(8,128)(2,1)S(1)} %joined.3.refs_0_), channel_id=1, source_target_pairs={{0,8},{4,12},{8,0},{12,4},{1,9},{5,13},{9,1},{13,5},{2,10},{6,14},... | collective-permute-start | bytes 3145736 | tf_op jit(solution)/shard_map/ppermute | solution.py:23
  44.2 2.2 %copy-done.3 = bf16[1,2048,1024]{2,1,0:T(8,128)(2,1)S(1)} copy-done((bf16[1,2048,1024]{2,1,0:T(8,128)(2,1)S(1)}, bf16[1,2048,1024]{2,1,0:T(8,128)(2,1)}, u32[]{:S(2)}) %copy-start.3) | copy-done | bytes 4194328
  46.4 3.2 %returned_blocks.1 = (bf16[64,2048]{1,0:T(8,128)(2,1)S(1)}, bf16[64,2048]{1,0:T(8,128)(2,1)S(1)}, bf16[64,2048]{1,0:T(8,128)(2,1)S(1)}, bf16[64,2048]{1,0:T(8,12...) custom-call(bf16[128,1024]{1,0:T(8,128)(2,1)S(1)} %bitcast.17, ...), custom_call_target="tpu_custom_call" | custom-call | flops 2147483648 | bytes 7340032 | tf_op jit(solution)/shard_map/returned_blocks/pallas_call | solution.py:247
  51.7 0.7 copy-done.22
  52.4 0.7 copy-done.24
  55.3 31.9 %all-to-all-done = bf16[4,512,512]{2,1,0:T(8,128)(2,1)S(1)} async-done(((bf16[4,512,512]{2,1,0:T(8,128)(2,1)}), bf16[4,512,512]{2,1,0:T(8,128)(2,1)S(1)}, u32[]{:S(2)}, u32[]{:S(2)}) %all-to-all-start) | async-done | bytes 2097184 | tf_op jit(solution)/shard_map/all_to_all | solution.py:402
  87.6 2.2 %copy-done.4 = bf16[1,2048,1024]{2,1,0:T(8,128)(2,1)S(1)} copy-done((bf16[1,2048,1024]{2,1,0:T(8,128)(2,1)S(1)}, bf16[1,2048,1024]{2,1,0:T(8,128)(2,1)}, u32[]{:S(2)}) %copy-start.4) | copy-done | bytes 4194328
  89.8 4.6 %weight_product.1 = (bf16[272,1024]{1,0:T(8,128)(2,1)S(1)}, bf16[272,1024]{1,0:T(8,128)(2,1)S(1)}) custom-call(s32[1]{0:T(128)} %bitcast.1.me_ref, s32[1]{0:T(128)} %bitcast.3.rep_ref, bf16[2048,512]{1,0:T(8,128)(2,1)S(1)} %bitcast.10, bf16[512,1024]{1,0:T(8,128)(2,1)S(1)} %joined.3.refs_0_, bf16[512,1024]{1,0:T(8,128)(2,1)} %collective-permute-done.6.refs_1_, ...), custom_call_target="tpu_custom_call" | custom-call | flops 2147483648 | bytes 8388608 | tf_op jit(solution)/shard_map/weight_product/pallas_call | solution.py:214
  94.5 1.1 collective-permute-start.11
  95.5 1.3 collective-permute-start.9
  96.8 3.0 %collective-permute-start.14 = (bf16[64,2048]{1,0:T(8,128)(2,1)S(1)}, bf16[64,2048]{1,0:T(8,128)(2,1)S(1)}, u32[]{:S(2)}, u32[]{:S(2)}) collective-permute-start(bf16[64,2048]{1,0:T(8,128)(2,1)S(1)} %copy-done.29), channel_id=1, source_target_pairs={{0,3},{1,0},{2,1},{3,2},{4,7},{5,4},{6,5},{7,6},{8,11},{9,8},{10,9... | collective-permute-start | bytes 786440 | tf_op jit(solution)/shard_map/ppermute | solution.py:18
  99.8 1.4 collective-permute-start.16
  101.2 5.4 %collective-permute-done.14.refs_1_ = bf16[64,2048]{1,0:T(8,128)(2,1)S(1)} collective-permute-done((bf16[64,2048]{1,0:T(8,128)(2,1)S(1)}, bf16[64,2048]{1,0:T(8,128)(2,1)S(1)}, u32[]{:S(2)}, u32[]{:S(2)}) %collective-permute-start.14) | collective-permute-done | bytes 262176 | tf_op jit(solution)/shard_map/ppermute | solution.py:18
  106.7 1.7 %collective-permute-start.17 = (bf16[64,2048]{1,0:T(8,128)(2,1)S(1)}, bf16[64,2048]{1,0:T(8,128)(2,1)S(1)}, u32[]{:S(2)}, u32[]{:S(2)}) collective-permute-start(bf16[64,2048]{1,0:T(8,128)(2,1)S(1)} %copy-done.23), channel_id=1, source_target_pairs={{0,1},{1,2},{2,3},{3,0},{4,5},{5,6},{6,7},{7,4},{8,9},{9,10},{10,1... | collective-permute-start | bytes 786440 | tf_op jit(solution)/shard_map/ppermute | solution.py:18
  108.6 0.9 collective-permute-start.12
  109.9 7.0 %collective-permute-done.15.refs_3_ = bf16[64,2048]{1,0:T(8,128)(2,1)S(1)} collective-permute-done((bf16[64,2048]{1,0:T(8,128)(2,1)S(1)}, bf16[64,2048]{1,0:T(8,128)(2,1)S(1)}, u32[]{:S(2)}, u32[]{:S(2)}) %collective-permute-start.15) | collective-permute-done | bytes 262176 | tf_op jit(solution)/shard_map/ppermute | solution.py:18
  116.9 2.8 %collective-permute-done.17.refs_3_ = bf16[64,2048]{1,0:T(8,128)(2,1)S(1)} collective-permute-done((bf16[64,2048]{1,0:T(8,128)(2,1)S(1)}, bf16[64,2048]{1,0:T(8,128)(2,1)S(1)}, u32[]{:S(2)}, u32[]{:S(2)}) %collective-permute-start.17) | collective-permute-done | bytes 262176 | tf_op jit(solution)/shard_map/ppermute | solution.py:18
  119.7 1.5 %row_gradient.2 = (bf16[64,8192]{1,0:T(8,128)(2,1)S(1)}, bf16[64,8192]{1,0:T(8,128)(2,1)S(1)}) custom-call(s32[1]{0:T(128)} %bitcast.1.me_ref, bf16[1,2,64,8192]{3,2,1,0:T(8,128)(2,1)S(1)} %copy-done.1, bf16[2,64,8192]{2,1,0:T(8,128)(2,1)S(1)} %copy-done.2, bf16[64,2048]{1,0:T(8,128)(2,1)S(1)} %copy-done.18, ...), custom_call_target="tpu_custom_call" | custom-call | flops 6291456 | bytes 5242880 | tf_op jit(solution)/shard_map/row_gradient/pallas_call | solution.py:292
  121.3 1.3 collective-permute-start.18
  122.6 2.5 %collective-permute-start.19 = (bf16[64,2048]{1,0:T(8,128)(2,1)S(1)}, bf16[64,2048]{1,0:T(8,128)(2,1)S(1)}, u32[]{:S(2)}, u32[]{:S(2)}) collective-permute-start(bf16[64,2048]{1,0:T(8,128)(2,1)S(1)} %copy-done.21), channel_id=1, source_target_pairs={{0,2},{1,3},{2,0},{3,1},{4,6},{5,7},{6,4},{7,5},{8,10},{9,11},{10,... | collective-permute-start | bytes 786440 | tf_op jit(solution)/shard_map/ppermute | solution.py:18
  125.1 1.4 finished_half.4
  126.5 1.4 finished_half.5
  127.9 2.5 %collective-permute-done.12.sum_ref = bf16[544,1024]{1,0:T(8,128)(2,1)S(1)} collective-permute-done((bf16[544,1024]{1,0:T(8,128)(2,1)S(1)}, bf16[544,1024]{1,0:T(8,128)(2,1)S(1)}, u32[]{:S(2)}, u32[]{:S(2)}) %collective-permute-start.12) | collective-permute-done | bytes 1114144 | tf_op jit(solution)/shard_map/ppermute | solution.py:23
  130.4 1.4 finished_half.6
  131.8 1.4 finished_half.7
  133.2 1.1 input_gradient.2.refs_0_
  134.3 3.8 %collective-permute-done.19.refs_2_ = bf16[64,2048]{1,0:T(8,128)(2,1)S(1)} collective-permute-done((bf16[64,2048]{1,0:T(8,128)(2,1)S(1)}, bf16[64,2048]{1,0:T(8,128)(2,1)S(1)}, u32[]{:S(2)}, u32[]{:S(2)}) %collective-permute-start.19) | collective-permute-done | bytes 262176 | tf_op jit(solution)/shard_map/ppermute | solution.py:18
  138.1 1.5 %row_gradient.3 = (bf16[64,8192]{1,0:T(8,128)(2,1)S(1)}, bf16[64,8192]{1,0:T(8,128)(2,1)S(1)}) custom-call(s32[1]{0:T(128)} %bitcast.1.me_ref, bf16[1,2,64,8192]{3,2,1,0:T(8,128)(2,1)S(1)} %copy-done.1, bf16[2,64,8192]{2,1,0:T(8,128)(2,1)S(1)} %copy-done.2, bf16[64,2048]{1,0:T(8,128)(2,1)S(1)} %copy-done.16, ...), custom_call_target="tpu_custom_call" | custom-call | flops 6291456 | bytes 5242880 | tf_op jit(solution)/shard_map/row_gradient/pallas_call | solution.py:292
  139.6 1.3 collective-permute-start.20
  140.9 3.3 %collective-permute-done.20.passed_ref = bf16[64,8192]{1,0:T(8,128)(2,1)S(1)} collective-permute-done((bf16[64,8192]{1,0:T(8,128)(2,1)S(1)}, bf16[64,8192]{1,0:T(8,128)(2,1)S(1)}, u32[]{:S(2)}, u32[]{:S(2)}) %collective-permute-start.20) | collective-permute-done | bytes 1048608 | tf_op jit(solution)/shard_map/ppermute | solution.py:435
  144.2 1.1 input_gradient.3
  (73 shorter events, 7.2 us)
Async XLA Ops:
  0.6 1.6 %copy-start = (bf16[1,2,64,8192]{3,2,1,0:T(8,128)(2,1)S(1)}, bf16[1,2,64,8192]{3,2,1,0:T(8,128)(2,1)}, u32[]{:S(2)}) copy-start(bf16[1,2,64,8192]{3,2,1,0:T(8,128)(2,1)} %x_ref.3) | copy-start | bytes 6291460
  2.2 1.1 copy-start.5
  3.3 12.3 %collective-permute-start = (bf16[128,1024]{1,0:T(8,128)(2,1)S(1)}, bf16[128,1024]{1,0:T(8,128)(2,1)S(1)}, u32[]{:S(2)}, u32[]{:S(2)}) collective-permute-start(bf16[128,1024]{1,0:T(8,128)(2,1)S(1)} %bitcast.13), channel_id=1, source_target_pairs={{0,1},{1,2},{2,3},{3,0},{4,5},{5,6},{6,7},{7,4},{8,9},{9,10},{10,1... | collective-permute-start | bytes 786440 | tf_op jit(solution)/shard_map/ppermute | solution.py:18
  6.4 24.6 %collective-permute-start.3 = (bf16[128,2048]{1,0:T(8,128)(2,1)S(1)}, bf16[128,2048]{1,0:T(8,128)(2,1)S(1)}, u32[]{:S(2)}, u32[]{:S(2)}) collective-permute-start(bf16[128,2048]{1,0:T(8,128)(2,1)S(1)} %get-tuple-element.47), channel_id=1, source_target_pairs={{0,4},{4,0},{8,12},{12,8},{1,5},{5,1},{9,13},{13,9},{2,6},{6,2},{1... | collective-permute-start | bytes 1572872 | tf_op jit(solution)/shard_map/ppermute | solution.py:23
  7.9 24.3 %collective-permute-start.4 = (bf16[128,2048]{1,0:T(8,128)(2,1)S(1)}, bf16[128,2048]{1,0:T(8,128)(2,1)S(1)}, u32[]{:S(2)}, u32[]{:S(2)}) collective-permute-start(bf16[128,2048]{1,0:T(8,128)(2,1)S(1)} %get-tuple-element.48), channel_id=1, source_target_pairs={{0,8},{4,12},{8,0},{12,4},{1,9},{5,13},{9,1},{13,5},{2,10},{6,14},... | collective-permute-start | bytes 1572872 | tf_op jit(solution)/shard_map/ppermute | solution.py:23
  9.4 22.8 %collective-permute-start.5 = (bf16[128,2048]{1,0:T(8,128)(2,1)S(1)}, bf16[128,2048]{1,0:T(8,128)(2,1)S(1)}, u32[]{:S(2)}, u32[]{:S(2)}) collective-permute-start(bf16[128,2048]{1,0:T(8,128)(2,1)S(1)} %get-tuple-element.49), channel_id=1, source_target_pairs={{0,12},{4,8},{8,4},{12,0},{1,13},{5,9},{9,5},{13,1},{2,14},{6,10},... | collective-permute-start | bytes 1572872 | tf_op jit(solution)/shard_map/ppermute | solution.py:23
  9.9 16.2 %collective-permute-start.1 = (bf16[128,1024]{1,0:T(8,128)(2,1)S(1)}, bf16[128,1024]{1,0:T(8,128)(2,1)S(1)}, u32[]{:S(2)}, u32[]{:S(2)}) collective-permute-start(bf16[128,1024]{1,0:T(8,128)(2,1)S(1)} %bitcast.14), channel_id=1, source_target_pairs={{0,2},{1,3},{2,0},{3,1},{4,6},{5,7},{6,4},{7,5},{8,10},{9,11},{10,... | collective-permute-start | bytes 786440 | tf_op jit(solution)/shard_map/ppermute | solution.py:18
  15.6 18.0 %copy-start.6 = (bf16[128,1024]{1,0:T(8,128)(2,1)}, bf16[128,1024]{1,0:T(8,128)(2,1)S(1)}, u32[]{:S(2)}) copy-start(bf16[128,1024]{1,0:T(8,128)(2,1)S(1)} %collective-permute-done.refs_1_) | copy-start | bytes 786436
  15.6 14.6 %collective-permute-start.2 = (bf16[128,1024]{1,0:T(8,128)(2,1)S(1)}, bf16[128,1024]{1,0:T(8,128)(2,1)S(1)}, u32[]{:S(2)}, u32[]{:S(2)}) collective-permute-start(bf16[128,1024]{1,0:T(8,128)(2,1)S(1)} %bitcast.15), channel_id=1, source_target_pairs={{0,3},{1,0},{2,1},{3,2},{4,7},{5,4},{6,5},{7,6},{8,11},{9,8},{10,9... | collective-permute-start | bytes 786440 | tf_op jit(solution)/shard_map/ppermute | solution.py:18
  26.0 7.6 %copy-start.9 = (bf16[128,1024]{1,0:T(8,128)(2,1)}, bf16[128,1024]{1,0:T(8,128)(2,1)S(1)}, u32[]{:S(2)}) copy-start(bf16[128,1024]{1,0:T(8,128)(2,1)S(1)} %collective-permute-done.1.refs_2_) | copy-start | bytes 786436
  33.7 53.5 %all-to-all-start = ((bf16[4,512,512]{2,1,0:T(8,128)(2,1)}), bf16[4,512,512]{2,1,0:T(8,128)(2,1)S(1)}, u32[]{:S(2)}, u32[]{:S(2)}) async-start(bf16[4,512,512]{2,1,0:T(8,128)(2,1)} %bitcast.6), calls=%async_computation | async-start | bytes 4194304 | tf_op jit(solution)/shard_map/all_to_all | solution.py:402
  37.7 0.9 copy-start.7
  38.6 0.9 copy-start.10
  39.6 0.9 copy-start.13
  40.5 3.7 %copy-start.8 = (bf16[128,1024]{1,0:T(8,128)(2,1)S(1)}, bf16[128,1024]{1,0:T(8,128)(2,1)}, u32[]{:S(2)}) copy-start(bf16[128,1024]{1,0:T(8,128)(2,1)} %copy-done.6) | copy-start | bytes 786436
  40.5 3.7 %copy-start.11 = (bf16[128,1024]{1,0:T(8,128)(2,1)S(1)}, bf16[128,1024]{1,0:T(8,128)(2,1)}, u32[]{:S(2)}) copy-start(bf16[128,1024]{1,0:T(8,128)(2,1)} %copy-done.9) | copy-start | bytes 786436
  40.5 3.7 %copy-start.14 = (bf16[128,1024]{1,0:T(8,128)(2,1)S(1)}, bf16[128,1024]{1,0:T(8,128)(2,1)}, u32[]{:S(2)}) copy-start(bf16[128,1024]{1,0:T(8,128)(2,1)} %copy-done.12) | copy-start | bytes 786436
  40.5 3.7 %copy-start.19 = (bf16[1,2048]{1,0:T(2,128)(2,1)S(1)}, bf16[1,2048]{1,0:T(2,128)(2,1)}, u32[]{:S(2)}) copy-start(bf16[1,2048]{1,0:T(2,128)(2,1)} %refs_5_.3) | copy-start | bytes 12292
  40.7 46.5 %collective-permute-start.6 = (bf16[512,1024]{1,0:T(8,128)(2,1)S(1)}, bf16[512,1024]{1,0:T(8,128)(2,1)}, u32[]{:S(2)}, u32[]{:S(2)}) collective-permute-start(bf16[512,1024]{1,0:T(8,128)(2,1)S(1)} %joined.3.refs_0_), channel_id=1, source_target_pairs={{0,4},{4,0},{8,12},{12,8},{1,5},{5,1},{9,13},{13,9},{2,6},{6,2},{1... | collective-permute-start | bytes 3145736 | tf_op jit(solution)/shard_map/ppermute | solution.py:23
  42.2 45.4 %collective-permute-start.7 = (bf16[512,1024]{1,0:T(8,128)(2,1)S(1)}, bf16[512,1024]{1,0:T(8,128)(2,1)}, u32[]{:S(2)}, u32[]{:S(2)}) collective-permute-start(bf16[512,1024]{1,0:T(8,128)(2,1)S(1)} %joined.3.refs_0_), channel_id=1, source_target_pairs={{0,8},{4,12},{8,0},{12,4},{1,9},{5,13},{9,1},{13,5},{2,10},{6,14},... | collective-permute-start | bytes 3145736 | tf_op jit(solution)/shard_map/ppermute | solution.py:23
  43.7 43.9 %collective-permute-start.8 = (bf16[512,1024]{1,0:T(8,128)(2,1)S(1)}, bf16[512,1024]{1,0:T(8,128)(2,1)}, u32[]{:S(2)}, u32[]{:S(2)}) collective-permute-start(bf16[512,1024]{1,0:T(8,128)(2,1)S(1)} %joined.3.refs_0_), channel_id=1, source_target_pairs={{0,12},{4,8},{8,4},{12,0},{1,13},{5,9},{9,5},{13,1},{2,14},{6,10},... | collective-permute-start | bytes 3145736 | tf_op jit(solution)/shard_map/ppermute | solution.py:23
  44.2 2.2 %copy-start.3 = (bf16[1,2048,1024]{2,1,0:T(8,128)(2,1)S(1)}, bf16[1,2048,1024]{2,1,0:T(8,128)(2,1)}, u32[]{:S(2)}) copy-start(bf16[1,2048,1024]{2,1,0:T(8,128)(2,1)} %param.7) | copy-start | bytes 12582916
  50.3 0.7 copy-start.17
  51.7 0.7 copy-start.22
  52.4 0.7 copy-start.24
  54.6 0.7 copy-start.30
  87.2 9.6 %collective-permute-start.13 = (bf16[64,2048]{1,0:T(8,128)(2,1)}, bf16[64,2048]{1,0:T(8,128)(2,1)S(1)}, u32[]{:S(2)}, u32[]{:S(2)}) collective-permute-start(bf16[64,2048]{1,0:T(8,128)(2,1)} %copy-done.30), channel_id=1, source_target_pairs={{0,2},{1,3},{2,0},{3,1},{4,6},{5,7},{6,4},{7,5},{8,10},{9,11},{10,... | collective-permute-start | bytes 786440 | tf_op jit(solution)/shard_map/ppermute | solution.py:18
  87.6 2.2 %copy-start.4 = (bf16[1,2048,1024]{2,1,0:T(8,128)(2,1)S(1)}, bf16[1,2048,1024]{2,1,0:T(8,128)(2,1)}, u32[]{:S(2)}) copy-start(bf16[1,2048,1024]{2,1,0:T(8,128)(2,1)} %param.7) | copy-start | bytes 12582916
  89.8 7.0 %copy-start.29 = (bf16[64,2048]{1,0:T(8,128)(2,1)S(1)}, bf16[64,2048]{1,0:T(8,128)(2,1)}, u32[]{:S(2)}) copy-start(bf16[64,2048]{1,0:T(8,128)(2,1)} %copy-done.28) | copy-start | bytes 786436
  89.8 10.0 %copy-start.25 = (bf16[64,2048]{1,0:T(8,128)(2,1)S(1)}, bf16[64,2048]{1,0:T(8,128)(2,1)}, u32[]{:S(2)}) copy-start(bf16[64,2048]{1,0:T(8,128)(2,1)} %copy-done.24) | copy-start | bytes 786436
  89.8 16.8 %copy-start.27 = (bf16[64,2048]{1,0:T(8,128)(2,1)S(1)}, bf16[64,2048]{1,0:T(8,128)(2,1)}, u32[]{:S(2)}) copy-start(bf16[64,2048]{1,0:T(8,128)(2,1)} %copy-done.26) | copy-start | bytes 786436
  89.8 16.8 %copy-start.23 = (bf16[64,2048]{1,0:T(8,128)(2,1)S(1)}, bf16[64,2048]{1,0:T(8,128)(2,1)}, u32[]{:S(2)}) copy-start(bf16[64,2048]{1,0:T(8,128)(2,1)} %copy-done.22) | copy-start | bytes 786436
  94.5 13.9 %collective-permute-start.11 = (bf16[272,1024]{1,0:T(8,128)(2,1)S(1)}, bf16[272,1024]{1,0:T(8,128)(2,1)S(1)}, u32[]{:S(2)}, u32[]{:S(2)}) collective-permute-start(bf16[272,1024]{1,0:T(8,128)(2,1)S(1)} %get-tuple-element.56.refs_0_), channel_id=1, source_target_pairs={{0,4},{4,0},{8,12},{12,8},{1,5},{5,1},{9,13},{13,9},{2,6},{6,2},{1... | collective-permute-start | bytes 1671176 | tf_op jit(solution)/shard_map/ppermute | solution.py:23
  95.5 13.9 %collective-permute-start.9 = (bf16[272,1024]{1,0:T(8,128)(2,1)S(1)}, bf16[272,1024]{1,0:T(8,128)(2,1)S(1)}, u32[]{:S(2)}, u32[]{:S(2)}) collective-permute-start(bf16[272,1024]{1,0:T(8,128)(2,1)S(1)} %get-tuple-element.55.refs_0_), channel_id=1, source_target_pairs={{0,8},{4,12},{8,0},{12,4},{1,9},{5,13},{9,1},{13,5},{2,10},{6,14},... | collective-permute-start | bytes 1671176 | tf_op jit(solution)/shard_map/ppermute | solution.py:23
  96.8 9.8 %collective-permute-start.14 = (bf16[64,2048]{1,0:T(8,128)(2,1)S(1)}, bf16[64,2048]{1,0:T(8,128)(2,1)S(1)}, u32[]{:S(2)}, u32[]{:S(2)}) collective-permute-start(bf16[64,2048]{1,0:T(8,128)(2,1)S(1)} %copy-done.29), channel_id=1, source_target_pairs={{0,3},{1,0},{2,1},{3,2},{4,7},{5,4},{6,5},{7,6},{8,11},{9,8},{10,9... | collective-permute-start | bytes 786440 | tf_op jit(solution)/shard_map/ppermute | solution.py:18
  99.8 17.1 %collective-permute-start.16 = (bf16[64,2048]{1,0:T(8,128)(2,1)S(1)}, bf16[64,2048]{1,0:T(8,128)(2,1)S(1)}, u32[]{:S(2)}, u32[]{:S(2)}) collective-permute-start(bf16[64,2048]{1,0:T(8,128)(2,1)S(1)} %copy-done.25), channel_id=1, source_target_pairs={{0,3},{1,0},{2,1},{3,2},{4,7},{5,4},{6,5},{7,6},{8,11},{9,8},{10,9... | collective-permute-start | bytes 786440 | tf_op jit(solution)/shard_map/ppermute | solution.py:18
  106.6 10.3 %collective-permute-start.15 = (bf16[64,2048]{1,0:T(8,128)(2,1)S(1)}, bf16[64,2048]{1,0:T(8,128)(2,1)S(1)}, u32[]{:S(2)}, u32[]{:S(2)}) collective-permute-start(bf16[64,2048]{1,0:T(8,128)(2,1)S(1)} %copy-done.27), channel_id=1, source_target_pairs={{0,1},{1,2},{2,3},{3,0},{4,5},{5,6},{6,7},{7,4},{8,9},{9,10},{10,1... | collective-permute-start | bytes 786440 | tf_op jit(solution)/shard_map/ppermute | solution.py:18
  106.6 13.1 %copy-start.1 = (bf16[1,2,64,8192]{3,2,1,0:T(8,128)(2,1)S(1)}, bf16[1,2,64,8192]{3,2,1,0:T(8,128)(2,1)}, u32[]{:S(2)}) copy-start(bf16[1,2,64,8192]{3,2,1,0:T(8,128)(2,1)} %x_ref.3) | copy-start | bytes 6291460
  106.6 13.1 %copy-start.2 = (bf16[2,64,8192]{2,1,0:T(8,128)(2,1)S(1)}, bf16[2,64,8192]{2,1,0:T(8,128)(2,1)}, u32[]{:S(2)}) copy-start(bf16[2,64,8192]{2,1,0:T(8,128)(2,1)} %top_ref.3) | copy-start | bytes 6291460
  106.7 13.1 %copy-start.18 = (bf16[64,2048]{1,0:T(8,128)(2,1)S(1)}, bf16[64,2048]{1,0:T(8,128)(2,1)}, u32[]{:S(2)}) copy-start(bf16[64,2048]{1,0:T(8,128)(2,1)} %copy-done.17) | copy-start | bytes 786436
  106.7 13.1 %collective-permute-start.17 = (bf16[64,2048]{1,0:T(8,128)(2,1)S(1)}, bf16[64,2048]{1,0:T(8,128)(2,1)S(1)}, u32[]{:S(2)}, u32[]{:S(2)}) collective-permute-start(bf16[64,2048]{1,0:T(8,128)(2,1)S(1)} %copy-done.23), channel_id=1, source_target_pairs={{0,1},{1,2},{2,3},{3,0},{4,5},{5,6},{6,7},{7,4},{8,9},{9,10},{10,1... | collective-permute-start | bytes 786440 | tf_op jit(solution)/shard_map/ppermute | solution.py:18
  108.6 21.8 %collective-permute-start.12 = (bf16[544,1024]{1,0:T(8,128)(2,1)S(1)}, bf16[544,1024]{1,0:T(8,128)(2,1)S(1)}, u32[]{:S(2)}, u32[]{:S(2)}) collective-permute-start(bf16[544,1024]{1,0:T(8,128)(2,1)S(1)} %joined.5.sum_ref), channel_id=1, source_target_pairs={{0,8},{4,12},{8,0},{12,4},{1,9},{5,13},{9,1},{13,5},{2,10},{6,14},... | collective-permute-start | bytes 3342344 | tf_op jit(solution)/shard_map/ppermute | solution.py:23
  109.6 12.9 %copy-start.21 = (bf16[64,2048]{1,0:T(8,128)(2,1)S(1)}, bf16[64,2048]{1,0:T(8,128)(2,1)}, u32[]{:S(2)}) copy-start(bf16[64,2048]{1,0:T(8,128)(2,1)} %copy-done.20) | copy-start | bytes 786436
  109.7 22.1 %collective-permute-start.10 = (bf16[544,1024]{1,0:T(8,128)(2,1)S(1)}, bf16[544,1024]{1,0:T(8,128)(2,1)S(1)}, u32[]{:S(2)}, u32[]{:S(2)}) collective-permute-start(bf16[544,1024]{1,0:T(8,128)(2,1)S(1)} %joined.4.sum_ref), channel_id=1, source_target_pairs={{0,4},{4,0},{8,12},{12,8},{1,5},{5,1},{9,13},{13,9},{2,6},{6,2},{1... | collective-permute-start | bytes 3342344 | tf_op jit(solution)/shard_map/ppermute | solution.py:23
  121.3 11.9 %collective-permute-start.18 = (bf16[64,8192]{1,0:T(8,128)(2,1)S(1)}, bf16[64,8192]{1,0:T(8,128)(2,1)S(1)}, u32[]{:S(2)}, u32[]{:S(2)}) collective-permute-start(bf16[64,8192]{1,0:T(8,128)(2,1)S(1)} %get-tuple-element.76.upper_ref), channel_id=1, source_target_pairs={{16,0},{17,1},{18,2},{19,3},{20,4},{21,5},{22,6},{23,7},{24,8},{25... | collective-permute-start | bytes 3145736 | tf_op jit(solution)/shard_map/ppermute | solution.py:435
  122.6 15.5 %collective-permute-start.19 = (bf16[64,2048]{1,0:T(8,128)(2,1)S(1)}, bf16[64,2048]{1,0:T(8,128)(2,1)S(1)}, u32[]{:S(2)}, u32[]{:S(2)}) collective-permute-start(bf16[64,2048]{1,0:T(8,128)(2,1)S(1)} %copy-done.21), channel_id=1, source_target_pairs={{0,2},{1,3},{2,0},{3,1},{4,6},{5,7},{6,4},{7,5},{8,10},{9,11},{10,... | collective-permute-start | bytes 786440 | tf_op jit(solution)/shard_map/ppermute | solution.py:18
  133.2 4.9 %copy-start.16 = (bf16[64,2048]{1,0:T(8,128)(2,1)S(1)}, bf16[64,2048]{1,0:T(8,128)(2,1)}, u32[]{:S(2)}) copy-start(bf16[64,2048]{1,0:T(8,128)(2,1)} %copy-done.15) | copy-start | bytes 786436
  139.6 4.6 %collective-permute-start.20 = (bf16[64,8192]{1,0:T(8,128)(2,1)S(1)}, bf16[64,8192]{1,0:T(8,128)(2,1)S(1)}, u32[]{:S(2)}, u32[]{:S(2)}) collective-permute-start(bf16[64,8192]{1,0:T(8,128)(2,1)S(1)} %get-tuple-element.81.upper_ref), channel_id=1, source_target_pairs={{16,0},{17,1},{18,2},{19,3},{20,4},{21,5},{22,6},{23,7},{24,8},{25... | collective-permute-start | bytes 3145736 | tf_op jit(solution)/shard_map/ppermute | solution.py:435
  (5 other events, 3.5 us)

commit v9 on v7

--- a/solution.py
+++ b/solution.py
@@ -405,10 +405,9 @@
     far = groups // 2
     near = [j for j in range(1, groups) if j != far]
     columns = list(sent)
-    columns[far] = cyclic(sent[far], "fsdp", far)
-    columns[near[0]] = cyclic(sent[near[0]], "fsdp", near[0])
-    for j in near[1:]:
-        columns[j] = cyclic(after(sent[j], back[0][0], columns[near[0]]), "fsdp", j)
+    for j in near:
+        columns[j] = cyclic(sent[j], "fsdp", j)
+    columns[far] = cyclic(after(sent[far], back[0][0], *[columns[j] for j in near]), "fsdp", far)
     held = after(joined(slots), sent[0])
     values = [held if e == 0 else flipped(held, "rep", e) for e in range(reps)]
 

time: 143 us -> 147 us (1.028); the launches traced: 140 us -> 147 us
  waiting for transfers between devices: 73.4 us -> 95.5 us
  starting transfers between devices: 45.8 us -> 30.3 us
    ppermute x12, waiting for transfers between devices: 58.5 us -> 88.2 us  [cyclic(): lax.ppermute(value, axis, [(i, (i + steps) % count) for i in range(count)])]
    ppermute x12, starting transfers between devices: 25.8 us -> 16.4 us  [cyclic(): lax.ppermute(value, axis, [(i, (i + steps) % count) for i in range(count)])]
    ppermute x10, waiting for transfers between devices: 11.6 us -> 4.07 us  [flipped(): return lax.ppermute(value, axis, [(i, i ^ mask) for i in range(count)])]
    ppermute x10, starting transfers between devices: 17.4 us -> 11.2 us  [flipped(): return lax.ppermute(value, axis, [(i, i ^ mask) for i in range(count)])]
where the time goes in v9:
time: 147 us
  waiting for transfers between devices  95.5 us (65%)
  starting transfers between devices  30.3 us (21%)
  Pallas kernels  18.8 us (13%)
  local copies, waits for them, and re-layouts  1.6 us (1%)
    ppermute x12, waiting for transfers between devices, cyclic(): lax.ppermute(value, axis, [(i, (i + steps) % count) for i in range(count)])  88.2 us
    ppermute x12, starting transfers between devices, cyclic(): lax.ppermute(value, axis, [(i, (i + steps) % count) for i in range(count)])  16.4 us
    ppermute x10, starting transfers between devices, flipped(): return lax.ppermute(value, axis, [(i, i ^ mask) for i in range(count)])  11.2 us
    pallas_call x4, Pallas kernels, finished_half(): pl.pallas_call(kernel, grid_spec=pltpu.PrefetchScalarGridSpec(num_scalar_...  5.61 us
    ppermute x10, waiting for transfers between devices, flipped(): return lax.ppermute(value, axis, [(i, i ^ mask) for i in range(count)])  4.07 us
    ppermute x2, waiting for transfers between devices, local(): passed = lax.ppermute(upper, 'section', [(1, 0)])  3.26 us
    pallas_call x1, Pallas kernels, returned_blocks(): pl.pallas_call(kernel, grid=(shard // tile,), out_shape=[jax.ShapeDtypeSt...  3.2 us
    pallas_call x2, Pallas kernels, row_gradient(): pl.pallas_call(kernel, grid=(rows // step,), out_shape=[jax.ShapeDtypeStr...  3.03 us
  transfers between devices with their start and end apart: 24, of which 15 were waited for; matrix products, arithmetic and copies ran while one was open for 0% of the time, Pallas kernels for 10%

profile of v9, /device:TPU:0, one launch (start us, length us, event | category | flops | bytes accessed | tf_op | source)
XLA Modules:
  0.0 146.9 jit_solution(7904481349597144745)
XLA Ops:
  0.6 1.6 %copy-done = bf16[1,2,64,8192]{3,2,1,0:T(8,128)(2,1)S(1)} copy-done((bf16[1,2,64,8192]{3,2,1,0:T(8,128)(2,1)S(1)}, bf16[1,2,64,8192]{3,2,1,0:T(8,128)(2,1)}, u32[]{:S(2)}) %copy-start) | copy-done | bytes 2097176
  2.2 1.1 scaled_blocks.1
  3.3 3.1 %collective-permute-start = (bf16[128,1024]{1,0:T(8,128)(2,1)S(1)}, bf16[128,1024]{1,0:T(8,128)(2,1)S(1)}, u32[]{:S(2)}, u32[]{:S(2)}) collective-permute-start(bf16[128,1024]{1,0:T(8,128)(2,1)S(1)} %bitcast.10), channel_id=1, source_target_pairs={{0,1},{1,2},{2,3},{3,0},{4,5},{5,6},{6,7},{7,4},{8,9},{9,10},{10,1... | collective-permute-start | bytes 786440 | tf_op jit(solution)/shard_map/ppermute | solution.py:18
  6.4 1.5 %collective-permute-start.3 = (bf16[128,2048]{1,0:T(8,128)(2,1)S(1)}, bf16[128,2048]{1,0:T(8,128)(2,1)S(1)}, u32[]{:S(2)}, u32[]{:S(2)}) collective-permute-start(bf16[128,2048]{1,0:T(8,128)(2,1)S(1)} %get-tuple-element.51), channel_id=1, source_target_pairs={{0,4},{4,0},{8,12},{12,8},{1,5},{5,1},{9,13},{13,9},{2,6},{6,2},{1... | collective-permute-start | bytes 1572872 | tf_op jit(solution)/shard_map/ppermute | solution.py:23
  7.9 1.5 %collective-permute-start.4 = (bf16[128,2048]{1,0:T(8,128)(2,1)S(1)}, bf16[128,2048]{1,0:T(8,128)(2,1)S(1)}, u32[]{:S(2)}, u32[]{:S(2)}) collective-permute-start(bf16[128,2048]{1,0:T(8,128)(2,1)S(1)} %get-tuple-element.52), channel_id=1, source_target_pairs={{0,8},{4,12},{8,0},{12,4},{1,9},{5,13},{9,1},{13,5},{2,10},{6,14},... | collective-permute-start | bytes 1572872 | tf_op jit(solution)/shard_map/ppermute | solution.py:23
  9.4 0.5 collective-permute-start.5
  9.9 2.6 %collective-permute-start.1 = (bf16[128,1024]{1,0:T(8,128)(2,1)S(1)}, bf16[128,1024]{1,0:T(8,128)(2,1)S(1)}, u32[]{:S(2)}, u32[]{:S(2)}) collective-permute-start(bf16[128,1024]{1,0:T(8,128)(2,1)S(1)} %bitcast.11), channel_id=1, source_target_pairs={{0,2},{1,3},{2,0},{3,1},{4,6},{5,7},{6,4},{7,5},{8,10},{9,11},{10,... | collective-permute-start | bytes 786440 | tf_op jit(solution)/shard_map/ppermute | solution.py:18
  12.5 3.2 %collective-permute-done.refs_1_ = bf16[128,1024]{1,0:T(8,128)(2,1)S(1)} collective-permute-done((bf16[128,1024]{1,0:T(8,128)(2,1)S(1)}, bf16[128,1024]{1,0:T(8,128)(2,1)S(1)}, u32[]{:S(2)}, u32[]{:S(2)}) %collective-permute-start) | collective-permute-done | bytes 262176 | tf_op jit(solution)/shard_map/ppermute | solution.py:18
  15.6 1.4 collective-permute-start.2
  17.0 9.0 %collective-permute-done.1.refs_2_ = bf16[128,1024]{1,0:T(8,128)(2,1)S(1)} collective-permute-done((bf16[128,1024]{1,0:T(8,128)(2,1)S(1)}, bf16[128,1024]{1,0:T(8,128)(2,1)S(1)}, u32[]{:S(2)}, u32[]{:S(2)}) %collective-permute-start.1) | collective-permute-done | bytes 262176 | tf_op jit(solution)/shard_map/ppermute | solution.py:18
  26.0 4.2 %collective-permute-done.2.refs_3_ = bf16[128,1024]{1,0:T(8,128)(2,1)S(1)} collective-permute-done((bf16[128,1024]{1,0:T(8,128)(2,1)S(1)}, bf16[128,1024]{1,0:T(8,128)(2,1)S(1)}, u32[]{:S(2)}, u32[]{:S(2)}) %collective-permute-start.2) | collective-permute-done | bytes 262176 | tf_op jit(solution)/shard_map/ppermute | solution.py:18
  30.3 2.0 %collective-permute-done.4.refs_2_ = bf16[128,2048]{1,0:T(8,128)(2,1)S(1)} collective-permute-done((bf16[128,2048]{1,0:T(8,128)(2,1)S(1)}, bf16[128,2048]{1,0:T(8,128)(2,1)S(1)}, u32[]{:S(2)}, u32[]{:S(2)}) %collective-permute-start.4) | collective-permute-done | bytes 524320 | tf_op jit(solution)/shard_map/ppermute | solution.py:23
  32.2 0.5 regrouped.1
  32.7 1.6 %collective-permute-start.6 = (bf16[512,512]{1,0:T(8,128)(2,1)S(1)}, bf16[512,512]{1,0:T(8,128)(2,1)S(1)}, u32[]{:S(2)}, u32[]{:S(2)}) collective-permute-start(bf16[512,512]{1,0:T(8,128)(2,1)S(1)} %get-tuple-element.55), channel_id=1, source_target_pairs={{0,1},{1,2},{2,3},{3,0},{4,5},{5,6},{6,7},{7,4},{8,9},{9,10},{10,1... | collective-permute-start | bytes 1572872 | tf_op jit(solution)/shard_map/ppermute | solution.py:18
  34.3 2.2 %collective-permute-start.7 = (bf16[512,512]{1,0:T(8,128)(2,1)S(1)}, bf16[512,512]{1,0:T(8,128)(2,1)S(1)}, u32[]{:S(2)}, u32[]{:S(2)}) collective-permute-start(bf16[512,512]{1,0:T(8,128)(2,1)S(1)} %get-tuple-element.58), channel_id=1, source_target_pairs={{0,3},{1,0},{2,1},{3,2},{4,7},{5,4},{6,5},{7,6},{8,11},{9,8},{10,9... | collective-permute-start | bytes 1572872 | tf_op jit(solution)/shard_map/ppermute | solution.py:18
  36.7 1.6 %collective-permute-start.10 = (bf16[512,1024]{1,0:T(8,128)(2,1)S(1)}, bf16[512,1024]{1,0:T(8,128)(2,1)S(1)}, u32[]{:S(2)}, u32[]{:S(2)}) collective-permute-start(bf16[512,1024]{1,0:T(8,128)(2,1)S(1)} %joined.3.refs_4_), channel_id=1, source_target_pairs={{0,8},{4,12},{8,0},{12,4},{1,9},{5,13},{9,1},{13,5},{2,10},{6,14},... | collective-permute-start | bytes 3145736 | tf_op jit(solution)/shard_map/ppermute | solution.py:23
  38.3 1.2 collective-permute-start.11
  39.5 0.8 collective-permute-start.9
  40.3 3.2 %returned_blocks.1 = (bf16[64,2048]{1,0:T(8,128)(2,1)S(1)}, bf16[64,2048]{1,0:T(8,128)(2,1)S(1)}, bf16[64,2048]{1,0:T(8,128)(2,1)S(1)}, bf16[64,2048]{1,0:T(8,12...) custom-call(bf16[128,1024]{1,0:T(8,128)(2,1)S(1)} %bitcast.14, ...), custom_call_target="tpu_custom_call" | custom-call | flops 2147483648 | bytes 7340032 | tf_op jit(solution)/shard_map/returned_blocks/pallas_call | solution.py:248
  43.5 5.9 %collective-permute-done.6.refs_1_ = bf16[512,512]{1,0:T(8,128)(2,1)S(1)} collective-permute-done((bf16[512,512]{1,0:T(8,128)(2,1)S(1)}, bf16[512,512]{1,0:T(8,128)(2,1)S(1)}, u32[]{:S(2)}, u32[]{:S(2)}) %collective-permute-start.6) | collective-permute-done | bytes 524320 | tf_op jit(solution)/shard_map/ppermute | solution.py:18
  49.4 8.1 %collective-permute-done.7.refs_3_ = bf16[512,512]{1,0:T(8,128)(2,1)S(1)} collective-permute-done((bf16[512,512]{1,0:T(8,128)(2,1)S(1)}, bf16[512,512]{1,0:T(8,128)(2,1)S(1)}, u32[]{:S(2)}, u32[]{:S(2)}) %collective-permute-start.7) | collective-permute-done | bytes 524320 | tf_op jit(solution)/shard_map/ppermute | solution.py:18
  57.5 1.3 collective-permute-start.8
  58.8 24.1 %collective-permute-done.8.refs_2_ = bf16[512,512]{1,0:T(8,128)(2,1)S(1)} collective-permute-done((bf16[512,512]{1,0:T(8,128)(2,1)S(1)}, bf16[512,512]{1,0:T(8,128)(2,1)S(1)}, u32[]{:S(2)}, u32[]{:S(2)}) %collective-permute-start.8) | collective-permute-done | bytes 524320 | tf_op jit(solution)/shard_map/ppermute | solution.py:18
  82.9 0.5 collective-permute-done.9.refs_5_
  83.4 2.7 %weight_product.1 = (bf16[272,1024]{1,0:T(8,128)(2,1)S(1)}, bf16[272,1024]{1,0:T(8,128)(2,1)S(1)}) custom-call(s32[1]{0:T(128)} %bitcast.3.rep_ref, bf16[512,512]{1,0:T(8,128)(2,1)S(1)} %get-tuple-element.54.refs_0_, bf16[512,512]{1,0:T(8,128)(2,1)S(1)} %collective-permute-done.6.refs_1_, bf16[512,512]{1,0:T(8,128)(2,1)S(1)} %collective-permute-done.8.refs_2_, ...), custom_call_target="tpu_custom_call" | custom-call | flops 2147483648 | bytes 8388608 | tf_op jit(solution)/shard_map/weight_product/pallas_call | solution.py:215
  86.1 1.5 %collective-permute-start.14 = (bf16[272,1024]{1,0:T(8,128)(2,1)S(1)}, bf16[272,1024]{1,0:T(8,128)(2,1)S(1)}, u32[]{:S(2)}, u32[]{:S(2)}) collective-permute-start(bf16[272,1024]{1,0:T(8,128)(2,1)S(1)} %get-tuple-element.62.refs_0_), channel_id=1, source_target_pairs={{0,4},{4,0},{8,12},{12,8},{1,5},{5,1},{9,13},{13,9},{2,6},{6,2},{1... | collective-permute-start | bytes 1671176 | tf_op jit(solution)/shard_map/ppermute | solution.py:23
  87.6 0.6 collective-permute-start.12
  88.2 8.0 %collective-permute-done.16.refs_2_ = bf16[64,2048]{1,0:T(8,128)(2,1)S(1)} collective-permute-done((bf16[64,2048]{1,0:T(8,128)(2,1)S(1)}, bf16[64,2048]{1,0:T(8,128)(2,1)S(1)}, u32[]{:S(2)}, u32[]{:S(2)}) %collective-permute-start.16) | collective-permute-done | bytes 262176 | tf_op jit(solution)/shard_map/ppermute | solution.py:18
  96.2 1.4 collective-permute-start.17
  97.7 7.7 %collective-permute-done.17.refs_1_ = bf16[64,2048]{1,0:T(8,128)(2,1)S(1)} collective-permute-done((bf16[64,2048]{1,0:T(8,128)(2,1)S(1)}, bf16[64,2048]{1,0:T(8,128)(2,1)S(1)}, u32[]{:S(2)}, u32[]{:S(2)}) %collective-permute-start.17) | collective-permute-done | bytes 262176 | tf_op jit(solution)/shard_map/ppermute | solution.py:18
  106.1 0.6 collective-permute-start.15
  106.8 1.6 %collective-permute-start.13 = (bf16[544,1024]{1,0:T(8,128)(2,1)S(1)}, bf16[544,1024]{1,0:T(8,128)(2,1)S(1)}, u32[]{:S(2)}, u32[]{:S(2)}) collective-permute-start(bf16[544,1024]{1,0:T(8,128)(2,1)S(1)} %joined.4.sum_ref), channel_id=1, source_target_pairs={{0,4},{4,0},{8,12},{12,8},{1,5},{5,1},{9,13},{13,9},{2,6},{6,2},{1... | collective-permute-start | bytes 3342344 | tf_op jit(solution)/shard_map/ppermute | solution.py:23
  108.4 8.2 %collective-permute-done.18.refs_3_ = bf16[64,2048]{1,0:T(8,128)(2,1)S(1)} collective-permute-done((bf16[64,2048]{1,0:T(8,128)(2,1)S(1)}, bf16[64,2048]{1,0:T(8,128)(2,1)S(1)}, u32[]{:S(2)}, u32[]{:S(2)}) %collective-permute-start.18) | collective-permute-done | bytes 262176 | tf_op jit(solution)/shard_map/ppermute | solution.py:18
  116.6 4.8 %collective-permute-done.19.refs_1_ = bf16[64,2048]{1,0:T(8,128)(2,1)S(1)} collective-permute-done((bf16[64,2048]{1,0:T(8,128)(2,1)S(1)}, bf16[64,2048]{1,0:T(8,128)(2,1)S(1)}, u32[]{:S(2)}, u32[]{:S(2)}) %collective-permute-start.19) | collective-permute-done | bytes 262176 | tf_op jit(solution)/shard_map/ppermute | solution.py:18
  121.3 1.5 %row_gradient.2 = (bf16[64,8192]{1,0:T(8,128)(2,1)S(1)}, bf16[64,8192]{1,0:T(8,128)(2,1)S(1)}) custom-call(s32[1]{0:T(128)} %bitcast.1.me_ref, bf16[1,2,64,8192]{3,2,1,0:T(8,128)(2,1)S(1)} %copy-done.1, bf16[2,64,8192]{2,1,0:T(8,128)(2,1)S(1)} %copy-done.2, bf16[64,2048]{1,0:T(8,128)(2,1)S(1)} %get-tuple-element.77.refs_0_, ...), custom_call_target="tpu_custom_call" | custom-call | flops 6291456 | bytes 5242880 | tf_op jit(solution)/shard_map/row_gradient/pallas_call | solution.py:293
  122.9 1.3 collective-permute-start.21
  124.2 2.3 %collective-permute-start.22 = (bf16[64,2048]{1,0:T(8,128)(2,1)S(1)}, bf16[64,2048]{1,0:T(8,128)(2,1)S(1)}, u32[]{:S(2)}, u32[]{:S(2)}) collective-permute-start(bf16[64,2048]{1,0:T(8,128)(2,1)S(1)} %get-tuple-element.86), channel_id=1, source_target_pairs={{0,2},{1,3},{2,0},{3,1},{4,6},{5,7},{6,4},{7,5},{8,10},{9,11},{10,... | collective-permute-start | bytes 786440 | tf_op jit(solution)/shard_map/ppermute | solution.py:18
  126.5 1.4 finished_half.4
  127.9 1.4 finished_half.5
  129.3 1.6 %collective-permute-done.15.sum_ref = bf16[544,1024]{1,0:T(8,128)(2,1)S(1)} collective-permute-done((bf16[544,1024]{1,0:T(8,128)(2,1)S(1)}, bf16[544,1024]{1,0:T(8,128)(2,1)S(1)}, u32[]{:S(2)}, u32[]{:S(2)}) %collective-permute-start.15) | collective-permute-done | bytes 1114144 | tf_op jit(solution)/shard_map/ppermute | solution.py:23
  130.9 1.4 finished_half.6
  132.3 1.4 finished_half.7
  133.7 1.1 input_gradient.2.refs_0_
  134.8 4.9 %collective-permute-done.22.refs_2_ = bf16[64,2048]{1,0:T(8,128)(2,1)S(1)} collective-permute-done((bf16[64,2048]{1,0:T(8,128)(2,1)S(1)}, bf16[64,2048]{1,0:T(8,128)(2,1)S(1)}, u32[]{:S(2)}, u32[]{:S(2)}) %collective-permute-start.22) | collective-permute-done | bytes 262176 | tf_op jit(solution)/shard_map/ppermute | solution.py:18
  139.7 1.5 %row_gradient.3 = (bf16[64,8192]{1,0:T(8,128)(2,1)S(1)}, bf16[64,8192]{1,0:T(8,128)(2,1)S(1)}) custom-call(s32[1]{0:T(128)} %bitcast.1.me_ref, bf16[1,2,64,8192]{3,2,1,0:T(8,128)(2,1)S(1)} %copy-done.1, bf16[2,64,8192]{2,1,0:T(8,128)(2,1)S(1)} %copy-done.2, bf16[64,2048]{1,0:T(8,128)(2,1)S(1)} %get-tuple-element.84.refs_0_, ...), custom_call_target="tpu_custom_call" | custom-call | flops 6291456 | bytes 5242880 | tf_op jit(solution)/shard_map/row_gradient/pallas_call | solution.py:293
  141.2 1.3 collective-permute-start.23
  142.5 3.3 %collective-permute-done.23.passed_ref = bf16[64,8192]{1,0:T(8,128)(2,1)S(1)} collective-permute-done((bf16[64,8192]{1,0:T(8,128)(2,1)S(1)}, bf16[64,8192]{1,0:T(8,128)(2,1)S(1)}, u32[]{:S(2)}, u32[]{:S(2)}) %collective-permute-start.23) | collective-permute-done | bytes 1048608 | tf_op jit(solution)/shard_map/ppermute | solution.py:439
  145.8 1.1 input_gradient.3
  (27 shorter events, 1.0 us)
Async XLA Ops:
  0.6 1.6 %copy-start = (bf16[1,2,64,8192]{3,2,1,0:T(8,128)(2,1)S(1)}, bf16[1,2,64,8192]{3,2,1,0:T(8,128)(2,1)}, u32[]{:S(2)}) copy-start(bf16[1,2,64,8192]{3,2,1,0:T(8,128)(2,1)} %x_ref.3) | copy-start | bytes 6291460
  2.2 1.1 copy-start.4
  3.3 12.3 %collective-permute-start = (bf16[128,1024]{1,0:T(8,128)(2,1)S(1)}, bf16[128,1024]{1,0:T(8,128)(2,1)S(1)}, u32[]{:S(2)}, u32[]{:S(2)}) collective-permute-start(bf16[128,1024]{1,0:T(8,128)(2,1)S(1)} %bitcast.10), channel_id=1, source_target_pairs={{0,1},{1,2},{2,3},{3,0},{4,5},{5,6},{6,7},{7,4},{8,9},{9,10},{10,1... | collective-permute-start | bytes 786440 | tf_op jit(solution)/shard_map/ppermute | solution.py:18
  6.4 23.9 %collective-permute-start.3 = (bf16[128,2048]{1,0:T(8,128)(2,1)S(1)}, bf16[128,2048]{1,0:T(8,128)(2,1)S(1)}, u32[]{:S(2)}, u32[]{:S(2)}) collective-permute-start(bf16[128,2048]{1,0:T(8,128)(2,1)S(1)} %get-tuple-element.51), channel_id=1, source_target_pairs={{0,4},{4,0},{8,12},{12,8},{1,5},{5,1},{9,13},{13,9},{2,6},{6,2},{1... | collective-permute-start | bytes 1572872 | tf_op jit(solution)/shard_map/ppermute | solution.py:23
  7.9 24.3 %collective-permute-start.4 = (bf16[128,2048]{1,0:T(8,128)(2,1)S(1)}, bf16[128,2048]{1,0:T(8,128)(2,1)S(1)}, u32[]{:S(2)}, u32[]{:S(2)}) collective-permute-start(bf16[128,2048]{1,0:T(8,128)(2,1)S(1)} %get-tuple-element.52), channel_id=1, source_target_pairs={{0,8},{4,12},{8,0},{12,4},{1,9},{5,13},{9,1},{13,5},{2,10},{6,14},... | collective-permute-start | bytes 1572872 | tf_op jit(solution)/shard_map/ppermute | solution.py:23
  9.4 30.9 %copy-start.5 = (bf16[1,2048]{1,0:T(2,128)(2,1)S(1)}, bf16[1,2048]{1,0:T(2,128)(2,1)}, u32[]{:S(2)}) copy-start(bf16[1,2048]{1,0:T(2,128)(2,1)} %refs_9_.1) | copy-start | bytes 12292
  9.4 30.9 %copy-start.3 = (bf16[1,2048,1024]{2,1,0:T(8,128)(2,1)S(1)}, bf16[1,2048,1024]{2,1,0:T(8,128)(2,1)}, u32[]{:S(2)}) copy-start(bf16[1,2048,1024]{2,1,0:T(8,128)(2,1)} %param.7) | copy-start | bytes 12582916
  9.4 22.8 %collective-permute-start.5 = (bf16[128,2048]{1,0:T(8,128)(2,1)S(1)}, bf16[128,2048]{1,0:T(8,128)(2,1)S(1)}, u32[]{:S(2)}, u32[]{:S(2)}) collective-permute-start(bf16[128,2048]{1,0:T(8,128)(2,1)S(1)} %get-tuple-element.53), channel_id=1, source_target_pairs={{0,12},{4,8},{8,4},{12,0},{1,13},{5,9},{9,5},{13,1},{2,14},{6,10},... | collective-permute-start | bytes 1572872 | tf_op jit(solution)/shard_map/ppermute | solution.py:23
  9.9 16.2 %collective-permute-start.1 = (bf16[128,1024]{1,0:T(8,128)(2,1)S(1)}, bf16[128,1024]{1,0:T(8,128)(2,1)S(1)}, u32[]{:S(2)}, u32[]{:S(2)}) collective-permute-start(bf16[128,1024]{1,0:T(8,128)(2,1)S(1)} %bitcast.11), channel_id=1, source_target_pairs={{0,2},{1,3},{2,0},{3,1},{4,6},{5,7},{6,4},{7,5},{8,10},{9,11},{10,... | collective-permute-start | bytes 786440 | tf_op jit(solution)/shard_map/ppermute | solution.py:18
  15.6 14.6 %collective-permute-start.2 = (bf16[128,1024]{1,0:T(8,128)(2,1)S(1)}, bf16[128,1024]{1,0:T(8,128)(2,1)S(1)}, u32[]{:S(2)}, u32[]{:S(2)}) collective-permute-start(bf16[128,1024]{1,0:T(8,128)(2,1)S(1)} %bitcast.12), channel_id=1, source_target_pairs={{0,3},{1,0},{2,1},{3,2},{4,7},{5,4},{6,5},{7,6},{8,11},{9,8},{10,9... | collective-permute-start | bytes 786440 | tf_op jit(solution)/shard_map/ppermute | solution.py:18
  32.7 16.7 %collective-permute-start.6 = (bf16[512,512]{1,0:T(8,128)(2,1)S(1)}, bf16[512,512]{1,0:T(8,128)(2,1)S(1)}, u32[]{:S(2)}, u32[]{:S(2)}) collective-permute-start(bf16[512,512]{1,0:T(8,128)(2,1)S(1)} %get-tuple-element.55), channel_id=1, source_target_pairs={{0,1},{1,2},{2,3},{3,0},{4,5},{5,6},{6,7},{7,4},{8,9},{9,10},{10,1... | collective-permute-start | bytes 1572872 | tf_op jit(solution)/shard_map/ppermute | solution.py:18
  34.3 23.2 %collective-permute-start.7 = (bf16[512,512]{1,0:T(8,128)(2,1)S(1)}, bf16[512,512]{1,0:T(8,128)(2,1)S(1)}, u32[]{:S(2)}, u32[]{:S(2)}) collective-permute-start(bf16[512,512]{1,0:T(8,128)(2,1)S(1)} %get-tuple-element.58), channel_id=1, source_target_pairs={{0,3},{1,0},{2,1},{3,2},{4,7},{5,4},{6,5},{7,6},{8,11},{9,8},{10,9... | collective-permute-start | bytes 1572872 | tf_op jit(solution)/shard_map/ppermute | solution.py:18
  36.7 46.2 %collective-permute-start.10 = (bf16[512,1024]{1,0:T(8,128)(2,1)S(1)}, bf16[512,1024]{1,0:T(8,128)(2,1)S(1)}, u32[]{:S(2)}, u32[]{:S(2)}) collective-permute-start(bf16[512,1024]{1,0:T(8,128)(2,1)S(1)} %joined.3.refs_4_), channel_id=1, source_target_pairs={{0,8},{4,12},{8,0},{12,4},{1,9},{5,13},{9,1},{13,5},{2,10},{6,14},... | collective-permute-start | bytes 3145736 | tf_op jit(solution)/shard_map/ppermute | solution.py:23
  38.3 44.6 %collective-permute-start.11 = (bf16[512,1024]{1,0:T(8,128)(2,1)S(1)}, bf16[512,1024]{1,0:T(8,128)(2,1)S(1)}, u32[]{:S(2)}, u32[]{:S(2)}) collective-permute-start(bf16[512,1024]{1,0:T(8,128)(2,1)S(1)} %joined.3.refs_4_), channel_id=1, source_target_pairs={{0,12},{4,8},{8,4},{12,0},{1,13},{5,9},{9,5},{13,1},{2,14},{6,10},... | collective-permute-start | bytes 3145736 | tf_op jit(solution)/shard_map/ppermute | solution.py:23
  39.5 43.9 %collective-permute-start.9 = (bf16[512,1024]{1,0:T(8,128)(2,1)S(1)}, bf16[512,1024]{1,0:T(8,128)(2,1)S(1)}, u32[]{:S(2)}, u32[]{:S(2)}) collective-permute-start(bf16[512,1024]{1,0:T(8,128)(2,1)S(1)} %joined.3.refs_4_), channel_id=1, source_target_pairs={{0,4},{4,0},{8,12},{12,8},{1,5},{5,1},{9,13},{13,9},{2,6},{6,2},{1... | collective-permute-start | bytes 3145736 | tf_op jit(solution)/shard_map/ppermute | solution.py:23
  57.5 25.4 %collective-permute-start.8 = (bf16[512,512]{1,0:T(8,128)(2,1)S(1)}, bf16[512,512]{1,0:T(8,128)(2,1)S(1)}, u32[]{:S(2)}, u32[]{:S(2)}) collective-permute-start(bf16[512,512]{1,0:T(8,128)(2,1)S(1)} %get-tuple-element.59), channel_id=1, source_target_pairs={{0,2},{1,3},{2,0},{3,1},{4,6},{5,7},{6,4},{7,5},{8,10},{9,11},{10,... | collective-permute-start | bytes 1572872 | tf_op jit(solution)/shard_map/ppermute | solution.py:18
  82.9 13.3 %collective-permute-start.16 = (bf16[64,2048]{1,0:T(8,128)(2,1)S(1)}, bf16[64,2048]{1,0:T(8,128)(2,1)S(1)}, u32[]{:S(2)}, u32[]{:S(2)}) collective-permute-start(bf16[64,2048]{1,0:T(8,128)(2,1)S(1)} %get-tuple-element.74), channel_id=1, source_target_pairs={{0,2},{1,3},{2,0},{3,1},{4,6},{5,7},{6,4},{7,5},{8,10},{9,11},{10,... | collective-permute-start | bytes 786440 | tf_op jit(solution)/shard_map/ppermute | solution.py:18
  86.1 19.7 %collective-permute-start.14 = (bf16[272,1024]{1,0:T(8,128)(2,1)S(1)}, bf16[272,1024]{1,0:T(8,128)(2,1)S(1)}, u32[]{:S(2)}, u32[]{:S(2)}) collective-permute-start(bf16[272,1024]{1,0:T(8,128)(2,1)S(1)} %get-tuple-element.62.refs_0_), channel_id=1, source_target_pairs={{0,4},{4,0},{8,12},{12,8},{1,5},{5,1},{9,13},{13,9},{2,6},{6,2},{1... | collective-permute-start | bytes 1671176 | tf_op jit(solution)/shard_map/ppermute | solution.py:23
  87.6 19.0 %collective-permute-start.12 = (bf16[272,1024]{1,0:T(8,128)(2,1)S(1)}, bf16[272,1024]{1,0:T(8,128)(2,1)S(1)}, u32[]{:S(2)}, u32[]{:S(2)}) collective-permute-start(bf16[272,1024]{1,0:T(8,128)(2,1)S(1)} %get-tuple-element.61.refs_0_), channel_id=1, source_target_pairs={{0,8},{4,12},{8,0},{12,4},{1,9},{5,13},{9,1},{13,5},{2,10},{6,14},... | collective-permute-start | bytes 1671176 | tf_op jit(solution)/shard_map/ppermute | solution.py:23
  96.2 9.2 %collective-permute-start.17 = (bf16[64,2048]{1,0:T(8,128)(2,1)S(1)}, bf16[64,2048]{1,0:T(8,128)(2,1)S(1)}, u32[]{:S(2)}, u32[]{:S(2)}) collective-permute-start(bf16[64,2048]{1,0:T(8,128)(2,1)S(1)} %get-tuple-element.75), channel_id=1, source_target_pairs={{0,3},{1,0},{2,1},{3,2},{4,7},{5,4},{6,5},{7,6},{8,11},{9,8},{10,9... | collective-permute-start | bytes 786440 | tf_op jit(solution)/shard_map/ppermute | solution.py:18
  97.6 23.7 %collective-permute-start.19 = (bf16[64,2048]{1,0:T(8,128)(2,1)S(1)}, bf16[64,2048]{1,0:T(8,128)(2,1)S(1)}, u32[]{:S(2)}, u32[]{:S(2)}) collective-permute-start(bf16[64,2048]{1,0:T(8,128)(2,1)S(1)} %get-tuple-element.79), channel_id=1, source_target_pairs={{0,3},{1,0},{2,1},{3,2},{4,7},{5,4},{6,5},{7,6},{8,11},{9,8},{10,9... | collective-permute-start | bytes 786440 | tf_op jit(solution)/shard_map/ppermute | solution.py:18
  105.4 11.1 %collective-permute-start.18 = (bf16[64,2048]{1,0:T(8,128)(2,1)S(1)}, bf16[64,2048]{1,0:T(8,128)(2,1)S(1)}, u32[]{:S(2)}, u32[]{:S(2)}) collective-permute-start(bf16[64,2048]{1,0:T(8,128)(2,1)S(1)} %get-tuple-element.76), channel_id=1, source_target_pairs={{0,1},{1,2},{2,3},{3,0},{4,5},{5,6},{6,7},{7,4},{8,9},{9,10},{10,1... | collective-permute-start | bytes 786440 | tf_op jit(solution)/shard_map/ppermute | solution.py:18
  105.4 15.9 %copy-start.1 = (bf16[1,2,64,8192]{3,2,1,0:T(8,128)(2,1)S(1)}, bf16[1,2,64,8192]{3,2,1,0:T(8,128)(2,1)}, u32[]{:S(2)}) copy-start(bf16[1,2,64,8192]{3,2,1,0:T(8,128)(2,1)} %x_ref.3) | copy-start | bytes 6291460
  105.4 15.9 %copy-start.2 = (bf16[2,64,8192]{2,1,0:T(8,128)(2,1)S(1)}, bf16[2,64,8192]{2,1,0:T(8,128)(2,1)}, u32[]{:S(2)}) copy-start(bf16[2,64,8192]{2,1,0:T(8,128)(2,1)} %top_ref.3) | copy-start | bytes 6291460
  105.4 15.9 %collective-permute-start.20 = (bf16[64,2048]{1,0:T(8,128)(2,1)S(1)}, bf16[64,2048]{1,0:T(8,128)(2,1)S(1)}, u32[]{:S(2)}, u32[]{:S(2)}) collective-permute-start(bf16[64,2048]{1,0:T(8,128)(2,1)S(1)} %get-tuple-element.81), channel_id=1, source_target_pairs={{0,1},{1,2},{2,3},{3,0},{4,5},{5,6},{6,7},{7,4},{8,9},{9,10},{10,1... | collective-permute-start | bytes 786440 | tf_op jit(solution)/shard_map/ppermute | solution.py:18
  106.1 24.8 %collective-permute-start.15 = (bf16[544,1024]{1,0:T(8,128)(2,1)S(1)}, bf16[544,1024]{1,0:T(8,128)(2,1)S(1)}, u32[]{:S(2)}, u32[]{:S(2)}) collective-permute-start(bf16[544,1024]{1,0:T(8,128)(2,1)S(1)} %joined.5.sum_ref), channel_id=1, source_target_pairs={{0,8},{4,12},{8,0},{12,4},{1,9},{5,13},{9,1},{13,5},{2,10},{6,14},... | collective-permute-start | bytes 3342344 | tf_op jit(solution)/shard_map/ppermute | solution.py:23
  106.8 25.5 %collective-permute-start.13 = (bf16[544,1024]{1,0:T(8,128)(2,1)S(1)}, bf16[544,1024]{1,0:T(8,128)(2,1)S(1)}, u32[]{:S(2)}, u32[]{:S(2)}) collective-permute-start(bf16[544,1024]{1,0:T(8,128)(2,1)S(1)} %joined.4.sum_ref), channel_id=1, source_target_pairs={{0,4},{4,0},{8,12},{12,8},{1,5},{5,1},{9,13},{13,9},{2,6},{6,2},{1... | collective-permute-start | bytes 3342344 | tf_op jit(solution)/shard_map/ppermute | solution.py:23
  122.9 10.9 %collective-permute-start.21 = (bf16[64,8192]{1,0:T(8,128)(2,1)S(1)}, bf16[64,8192]{1,0:T(8,128)(2,1)S(1)}, u32[]{:S(2)}, u32[]{:S(2)}) collective-permute-start(bf16[64,8192]{1,0:T(8,128)(2,1)S(1)} %get-tuple-element.82.upper_ref), channel_id=1, source_target_pairs={{16,0},{17,1},{18,2},{19,3},{20,4},{21,5},{22,6},{23,7},{24,8},{25... | collective-permute-start | bytes 3145736 | tf_op jit(solution)/shard_map/ppermute | solution.py:439
  124.2 15.5 %collective-permute-start.22 = (bf16[64,2048]{1,0:T(8,128)(2,1)S(1)}, bf16[64,2048]{1,0:T(8,128)(2,1)S(1)}, u32[]{:S(2)}, u32[]{:S(2)}) collective-permute-start(bf16[64,2048]{1,0:T(8,128)(2,1)S(1)} %get-tuple-element.86), channel_id=1, source_target_pairs={{0,2},{1,3},{2,0},{3,1},{4,6},{5,7},{6,4},{7,5},{8,10},{9,11},{10,... | collective-permute-start | bytes 786440 | tf_op jit(solution)/shard_map/ppermute | solution.py:18
  141.2 4.6 %collective-permute-start.23 = (bf16[64,8192]{1,0:T(8,128)(2,1)S(1)}, bf16[64,8192]{1,0:T(8,128)(2,1)S(1)}, u32[]{:S(2)}, u32[]{:S(2)}) collective-permute-start(bf16[64,8192]{1,0:T(8,128)(2,1)S(1)} %get-tuple-element.87.upper_ref), channel_id=1, source_target_pairs={{16,0},{17,1},{18,2},{19,3},{20,4},{21,5},{22,6},{23,7},{24,8},{25... | collective-permute-start | bytes 3145736 | tf_op jit(solution)/shard_map/ppermute | solution.py:439

commit v10 on v6

--- a/solution.py
+++ b/solution.py
@@ -224,10 +224,12 @@
     )(rep, *columns, *values, weight, gain)
 
 
-def returned_blocks(slots, weight, gain, micro):
+def returned_blocks(slots, weight, gain, micro, far):
     groups = len(slots)
     tokens, features = slots[0].shape
-    rows = tokens // micro
+    counts = [micro if j == far else 1 for j in range(groups)]
+    starts = [sum(counts[:j]) for j in range(groups)]
+    parts = [tokens // n for n in counts for _ in range(n)]
     shard = weight.shape[0]
     tile = min(shard, 512)
 
@@ -236,34 +238,41 @@
         out_refs = refs[groups + 2 :]
         factor = gain_ref[...].astype(f32)
         pair = 2 if groups % 2 == 0 else 1
+        out_refs = [out_refs[at : at + n] for at, n in zip(starts, counts)]
         for j in range(0, groups, pair):
             values = jnp.concatenate([slot_refs[j + i][...] for i in range(pair)], axis=0)
             back = lax.dot_general(values, weight_ref[...], (((1,), (1,)), ((), ())), preferred_element_type=f32)
             back = (back * factor).astype(bf16)
             for i in range(pair):
-                for m in range(micro):
-                    at = i * tokens + m * rows
-                    out_refs[(j + i) * micro + m][...] = back[at : at + rows, :]
+                part = tokens // counts[j + i]
+                for m in range(counts[j + i]):
+                    at = i * tokens + m * part
+                    out_refs[j + i][m][...] = back[at : at + part, :]
 
     outs = pl.pallas_call(
         kernel,
         grid=(shard // tile,),
-        out_shape=[jax.ShapeDtypeStruct((rows, shard), bf16)] * (groups * micro),
+        out_shape=[jax.ShapeDtypeStruct((part, shard), bf16) for part in parts],
         in_specs=[pl.BlockSpec((tokens, features), lambda i: (0, 0))] * groups
         + [pl.BlockSpec((tile, features), lambda i: (i, 0)), pl.BlockSpec((1, tile), lambda i: (0, i))],
-        out_specs=[pl.BlockSpec((rows, tile), lambda i: (0, i))] * (groups * micro),
+        out_specs=[pl.BlockSpec((part, tile), lambda i: (0, i)) for part in parts],
         compiler_params=params(8),
         cost_estimate=cost(2 * groups * tokens * shard * features, 2 * groups * tokens * (shard + features) + 2 * shard * features),
         name="returned_blocks",
     )(*slots, weight, gain)
-    return [list(outs[j * micro : (j + 1) * micro]) for j in range(groups)]
+    return [list(outs[at : at + n]) for at, n in zip(starts, counts)]
 
 
 def row_gradient(x, top, blocks, me, m):
     groups = len(blocks)
-    rows, shard = blocks[0].shape
+    shard = blocks[0].shape[1]
+    rows = x.shape[2]
     width = shard * groups
     step = 16
+
+    def block_spec(block):
+        base = m * rows // step if block.shape[0] > rows else 0
+        return pl.BlockSpec((step, shard), lambda i: (base + i, 0))
 
     def kernel(me_ref, x_ref, top_ref, *refs):
         block_refs, upper_ref, piece_ref = refs[:groups], refs[groups], refs[groups + 1]
@@ -299,7 +308,7 @@
             pl.BlockSpec((1, 1, step, width), lambda i: (0, m, i, 0)),
             pl.BlockSpec((1, step, width), lambda i: (m, i, 0)),
         ]
-        + [pl.BlockSpec((step, shard), lambda i: (i, 0))] * groups,
+        + [block_spec(block) for block in blocks],
         out_specs=[pl.BlockSpec((step, width), lambda i: (i, 0))] * 2,
         compiler_params=params(8),
         cost_estimate=cost(12 * rows * width, 10 * rows * width),
@@ -400,10 +409,9 @@
 
     plane[0] = after(plane[0], *slots[1:])
     sent = regrouped(plane, groups)
-    back = returned_blocks(slots, weight, norm_gain, micro)
-    lines = [[back[j][m] for j in range(groups)] for m in range(micro)]
     far = groups // 2
     near = [j for j in range(1, groups) if j != far]
+    back = returned_blocks(slots, weight, norm_gain, micro, far)
     columns = list(sent)
     columns[far] = cyclic(sent[far], "fsdp", far)
     columns[near[0]] = cyclic(sent[near[0]], "fsdp", near[0])
@@ -412,15 +420,17 @@
     held = after(joined(slots), sent[0])
     values = [held if e == 0 else flipped(held, "rep", e) for e in range(reps)]
 
-    def send_back(m, j, *ties):
-        lines[m][j] = cyclic(after(lines[m][j], *ties), "fsdp", -j)
-
-    send_back(0, near[0], columns[far])
-    for m, j in [(0, far), *((0, j) for j in near[1:]), (1, near[0])]:
-        send_back(m, j, columns[near[-1]])
-    for j in [far, *near[1:]]:
-        send_back(1, j, *lines[0][1:], lines[1][near[0]])
-    columns[0] = after(columns[0], lines[0][near[0]])
+    lines = [list(arrays) for arrays in back]
+
+    def send_back(j, m, *ties):
+        lines[j][m] = cyclic(after(lines[j][m], *ties), "fsdp", -j)
+
+    send_back(far, 0, columns[far])
+    send_back(near[-1], 0, columns[far])
+    for j in near[:-1]:
+        send_back(j, 0, lines[far][0])
+    for m in range(1, micro):
+        send_back(far, m, lines[far][m - 1])
     sums = weight_product(columns, values, weight, norm_gain, rep, groups, chunks, norm_scale)
     gathered = [doubled(sums[c], orders[c]) for c in range(chunks)]
     finished = ()
@@ -431,12 +441,16 @@
             early = finished
     weight_grad, gain_grad = finished
 
+    uppers = []
+    for m in range(micro):
+        line = [arrays[m if j == far else 0] for j, arrays in enumerate(lines)]
+        line[0] = after(line[0], *([*early] if m else [*early]))
+        line[0] = after(line[0], *[u for u, _ in uppers])
+        uppers.append(row_gradient(layer_input, top_grad, line, me, m))
     result = ()
-    for m in range(micro):
-        ties = [lines[-1][near[0]], *[g[0] for g in gathered]] if m == 0 else [*finished, *result]
-        lines[m][0] = after(lines[m][0], *ties)
-        upper, piece = row_gradient(layer_input, top_grad, lines[m], me, m)
+    for m, (upper, piece) in enumerate(uppers):
         passed = lax.ppermute(upper, "section", [(1, 0)])
+        piece = after(piece, *finished)
         result = (input_gradient(upper, piece, passed, is_upper, layer_input.shape, m, result),)
     return (result[0], weight_grad[None], gain_grad)
 

time: 146 us -> 135 us (0.925)
  waiting for transfers between devices: 82.1 us -> 72.4 us
  starting transfers between devices: 42.6 us -> 40.2 us
    ppermute x12 -> x10, starting transfers between devices: 30.5 us -> 23.8 us  [cyclic(): lax.ppermute(value, axis, [(i, (i + steps) % count) for i in range(count)])]
    ppermute x12 -> x10, waiting for transfers between devices: 66.9 us -> 62 us  [cyclic(): lax.ppermute(value, axis, [(i, (i + steps) % count) for i in range(count)])]
    ppermute x10, starting transfers between devices: 9.48 us -> 13.8 us  [flipped(): return lax.ppermute(value, axis, [(i, i ^ mask) for i in range(count)])]
    ppermute x2, waiting for transfers between devices: 3.26 us -> 0.01 us  [local(): passed = lax.ppermute(upper, 'section', [(1, 0)])]
    ppermute x10, waiting for transfers between devices: 12 us -> 10.4 us  [flipped(): return lax.ppermute(value, axis, [(i, i ^ mask) for i in range(count)])]
  transfers between devices with their start and end apart: 24 -> 22, of which waited for: 13 -> 11; matrix products, arithmetic and copies ran while one was open for 0% -> 0% of each run, Pallas kernels for 8% -> 12%
where the time goes in v10:
time: 135 us; the launch traced here: 134 us
  waiting for transfers between devices  72.4 us (54%)
  starting transfers between devices  40.2 us (30%)
  Pallas kernels  18.8 us (14%)
  local copies, waits for them, and re-layouts  1.6 us (1%)
    ppermute x10, waiting for transfers between devices, cyclic(): lax.ppermute(value, axis, [(i, (i + steps) % count) for i in range(count)])  62 us
    ppermute x10, starting transfers between devices, cyclic(): lax.ppermute(value, axis, [(i, (i + steps) % count) for i in range(count)])  23.8 us
    ppermute x10, starting transfers between devices, flipped(): return lax.ppermute(value, axis, [(i, i ^ mask) for i in range(count)])  13.8 us
    ppermute x10, waiting for transfers between devices, flipped(): return lax.ppermute(value, axis, [(i, i ^ mask) for i in range(count)])  10.4 us
    pallas_call x4, Pallas kernels, finished_half(): pl.pallas_call(kernel, grid_spec=pltpu.PrefetchScalarGridSpec(num_scalar_...  5.74 us
    pallas_call x1, Pallas kernels, returned_blocks(): pl.pallas_call(kernel, grid=(shard // tile,), out_shape=[jax.ShapeDtypeSt...  3.17 us
    pallas_call x2, Pallas kernels, row_gradient(): pl.pallas_call(kernel, grid=(rows // step,), out_shape=[jax.ShapeDtypeStr...  2.99 us
    pallas_call x1, Pallas kernels, weight_product(): pl.pallas_call(kernel, out_shape=[jax.ShapeDtypeStruct((chunk + 16, featu...  2.73 us
  transfers between devices with their start and end apart: 22, of which 11 were waited for; matrix products, arithmetic and copies ran while one was open for 0% of the time, Pallas kernels for 12%

profile of v10, /device:TPU:0, one launch (start us, length us, event | category | flops | bytes accessed | tf_op | source)
XLA Modules:
  0.0 133.8 jit_solution(14642806394803091009)
XLA Ops:
  0.6 0.0 copy-start
  0.6 1.6 %copy-done = bf16[1,2,64,8192]{3,2,1,0:T(8,128)(2,1)S(1)} copy-done((bf16[1,2,64,8192]{3,2,1,0:T(8,128)(2,1)S(1)}, bf16[1,2,64,8192]{3,2,1,0:T(8,128)(2,1)}, u32[]{:S(2)}) %copy-start) | copy-done | bytes 2097176
  2.2 1.1 scaled_blocks.1
  3.3 3.1 %collective-permute-start = (bf16[128,1024]{1,0:T(8,128)(2,1)S(1)}, bf16[128,1024]{1,0:T(8,128)(2,1)S(1)}, u32[]{:S(2)}, u32[]{:S(2)}) collective-permute-start(bf16[128,1024]{1,0:T(8,128)(2,1)S(1)} %bitcast.10), channel_id=1, source_target_pairs={{0,1},{1,2},{2,3},{3,0},{4,5},{5,6},{6,7},{7,4},{8,9},{9,10},{10,1... | collective-permute-start | bytes 786440 | tf_op jit(solution)/shard_map/ppermute | solution.py:18
  6.4 1.5 %collective-permute-start.3 = (bf16[128,2048]{1,0:T(8,128)(2,1)S(1)}, bf16[128,2048]{1,0:T(8,128)(2,1)S(1)}, u32[]{:S(2)}, u32[]{:S(2)}) collective-permute-start(bf16[128,2048]{1,0:T(8,128)(2,1)S(1)} %get-tuple-element.48), channel_id=1, source_target_pairs={{0,4},{4,0},{8,12},{12,8},{1,5},{5,1},{9,13},{13,9},{2,6},{6,2},{1... | collective-permute-start | bytes 1572872 | tf_op jit(solution)/shard_map/ppermute | solution.py:23
  7.9 1.5 %collective-permute-start.4 = (bf16[128,2048]{1,0:T(8,128)(2,1)S(1)}, bf16[128,2048]{1,0:T(8,128)(2,1)S(1)}, u32[]{:S(2)}, u32[]{:S(2)}) collective-permute-start(bf16[128,2048]{1,0:T(8,128)(2,1)S(1)} %get-tuple-element.49), channel_id=1, source_target_pairs={{0,8},{4,12},{8,0},{12,4},{1,9},{5,13},{9,1},{13,5},{2,10},{6,14},... | collective-permute-start | bytes 1572872 | tf_op jit(solution)/shard_map/ppermute | solution.py:23
  9.4 0.5 collective-permute-start.5
  9.9 2.6 %collective-permute-start.1 = (bf16[128,1024]{1,0:T(8,128)(2,1)S(1)}, bf16[128,1024]{1,0:T(8,128)(2,1)S(1)}, u32[]{:S(2)}, u32[]{:S(2)}) collective-permute-start(bf16[128,1024]{1,0:T(8,128)(2,1)S(1)} %bitcast.11), channel_id=1, source_target_pairs={{0,2},{1,3},{2,0},{3,1},{4,6},{5,7},{6,4},{7,5},{8,10},{9,11},{10,... | collective-permute-start | bytes 786440 | tf_op jit(solution)/shard_map/ppermute | solution.py:18
  12.5 3.2 %collective-permute-done.refs_1_ = bf16[128,1024]{1,0:T(8,128)(2,1)S(1)} collective-permute-done((bf16[128,1024]{1,0:T(8,128)(2,1)S(1)}, bf16[128,1024]{1,0:T(8,128)(2,1)S(1)}, u32[]{:S(2)}, u32[]{:S(2)}) %collective-permute-start) | collective-permute-done | bytes 262176 | tf_op jit(solution)/shard_map/ppermute | solution.py:18
  15.6 1.4 %collective-permute-start.2 = (bf16[128,1024]{1,0:T(8,128)(2,1)S(1)}, bf16[128,1024]{1,0:T(8,128)(2,1)S(1)}, u32[]{:S(2)}, u32[]{:S(2)}) collective-permute-start(bf16[128,1024]{1,0:T(8,128)(2,1)S(1)} %bitcast.12), channel_id=1, source_target_pairs={{0,3},{1,0},{2,1},{3,2},{4,7},{5,4},{6,5},{7,6},{8,11},{9,8},{10,9... | collective-permute-start | bytes 786440 | tf_op jit(solution)/shard_map/ppermute | solution.py:18
  17.0 9.0 %collective-permute-done.1.refs_2_ = bf16[128,1024]{1,0:T(8,128)(2,1)S(1)} collective-permute-done((bf16[128,1024]{1,0:T(8,128)(2,1)S(1)}, bf16[128,1024]{1,0:T(8,128)(2,1)S(1)}, u32[]{:S(2)}, u32[]{:S(2)}) %collective-permute-start.1) | collective-permute-done | bytes 262176 | tf_op jit(solution)/shard_map/ppermute | solution.py:18
  26.0 4.2 %collective-permute-done.2.refs_3_ = bf16[128,1024]{1,0:T(8,128)(2,1)S(1)} collective-permute-done((bf16[128,1024]{1,0:T(8,128)(2,1)S(1)}, bf16[128,1024]{1,0:T(8,128)(2,1)S(1)}, u32[]{:S(2)}, u32[]{:S(2)}) %collective-permute-start.2) | collective-permute-done | bytes 262176 | tf_op jit(solution)/shard_map/ppermute | solution.py:18
  30.3 0.1 joined.3.refs_4_
  30.4 1.8 %collective-permute-done.4.refs_2_ = bf16[128,2048]{1,0:T(8,128)(2,1)S(1)} collective-permute-done((bf16[128,2048]{1,0:T(8,128)(2,1)S(1)}, bf16[128,2048]{1,0:T(8,128)(2,1)S(1)}, u32[]{:S(2)}, u32[]{:S(2)}) %collective-permute-start.4) | collective-permute-done | bytes 524320 | tf_op jit(solution)/shard_map/ppermute | solution.py:23
  32.2 0.5 regrouped.1
  32.7 1.6 %collective-permute-start.6 = (bf16[512,512]{1,0:T(8,128)(2,1)S(1)}, bf16[512,512]{1,0:T(8,128)(2,1)S(1)}, u32[]{:S(2)}, u32[]{:S(2)}) collective-permute-start(bf16[512,512]{1,0:T(8,128)(2,1)S(1)} %get-tuple-element.52), channel_id=1, source_target_pairs={{0,1},{1,2},{2,3},{3,0},{4,5},{5,6},{6,7},{7,4},{8,9},{9,10},{10,1... | collective-permute-start | bytes 1572872 | tf_op jit(solution)/shard_map/ppermute | solution.py:18
  34.3 1.5 %collective-permute-start.10 = (bf16[512,1024]{1,0:T(8,128)(2,1)S(1)}, bf16[512,1024]{1,0:T(8,128)(2,1)S(1)}, u32[]{:S(2)}, u32[]{:S(2)}) collective-permute-start(bf16[512,1024]{1,0:T(8,128)(2,1)S(1)} %joined.3.refs_4_), channel_id=1, source_target_pairs={{0,8},{4,12},{8,0},{12,4},{1,9},{5,13},{9,1},{13,5},{2,10},{6,14},... | collective-permute-start | bytes 3145736 | tf_op jit(solution)/shard_map/ppermute | solution.py:23
  35.8 1.2 collective-permute-start.11
  37.0 0.8 collective-permute-start.9
  37.8 1.4 %collective-permute-start.7 = (bf16[512,512]{1,0:T(8,128)(2,1)S(1)}, bf16[512,512]{1,0:T(8,128)(2,1)S(1)}, u32[]{:S(2)}, u32[]{:S(2)}) collective-permute-start(bf16[512,512]{1,0:T(8,128)(2,1)S(1)} %get-tuple-element.53), channel_id=1, source_target_pairs={{0,2},{1,3},{2,0},{3,1},{4,6},{5,7},{6,4},{7,5},{8,10},{9,11},{10,... | collective-permute-start | bytes 1572872 | tf_op jit(solution)/shard_map/ppermute | solution.py:18
  39.2 3.2 %returned_blocks.1 = (bf16[128,2048]{1,0:T(8,128)(2,1)S(1)}, bf16[128,2048]{1,0:T(8,128)(2,1)S(1)}, bf16[64,2048]{1,0:T(8,128)(2,1)S(1)}, bf16[64,2048]{1,0:T(8,128)(2,1)S(1)}, bf16[128,2048]{1,0:T(8,128)(2,1)S(1)}) custom-call(bf16[128,1024]{1,0:T(8,128)(2,1)S(1)} %bitcast.14, bf16[128,1024]{1,0:T(8,128)(2,1)S(1)} %collective-permute-done.refs_1_, ...), custom_call_target="tpu_custom_call" | custom-call | flops 2147483648 | bytes 7340032 | tf_op jit(solution)/shard_map/returned_blocks/pallas_call | solution.py:252
  42.4 7.1 %collective-permute-done.6.refs_1_ = bf16[512,512]{1,0:T(8,128)(2,1)S(1)} collective-permute-done((bf16[512,512]{1,0:T(8,128)(2,1)S(1)}, bf16[512,512]{1,0:T(8,128)(2,1)S(1)}, u32[]{:S(2)}, u32[]{:S(2)}) %collective-permute-start.6) | collective-permute-done | bytes 524320 | tf_op jit(solution)/shard_map/ppermute | solution.py:18
  49.5 19.9 %collective-permute-done.7.refs_2_ = bf16[512,512]{1,0:T(8,128)(2,1)S(1)} collective-permute-done((bf16[512,512]{1,0:T(8,128)(2,1)S(1)}, bf16[512,512]{1,0:T(8,128)(2,1)S(1)}, u32[]{:S(2)}, u32[]{:S(2)}) %collective-permute-start.7) | collective-permute-done | bytes 524320 | tf_op jit(solution)/shard_map/ppermute | solution.py:18
  69.4 3.3 %collective-permute-start.14 = (bf16[64,2048]{1,0:T(8,128)(2,1)S(1)}, bf16[64,2048]{1,0:T(8,128)(2,1)S(1)}, u32[]{:S(2)}, u32[]{:S(2)}) collective-permute-start(bf16[64,2048]{1,0:T(8,128)(2,1)S(1)} %get-tuple-element.66), channel_id=1, source_target_pairs={{0,2},{1,3},{2,0},{3,1},{4,6},{5,7},{6,4},{7,5},{8,10},{9,11},{10,... | collective-permute-start | bytes 786440 | tf_op jit(solution)/shard_map/ppermute | solution.py:18
  72.7 7.3 %collective-permute-done.10.refs_6_ = bf16[512,1024]{1,0:T(8,128)(2,1)S(1)} collective-permute-done((bf16[512,1024]{1,0:T(8,128)(2,1)S(1)}, bf16[512,1024]{1,0:T(8,128)(2,1)S(1)}, u32[]{:S(2)}, u32[]{:S(2)}) %collective-permute-start.10) | collective-permute-done | bytes 1048608 | tf_op jit(solution)/shard_map/ppermute | solution.py:23
  80.0 1.2 collective-permute-done.9.refs_5_
  81.2 2.7 %weight_product.1 = (bf16[272,1024]{1,0:T(8,128)(2,1)S(1)}, bf16[272,1024]{1,0:T(8,128)(2,1)S(1)}) custom-call(s32[1]{0:T(128)} %bitcast.3.rep_ref, bf16[512,512]{1,0:T(8,128)(2,1)S(1)} %get-tuple-element.51.refs_0_, bf16[512,512]{1,0:T(8,128)(2,1)S(1)} %collective-permute-done.6.refs_1_, bf16[512,512]{1,0:T(8,128)(2,1)S(1)} %collective-permute-done.7.refs_2_, ...), custom_call_target="tpu_custom_call" | custom-call | flops 2147483648 | bytes 8388608 | tf_op jit(solution)/shard_map/weight_product/pallas_call | solution.py:215
  84.0 1.5 %collective-permute-start.13 = (bf16[272,1024]{1,0:T(8,128)(2,1)S(1)}, bf16[272,1024]{1,0:T(8,128)(2,1)S(1)}, u32[]{:S(2)}, u32[]{:S(2)}) collective-permute-start(bf16[272,1024]{1,0:T(8,128)(2,1)S(1)} %get-tuple-element.58.refs_0_), channel_id=1, source_target_pairs={{0,4},{4,0},{8,12},{12,8},{1,5},{5,1},{9,13},{13,9},{2,6},{6,2},{1... | collective-permute-start | bytes 1671176 | tf_op jit(solution)/shard_map/ppermute | solution.py:23
  85.5 1.2 collective-permute-start.12
  86.7 7.8 %collective-permute-start.16 = (bf16[128,2048]{1,0:T(8,128)(2,1)S(1)}, bf16[128,2048]{1,0:T(8,128)(2,1)S(1)}, u32[]{:S(2)}, u32[]{:S(2)}) collective-permute-start(bf16[128,2048]{1,0:T(8,128)(2,1)S(1)} %get-tuple-element.69), channel_id=1, source_target_pairs={{0,1},{1,2},{2,3},{3,0},{4,5},{5,6},{6,7},{7,4},{8,9},{9,10},{10,1... | collective-permute-start | bytes 1572872 | tf_op jit(solution)/shard_map/ppermute | solution.py:18
  94.6 2.6 %collective-permute-start.15 = (bf16[128,2048]{1,0:T(8,128)(2,1)S(1)}, bf16[128,2048]{1,0:T(8,128)(2,1)S(1)}, u32[]{:S(2)}, u32[]{:S(2)}) collective-permute-start(bf16[128,2048]{1,0:T(8,128)(2,1)S(1)} %get-tuple-element.67), channel_id=1, source_target_pairs={{0,3},{1,0},{2,1},{3,2},{4,7},{5,4},{6,5},{7,6},{8,11},{9,8},{10,9... | collective-permute-start | bytes 1572872 | tf_op jit(solution)/shard_map/ppermute | solution.py:18
  97.2 0.2 joined.5.sum_ref
  97.4 4.0 %collective-permute-start.19 = (bf16[544,1024]{1,0:T(8,128)(2,1)S(1)}, bf16[544,1024]{1,0:T(8,128)(2,1)S(1)}, u32[]{:S(2)}, u32[]{:S(2)}) collective-permute-start(bf16[544,1024]{1,0:T(8,128)(2,1)S(1)} %joined.5.sum_ref), channel_id=1, source_target_pairs={{0,8},{4,12},{8,0},{12,4},{1,9},{5,13},{9,1},{13,5},{2,10},{6,14},... | collective-permute-start | bytes 3342344 | tf_op jit(solution)/shard_map/ppermute | solution.py:23
  101.4 0.2 joined.4.sum_ref
  101.6 0.1 collective-permute-start.18
  101.6 1.4 %finished_half.4 = (f32[2048,1024]{1,0:T(8,128)}, f32[1,2048]{1,0:T(1,128)}) custom-call(s32[1]{0:T(128)} %bitcast.3.rep_ref, bf16[544,1024]{1,0:T(8,128)(2,1)S(1)} %joined.5.sum_ref), custom_call_target="tpu_custom_call" | custom-call | flops 557056 | bytes 3342336 | tf_op jit(solution)/shard_map/finished_half/pallas_call | solution.py:368
  103.1 1.4 %finished_half.5 = (f32[2048,1024]{1,0:T(8,128)}, f32[1,2048]{1,0:T(1,128)}) custom-call(s32[1]{0:T(128)} %bitcast.3.rep_ref, bf16[544,1024]{1,0:T(8,128)(2,1)S(1)} %joined.4.sum_ref, f32[2048,1024]{1,0:T(8,128)} %get-tuple-element.59.refs_0_, f32[1,2048]{1,0:T(1,128)} %get-tuple-element.60.refs_1_), custom_call_target="tpu_custom_call", output_to_operand_aliasing={{0}: (2, {}), {1}: (3, {})} | custom-call | flops 557056 | bytes 3342336 | tf_op jit(solution)/shard_map/finished_half/pallas_call | solution.py:368
  104.5 2.4 %collective-permute-done.16.refs_3_ = bf16[128,2048]{1,0:T(8,128)(2,1)S(1)} collective-permute-done((bf16[128,2048]{1,0:T(8,128)(2,1)S(1)}, bf16[128,2048]{1,0:T(8,128)(2,1)S(1)}, u32[]{:S(2)}, u32[]{:S(2)}) %collective-permute-start.16) | collective-permute-done | bytes 524320 | tf_op jit(solution)/shard_map/ppermute | solution.py:18
  106.9 8.3 %collective-permute-done.15.refs_1_ = bf16[128,2048]{1,0:T(8,128)(2,1)S(1)} collective-permute-done((bf16[128,2048]{1,0:T(8,128)(2,1)S(1)}, bf16[128,2048]{1,0:T(8,128)(2,1)S(1)}, u32[]{:S(2)}, u32[]{:S(2)}) %collective-permute-start.15) | collective-permute-done | bytes 524320 | tf_op jit(solution)/shard_map/ppermute | solution.py:18
  115.2 1.5 %row_gradient.2 = (bf16[64,8192]{1,0:T(8,128)(2,1)S(1)}, bf16[64,8192]{1,0:T(8,128)(2,1)S(1)}) custom-call(s32[1]{0:T(128)} %bitcast.1.me_ref, bf16[1,2,64,8192]{3,2,1,0:T(8,128)(2,1)S(1)} %copy-done.1, bf16[2,64,8192]{2,1,0:T(8,128)(2,1)S(1)} %copy-done.2, bf16[128,2048]{1,0:T(8,128)(2,1)S(1)} %get-tuple-element.71.refs_0_, ...), custom_call_target="tpu_custom_call" | custom-call | flops 6291456 | bytes 5242880 | tf_op jit(solution)/shard_map/row_gradient/pallas_call | solution.py:302
  116.7 1.3 collective-permute-start.21
  118.0 7.8 %collective-permute-done.17.refs_2_ = bf16[64,2048]{1,0:T(8,128)(2,1)S(1)} collective-permute-done((bf16[64,2048]{1,0:T(8,128)(2,1)S(1)}, bf16[64,2048]{1,0:T(8,128)(2,1)S(1)}, u32[]{:S(2)}, u32[]{:S(2)}) %collective-permute-start.17) | collective-permute-done | bytes 262176 | tf_op jit(solution)/shard_map/ppermute | solution.py:18
  125.9 1.5 %row_gradient.3 = (bf16[64,8192]{1,0:T(8,128)(2,1)S(1)}, bf16[64,8192]{1,0:T(8,128)(2,1)S(1)}) custom-call(s32[1]{0:T(128)} %bitcast.1.me_ref, bf16[1,2,64,8192]{3,2,1,0:T(8,128)(2,1)S(1)} %copy-done.1, bf16[2,64,8192]{2,1,0:T(8,128)(2,1)S(1)} %copy-done.2, bf16[128,2048]{1,0:T(8,128)(2,1)S(1)} %get-tuple-element.71.refs_0_, ...), custom_call_target="tpu_custom_call" | custom-call | flops 6291456 | bytes 5242880 | tf_op jit(solution)/shard_map/row_gradient/pallas_call | solution.py:302
  127.4 1.3 collective-permute-start.20
  128.7 1.4 %finished_half.6 = (f32[2048,1024]{1,0:T(8,128)}, f32[1,2048]{1,0:T(1,128)}) custom-call(s32[1]{0:T(128)} %bitcast.3.rep_ref, bf16[544,1024]{1,0:T(8,128)(2,1)S(1)} %collective-permute-done.19.sum_ref, f32[2048,1024]{1,0:T(8,128)} %get-tuple-element.61.refs_0_, f32[1,2048]{1,0:T(1,128)} %get-tuple-element.62.refs_1_), custom_call_target="tpu_custom_call", output_to_operand_aliasing={{0}: (2, {}), {1}: (3, {})} | custom-call | flops 557056 | bytes 3342336 | tf_op jit(solution)/shard_map/finished_half/pallas_call | solution.py:368
  130.1 1.4 %finished_half.7 = (f32[2048,1024]{1,0:T(8,128)}, f32[1,2048]{1,0:T(1,128)}) custom-call(s32[1]{0:T(128)} %bitcast.3.rep_ref, bf16[544,1024]{1,0:T(8,128)(2,1)S(1)} %collective-permute-done.18.sum_ref, f32[2048,1024]{1,0:T(8,128)} %get-tuple-element.76.refs_0_, f32[1,2048]{1,0:T(1,128)} %get-tuple-element.77.refs_1_), custom_call_target="tpu_custom_call", output_to_operand_aliasing={{0}: (2, {}), {1}: (3, {})} | custom-call | flops 557056 | bytes 3342336 | tf_op jit(solution)/shard_map/finished_half/pallas_call | solution.py:368
  131.6 1.1 input_gradient.2.refs_0_
  132.7 1.1 input_gradient.3
  (23 shorter events, 0.1 us)
Async XLA Ops:
  0.6 1.6 %copy-start = (bf16[1,2,64,8192]{3,2,1,0:T(8,128)(2,1)S(1)}, bf16[1,2,64,8192]{3,2,1,0:T(8,128)(2,1)}, u32[]{:S(2)}) copy-start(bf16[1,2,64,8192]{3,2,1,0:T(8,128)(2,1)} %x_ref.3) | copy-start | bytes 6291460
  2.2 1.1 copy-start.4
  3.3 12.3 %collective-permute-start = (bf16[128,1024]{1,0:T(8,128)(2,1)S(1)}, bf16[128,1024]{1,0:T(8,128)(2,1)S(1)}, u32[]{:S(2)}, u32[]{:S(2)}) collective-permute-start(bf16[128,1024]{1,0:T(8,128)(2,1)S(1)} %bitcast.10), channel_id=1, source_target_pairs={{0,1},{1,2},{2,3},{3,0},{4,5},{5,6},{6,7},{7,4},{8,9},{9,10},{10,1... | collective-permute-start | bytes 786440 | tf_op jit(solution)/shard_map/ppermute | solution.py:18
  6.4 24.0 %collective-permute-start.3 = (bf16[128,2048]{1,0:T(8,128)(2,1)S(1)}, bf16[128,2048]{1,0:T(8,128)(2,1)S(1)}, u32[]{:S(2)}, u32[]{:S(2)}) collective-permute-start(bf16[128,2048]{1,0:T(8,128)(2,1)S(1)} %get-tuple-element.48), channel_id=1, source_target_pairs={{0,4},{4,0},{8,12},{12,8},{1,5},{5,1},{9,13},{13,9},{2,6},{6,2},{1... | collective-permute-start | bytes 1572872 | tf_op jit(solution)/shard_map/ppermute | solution.py:23
  7.9 24.3 %collective-permute-start.4 = (bf16[128,2048]{1,0:T(8,128)(2,1)S(1)}, bf16[128,2048]{1,0:T(8,128)(2,1)S(1)}, u32[]{:S(2)}, u32[]{:S(2)}) collective-permute-start(bf16[128,2048]{1,0:T(8,128)(2,1)S(1)} %get-tuple-element.49), channel_id=1, source_target_pairs={{0,8},{4,12},{8,0},{12,4},{1,9},{5,13},{9,1},{13,5},{2,10},{6,14},... | collective-permute-start | bytes 1572872 | tf_op jit(solution)/shard_map/ppermute | solution.py:23
  9.4 29.8 %copy-start.5 = (bf16[1,2048]{1,0:T(2,128)(2,1)S(1)}, bf16[1,2048]{1,0:T(2,128)(2,1)}, u32[]{:S(2)}) copy-start(bf16[1,2048]{1,0:T(2,128)(2,1)} %refs_9_.1) | copy-start | bytes 12292
  9.4 29.8 %copy-start.3 = (bf16[1,2048,1024]{2,1,0:T(8,128)(2,1)S(1)}, bf16[1,2048,1024]{2,1,0:T(8,128)(2,1)}, u32[]{:S(2)}) copy-start(bf16[1,2048,1024]{2,1,0:T(8,128)(2,1)} %param.7) | copy-start | bytes 12582916
  9.4 22.8 %collective-permute-start.5 = (bf16[128,2048]{1,0:T(8,128)(2,1)S(1)}, bf16[128,2048]{1,0:T(8,128)(2,1)S(1)}, u32[]{:S(2)}, u32[]{:S(2)}) collective-permute-start(bf16[128,2048]{1,0:T(8,128)(2,1)S(1)} %get-tuple-element.50), channel_id=1, source_target_pairs={{0,12},{4,8},{8,4},{12,0},{1,13},{5,9},{9,5},{13,1},{2,14},{6,10},... | collective-permute-start | bytes 1572872 | tf_op jit(solution)/shard_map/ppermute | solution.py:23
  9.9 16.2 %collective-permute-start.1 = (bf16[128,1024]{1,0:T(8,128)(2,1)S(1)}, bf16[128,1024]{1,0:T(8,128)(2,1)S(1)}, u32[]{:S(2)}, u32[]{:S(2)}) collective-permute-start(bf16[128,1024]{1,0:T(8,128)(2,1)S(1)} %bitcast.11), channel_id=1, source_target_pairs={{0,2},{1,3},{2,0},{3,1},{4,6},{5,7},{6,4},{7,5},{8,10},{9,11},{10,... | collective-permute-start | bytes 786440 | tf_op jit(solution)/shard_map/ppermute | solution.py:18
  15.6 14.6 %collective-permute-start.2 = (bf16[128,1024]{1,0:T(8,128)(2,1)S(1)}, bf16[128,1024]{1,0:T(8,128)(2,1)S(1)}, u32[]{:S(2)}, u32[]{:S(2)}) collective-permute-start(bf16[128,1024]{1,0:T(8,128)(2,1)S(1)} %bitcast.12), channel_id=1, source_target_pairs={{0,3},{1,0},{2,1},{3,2},{4,7},{5,4},{6,5},{7,6},{8,11},{9,8},{10,9... | collective-permute-start | bytes 786440 | tf_op jit(solution)/shard_map/ppermute | solution.py:18
  32.7 16.8 %collective-permute-start.6 = (bf16[512,512]{1,0:T(8,128)(2,1)S(1)}, bf16[512,512]{1,0:T(8,128)(2,1)S(1)}, u32[]{:S(2)}, u32[]{:S(2)}) collective-permute-start(bf16[512,512]{1,0:T(8,128)(2,1)S(1)} %get-tuple-element.52), channel_id=1, source_target_pairs={{0,1},{1,2},{2,3},{3,0},{4,5},{5,6},{6,7},{7,4},{8,9},{9,10},{10,1... | collective-permute-start | bytes 1572872 | tf_op jit(solution)/shard_map/ppermute | solution.py:18
  34.3 45.7 %collective-permute-start.10 = (bf16[512,1024]{1,0:T(8,128)(2,1)S(1)}, bf16[512,1024]{1,0:T(8,128)(2,1)S(1)}, u32[]{:S(2)}, u32[]{:S(2)}) collective-permute-start(bf16[512,1024]{1,0:T(8,128)(2,1)S(1)} %joined.3.refs_4_), channel_id=1, source_target_pairs={{0,8},{4,12},{8,0},{12,4},{1,9},{5,13},{9,1},{13,5},{2,10},{6,14},... | collective-permute-start | bytes 3145736 | tf_op jit(solution)/shard_map/ppermute | solution.py:23
  35.8 44.2 %collective-permute-start.11 = (bf16[512,1024]{1,0:T(8,128)(2,1)S(1)}, bf16[512,1024]{1,0:T(8,128)(2,1)S(1)}, u32[]{:S(2)}, u32[]{:S(2)}) collective-permute-start(bf16[512,1024]{1,0:T(8,128)(2,1)S(1)} %joined.3.refs_4_), channel_id=1, source_target_pairs={{0,12},{4,8},{8,4},{12,0},{1,13},{5,9},{9,5},{13,1},{2,14},{6,10},... | collective-permute-start | bytes 3145736 | tf_op jit(solution)/shard_map/ppermute | solution.py:23
  37.0 44.2 %collective-permute-start.9 = (bf16[512,1024]{1,0:T(8,128)(2,1)S(1)}, bf16[512,1024]{1,0:T(8,128)(2,1)S(1)}, u32[]{:S(2)}, u32[]{:S(2)}) collective-permute-start(bf16[512,1024]{1,0:T(8,128)(2,1)S(1)} %joined.3.refs_4_), channel_id=1, source_target_pairs={{0,4},{4,0},{8,12},{12,8},{1,5},{5,1},{9,13},{13,9},{2,6},{6,2},{1... | collective-permute-start | bytes 3145736 | tf_op jit(solution)/shard_map/ppermute | solution.py:23
  37.8 31.6 %collective-permute-start.7 = (bf16[512,512]{1,0:T(8,128)(2,1)S(1)}, bf16[512,512]{1,0:T(8,128)(2,1)S(1)}, u32[]{:S(2)}, u32[]{:S(2)}) collective-permute-start(bf16[512,512]{1,0:T(8,128)(2,1)S(1)} %get-tuple-element.53), channel_id=1, source_target_pairs={{0,2},{1,3},{2,0},{3,1},{4,6},{5,7},{6,4},{7,5},{8,10},{9,11},{10,... | collective-permute-start | bytes 1572872 | tf_op jit(solution)/shard_map/ppermute | solution.py:18
  49.5 31.7 %collective-permute-start.8 = (bf16[512,512]{1,0:T(8,128)(2,1)S(1)}, bf16[512,512]{1,0:T(8,128)(2,1)S(1)}, u32[]{:S(2)}, u32[]{:S(2)}) collective-permute-start(bf16[512,512]{1,0:T(8,128)(2,1)S(1)} %get-tuple-element.55), channel_id=1, source_target_pairs={{0,3},{1,0},{2,1},{3,2},{4,7},{5,4},{6,5},{7,6},{8,11},{9,8},{10,9... | collective-permute-start | bytes 1572872 | tf_op jit(solution)/shard_map/ppermute | solution.py:18
  69.4 25.2 %collective-permute-start.14 = (bf16[64,2048]{1,0:T(8,128)(2,1)S(1)}, bf16[64,2048]{1,0:T(8,128)(2,1)S(1)}, u32[]{:S(2)}, u32[]{:S(2)}) collective-permute-start(bf16[64,2048]{1,0:T(8,128)(2,1)S(1)} %get-tuple-element.66), channel_id=1, source_target_pairs={{0,2},{1,3},{2,0},{3,1},{4,6},{5,7},{6,4},{7,5},{8,10},{9,11},{10,... | collective-permute-start | bytes 786440 | tf_op jit(solution)/shard_map/ppermute | solution.py:18
  84.0 13.2 %collective-permute-start.13 = (bf16[272,1024]{1,0:T(8,128)(2,1)S(1)}, bf16[272,1024]{1,0:T(8,128)(2,1)S(1)}, u32[]{:S(2)}, u32[]{:S(2)}) collective-permute-start(bf16[272,1024]{1,0:T(8,128)(2,1)S(1)} %get-tuple-element.58.refs_0_), channel_id=1, source_target_pairs={{0,4},{4,0},{8,12},{12,8},{1,5},{5,1},{9,13},{13,9},{2,6},{6,2},{1... | collective-permute-start | bytes 1671176 | tf_op jit(solution)/shard_map/ppermute | solution.py:23
  85.5 15.9 %collective-permute-start.12 = (bf16[272,1024]{1,0:T(8,128)(2,1)S(1)}, bf16[272,1024]{1,0:T(8,128)(2,1)S(1)}, u32[]{:S(2)}, u32[]{:S(2)}) collective-permute-start(bf16[272,1024]{1,0:T(8,128)(2,1)S(1)} %get-tuple-element.57.refs_0_), channel_id=1, source_target_pairs={{0,8},{4,12},{8,0},{12,4},{1,9},{5,13},{9,1},{13,5},{2,10},{6,14},... | collective-permute-start | bytes 1671176 | tf_op jit(solution)/shard_map/ppermute | solution.py:23
  86.7 20.2 %collective-permute-start.16 = (bf16[128,2048]{1,0:T(8,128)(2,1)S(1)}, bf16[128,2048]{1,0:T(8,128)(2,1)S(1)}, u32[]{:S(2)}, u32[]{:S(2)}) collective-permute-start(bf16[128,2048]{1,0:T(8,128)(2,1)S(1)} %get-tuple-element.69), channel_id=1, source_target_pairs={{0,1},{1,2},{2,3},{3,0},{4,5},{5,6},{6,7},{7,4},{8,9},{9,10},{10,1... | collective-permute-start | bytes 1572872 | tf_op jit(solution)/shard_map/ppermute | solution.py:18
  94.6 20.7 %collective-permute-start.15 = (bf16[128,2048]{1,0:T(8,128)(2,1)S(1)}, bf16[128,2048]{1,0:T(8,128)(2,1)S(1)}, u32[]{:S(2)}, u32[]{:S(2)}) collective-permute-start(bf16[128,2048]{1,0:T(8,128)(2,1)S(1)} %get-tuple-element.67), channel_id=1, source_target_pairs={{0,3},{1,0},{2,1},{3,2},{4,7},{5,4},{6,5},{7,6},{8,11},{9,8},{10,9... | collective-permute-start | bytes 1572872 | tf_op jit(solution)/shard_map/ppermute | solution.py:18
  97.2 28.7 %collective-permute-start.17 = (bf16[64,2048]{1,0:T(8,128)(2,1)S(1)}, bf16[64,2048]{1,0:T(8,128)(2,1)S(1)}, u32[]{:S(2)}, u32[]{:S(2)}) collective-permute-start(bf16[64,2048]{1,0:T(8,128)(2,1)S(1)} %get-tuple-element.73), channel_id=1, source_target_pairs={{0,2},{1,3},{2,0},{3,1},{4,6},{5,7},{6,4},{7,5},{8,10},{9,11},{10,... | collective-permute-start | bytes 786440 | tf_op jit(solution)/shard_map/ppermute | solution.py:18
  97.4 31.3 %collective-permute-start.19 = (bf16[544,1024]{1,0:T(8,128)(2,1)S(1)}, bf16[544,1024]{1,0:T(8,128)(2,1)S(1)}, u32[]{:S(2)}, u32[]{:S(2)}) collective-permute-start(bf16[544,1024]{1,0:T(8,128)(2,1)S(1)} %joined.5.sum_ref), channel_id=1, source_target_pairs={{0,8},{4,12},{8,0},{12,4},{1,9},{5,13},{9,1},{13,5},{2,10},{6,14},... | collective-permute-start | bytes 3342344 | tf_op jit(solution)/shard_map/ppermute | solution.py:23
  101.6 28.6 %collective-permute-start.18 = (bf16[544,1024]{1,0:T(8,128)(2,1)S(1)}, bf16[544,1024]{1,0:T(8,128)(2,1)S(1)}, u32[]{:S(2)}, u32[]{:S(2)}) collective-permute-start(bf16[544,1024]{1,0:T(8,128)(2,1)S(1)} %joined.4.sum_ref), channel_id=1, source_target_pairs={{0,4},{4,0},{8,12},{12,8},{1,5},{5,1},{9,13},{13,9},{2,6},{6,2},{1... | collective-permute-start | bytes 3342344 | tf_op jit(solution)/shard_map/ppermute | solution.py:23
  103.1 12.2 %copy-start.1 = (bf16[1,2,64,8192]{3,2,1,0:T(8,128)(2,1)S(1)}, bf16[1,2,64,8192]{3,2,1,0:T(8,128)(2,1)}, u32[]{:S(2)}) copy-start(bf16[1,2,64,8192]{3,2,1,0:T(8,128)(2,1)} %x_ref.3) | copy-start | bytes 6291460
  103.1 12.2 %copy-start.2 = (bf16[2,64,8192]{2,1,0:T(8,128)(2,1)S(1)}, bf16[2,64,8192]{2,1,0:T(8,128)(2,1)}, u32[]{:S(2)}) copy-start(bf16[2,64,8192]{2,1,0:T(8,128)(2,1)} %top_ref.3) | copy-start | bytes 6291460
  116.7 14.8 %collective-permute-start.21 = (bf16[64,8192]{1,0:T(8,128)(2,1)S(1)}, bf16[64,8192]{1,0:T(8,128)(2,1)S(1)}, u32[]{:S(2)}, u32[]{:S(2)}) collective-permute-start(bf16[64,8192]{1,0:T(8,128)(2,1)S(1)} %get-tuple-element.70.upper_ref), channel_id=1, source_target_pairs={{16,0},{17,1},{18,2},{19,3},{20,4},{21,5},{22,6},{23,7},{24,8},{25... | collective-permute-start | bytes 3145736 | tf_op jit(solution)/shard_map/ppermute | solution.py:452
  127.4 5.3 %collective-permute-start.20 = (bf16[64,8192]{1,0:T(8,128)(2,1)S(1)}, bf16[64,8192]{1,0:T(8,128)(2,1)S(1)}, u32[]{:S(2)}, u32[]{:S(2)}) collective-permute-start(bf16[64,8192]{1,0:T(8,128)(2,1)S(1)} %get-tuple-element.74.upper_ref), channel_id=1, source_target_pairs={{16,0},{17,1},{18,2},{19,3},{20,4},{21,5},{22,6},{23,7},{24,8},{25... | collective-permute-start | bytes 3145736 | tf_op jit(solution)/shard_map/ppermute | solution.py:452

commit v11 on v10

--- a/solution.py
+++ b/solution.py
@@ -413,10 +413,9 @@
     near = [j for j in range(1, groups) if j != far]
     back = returned_blocks(slots, weight, norm_gain, micro, far)
     columns = list(sent)
-    columns[far] = cyclic(sent[far], "fsdp", far)
-    columns[near[0]] = cyclic(sent[near[0]], "fsdp", near[0])
-    for j in near[1:]:
-        columns[j] = cyclic(after(sent[j], back[0][0], columns[near[0]]), "fsdp", j)
+    for j in near:
+        columns[j] = cyclic(sent[j], "fsdp", j)
+    columns[far] = cyclic(after(sent[far], back[0][0], *[columns[j] for j in near]), "fsdp", far)
     held = after(joined(slots), sent[0])
     values = [held if e == 0 else flipped(held, "rep", e) for e in range(reps)]
 

time: 135 us -> 139 us (1.030); the launches traced: 134 us -> 139 us
  waiting for transfers between devices: 72.4 us -> 90.6 us
  starting transfers between devices: 40.2 us -> 27.5 us
    ppermute x10, waiting for transfers between devices: 62 us -> 87.1 us  [cyclic(): lax.ppermute(value, axis, [(i, (i + steps) % count) for i in range(count)])]
    ppermute x10, starting transfers between devices: 23.8 us -> 13.7 us  [cyclic(): lax.ppermute(value, axis, [(i, (i + steps) % count) for i in range(count)])]
    ppermute x10, waiting for transfers between devices: 10.4 us -> 3.53 us  [flipped(): return lax.ppermute(value, axis, [(i, i ^ mask) for i in range(count)])]
    ppermute x10, starting transfers between devices: 13.8 us -> 11.2 us  [flipped(): return lax.ppermute(value, axis, [(i, i ^ mask) for i in range(count)])]
  transfers between devices with their start and end apart: 22 -> 22, of which waited for: 11 -> 12; matrix products, arithmetic and copies ran while one was open for 0% -> 0% of each run, Pallas kernels for 12% -> 12%
where the time goes in v11:
time: 139 us
  waiting for transfers between devices  90.6 us (65%)
  starting transfers between devices  27.5 us (20%)
  Pallas kernels  18.7 us (13%)
  local copies, waits for them, and re-layouts  1.6 us (1%)
    ppermute x10, waiting for transfers between devices, cyclic(): lax.ppermute(value, axis, [(i, (i + steps) % count) for i in range(count)])  87.1 us
    ppermute x10, starting transfers between devices, cyclic(): lax.ppermute(value, axis, [(i, (i + steps) % count) for i in range(count)])  13.7 us
    ppermute x10, starting transfers between devices, flipped(): return lax.ppermute(value, axis, [(i, i ^ mask) for i in range(count)])  11.2 us
    pallas_call x4, Pallas kernels, finished_half(): pl.pallas_call(kernel, grid_spec=pltpu.PrefetchScalarGridSpec(num_scalar_...  5.65 us
    ppermute x10, waiting for transfers between devices, flipped(): return lax.ppermute(value, axis, [(i, i ^ mask) for i in range(count)])  3.53 us
    pallas_call x1, Pallas kernels, returned_blocks(): pl.pallas_call(kernel, grid=(shard // tile,), out_shape=[jax.ShapeDtypeSt...  3.17 us
    pallas_call x2, Pallas kernels, row_gradient(): pl.pallas_call(kernel, grid=(rows // step,), out_shape=[jax.ShapeDtypeStr...  2.99 us
  transfers between devices with their start and end apart: 22, of which 12 were waited for; matrix products, arithmetic and copies ran while one was open for 0% of the time, Pallas kernels for 12%

profile of v11, /device:TPU:0, one launch (start us, length us, event | category | flops | bytes accessed | tf_op | source)
XLA Modules:
  0.0 139.3 jit_solution(9598766026395531888)
XLA Ops:
  0.6 0.0 copy-start
  0.6 1.6 %copy-done = bf16[1,2,64,8192]{3,2,1,0:T(8,128)(2,1)S(1)} copy-done((bf16[1,2,64,8192]{3,2,1,0:T(8,128)(2,1)S(1)}, bf16[1,2,64,8192]{3,2,1,0:T(8,128)(2,1)}, u32[]{:S(2)}) %copy-start) | copy-done | bytes 2097176
  2.2 1.1 scaled_blocks.1
  3.3 3.1 %collective-permute-start = (bf16[128,1024]{1,0:T(8,128)(2,1)S(1)}, bf16[128,1024]{1,0:T(8,128)(2,1)S(1)}, u32[]{:S(2)}, u32[]{:S(2)}) collective-permute-start(bf16[128,1024]{1,0:T(8,128)(2,1)S(1)} %bitcast.10), channel_id=1, source_target_pairs={{0,1},{1,2},{2,3},{3,0},{4,5},{5,6},{6,7},{7,4},{8,9},{9,10},{10,1... | collective-permute-start | bytes 786440 | tf_op jit(solution)/shard_map/ppermute | solution.py:18
  6.4 1.5 %collective-permute-start.3 = (bf16[128,2048]{1,0:T(8,128)(2,1)S(1)}, bf16[128,2048]{1,0:T(8,128)(2,1)S(1)}, u32[]{:S(2)}, u32[]{:S(2)}) collective-permute-start(bf16[128,2048]{1,0:T(8,128)(2,1)S(1)} %get-tuple-element.48), channel_id=1, source_target_pairs={{0,4},{4,0},{8,12},{12,8},{1,5},{5,1},{9,13},{13,9},{2,6},{6,2},{1... | collective-permute-start | bytes 1572872 | tf_op jit(solution)/shard_map/ppermute | solution.py:23
  7.9 1.5 %collective-permute-start.4 = (bf16[128,2048]{1,0:T(8,128)(2,1)S(1)}, bf16[128,2048]{1,0:T(8,128)(2,1)S(1)}, u32[]{:S(2)}, u32[]{:S(2)}) collective-permute-start(bf16[128,2048]{1,0:T(8,128)(2,1)S(1)} %get-tuple-element.49), channel_id=1, source_target_pairs={{0,8},{4,12},{8,0},{12,4},{1,9},{5,13},{9,1},{13,5},{2,10},{6,14},... | collective-permute-start | bytes 1572872 | tf_op jit(solution)/shard_map/ppermute | solution.py:23
  9.4 0.5 collective-permute-start.5
  9.9 2.6 %collective-permute-start.1 = (bf16[128,1024]{1,0:T(8,128)(2,1)S(1)}, bf16[128,1024]{1,0:T(8,128)(2,1)S(1)}, u32[]{:S(2)}, u32[]{:S(2)}) collective-permute-start(bf16[128,1024]{1,0:T(8,128)(2,1)S(1)} %bitcast.11), channel_id=1, source_target_pairs={{0,2},{1,3},{2,0},{3,1},{4,6},{5,7},{6,4},{7,5},{8,10},{9,11},{10,... | collective-permute-start | bytes 786440 | tf_op jit(solution)/shard_map/ppermute | solution.py:18
  12.5 3.2 %collective-permute-done.refs_1_ = bf16[128,1024]{1,0:T(8,128)(2,1)S(1)} collective-permute-done((bf16[128,1024]{1,0:T(8,128)(2,1)S(1)}, bf16[128,1024]{1,0:T(8,128)(2,1)S(1)}, u32[]{:S(2)}, u32[]{:S(2)}) %collective-permute-start) | collective-permute-done | bytes 262176 | tf_op jit(solution)/shard_map/ppermute | solution.py:18
  15.6 1.4 collective-permute-start.2
  17.0 9.0 %collective-permute-done.1.refs_2_ = bf16[128,1024]{1,0:T(8,128)(2,1)S(1)} collective-permute-done((bf16[128,1024]{1,0:T(8,128)(2,1)S(1)}, bf16[128,1024]{1,0:T(8,128)(2,1)S(1)}, u32[]{:S(2)}, u32[]{:S(2)}) %collective-permute-start.1) | collective-permute-done | bytes 262176 | tf_op jit(solution)/shard_map/ppermute | solution.py:18
  26.0 4.2 %collective-permute-done.2.refs_3_ = bf16[128,1024]{1,0:T(8,128)(2,1)S(1)} collective-permute-done((bf16[128,1024]{1,0:T(8,128)(2,1)S(1)}, bf16[128,1024]{1,0:T(8,128)(2,1)S(1)}, u32[]{:S(2)}, u32[]{:S(2)}) %collective-permute-start.2) | collective-permute-done | bytes 262176 | tf_op jit(solution)/shard_map/ppermute | solution.py:18
  30.3 2.0 %collective-permute-done.4.refs_2_ = bf16[128,2048]{1,0:T(8,128)(2,1)S(1)} collective-permute-done((bf16[128,2048]{1,0:T(8,128)(2,1)S(1)}, bf16[128,2048]{1,0:T(8,128)(2,1)S(1)}, u32[]{:S(2)}, u32[]{:S(2)}) %collective-permute-start.4) | collective-permute-done | bytes 524320 | tf_op jit(solution)/shard_map/ppermute | solution.py:23
  32.2 0.5 regrouped.1
  32.7 1.6 %collective-permute-start.6 = (bf16[512,512]{1,0:T(8,128)(2,1)S(1)}, bf16[512,512]{1,0:T(8,128)(2,1)S(1)}, u32[]{:S(2)}, u32[]{:S(2)}) collective-permute-start(bf16[512,512]{1,0:T(8,128)(2,1)S(1)} %get-tuple-element.52), channel_id=1, source_target_pairs={{0,1},{1,2},{2,3},{3,0},{4,5},{5,6},{6,7},{7,4},{8,9},{9,10},{10,1... | collective-permute-start | bytes 1572872 | tf_op jit(solution)/shard_map/ppermute | solution.py:18
  34.3 2.2 %collective-permute-start.7 = (bf16[512,512]{1,0:T(8,128)(2,1)S(1)}, bf16[512,512]{1,0:T(8,128)(2,1)S(1)}, u32[]{:S(2)}, u32[]{:S(2)}) collective-permute-start(bf16[512,512]{1,0:T(8,128)(2,1)S(1)} %get-tuple-element.54), channel_id=1, source_target_pairs={{0,3},{1,0},{2,1},{3,2},{4,7},{5,4},{6,5},{7,6},{8,11},{9,8},{10,9... | collective-permute-start | bytes 1572872 | tf_op jit(solution)/shard_map/ppermute | solution.py:18
  36.6 0.1 joined.3.refs_4_
  36.7 1.6 %collective-permute-start.10 = (bf16[512,1024]{1,0:T(8,128)(2,1)S(1)}, bf16[512,1024]{1,0:T(8,128)(2,1)S(1)}, u32[]{:S(2)}, u32[]{:S(2)}) collective-permute-start(bf16[512,1024]{1,0:T(8,128)(2,1)S(1)} %joined.3.refs_4_), channel_id=1, source_target_pairs={{0,8},{4,12},{8,0},{12,4},{1,9},{5,13},{9,1},{13,5},{2,10},{6,14},... | collective-permute-start | bytes 3145736 | tf_op jit(solution)/shard_map/ppermute | solution.py:23
  38.3 1.2 collective-permute-start.11
  39.5 0.8 collective-permute-start.9
  40.3 3.2 %returned_blocks.1 = (bf16[128,2048]{1,0:T(8,128)(2,1)S(1)}, bf16[128,2048]{1,0:T(8,128)(2,1)S(1)}, bf16[64,2048]{1,0:T(8,128)(2,1)S(1)}, bf16[64,2048]{1,0:T(8,128)(2,1)S(1)}, bf16[128,2048]{1,0:T(8,128)(2,1)S(1)}) custom-call(bf16[128,1024]{1,0:T(8,128)(2,1)S(1)} %bitcast.14, bf16[128,1024]{1,0:T(8,128)(2,1)S(1)} %collective-permute-done.refs_1_, ...), custom_call_target="tpu_custom_call" | custom-call | flops 2147483648 | bytes 7340032 | tf_op jit(solution)/shard_map/returned_blocks/pallas_call | solution.py:252
  43.4 6.0 %collective-permute-done.6.refs_1_ = bf16[512,512]{1,0:T(8,128)(2,1)S(1)} collective-permute-done((bf16[512,512]{1,0:T(8,128)(2,1)S(1)}, bf16[512,512]{1,0:T(8,128)(2,1)S(1)}, u32[]{:S(2)}, u32[]{:S(2)}) %collective-permute-start.6) | collective-permute-done | bytes 524320 | tf_op jit(solution)/shard_map/ppermute | solution.py:18
  49.4 8.1 %collective-permute-done.7.refs_3_ = bf16[512,512]{1,0:T(8,128)(2,1)S(1)} collective-permute-done((bf16[512,512]{1,0:T(8,128)(2,1)S(1)}, bf16[512,512]{1,0:T(8,128)(2,1)S(1)}, u32[]{:S(2)}, u32[]{:S(2)}) %collective-permute-start.7) | collective-permute-done | bytes 524320 | tf_op jit(solution)/shard_map/ppermute | solution.py:18
  57.5 1.3 collective-permute-start.8
  58.8 24.1 %collective-permute-done.8.refs_2_ = bf16[512,512]{1,0:T(8,128)(2,1)S(1)} collective-permute-done((bf16[512,512]{1,0:T(8,128)(2,1)S(1)}, bf16[512,512]{1,0:T(8,128)(2,1)S(1)}, u32[]{:S(2)}, u32[]{:S(2)}) %collective-permute-start.8) | collective-permute-done | bytes 524320 | tf_op jit(solution)/shard_map/ppermute | solution.py:18
  82.9 0.5 collective-permute-done.9.refs_5_
  83.4 2.7 %weight_product.1 = (bf16[272,1024]{1,0:T(8,128)(2,1)S(1)}, bf16[272,1024]{1,0:T(8,128)(2,1)S(1)}) custom-call(s32[1]{0:T(128)} %bitcast.3.rep_ref, bf16[512,512]{1,0:T(8,128)(2,1)S(1)} %get-tuple-element.51.refs_0_, bf16[512,512]{1,0:T(8,128)(2,1)S(1)} %collective-permute-done.6.refs_1_, bf16[512,512]{1,0:T(8,128)(2,1)S(1)} %collective-permute-done.8.refs_2_, ...), custom_call_target="tpu_custom_call" | custom-call | flops 2147483648 | bytes 8388608 | tf_op jit(solution)/shard_map/weight_product/pallas_call | solution.py:215
  86.1 1.5 %collective-permute-start.13 = (bf16[272,1024]{1,0:T(8,128)(2,1)S(1)}, bf16[272,1024]{1,0:T(8,128)(2,1)S(1)}, u32[]{:S(2)}, u32[]{:S(2)}) collective-permute-start(bf16[272,1024]{1,0:T(8,128)(2,1)S(1)} %get-tuple-element.58.refs_0_), channel_id=1, source_target_pairs={{0,4},{4,0},{8,12},{12,8},{1,5},{5,1},{9,13},{13,9},{2,6},{6,2},{1... | collective-permute-start | bytes 1671176 | tf_op jit(solution)/shard_map/ppermute | solution.py:23
  87.6 0.6 collective-permute-start.12
  88.2 1.5 %collective-permute-start.16 = (bf16[128,2048]{1,0:T(8,128)(2,1)S(1)}, bf16[128,2048]{1,0:T(8,128)(2,1)S(1)}, u32[]{:S(2)}, u32[]{:S(2)}) collective-permute-start(bf16[128,2048]{1,0:T(8,128)(2,1)S(1)} %get-tuple-element.69), channel_id=1, source_target_pairs={{0,1},{1,2},{2,3},{3,0},{4,5},{5,6},{6,7},{7,4},{8,9},{9,10},{10,1... | collective-permute-start | bytes 1572872 | tf_op jit(solution)/shard_map/ppermute | solution.py:18
  89.7 17.8 %collective-permute-done.14.refs_2_ = bf16[64,2048]{1,0:T(8,128)(2,1)S(1)} collective-permute-done((bf16[64,2048]{1,0:T(8,128)(2,1)S(1)}, bf16[64,2048]{1,0:T(8,128)(2,1)S(1)}, u32[]{:S(2)}, u32[]{:S(2)}) %collective-permute-start.14) | collective-permute-done | bytes 262176 | tf_op jit(solution)/shard_map/ppermute | solution.py:18
  107.5 0.2 joined.5.sum_ref
  107.7 0.6 collective-permute-start.19
  108.3 0.2 joined.4.sum_ref
  108.4 1.6 %collective-permute-start.18 = (bf16[544,1024]{1,0:T(8,128)(2,1)S(1)}, bf16[544,1024]{1,0:T(8,128)(2,1)S(1)}, u32[]{:S(2)}, u32[]{:S(2)}) collective-permute-start(bf16[544,1024]{1,0:T(8,128)(2,1)S(1)} %joined.4.sum_ref), channel_id=1, source_target_pairs={{0,4},{4,0},{8,12},{12,8},{1,5},{5,1},{9,13},{13,9},{2,6},{6,2},{1... | collective-permute-start | bytes 3342344 | tf_op jit(solution)/shard_map/ppermute | solution.py:23
  110.0 1.4 finished_half.4
  111.4 1.4 %finished_half.5 = (f32[2048,1024]{1,0:T(8,128)}, f32[1,2048]{1,0:T(1,128)}) custom-call(s32[1]{0:T(128)} %bitcast.3.rep_ref, bf16[544,1024]{1,0:T(8,128)(2,1)S(1)} %joined.4.sum_ref, f32[2048,1024]{1,0:T(8,128)} %get-tuple-element.59.refs_0_, f32[1,2048]{1,0:T(1,128)} %get-tuple-element.60.refs_1_), custom_call_target="tpu_custom_call", output_to_operand_aliasing={{0}: (2, {}), {1}: (3, {})} | custom-call | flops 557056 | bytes 3342336 | tf_op jit(solution)/shard_map/finished_half/pallas_call | solution.py:368
  112.8 9.8 %collective-permute-done.15.refs_1_ = bf16[128,2048]{1,0:T(8,128)(2,1)S(1)} collective-permute-done((bf16[128,2048]{1,0:T(8,128)(2,1)S(1)}, bf16[128,2048]{1,0:T(8,128)(2,1)S(1)}, u32[]{:S(2)}, u32[]{:S(2)}) %collective-permute-start.15) | collective-permute-done | bytes 524320 | tf_op jit(solution)/shard_map/ppermute | solution.py:18
  122.6 1.5 %row_gradient.2 = (bf16[64,8192]{1,0:T(8,128)(2,1)S(1)}, bf16[64,8192]{1,0:T(8,128)(2,1)S(1)}) custom-call(s32[1]{0:T(128)} %bitcast.1.me_ref, bf16[1,2,64,8192]{3,2,1,0:T(8,128)(2,1)S(1)} %copy-done.1, bf16[2,64,8192]{2,1,0:T(8,128)(2,1)S(1)} %copy-done.2, bf16[128,2048]{1,0:T(8,128)(2,1)S(1)} %get-tuple-element.71.refs_0_, ...), custom_call_target="tpu_custom_call" | custom-call | flops 6291456 | bytes 5242880 | tf_op jit(solution)/shard_map/row_gradient/pallas_call | solution.py:302
  124.1 1.3 collective-permute-start.21
  125.4 4.9 %collective-permute-done.17.refs_2_ = bf16[64,2048]{1,0:T(8,128)(2,1)S(1)} collective-permute-done((bf16[64,2048]{1,0:T(8,128)(2,1)S(1)}, bf16[64,2048]{1,0:T(8,128)(2,1)S(1)}, u32[]{:S(2)}, u32[]{:S(2)}) %collective-permute-start.17) | collective-permute-done | bytes 262176 | tf_op jit(solution)/shard_map/ppermute | solution.py:18
  130.4 1.5 %row_gradient.3 = (bf16[64,8192]{1,0:T(8,128)(2,1)S(1)}, bf16[64,8192]{1,0:T(8,128)(2,1)S(1)}) custom-call(s32[1]{0:T(128)} %bitcast.1.me_ref, bf16[1,2,64,8192]{3,2,1,0:T(8,128)(2,1)S(1)} %copy-done.1, bf16[2,64,8192]{2,1,0:T(8,128)(2,1)S(1)} %copy-done.2, bf16[128,2048]{1,0:T(8,128)(2,1)S(1)} %get-tuple-element.71.refs_0_, ...), custom_call_target="tpu_custom_call" | custom-call | flops 6291456 | bytes 5242880 | tf_op jit(solution)/shard_map/row_gradient/pallas_call | solution.py:302
  131.9 1.3 collective-permute-start.20
  133.2 1.1 collective-permute-done.19.sum_ref
  134.2 1.4 %finished_half.6 = (f32[2048,1024]{1,0:T(8,128)}, f32[1,2048]{1,0:T(1,128)}) custom-call(s32[1]{0:T(128)} %bitcast.3.rep_ref, bf16[544,1024]{1,0:T(8,128)(2,1)S(1)} %collective-permute-done.19.sum_ref, f32[2048,1024]{1,0:T(8,128)} %get-tuple-element.61.refs_0_, f32[1,2048]{1,0:T(1,128)} %get-tuple-element.62.refs_1_), custom_call_target="tpu_custom_call", output_to_operand_aliasing={{0}: (2, {}), {1}: (3, {})} | custom-call | flops 557056 | bytes 3342336 | tf_op jit(solution)/shard_map/finished_half/pallas_call | solution.py:368
  135.6 1.4 %finished_half.7 = (f32[2048,1024]{1,0:T(8,128)}, f32[1,2048]{1,0:T(1,128)}) custom-call(s32[1]{0:T(128)} %bitcast.3.rep_ref, bf16[544,1024]{1,0:T(8,128)(2,1)S(1)} %collective-permute-done.18.sum_ref, f32[2048,1024]{1,0:T(8,128)} %get-tuple-element.76.refs_0_, f32[1,2048]{1,0:T(1,128)} %get-tuple-element.77.refs_1_), custom_call_target="tpu_custom_call", output_to_operand_aliasing={{0}: (2, {}), {1}: (3, {})} | custom-call | flops 557056 | bytes 3342336 | tf_op jit(solution)/shard_map/finished_half/pallas_call | solution.py:368
  137.1 1.1 input_gradient.2.refs_0_
  138.2 1.1 input_gradient.3
  (23 shorter events, 0.1 us)
Async XLA Ops:
  0.6 1.6 %copy-start = (bf16[1,2,64,8192]{3,2,1,0:T(8,128)(2,1)S(1)}, bf16[1,2,64,8192]{3,2,1,0:T(8,128)(2,1)}, u32[]{:S(2)}) copy-start(bf16[1,2,64,8192]{3,2,1,0:T(8,128)(2,1)} %x_ref.3) | copy-start | bytes 6291460
  2.2 1.1 copy-start.4
  3.3 12.3 %collective-permute-start = (bf16[128,1024]{1,0:T(8,128)(2,1)S(1)}, bf16[128,1024]{1,0:T(8,128)(2,1)S(1)}, u32[]{:S(2)}, u32[]{:S(2)}) collective-permute-start(bf16[128,1024]{1,0:T(8,128)(2,1)S(1)} %bitcast.10), channel_id=1, source_target_pairs={{0,1},{1,2},{2,3},{3,0},{4,5},{5,6},{6,7},{7,4},{8,9},{9,10},{10,1... | collective-permute-start | bytes 786440 | tf_op jit(solution)/shard_map/ppermute | solution.py:18
  6.4 23.9 %collective-permute-start.3 = (bf16[128,2048]{1,0:T(8,128)(2,1)S(1)}, bf16[128,2048]{1,0:T(8,128)(2,1)S(1)}, u32[]{:S(2)}, u32[]{:S(2)}) collective-permute-start(bf16[128,2048]{1,0:T(8,128)(2,1)S(1)} %get-tuple-element.48), channel_id=1, source_target_pairs={{0,4},{4,0},{8,12},{12,8},{1,5},{5,1},{9,13},{13,9},{2,6},{6,2},{1... | collective-permute-start | bytes 1572872 | tf_op jit(solution)/shard_map/ppermute | solution.py:23
  7.9 24.3 %collective-permute-start.4 = (bf16[128,2048]{1,0:T(8,128)(2,1)S(1)}, bf16[128,2048]{1,0:T(8,128)(2,1)S(1)}, u32[]{:S(2)}, u32[]{:S(2)}) collective-permute-start(bf16[128,2048]{1,0:T(8,128)(2,1)S(1)} %get-tuple-element.49), channel_id=1, source_target_pairs={{0,8},{4,12},{8,0},{12,4},{1,9},{5,13},{9,1},{13,5},{2,10},{6,14},... | collective-permute-start | bytes 1572872 | tf_op jit(solution)/shard_map/ppermute | solution.py:23
  9.4 30.9 %copy-start.5 = (bf16[1,2048]{1,0:T(2,128)(2,1)S(1)}, bf16[1,2048]{1,0:T(2,128)(2,1)}, u32[]{:S(2)}) copy-start(bf16[1,2048]{1,0:T(2,128)(2,1)} %refs_9_.1) | copy-start | bytes 12292
  9.4 30.9 %copy-start.3 = (bf16[1,2048,1024]{2,1,0:T(8,128)(2,1)S(1)}, bf16[1,2048,1024]{2,1,0:T(8,128)(2,1)}, u32[]{:S(2)}) copy-start(bf16[1,2048,1024]{2,1,0:T(8,128)(2,1)} %param.7) | copy-start | bytes 12582916
  9.4 22.8 %collective-permute-start.5 = (bf16[128,2048]{1,0:T(8,128)(2,1)S(1)}, bf16[128,2048]{1,0:T(8,128)(2,1)S(1)}, u32[]{:S(2)}, u32[]{:S(2)}) collective-permute-start(bf16[128,2048]{1,0:T(8,128)(2,1)S(1)} %get-tuple-element.50), channel_id=1, source_target_pairs={{0,12},{4,8},{8,4},{12,0},{1,13},{5,9},{9,5},{13,1},{2,14},{6,10},... | collective-permute-start | bytes 1572872 | tf_op jit(solution)/shard_map/ppermute | solution.py:23
  9.9 16.2 %collective-permute-start.1 = (bf16[128,1024]{1,0:T(8,128)(2,1)S(1)}, bf16[128,1024]{1,0:T(8,128)(2,1)S(1)}, u32[]{:S(2)}, u32[]{:S(2)}) collective-permute-start(bf16[128,1024]{1,0:T(8,128)(2,1)S(1)} %bitcast.11), channel_id=1, source_target_pairs={{0,2},{1,3},{2,0},{3,1},{4,6},{5,7},{6,4},{7,5},{8,10},{9,11},{10,... | collective-permute-start | bytes 786440 | tf_op jit(solution)/shard_map/ppermute | solution.py:18
  15.6 14.6 %collective-permute-start.2 = (bf16[128,1024]{1,0:T(8,128)(2,1)S(1)}, bf16[128,1024]{1,0:T(8,128)(2,1)S(1)}, u32[]{:S(2)}, u32[]{:S(2)}) collective-permute-start(bf16[128,1024]{1,0:T(8,128)(2,1)S(1)} %bitcast.12), channel_id=1, source_target_pairs={{0,3},{1,0},{2,1},{3,2},{4,7},{5,4},{6,5},{7,6},{8,11},{9,8},{10,9... | collective-permute-start | bytes 786440 | tf_op jit(solution)/shard_map/ppermute | solution.py:18
  32.7 16.7 %collective-permute-start.6 = (bf16[512,512]{1,0:T(8,128)(2,1)S(1)}, bf16[512,512]{1,0:T(8,128)(2,1)S(1)}, u32[]{:S(2)}, u32[]{:S(2)}) collective-permute-start(bf16[512,512]{1,0:T(8,128)(2,1)S(1)} %get-tuple-element.52), channel_id=1, source_target_pairs={{0,1},{1,2},{2,3},{3,0},{4,5},{5,6},{6,7},{7,4},{8,9},{9,10},{10,1... | collective-permute-start | bytes 1572872 | tf_op jit(solution)/shard_map/ppermute | solution.py:18
  34.3 23.2 %collective-permute-start.7 = (bf16[512,512]{1,0:T(8,128)(2,1)S(1)}, bf16[512,512]{1,0:T(8,128)(2,1)S(1)}, u32[]{:S(2)}, u32[]{:S(2)}) collective-permute-start(bf16[512,512]{1,0:T(8,128)(2,1)S(1)} %get-tuple-element.54), channel_id=1, source_target_pairs={{0,3},{1,0},{2,1},{3,2},{4,7},{5,4},{6,5},{7,6},{8,11},{9,8},{10,9... | collective-permute-start | bytes 1572872 | tf_op jit(solution)/shard_map/ppermute | solution.py:18
  36.7 46.2 %collective-permute-start.10 = (bf16[512,1024]{1,0:T(8,128)(2,1)S(1)}, bf16[512,1024]{1,0:T(8,128)(2,1)S(1)}, u32[]{:S(2)}, u32[]{:S(2)}) collective-permute-start(bf16[512,1024]{1,0:T(8,128)(2,1)S(1)} %joined.3.refs_4_), channel_id=1, source_target_pairs={{0,8},{4,12},{8,0},{12,4},{1,9},{5,13},{9,1},{13,5},{2,10},{6,14},... | collective-permute-start | bytes 3145736 | tf_op jit(solution)/shard_map/ppermute | solution.py:23
  38.3 44.6 %collective-permute-start.11 = (bf16[512,1024]{1,0:T(8,128)(2,1)S(1)}, bf16[512,1024]{1,0:T(8,128)(2,1)S(1)}, u32[]{:S(2)}, u32[]{:S(2)}) collective-permute-start(bf16[512,1024]{1,0:T(8,128)(2,1)S(1)} %joined.3.refs_4_), channel_id=1, source_target_pairs={{0,12},{4,8},{8,4},{12,0},{1,13},{5,9},{9,5},{13,1},{2,14},{6,10},... | collective-permute-start | bytes 3145736 | tf_op jit(solution)/shard_map/ppermute | solution.py:23
  39.5 43.9 %collective-permute-start.9 = (bf16[512,1024]{1,0:T(8,128)(2,1)S(1)}, bf16[512,1024]{1,0:T(8,128)(2,1)S(1)}, u32[]{:S(2)}, u32[]{:S(2)}) collective-permute-start(bf16[512,1024]{1,0:T(8,128)(2,1)S(1)} %joined.3.refs_4_), channel_id=1, source_target_pairs={{0,4},{4,0},{8,12},{12,8},{1,5},{5,1},{9,13},{13,9},{2,6},{6,2},{1... | collective-permute-start | bytes 3145736 | tf_op jit(solution)/shard_map/ppermute | solution.py:23
  57.5 25.4 %collective-permute-start.8 = (bf16[512,512]{1,0:T(8,128)(2,1)S(1)}, bf16[512,512]{1,0:T(8,128)(2,1)S(1)}, u32[]{:S(2)}, u32[]{:S(2)}) collective-permute-start(bf16[512,512]{1,0:T(8,128)(2,1)S(1)} %get-tuple-element.55), channel_id=1, source_target_pairs={{0,2},{1,3},{2,0},{3,1},{4,6},{5,7},{6,4},{7,5},{8,10},{9,11},{10,... | collective-permute-start | bytes 1572872 | tf_op jit(solution)/shard_map/ppermute | solution.py:18
  82.9 24.6 %collective-permute-start.14 = (bf16[64,2048]{1,0:T(8,128)(2,1)S(1)}, bf16[64,2048]{1,0:T(8,128)(2,1)S(1)}, u32[]{:S(2)}, u32[]{:S(2)}) collective-permute-start(bf16[64,2048]{1,0:T(8,128)(2,1)S(1)} %get-tuple-element.66), channel_id=1, source_target_pairs={{0,2},{1,3},{2,0},{3,1},{4,6},{5,7},{6,4},{7,5},{8,10},{9,11},{10,... | collective-permute-start | bytes 786440 | tf_op jit(solution)/shard_map/ppermute | solution.py:18
  86.1 21.4 %collective-permute-start.13 = (bf16[272,1024]{1,0:T(8,128)(2,1)S(1)}, bf16[272,1024]{1,0:T(8,128)(2,1)S(1)}, u32[]{:S(2)}, u32[]{:S(2)}) collective-permute-start(bf16[272,1024]{1,0:T(8,128)(2,1)S(1)} %get-tuple-element.58.refs_0_), channel_id=1, source_target_pairs={{0,4},{4,0},{8,12},{12,8},{1,5},{5,1},{9,13},{13,9},{2,6},{6,2},{1... | collective-permute-start | bytes 1671176 | tf_op jit(solution)/shard_map/ppermute | solution.py:23
  87.6 20.6 %collective-permute-start.12 = (bf16[272,1024]{1,0:T(8,128)(2,1)S(1)}, bf16[272,1024]{1,0:T(8,128)(2,1)S(1)}, u32[]{:S(2)}, u32[]{:S(2)}) collective-permute-start(bf16[272,1024]{1,0:T(8,128)(2,1)S(1)} %get-tuple-element.57.refs_0_), channel_id=1, source_target_pairs={{0,8},{4,12},{8,0},{12,4},{1,9},{5,13},{9,1},{13,5},{2,10},{6,14},... | collective-permute-start | bytes 1671176 | tf_op jit(solution)/shard_map/ppermute | solution.py:23
  88.2 24.6 %collective-permute-start.16 = (bf16[128,2048]{1,0:T(8,128)(2,1)S(1)}, bf16[128,2048]{1,0:T(8,128)(2,1)S(1)}, u32[]{:S(2)}, u32[]{:S(2)}) collective-permute-start(bf16[128,2048]{1,0:T(8,128)(2,1)S(1)} %get-tuple-element.69), channel_id=1, source_target_pairs={{0,1},{1,2},{2,3},{3,0},{4,5},{5,6},{6,7},{7,4},{8,9},{9,10},{10,1... | collective-permute-start | bytes 1572872 | tf_op jit(solution)/shard_map/ppermute | solution.py:18
  107.5 15.1 %collective-permute-start.15 = (bf16[128,2048]{1,0:T(8,128)(2,1)S(1)}, bf16[128,2048]{1,0:T(8,128)(2,1)S(1)}, u32[]{:S(2)}, u32[]{:S(2)}) collective-permute-start(bf16[128,2048]{1,0:T(8,128)(2,1)S(1)} %get-tuple-element.67), channel_id=1, source_target_pairs={{0,3},{1,0},{2,1},{3,2},{4,7},{5,4},{6,5},{7,6},{8,11},{9,8},{10,9... | collective-permute-start | bytes 1572872 | tf_op jit(solution)/shard_map/ppermute | solution.py:18
  107.5 22.9 %collective-permute-start.17 = (bf16[64,2048]{1,0:T(8,128)(2,1)S(1)}, bf16[64,2048]{1,0:T(8,128)(2,1)S(1)}, u32[]{:S(2)}, u32[]{:S(2)}) collective-permute-start(bf16[64,2048]{1,0:T(8,128)(2,1)S(1)} %get-tuple-element.73), channel_id=1, source_target_pairs={{0,2},{1,3},{2,0},{3,1},{4,6},{5,7},{6,4},{7,5},{8,10},{9,11},{10,... | collective-permute-start | bytes 786440 | tf_op jit(solution)/shard_map/ppermute | solution.py:18
  107.7 26.6 %collective-permute-start.19 = (bf16[544,1024]{1,0:T(8,128)(2,1)S(1)}, bf16[544,1024]{1,0:T(8,128)(2,1)S(1)}, u32[]{:S(2)}, u32[]{:S(2)}) collective-permute-start(bf16[544,1024]{1,0:T(8,128)(2,1)S(1)} %joined.5.sum_ref), channel_id=1, source_target_pairs={{0,8},{4,12},{8,0},{12,4},{1,9},{5,13},{9,1},{13,5},{2,10},{6,14},... | collective-permute-start | bytes 3342344 | tf_op jit(solution)/shard_map/ppermute | solution.py:23
  108.4 27.2 %collective-permute-start.18 = (bf16[544,1024]{1,0:T(8,128)(2,1)S(1)}, bf16[544,1024]{1,0:T(8,128)(2,1)S(1)}, u32[]{:S(2)}, u32[]{:S(2)}) collective-permute-start(bf16[544,1024]{1,0:T(8,128)(2,1)S(1)} %joined.4.sum_ref), channel_id=1, source_target_pairs={{0,4},{4,0},{8,12},{12,8},{1,5},{5,1},{9,13},{13,9},{2,6},{6,2},{1... | collective-permute-start | bytes 3342344 | tf_op jit(solution)/shard_map/ppermute | solution.py:23
  111.4 11.2 %copy-start.1 = (bf16[1,2,64,8192]{3,2,1,0:T(8,128)(2,1)S(1)}, bf16[1,2,64,8192]{3,2,1,0:T(8,128)(2,1)}, u32[]{:S(2)}) copy-start(bf16[1,2,64,8192]{3,2,1,0:T(8,128)(2,1)} %x_ref.3) | copy-start | bytes 6291460
  111.4 11.2 %copy-start.2 = (bf16[2,64,8192]{2,1,0:T(8,128)(2,1)S(1)}, bf16[2,64,8192]{2,1,0:T(8,128)(2,1)}, u32[]{:S(2)}) copy-start(bf16[2,64,8192]{2,1,0:T(8,128)(2,1)} %top_ref.3) | copy-start | bytes 6291460
  124.1 12.9 %collective-permute-start.21 = (bf16[64,8192]{1,0:T(8,128)(2,1)S(1)}, bf16[64,8192]{1,0:T(8,128)(2,1)S(1)}, u32[]{:S(2)}, u32[]{:S(2)}) collective-permute-start(bf16[64,8192]{1,0:T(8,128)(2,1)S(1)} %get-tuple-element.70.upper_ref), channel_id=1, source_target_pairs={{16,0},{17,1},{18,2},{19,3},{20,4},{21,5},{22,6},{23,7},{24,8},{25... | collective-permute-start | bytes 3145736 | tf_op jit(solution)/shard_map/ppermute | solution.py:451
  131.9 6.3 %collective-permute-start.20 = (bf16[64,8192]{1,0:T(8,128)(2,1)S(1)}, bf16[64,8192]{1,0:T(8,128)(2,1)S(1)}, u32[]{:S(2)}, u32[]{:S(2)}) collective-permute-start(bf16[64,8192]{1,0:T(8,128)(2,1)S(1)} %get-tuple-element.74.upper_ref), channel_id=1, source_target_pairs={{16,0},{17,1},{18,2},{19,3},{20,4},{21,5},{22,6},{23,7},{24,8},{25... | collective-permute-start | bytes 3145736 | tf_op jit(solution)/shard_map/ppermute | solution.py:451

commit v12 on v10

--- a/solution.py
+++ b/solution.py
@@ -405,9 +405,9 @@
     for e in range(1, reps):
         plane[e] = flipped(hats[e], "rep", e)
     grads = after(value_grad[0].reshape(tokens, -1), hats[0])
-    slots = [grads] + [cyclic(grads, "fsdp", j) for j in range(1, groups)]
-
-    plane[0] = after(plane[0], *slots[1:])
+    slots = [grads] + [cyclic(after(grads, plane[1]) if j == groups - 1 else grads, "fsdp", j) for j in range(1, groups)]
+
+    plane[0] = after(plane[0], *slots[1:-1])
     sent = regrouped(plane, groups)
     far = groups // 2
     near = [j for j in range(1, groups) if j != far]

time: 135 us -> 134 us (level)
  waiting for transfers between devices: 72.4 us -> 70.1 us
  starting transfers between devices: 40.2 us -> 41.9 us
    ppermute x10, waiting for transfers between devices: 62 us -> 57.8 us  [cyclic(): lax.ppermute(value, axis, [(i, (i + steps) % count) for i in range(count)])]
    ppermute x10, starting transfers between devices: 13.8 us -> 16 us  [flipped(): return lax.ppermute(value, axis, [(i, i ^ mask) for i in range(count)])]
    ppermute x10, waiting for transfers between devices: 10.4 us -> 12.3 us  [flipped(): return lax.ppermute(value, axis, [(i, i ^ mask) for i in range(count)])]
where the time goes in v12:
time: 134 us; the launch traced here: 133 us
  waiting for transfers between devices  70.1 us (52%)
  starting transfers between devices  41.9 us (31%)
  Pallas kernels  18.8 us (14%)
  local copies, waits for them, and re-layouts  1.6 us (1%)
    ppermute x10, waiting for transfers between devices, cyclic(): lax.ppermute(value, axis, [(i, (i + steps) % count) for i in range(count)])  57.8 us
    ppermute x10, starting transfers between devices, cyclic(): lax.ppermute(value, axis, [(i, (i + steps) % count) for i in range(count)])  23.3 us
    ppermute x10, starting transfers between devices, flipped(): return lax.ppermute(value, axis, [(i, i ^ mask) for i in range(count)])  16 us
    ppermute x10, waiting for transfers between devices, flipped(): return lax.ppermute(value, axis, [(i, i ^ mask) for i in range(count)])  12.3 us
    pallas_call x4, Pallas kernels, finished_half(): pl.pallas_call(kernel, grid_spec=pltpu.PrefetchScalarGridSpec(num_scalar_...  5.7 us
    pallas_call x1, Pallas kernels, returned_blocks(): pl.pallas_call(kernel, grid=(shard // tile,), out_shape=[jax.ShapeDtypeSt...  3.17 us
    pallas_call x2, Pallas kernels, row_gradient(): pl.pallas_call(kernel, grid=(rows // step,), out_shape=[jax.ShapeDtypeStr...  2.99 us
    pallas_call x1, Pallas kernels, weight_product(): pl.pallas_call(kernel, out_shape=[jax.ShapeDtypeStruct((chunk + 16, featu...  2.73 us
  transfers between devices with their start and end apart: 22, of which 11 were waited for; matrix products, arithmetic and copies ran while one was open for 0% of the time, Pallas kernels for 12%

profile of v12, /device:TPU:0, one launch (start us, length us, event | category | flops | bytes accessed | tf_op | source)
XLA Modules:
  0.0 133.1 jit_solution(5956645049570424155)
XLA Ops:
  0.6 0.0 copy-start
  0.6 1.6 %copy-done = bf16[1,2,64,8192]{3,2,1,0:T(8,128)(2,1)S(1)} copy-done((bf16[1,2,64,8192]{3,2,1,0:T(8,128)(2,1)S(1)}, bf16[1,2,64,8192]{3,2,1,0:T(8,128)(2,1)}, u32[]{:S(2)}) %copy-start) | copy-done | bytes 2097176
  2.2 1.1 scaled_blocks.1
  3.3 3.0 %collective-permute-start.2 = (bf16[128,2048]{1,0:T(8,128)(2,1)S(1)}, bf16[128,2048]{1,0:T(8,128)(2,1)S(1)}, u32[]{:S(2)}, u32[]{:S(2)}) collective-permute-start(bf16[128,2048]{1,0:T(8,128)(2,1)S(1)} %get-tuple-element.47), channel_id=1, source_target_pairs={{0,4},{4,0},{8,12},{12,8},{1,5},{5,1},{9,13},{13,9},{2,6},{6,2},{1... | collective-permute-start | bytes 1572872 | tf_op jit(solution)/shard_map/ppermute | solution.py:23
  6.3 1.5 %collective-permute-start.4 = (bf16[128,2048]{1,0:T(8,128)(2,1)S(1)}, bf16[128,2048]{1,0:T(8,128)(2,1)S(1)}, u32[]{:S(2)}, u32[]{:S(2)}) collective-permute-start(bf16[128,2048]{1,0:T(8,128)(2,1)S(1)} %get-tuple-element.51), channel_id=1, source_target_pairs={{0,8},{4,12},{8,0},{12,4},{1,9},{5,13},{9,1},{13,5},{2,10},{6,14},... | collective-permute-start | bytes 1572872 | tf_op jit(solution)/shard_map/ppermute | solution.py:23
  7.8 0.0 collective-permute-start.5
  7.9 2.0 %collective-permute-start = (bf16[128,1024]{1,0:T(8,128)(2,1)S(1)}, bf16[128,1024]{1,0:T(8,128)(2,1)S(1)}, u32[]{:S(2)}, u32[]{:S(2)}) collective-permute-start(bf16[128,1024]{1,0:T(8,128)(2,1)S(1)} %bitcast.10), channel_id=1, source_target_pairs={{0,1},{1,2},{2,3},{3,0},{4,5},{5,6},{6,7},{7,4},{8,9},{9,10},{10,1... | collective-permute-start | bytes 786440 | tf_op jit(solution)/shard_map/ppermute | solution.py:18
  9.9 2.6 %collective-permute-start.1 = (bf16[128,1024]{1,0:T(8,128)(2,1)S(1)}, bf16[128,1024]{1,0:T(8,128)(2,1)S(1)}, u32[]{:S(2)}, u32[]{:S(2)}) collective-permute-start(bf16[128,1024]{1,0:T(8,128)(2,1)S(1)} %bitcast.11), channel_id=1, source_target_pairs={{0,2},{1,3},{2,0},{3,1},{4,6},{5,7},{6,4},{7,5},{8,10},{9,11},{10,... | collective-permute-start | bytes 786440 | tf_op jit(solution)/shard_map/ppermute | solution.py:18
  12.5 6.6 %collective-permute-done.2.refs_1_ = bf16[128,2048]{1,0:T(8,128)(2,1)S(1)} collective-permute-done((bf16[128,2048]{1,0:T(8,128)(2,1)S(1)}, bf16[128,2048]{1,0:T(8,128)(2,1)S(1)}, u32[]{:S(2)}, u32[]{:S(2)}) %collective-permute-start.2) | collective-permute-done | bytes 524320 | tf_op jit(solution)/shard_map/ppermute | solution.py:23
  19.1 4.2 %collective-permute-start.3 = (bf16[128,1024]{1,0:T(8,128)(2,1)S(1)}, bf16[128,1024]{1,0:T(8,128)(2,1)S(1)}, u32[]{:S(2)}, u32[]{:S(2)}) collective-permute-start(bf16[128,1024]{1,0:T(8,128)(2,1)S(1)} %bitcast.12), channel_id=1, source_target_pairs={{0,3},{1,0},{2,1},{3,2},{4,7},{5,4},{6,5},{7,6},{8,11},{9,8},{10,9... | collective-permute-start | bytes 786440 | tf_op jit(solution)/shard_map/ppermute | solution.py:18
  23.2 5.5 %collective-permute-done.1.refs_2_ = bf16[128,1024]{1,0:T(8,128)(2,1)S(1)} collective-permute-done((bf16[128,1024]{1,0:T(8,128)(2,1)S(1)}, bf16[128,1024]{1,0:T(8,128)(2,1)S(1)}, u32[]{:S(2)}, u32[]{:S(2)}) %collective-permute-start.1) | collective-permute-done | bytes 262176 | tf_op jit(solution)/shard_map/ppermute | solution.py:18
  28.7 2.2 %collective-permute-done.4.refs_2_ = bf16[128,2048]{1,0:T(8,128)(2,1)S(1)} collective-permute-done((bf16[128,2048]{1,0:T(8,128)(2,1)S(1)}, bf16[128,2048]{1,0:T(8,128)(2,1)S(1)}, u32[]{:S(2)}, u32[]{:S(2)}) %collective-permute-start.4) | collective-permute-done | bytes 524320 | tf_op jit(solution)/shard_map/ppermute | solution.py:23
  30.9 0.5 regrouped.1
  31.4 2.2 %collective-permute-start.6 = (bf16[512,512]{1,0:T(8,128)(2,1)S(1)}, bf16[512,512]{1,0:T(8,128)(2,1)S(1)}, u32[]{:S(2)}, u32[]{:S(2)}) collective-permute-start(bf16[512,512]{1,0:T(8,128)(2,1)S(1)} %get-tuple-element.54), channel_id=1, source_target_pairs={{0,1},{1,2},{2,3},{3,0},{4,5},{5,6},{6,7},{7,4},{8,9},{9,10},{10,1... | collective-permute-start | bytes 1572872 | tf_op jit(solution)/shard_map/ppermute | solution.py:18
  33.6 0.0 collective-permute-done.3.refs_3_
  33.6 0.1 joined.3.refs_4_
  33.7 2.1 %collective-permute-start.10 = (bf16[512,1024]{1,0:T(8,128)(2,1)S(1)}, bf16[512,1024]{1,0:T(8,128)(2,1)S(1)}, u32[]{:S(2)}, u32[]{:S(2)}) collective-permute-start(bf16[512,1024]{1,0:T(8,128)(2,1)S(1)} %joined.3.refs_4_), channel_id=1, source_target_pairs={{0,8},{4,12},{8,0},{12,4},{1,9},{5,13},{9,1},{13,5},{2,10},{6,14},... | collective-permute-start | bytes 3145736 | tf_op jit(solution)/shard_map/ppermute | solution.py:23
  35.8 1.0 collective-permute-start.11
  36.8 0.5 collective-permute-start.9
  37.3 3.4 %collective-permute-start.7 = (bf16[512,512]{1,0:T(8,128)(2,1)S(1)}, bf16[512,512]{1,0:T(8,128)(2,1)S(1)}, u32[]{:S(2)}, u32[]{:S(2)}) collective-permute-start(bf16[512,512]{1,0:T(8,128)(2,1)S(1)} %get-tuple-element.55), channel_id=1, source_target_pairs={{0,2},{1,3},{2,0},{3,1},{4,6},{5,7},{6,4},{7,5},{8,10},{9,11},{10,... | collective-permute-start | bytes 1572872 | tf_op jit(solution)/shard_map/ppermute | solution.py:18
  40.7 3.2 %returned_blocks.1 = (bf16[128,2048]{1,0:T(8,128)(2,1)S(1)}, bf16[128,2048]{1,0:T(8,128)(2,1)S(1)}, bf16[64,2048]{1,0:T(8,128)(2,1)S(1)}, bf16[64,2048]{1,0:T(8,128)(2,1)S(1)}, bf16[128,2048]{1,0:T(8,128)(2,1)S(1)}) custom-call(bf16[128,1024]{1,0:T(8,128)(2,1)S(1)} %bitcast.14, bf16[128,1024]{1,0:T(8,128)(2,1)S(1)} %collective-permute-done.refs_1_, ...), custom_call_target="tpu_custom_call" | custom-call | flops 2147483648 | bytes 7340032 | tf_op jit(solution)/shard_map/returned_blocks/pallas_call | solution.py:252
  43.9 5.4 %collective-permute-done.6.refs_1_ = bf16[512,512]{1,0:T(8,128)(2,1)S(1)} collective-permute-done((bf16[512,512]{1,0:T(8,128)(2,1)S(1)}, bf16[512,512]{1,0:T(8,128)(2,1)S(1)}, u32[]{:S(2)}, u32[]{:S(2)}) %collective-permute-start.6) | collective-permute-done | bytes 524320 | tf_op jit(solution)/shard_map/ppermute | solution.py:18
  49.3 19.8 %collective-permute-done.7.refs_2_ = bf16[512,512]{1,0:T(8,128)(2,1)S(1)} collective-permute-done((bf16[512,512]{1,0:T(8,128)(2,1)S(1)}, bf16[512,512]{1,0:T(8,128)(2,1)S(1)}, u32[]{:S(2)}, u32[]{:S(2)}) %collective-permute-start.7) | collective-permute-done | bytes 524320 | tf_op jit(solution)/shard_map/ppermute | solution.py:18
  69.1 2.3 %collective-permute-start.14 = (bf16[64,2048]{1,0:T(8,128)(2,1)S(1)}, bf16[64,2048]{1,0:T(8,128)(2,1)S(1)}, u32[]{:S(2)}, u32[]{:S(2)}) collective-permute-start(bf16[64,2048]{1,0:T(8,128)(2,1)S(1)} %get-tuple-element.68), channel_id=1, source_target_pairs={{0,2},{1,3},{2,0},{3,1},{4,6},{5,7},{6,4},{7,5},{8,10},{9,11},{10,... | collective-permute-start | bytes 786440 | tf_op jit(solution)/shard_map/ppermute | solution.py:18
  71.4 5.6 %collective-permute-done.8.refs_3_ = bf16[512,512]{1,0:T(8,128)(2,1)S(1)} collective-permute-done((bf16[512,512]{1,0:T(8,128)(2,1)S(1)}, bf16[512,512]{1,0:T(8,128)(2,1)S(1)}, u32[]{:S(2)}, u32[]{:S(2)}) %collective-permute-start.8) | collective-permute-done | bytes 524320 | tf_op jit(solution)/shard_map/ppermute | solution.py:18
  76.9 2.3 %collective-permute-done.10.refs_6_ = bf16[512,1024]{1,0:T(8,128)(2,1)S(1)} collective-permute-done((bf16[512,1024]{1,0:T(8,128)(2,1)S(1)}, bf16[512,1024]{1,0:T(8,128)(2,1)S(1)}, u32[]{:S(2)}, u32[]{:S(2)}) %collective-permute-start.10) | collective-permute-done | bytes 1048608 | tf_op jit(solution)/shard_map/ppermute | solution.py:23
  79.2 1.2 collective-permute-done.9.refs_5_
  80.5 2.7 %weight_product.1 = (bf16[272,1024]{1,0:T(8,128)(2,1)S(1)}, bf16[272,1024]{1,0:T(8,128)(2,1)S(1)}) custom-call(s32[1]{0:T(128)} %bitcast.3.rep_ref, bf16[512,512]{1,0:T(8,128)(2,1)S(1)} %get-tuple-element.53.refs_0_, bf16[512,512]{1,0:T(8,128)(2,1)S(1)} %collective-permute-done.6.refs_1_, bf16[512,512]{1,0:T(8,128)(2,1)S(1)} %collective-permute-done.7.refs_2_, ...), custom_call_target="tpu_custom_call" | custom-call | flops 2147483648 | bytes 8388608 | tf_op jit(solution)/shard_map/weight_product/pallas_call | solution.py:215
  83.2 1.5 %collective-permute-start.13 = (bf16[272,1024]{1,0:T(8,128)(2,1)S(1)}, bf16[272,1024]{1,0:T(8,128)(2,1)S(1)}, u32[]{:S(2)}, u32[]{:S(2)}) collective-permute-start(bf16[272,1024]{1,0:T(8,128)(2,1)S(1)} %get-tuple-element.60.refs_0_), channel_id=1, source_target_pairs={{0,4},{4,0},{8,12},{12,8},{1,5},{5,1},{9,13},{13,9},{2,6},{6,2},{1... | collective-permute-start | bytes 1671176 | tf_op jit(solution)/shard_map/ppermute | solution.py:23
  84.7 1.4 %collective-permute-start.12 = (bf16[272,1024]{1,0:T(8,128)(2,1)S(1)}, bf16[272,1024]{1,0:T(8,128)(2,1)S(1)}, u32[]{:S(2)}, u32[]{:S(2)}) collective-permute-start(bf16[272,1024]{1,0:T(8,128)(2,1)S(1)} %get-tuple-element.59.refs_0_), channel_id=1, source_target_pairs={{0,8},{4,12},{8,0},{12,4},{1,9},{5,13},{9,1},{13,5},{2,10},{6,14},... | collective-permute-start | bytes 1671176 | tf_op jit(solution)/shard_map/ppermute | solution.py:23
  86.1 6.7 %collective-permute-start.16 = (bf16[128,2048]{1,0:T(8,128)(2,1)S(1)}, bf16[128,2048]{1,0:T(8,128)(2,1)S(1)}, u32[]{:S(2)}, u32[]{:S(2)}) collective-permute-start(bf16[128,2048]{1,0:T(8,128)(2,1)S(1)} %get-tuple-element.71), channel_id=1, source_target_pairs={{0,1},{1,2},{2,3},{3,0},{4,5},{5,6},{6,7},{7,4},{8,9},{9,10},{10,1... | collective-permute-start | bytes 1572872 | tf_op jit(solution)/shard_map/ppermute | solution.py:18
  92.8 7.9 %collective-permute-done.14.refs_2_ = bf16[64,2048]{1,0:T(8,128)(2,1)S(1)} collective-permute-done((bf16[64,2048]{1,0:T(8,128)(2,1)S(1)}, bf16[64,2048]{1,0:T(8,128)(2,1)S(1)}, u32[]{:S(2)}, u32[]{:S(2)}) %collective-permute-start.14) | collective-permute-done | bytes 262176 | tf_op jit(solution)/shard_map/ppermute | solution.py:18
  100.8 0.2 joined.5.sum_ref
  100.9 3.2 %collective-permute-start.19 = (bf16[544,1024]{1,0:T(8,128)(2,1)S(1)}, bf16[544,1024]{1,0:T(8,128)(2,1)S(1)}, u32[]{:S(2)}, u32[]{:S(2)}) collective-permute-start(bf16[544,1024]{1,0:T(8,128)(2,1)S(1)} %joined.5.sum_ref), channel_id=1, source_target_pairs={{0,8},{4,12},{8,0},{12,4},{1,9},{5,13},{9,1},{13,5},{2,10},{6,14},... | collective-permute-start | bytes 3342344 | tf_op jit(solution)/shard_map/ppermute | solution.py:23
  104.2 0.2 joined.4.sum_ref
  104.3 1.7 %collective-permute-start.18 = (bf16[544,1024]{1,0:T(8,128)(2,1)S(1)}, bf16[544,1024]{1,0:T(8,128)(2,1)S(1)}, u32[]{:S(2)}, u32[]{:S(2)}) collective-permute-start(bf16[544,1024]{1,0:T(8,128)(2,1)S(1)} %joined.4.sum_ref), channel_id=1, source_target_pairs={{0,4},{4,0},{8,12},{12,8},{1,5},{5,1},{9,13},{13,9},{2,6},{6,2},{1... | collective-permute-start | bytes 3342344 | tf_op jit(solution)/shard_map/ppermute | solution.py:23
  106.0 1.4 %finished_half.4 = (f32[2048,1024]{1,0:T(8,128)}, f32[1,2048]{1,0:T(1,128)}) custom-call(s32[1]{0:T(128)} %bitcast.3.rep_ref, bf16[544,1024]{1,0:T(8,128)(2,1)S(1)} %joined.5.sum_ref), custom_call_target="tpu_custom_call" | custom-call | flops 557056 | bytes 3342336 | tf_op jit(solution)/shard_map/finished_half/pallas_call | solution.py:368
  107.4 1.4 %finished_half.5 = (f32[2048,1024]{1,0:T(8,128)}, f32[1,2048]{1,0:T(1,128)}) custom-call(s32[1]{0:T(128)} %bitcast.3.rep_ref, bf16[544,1024]{1,0:T(8,128)(2,1)S(1)} %joined.4.sum_ref, f32[2048,1024]{1,0:T(8,128)} %get-tuple-element.61.refs_0_, f32[1,2048]{1,0:T(1,128)} %get-tuple-element.62.refs_1_), custom_call_target="tpu_custom_call", output_to_operand_aliasing={{0}: (2, {}), {1}: (3, {})} | custom-call | flops 557056 | bytes 3342336 | tf_op jit(solution)/shard_map/finished_half/pallas_call | solution.py:368
  108.8 6.5 %collective-permute-done.15.refs_1_ = bf16[128,2048]{1,0:T(8,128)(2,1)S(1)} collective-permute-done((bf16[128,2048]{1,0:T(8,128)(2,1)S(1)}, bf16[128,2048]{1,0:T(8,128)(2,1)S(1)}, u32[]{:S(2)}, u32[]{:S(2)}) %collective-permute-start.15) | collective-permute-done | bytes 524320 | tf_op jit(solution)/shard_map/ppermute | solution.py:18
  115.3 1.5 %row_gradient.2 = (bf16[64,8192]{1,0:T(8,128)(2,1)S(1)}, bf16[64,8192]{1,0:T(8,128)(2,1)S(1)}) custom-call(s32[1]{0:T(128)} %bitcast.1.me_ref, bf16[1,2,64,8192]{3,2,1,0:T(8,128)(2,1)S(1)} %copy-done.1, bf16[2,64,8192]{2,1,0:T(8,128)(2,1)S(1)} %copy-done.2, bf16[128,2048]{1,0:T(8,128)(2,1)S(1)} %get-tuple-element.73.refs_0_, ...), custom_call_target="tpu_custom_call" | custom-call | flops 6291456 | bytes 5242880 | tf_op jit(solution)/shard_map/row_gradient/pallas_call | solution.py:302
  116.8 1.3 collective-permute-start.21
  118.1 7.1 %collective-permute-done.17.refs_2_ = bf16[64,2048]{1,0:T(8,128)(2,1)S(1)} collective-permute-done((bf16[64,2048]{1,0:T(8,128)(2,1)S(1)}, bf16[64,2048]{1,0:T(8,128)(2,1)S(1)}, u32[]{:S(2)}, u32[]{:S(2)}) %collective-permute-start.17) | collective-permute-done | bytes 262176 | tf_op jit(solution)/shard_map/ppermute | solution.py:18
  125.2 1.5 %row_gradient.3 = (bf16[64,8192]{1,0:T(8,128)(2,1)S(1)}, bf16[64,8192]{1,0:T(8,128)(2,1)S(1)}) custom-call(s32[1]{0:T(128)} %bitcast.1.me_ref, bf16[1,2,64,8192]{3,2,1,0:T(8,128)(2,1)S(1)} %copy-done.1, bf16[2,64,8192]{2,1,0:T(8,128)(2,1)S(1)} %copy-done.2, bf16[128,2048]{1,0:T(8,128)(2,1)S(1)} %get-tuple-element.73.refs_0_, ...), custom_call_target="tpu_custom_call" | custom-call | flops 6291456 | bytes 5242880 | tf_op jit(solution)/shard_map/row_gradient/pallas_call | solution.py:302
  126.7 1.3 collective-permute-start.20
  128.0 1.4 %finished_half.6 = (f32[2048,1024]{1,0:T(8,128)}, f32[1,2048]{1,0:T(1,128)}) custom-call(s32[1]{0:T(128)} %bitcast.3.rep_ref, bf16[544,1024]{1,0:T(8,128)(2,1)S(1)} %collective-permute-done.19.sum_ref, f32[2048,1024]{1,0:T(8,128)} %get-tuple-element.63.refs_0_, f32[1,2048]{1,0:T(1,128)} %get-tuple-element.64.refs_1_), custom_call_target="tpu_custom_call", output_to_operand_aliasing={{0}: (2, {}), {1}: (3, {})} | custom-call | flops 557056 | bytes 3342336 | tf_op jit(solution)/shard_map/finished_half/pallas_call | solution.py:368
  129.5 1.4 %finished_half.7 = (f32[2048,1024]{1,0:T(8,128)}, f32[1,2048]{1,0:T(1,128)}) custom-call(s32[1]{0:T(128)} %bitcast.3.rep_ref, bf16[544,1024]{1,0:T(8,128)(2,1)S(1)} %collective-permute-done.18.sum_ref, f32[2048,1024]{1,0:T(8,128)} %get-tuple-element.78.refs_0_, f32[1,2048]{1,0:T(1,128)} %get-tuple-element.79.refs_1_), custom_call_target="tpu_custom_call", output_to_operand_aliasing={{0}: (2, {}), {1}: (3, {})} | custom-call | flops 557056 | bytes 3342336 | tf_op jit(solution)/shard_map/finished_half/pallas_call | solution.py:368
  130.9 1.1 input_gradient.2.refs_0_
  132.0 1.1 input_gradient.3
  (23 shorter events, 0.1 us)
Async XLA Ops:
  0.6 1.6 %copy-start = (bf16[1,2,64,8192]{3,2,1,0:T(8,128)(2,1)S(1)}, bf16[1,2,64,8192]{3,2,1,0:T(8,128)(2,1)}, u32[]{:S(2)}) copy-start(bf16[1,2,64,8192]{3,2,1,0:T(8,128)(2,1)} %x_ref.3) | copy-start | bytes 6291460
  2.2 5.6 %copy-start.4 = (bf16[1,2,64,1024]{3,2,1,0:T(8,128)(2,1)S(1)}, bf16[1,2,64,1024]{3,2,1,0:T(8,128)(2,1)}, u32[]{:S(2)}) copy-start(bf16[1,2,64,1024]{3,2,1,0:T(8,128)(2,1)} %param.6) | copy-start | bytes 786436
  3.3 15.8 %collective-permute-start.2 = (bf16[128,2048]{1,0:T(8,128)(2,1)S(1)}, bf16[128,2048]{1,0:T(8,128)(2,1)S(1)}, u32[]{:S(2)}, u32[]{:S(2)}) collective-permute-start(bf16[128,2048]{1,0:T(8,128)(2,1)S(1)} %get-tuple-element.47), channel_id=1, source_target_pairs={{0,4},{4,0},{8,12},{12,8},{1,5},{5,1},{9,13},{13,9},{2,6},{6,2},{1... | collective-permute-start | bytes 1572872 | tf_op jit(solution)/shard_map/ppermute | solution.py:23
  6.3 24.6 %collective-permute-start.4 = (bf16[128,2048]{1,0:T(8,128)(2,1)S(1)}, bf16[128,2048]{1,0:T(8,128)(2,1)S(1)}, u32[]{:S(2)}, u32[]{:S(2)}) collective-permute-start(bf16[128,2048]{1,0:T(8,128)(2,1)S(1)} %get-tuple-element.51), channel_id=1, source_target_pairs={{0,8},{4,12},{8,0},{12,4},{1,9},{5,13},{9,1},{13,5},{2,10},{6,14},... | collective-permute-start | bytes 1572872 | tf_op jit(solution)/shard_map/ppermute | solution.py:23
  7.8 23.1 %collective-permute-start.5 = (bf16[128,2048]{1,0:T(8,128)(2,1)S(1)}, bf16[128,2048]{1,0:T(8,128)(2,1)S(1)}, u32[]{:S(2)}, u32[]{:S(2)}) collective-permute-start(bf16[128,2048]{1,0:T(8,128)(2,1)S(1)} %get-tuple-element.52), channel_id=1, source_target_pairs={{0,12},{4,8},{8,4},{12,0},{1,13},{5,9},{9,5},{13,1},{2,14},{6,10},... | collective-permute-start | bytes 1572872 | tf_op jit(solution)/shard_map/ppermute | solution.py:23
  7.8 32.9 %copy-start.5 = (bf16[1,2048]{1,0:T(2,128)(2,1)S(1)}, bf16[1,2048]{1,0:T(2,128)(2,1)}, u32[]{:S(2)}) copy-start(bf16[1,2048]{1,0:T(2,128)(2,1)} %refs_9_.1) | copy-start | bytes 12292
  7.8 32.9 %copy-start.3 = (bf16[1,2048,1024]{2,1,0:T(8,128)(2,1)S(1)}, bf16[1,2048,1024]{2,1,0:T(8,128)(2,1)}, u32[]{:S(2)}) copy-start(bf16[1,2048,1024]{2,1,0:T(8,128)(2,1)} %param.7) | copy-start | bytes 12582916
  7.9 15.4 %collective-permute-start = (bf16[128,1024]{1,0:T(8,128)(2,1)S(1)}, bf16[128,1024]{1,0:T(8,128)(2,1)S(1)}, u32[]{:S(2)}, u32[]{:S(2)}) collective-permute-start(bf16[128,1024]{1,0:T(8,128)(2,1)S(1)} %bitcast.10), channel_id=1, source_target_pairs={{0,1},{1,2},{2,3},{3,0},{4,5},{5,6},{6,7},{7,4},{8,9},{9,10},{10,1... | collective-permute-start | bytes 786440 | tf_op jit(solution)/shard_map/ppermute | solution.py:18
  9.9 18.9 %collective-permute-start.1 = (bf16[128,1024]{1,0:T(8,128)(2,1)S(1)}, bf16[128,1024]{1,0:T(8,128)(2,1)S(1)}, u32[]{:S(2)}, u32[]{:S(2)}) collective-permute-start(bf16[128,1024]{1,0:T(8,128)(2,1)S(1)} %bitcast.11), channel_id=1, source_target_pairs={{0,2},{1,3},{2,0},{3,1},{4,6},{5,7},{6,4},{7,5},{8,10},{9,11},{10,... | collective-permute-start | bytes 786440 | tf_op jit(solution)/shard_map/ppermute | solution.py:18
  19.1 14.5 %collective-permute-start.3 = (bf16[128,1024]{1,0:T(8,128)(2,1)S(1)}, bf16[128,1024]{1,0:T(8,128)(2,1)S(1)}, u32[]{:S(2)}, u32[]{:S(2)}) collective-permute-start(bf16[128,1024]{1,0:T(8,128)(2,1)S(1)} %bitcast.12), channel_id=1, source_target_pairs={{0,3},{1,0},{2,1},{3,2},{4,7},{5,4},{6,5},{7,6},{8,11},{9,8},{10,9... | collective-permute-start | bytes 786440 | tf_op jit(solution)/shard_map/ppermute | solution.py:18
  31.4 17.9 %collective-permute-start.6 = (bf16[512,512]{1,0:T(8,128)(2,1)S(1)}, bf16[512,512]{1,0:T(8,128)(2,1)S(1)}, u32[]{:S(2)}, u32[]{:S(2)}) collective-permute-start(bf16[512,512]{1,0:T(8,128)(2,1)S(1)} %get-tuple-element.54), channel_id=1, source_target_pairs={{0,1},{1,2},{2,3},{3,0},{4,5},{5,6},{6,7},{7,4},{8,9},{9,10},{10,1... | collective-permute-start | bytes 1572872 | tf_op jit(solution)/shard_map/ppermute | solution.py:18
  33.7 45.5 %collective-permute-start.10 = (bf16[512,1024]{1,0:T(8,128)(2,1)S(1)}, bf16[512,1024]{1,0:T(8,128)(2,1)S(1)}, u32[]{:S(2)}, u32[]{:S(2)}) collective-permute-start(bf16[512,1024]{1,0:T(8,128)(2,1)S(1)} %joined.3.refs_4_), channel_id=1, source_target_pairs={{0,8},{4,12},{8,0},{12,4},{1,9},{5,13},{9,1},{13,5},{2,10},{6,14},... | collective-permute-start | bytes 3145736 | tf_op jit(solution)/shard_map/ppermute | solution.py:23
  35.8 43.4 %collective-permute-start.11 = (bf16[512,1024]{1,0:T(8,128)(2,1)S(1)}, bf16[512,1024]{1,0:T(8,128)(2,1)S(1)}, u32[]{:S(2)}, u32[]{:S(2)}) collective-permute-start(bf16[512,1024]{1,0:T(8,128)(2,1)S(1)} %joined.3.refs_4_), channel_id=1, source_target_pairs={{0,12},{4,8},{8,4},{12,0},{1,13},{5,9},{9,5},{13,1},{2,14},{6,10},... | collective-permute-start | bytes 3145736 | tf_op jit(solution)/shard_map/ppermute | solution.py:23
  36.8 43.7 %collective-permute-start.9 = (bf16[512,1024]{1,0:T(8,128)(2,1)S(1)}, bf16[512,1024]{1,0:T(8,128)(2,1)S(1)}, u32[]{:S(2)}, u32[]{:S(2)}) collective-permute-start(bf16[512,1024]{1,0:T(8,128)(2,1)S(1)} %joined.3.refs_4_), channel_id=1, source_target_pairs={{0,4},{4,0},{8,12},{12,8},{1,5},{5,1},{9,13},{13,9},{2,6},{6,2},{1... | collective-permute-start | bytes 3145736 | tf_op jit(solution)/shard_map/ppermute | solution.py:23
  37.3 31.8 %collective-permute-start.7 = (bf16[512,512]{1,0:T(8,128)(2,1)S(1)}, bf16[512,512]{1,0:T(8,128)(2,1)S(1)}, u32[]{:S(2)}, u32[]{:S(2)}) collective-permute-start(bf16[512,512]{1,0:T(8,128)(2,1)S(1)} %get-tuple-element.55), channel_id=1, source_target_pairs={{0,2},{1,3},{2,0},{3,1},{4,6},{5,7},{6,4},{7,5},{8,10},{9,11},{10,... | collective-permute-start | bytes 1572872 | tf_op jit(solution)/shard_map/ppermute | solution.py:18
  49.3 27.6 %collective-permute-start.8 = (bf16[512,512]{1,0:T(8,128)(2,1)S(1)}, bf16[512,512]{1,0:T(8,128)(2,1)S(1)}, u32[]{:S(2)}, u32[]{:S(2)}) collective-permute-start(bf16[512,512]{1,0:T(8,128)(2,1)S(1)} %get-tuple-element.57), channel_id=1, source_target_pairs={{0,3},{1,0},{2,1},{3,2},{4,7},{5,4},{6,5},{7,6},{8,11},{9,8},{10,9... | collective-permute-start | bytes 1572872 | tf_op jit(solution)/shard_map/ppermute | solution.py:18
  69.1 31.6 %collective-permute-start.14 = (bf16[64,2048]{1,0:T(8,128)(2,1)S(1)}, bf16[64,2048]{1,0:T(8,128)(2,1)S(1)}, u32[]{:S(2)}, u32[]{:S(2)}) collective-permute-start(bf16[64,2048]{1,0:T(8,128)(2,1)S(1)} %get-tuple-element.68), channel_id=1, source_target_pairs={{0,2},{1,3},{2,0},{3,1},{4,6},{5,7},{6,4},{7,5},{8,10},{9,11},{10,... | collective-permute-start | bytes 786440 | tf_op jit(solution)/shard_map/ppermute | solution.py:18
  83.2 17.6 %collective-permute-start.13 = (bf16[272,1024]{1,0:T(8,128)(2,1)S(1)}, bf16[272,1024]{1,0:T(8,128)(2,1)S(1)}, u32[]{:S(2)}, u32[]{:S(2)}) collective-permute-start(bf16[272,1024]{1,0:T(8,128)(2,1)S(1)} %get-tuple-element.60.refs_0_), channel_id=1, source_target_pairs={{0,4},{4,0},{8,12},{12,8},{1,5},{5,1},{9,13},{13,9},{2,6},{6,2},{1... | collective-permute-start | bytes 1671176 | tf_op jit(solution)/shard_map/ppermute | solution.py:23
  84.7 19.5 %collective-permute-start.12 = (bf16[272,1024]{1,0:T(8,128)(2,1)S(1)}, bf16[272,1024]{1,0:T(8,128)(2,1)S(1)}, u32[]{:S(2)}, u32[]{:S(2)}) collective-permute-start(bf16[272,1024]{1,0:T(8,128)(2,1)S(1)} %get-tuple-element.59.refs_0_), channel_id=1, source_target_pairs={{0,8},{4,12},{8,0},{12,4},{1,9},{5,13},{9,1},{13,5},{2,10},{6,14},... | collective-permute-start | bytes 1671176 | tf_op jit(solution)/shard_map/ppermute | solution.py:23
  86.1 22.7 %collective-permute-start.16 = (bf16[128,2048]{1,0:T(8,128)(2,1)S(1)}, bf16[128,2048]{1,0:T(8,128)(2,1)S(1)}, u32[]{:S(2)}, u32[]{:S(2)}) collective-permute-start(bf16[128,2048]{1,0:T(8,128)(2,1)S(1)} %get-tuple-element.71), channel_id=1, source_target_pairs={{0,1},{1,2},{2,3},{3,0},{4,5},{5,6},{6,7},{7,4},{8,9},{9,10},{10,1... | collective-permute-start | bytes 1572872 | tf_op jit(solution)/shard_map/ppermute | solution.py:18
  100.7 14.6 %collective-permute-start.15 = (bf16[128,2048]{1,0:T(8,128)(2,1)S(1)}, bf16[128,2048]{1,0:T(8,128)(2,1)S(1)}, u32[]{:S(2)}, u32[]{:S(2)}) collective-permute-start(bf16[128,2048]{1,0:T(8,128)(2,1)S(1)} %get-tuple-element.69), channel_id=1, source_target_pairs={{0,3},{1,0},{2,1},{3,2},{4,7},{5,4},{6,5},{7,6},{8,11},{9,8},{10,9... | collective-permute-start | bytes 1572872 | tf_op jit(solution)/shard_map/ppermute | solution.py:18
  100.7 24.5 %collective-permute-start.17 = (bf16[64,2048]{1,0:T(8,128)(2,1)S(1)}, bf16[64,2048]{1,0:T(8,128)(2,1)S(1)}, u32[]{:S(2)}, u32[]{:S(2)}) collective-permute-start(bf16[64,2048]{1,0:T(8,128)(2,1)S(1)} %get-tuple-element.75), channel_id=1, source_target_pairs={{0,2},{1,3},{2,0},{3,1},{4,6},{5,7},{6,4},{7,5},{8,10},{9,11},{10,... | collective-permute-start | bytes 786440 | tf_op jit(solution)/shard_map/ppermute | solution.py:18
  100.9 27.1 %collective-permute-start.19 = (bf16[544,1024]{1,0:T(8,128)(2,1)S(1)}, bf16[544,1024]{1,0:T(8,128)(2,1)S(1)}, u32[]{:S(2)}, u32[]{:S(2)}) collective-permute-start(bf16[544,1024]{1,0:T(8,128)(2,1)S(1)} %joined.5.sum_ref), channel_id=1, source_target_pairs={{0,8},{4,12},{8,0},{12,4},{1,9},{5,13},{9,1},{13,5},{2,10},{6,14},... | collective-permute-start | bytes 3342344 | tf_op jit(solution)/shard_map/ppermute | solution.py:23
  104.3 25.2 %collective-permute-start.18 = (bf16[544,1024]{1,0:T(8,128)(2,1)S(1)}, bf16[544,1024]{1,0:T(8,128)(2,1)S(1)}, u32[]{:S(2)}, u32[]{:S(2)}) collective-permute-start(bf16[544,1024]{1,0:T(8,128)(2,1)S(1)} %joined.4.sum_ref), channel_id=1, source_target_pairs={{0,4},{4,0},{8,12},{12,8},{1,5},{5,1},{9,13},{13,9},{2,6},{6,2},{1... | collective-permute-start | bytes 3342344 | tf_op jit(solution)/shard_map/ppermute | solution.py:23
  107.4 7.9 %copy-start.1 = (bf16[1,2,64,8192]{3,2,1,0:T(8,128)(2,1)S(1)}, bf16[1,2,64,8192]{3,2,1,0:T(8,128)(2,1)}, u32[]{:S(2)}) copy-start(bf16[1,2,64,8192]{3,2,1,0:T(8,128)(2,1)} %x_ref.3) | copy-start | bytes 6291460
  107.4 7.9 %copy-start.2 = (bf16[2,64,8192]{2,1,0:T(8,128)(2,1)S(1)}, bf16[2,64,8192]{2,1,0:T(8,128)(2,1)}, u32[]{:S(2)}) copy-start(bf16[2,64,8192]{2,1,0:T(8,128)(2,1)} %top_ref.3) | copy-start | bytes 6291460
  116.8 14.1 %collective-permute-start.21 = (bf16[64,8192]{1,0:T(8,128)(2,1)S(1)}, bf16[64,8192]{1,0:T(8,128)(2,1)S(1)}, u32[]{:S(2)}, u32[]{:S(2)}) collective-permute-start(bf16[64,8192]{1,0:T(8,128)(2,1)S(1)} %get-tuple-element.72.upper_ref), channel_id=1, source_target_pairs={{16,0},{17,1},{18,2},{19,3},{20,4},{21,5},{22,6},{23,7},{24,8},{25... | collective-permute-start | bytes 3145736 | tf_op jit(solution)/shard_map/ppermute | solution.py:452
  126.7 5.3 %collective-permute-start.20 = (bf16[64,8192]{1,0:T(8,128)(2,1)S(1)}, bf16[64,8192]{1,0:T(8,128)(2,1)S(1)}, u32[]{:S(2)}, u32[]{:S(2)}) collective-permute-start(bf16[64,8192]{1,0:T(8,128)(2,1)S(1)} %get-tuple-element.76.upper_ref), channel_id=1, source_target_pairs={{16,0},{17,1},{18,2},{19,3},{20,4},{21,5},{22,6},{23,7},{24,8},{25... | collective-permute-start | bytes 3145736 | tf_op jit(solution)/shard_map/ppermute | solution.py:452

commit v13 on v12

--- a/solution.py
+++ b/solution.py
@@ -73,7 +73,7 @@
         out_shape=[jax.ShapeDtypeStruct((tokens, groups * chunk), bf16)] * (chunks * reps),
         in_specs=[SMEM_ARG, SMEM_ARG, pl.BlockSpec((block, width), lambda i: (i, 0))],
         out_specs=[pl.BlockSpec((block, groups * chunk), lambda i: (i, 0))] * (chunks * reps),
-        compiler_params=params(8),
+        compiler_params=params(56),
         cost_estimate=cost(6 * x.size, 4 * x.size),
         name="scaled_blocks",
     )(me, rep, x)

time: 134 us -> 137 us (1.022)
  Pallas kernels: 18.8 us -> 21.9 us
    pallas_call x1, Pallas kernels: 1.06 us -> 4.17 us  [scaled_blocks(): pl.pallas_call(kernel, grid=(tokens // block,), out_shape=[jax.ShapeDtype...]
where the time goes in v13:
time: 137 us; the launch traced here: 136 us
  waiting for transfers between devices  69.4 us (51%)
  starting transfers between devices  42.4 us (31%)
  Pallas kernels  21.9 us (16%)
    ppermute x10, waiting for transfers between devices, cyclic(): lax.ppermute(value, axis, [(i, (i + steps) % count) for i in range(count)])  57.1 us
    ppermute x10, starting transfers between devices, cyclic(): lax.ppermute(value, axis, [(i, (i + steps) % count) for i in range(count)])  22.9 us
    ppermute x10, starting transfers between devices, flipped(): return lax.ppermute(value, axis, [(i, i ^ mask) for i in range(count)])  16.9 us
    ppermute x10, waiting for transfers between devices, flipped(): return lax.ppermute(value, axis, [(i, i ^ mask) for i in range(count)])  12.3 us
    pallas_call x4, Pallas kernels, finished_half(): pl.pallas_call(kernel, grid_spec=pltpu.PrefetchScalarGridSpec(num_scalar_...  5.7 us
    pallas_call x1, Pallas kernels, scaled_blocks(): pl.pallas_call(kernel, grid=(tokens // block,), out_shape=[jax.ShapeDtype...  4.17 us
    pallas_call x1, Pallas kernels, returned_blocks(): pl.pallas_call(kernel, grid=(shard // tile,), out_shape=[jax.ShapeDtypeSt...  3.21 us
    pallas_call x2, Pallas kernels, row_gradient(): pl.pallas_call(kernel, grid=(rows // step,), out_shape=[jax.ShapeDtypeStr...  2.99 us
  transfers between devices with their start and end apart: 22, of which 11 were waited for; matrix products, arithmetic and copies ran while one was open for 0% of the time, Pallas kernels for 12%

profile of v13, /device:TPU:0, one launch (start us, length us, event | category | flops | bytes accessed | tf_op | source)
XLA Modules:
  0.0 135.6 jit_solution(11863251685151901989)
XLA Ops:
  0.6 4.2 %scaled_blocks.1 = (bf16[128,2048]{1,0:T(8,128)(2,1)}, bf16[128,2048]{1,0:T(8,128)(2,1)}, bf16[128,2048]{1,0:T(8,128)(2,1)}, bf16[128,2048]{1,0:T(8,128)(2,1)}) custom-call(s32[1]{0:T(128)} %bitcast.1.me_ref, s32[1]{0:T(128)} %bitcast.3.rep_ref, bf16[128,8192]{1,0:T(8,128)(2,1)} %bitcast.7), custom_call_target="tpu_custom_call" | custom-call | flops 6291456 | bytes 4194304 | tf_op jit(solution)/shard_map/scaled_blocks/pallas_call | solution.py:70
  4.8 3.0 %collective-permute-start.2 = (bf16[128,2048]{1,0:T(8,128)(2,1)}, bf16[128,2048]{1,0:T(8,128)(2,1)S(1)}, u32[]{:S(2)}, u32[]{:S(2)}) collective-permute-start(bf16[128,2048]{1,0:T(8,128)(2,1)} %get-tuple-element.47), channel_id=1, source_target_pairs={{0,4},{4,0},{8,12},{12,8},{1,5},{5,1},{9,13},{13,9},{2,6},{6,2},{1... | collective-permute-start | bytes 1572872 | tf_op jit(solution)/shard_map/ppermute | solution.py:23
  7.8 1.5 %collective-permute-start.4 = (bf16[128,2048]{1,0:T(8,128)(2,1)}, bf16[128,2048]{1,0:T(8,128)(2,1)S(1)}, u32[]{:S(2)}, u32[]{:S(2)}) collective-permute-start(bf16[128,2048]{1,0:T(8,128)(2,1)} %get-tuple-element.51), channel_id=1, source_target_pairs={{0,8},{4,12},{8,0},{12,4},{1,9},{5,13},{9,1},{13,5},{2,10},{6,14},... | collective-permute-start | bytes 1572872 | tf_op jit(solution)/shard_map/ppermute | solution.py:23
  9.3 0.0 collective-permute-start.5
  9.3 2.0 %collective-permute-start = (bf16[128,1024]{1,0:T(8,128)(2,1)S(1)}, bf16[128,1024]{1,0:T(8,128)(2,1)S(1)}, u32[]{:S(2)}, u32[]{:S(2)}) collective-permute-start(bf16[128,1024]{1,0:T(8,128)(2,1)S(1)} %bitcast.10), channel_id=1, source_target_pairs={{0,1},{1,2},{2,3},{3,0},{4,5},{5,6},{6,7},{7,4},{8,9},{9,10},{10,1... | collective-permute-start | bytes 786440 | tf_op jit(solution)/shard_map/ppermute | solution.py:18
  11.4 2.6 %collective-permute-start.1 = (bf16[128,1024]{1,0:T(8,128)(2,1)S(1)}, bf16[128,1024]{1,0:T(8,128)(2,1)S(1)}, u32[]{:S(2)}, u32[]{:S(2)}) collective-permute-start(bf16[128,1024]{1,0:T(8,128)(2,1)S(1)} %bitcast.11), channel_id=1, source_target_pairs={{0,2},{1,3},{2,0},{3,1},{4,6},{5,7},{6,4},{7,5},{8,10},{9,11},{10,... | collective-permute-start | bytes 786440 | tf_op jit(solution)/shard_map/ppermute | solution.py:18
  13.9 6.8 %collective-permute-done.2.refs_1_ = bf16[128,2048]{1,0:T(8,128)(2,1)S(1)} collective-permute-done((bf16[128,2048]{1,0:T(8,128)(2,1)}, bf16[128,2048]{1,0:T(8,128)(2,1)S(1)}, u32[]{:S(2)}, u32[]{:S(2)}) %collective-permute-start.2) | collective-permute-done | bytes 524320 | tf_op jit(solution)/shard_map/ppermute | solution.py:23
  20.7 4.2 %collective-permute-start.3 = (bf16[128,1024]{1,0:T(8,128)(2,1)S(1)}, bf16[128,1024]{1,0:T(8,128)(2,1)S(1)}, u32[]{:S(2)}, u32[]{:S(2)}) collective-permute-start(bf16[128,1024]{1,0:T(8,128)(2,1)S(1)} %bitcast.12), channel_id=1, source_target_pairs={{0,3},{1,0},{2,1},{3,2},{4,7},{5,4},{6,5},{7,6},{8,11},{9,8},{10,9... | collective-permute-start | bytes 786440 | tf_op jit(solution)/shard_map/ppermute | solution.py:18
  24.9 5.3 %collective-permute-done.1.refs_2_ = bf16[128,1024]{1,0:T(8,128)(2,1)S(1)} collective-permute-done((bf16[128,1024]{1,0:T(8,128)(2,1)S(1)}, bf16[128,1024]{1,0:T(8,128)(2,1)S(1)}, u32[]{:S(2)}, u32[]{:S(2)}) %collective-permute-start.1) | collective-permute-done | bytes 262176 | tf_op jit(solution)/shard_map/ppermute | solution.py:18
  30.2 2.4 %collective-permute-done.4.refs_2_ = bf16[128,2048]{1,0:T(8,128)(2,1)S(1)} collective-permute-done((bf16[128,2048]{1,0:T(8,128)(2,1)}, bf16[128,2048]{1,0:T(8,128)(2,1)S(1)}, u32[]{:S(2)}, u32[]{:S(2)}) %collective-permute-start.4) | collective-permute-done | bytes 524320 | tf_op jit(solution)/shard_map/ppermute | solution.py:23
  32.6 1.0 copy-done.3
  33.7 0.5 regrouped.1
  34.1 2.0 %collective-permute-start.6 = (bf16[512,512]{1,0:T(8,128)(2,1)S(1)}, bf16[512,512]{1,0:T(8,128)(2,1)S(1)}, u32[]{:S(2)}, u32[]{:S(2)}) collective-permute-start(bf16[512,512]{1,0:T(8,128)(2,1)S(1)} %get-tuple-element.54), channel_id=1, source_target_pairs={{0,1},{1,2},{2,3},{3,0},{4,5},{5,6},{6,7},{7,4},{8,9},{9,10},{10,1... | collective-permute-start | bytes 1572872 | tf_op jit(solution)/shard_map/ppermute | solution.py:18
  36.1 0.0 collective-permute-done.3.refs_3_
  36.1 0.1 joined.3.refs_4_
  36.2 1.6 %collective-permute-start.10 = (bf16[512,1024]{1,0:T(8,128)(2,1)S(1)}, bf16[512,1024]{1,0:T(8,128)(2,1)S(1)}, u32[]{:S(2)}, u32[]{:S(2)}) collective-permute-start(bf16[512,1024]{1,0:T(8,128)(2,1)S(1)} %joined.3.refs_4_), channel_id=1, source_target_pairs={{0,8},{4,12},{8,0},{12,4},{1,9},{5,13},{9,1},{13,5},{2,10},{6,14},... | collective-permute-start | bytes 3145736 | tf_op jit(solution)/shard_map/ppermute | solution.py:23
  37.8 1.4 %collective-permute-start.11 = (bf16[512,1024]{1,0:T(8,128)(2,1)S(1)}, bf16[512,1024]{1,0:T(8,128)(2,1)S(1)}, u32[]{:S(2)}, u32[]{:S(2)}) collective-permute-start(bf16[512,1024]{1,0:T(8,128)(2,1)S(1)} %joined.3.refs_4_), channel_id=1, source_target_pairs={{0,12},{4,8},{8,4},{12,0},{1,13},{5,9},{9,5},{13,1},{2,14},{6,10},... | collective-permute-start | bytes 3145736 | tf_op jit(solution)/shard_map/ppermute | solution.py:23
  39.2 0.5 collective-permute-start.9
  39.8 3.4 %collective-permute-start.7 = (bf16[512,512]{1,0:T(8,128)(2,1)S(1)}, bf16[512,512]{1,0:T(8,128)(2,1)S(1)}, u32[]{:S(2)}, u32[]{:S(2)}) collective-permute-start(bf16[512,512]{1,0:T(8,128)(2,1)S(1)} %get-tuple-element.55), channel_id=1, source_target_pairs={{0,2},{1,3},{2,0},{3,1},{4,6},{5,7},{6,4},{7,5},{8,10},{9,11},{10,... | collective-permute-start | bytes 1572872 | tf_op jit(solution)/shard_map/ppermute | solution.py:18
  43.2 3.2 %returned_blocks.1 = (bf16[128,2048]{1,0:T(8,128)(2,1)S(1)}, bf16[128,2048]{1,0:T(8,128)(2,1)S(1)}, bf16[64,2048]{1,0:T(8,128)(2,1)S(1)}, bf16[64,2048]{1,0:T(8,128)(2,1)S(1)}, bf16[128,2048]{1,0:T(8,128)(2,1)S(1)}) custom-call(bf16[128,1024]{1,0:T(8,128)(2,1)S(1)} %bitcast.14, bf16[128,1024]{1,0:T(8,128)(2,1)S(1)} %collective-permute-done.refs_1_, ...), custom_call_target="tpu_custom_call" | custom-call | flops 2147483648 | bytes 7340032 | tf_op jit(solution)/shard_map/returned_blocks/pallas_call | solution.py:252
  46.4 5.5 %collective-permute-done.6.refs_1_ = bf16[512,512]{1,0:T(8,128)(2,1)S(1)} collective-permute-done((bf16[512,512]{1,0:T(8,128)(2,1)S(1)}, bf16[512,512]{1,0:T(8,128)(2,1)S(1)}, u32[]{:S(2)}, u32[]{:S(2)}) %collective-permute-start.6) | collective-permute-done | bytes 524320 | tf_op jit(solution)/shard_map/ppermute | solution.py:18
  51.8 0.0 collective-permute-start.8
  51.9 19.8 %collective-permute-done.7.refs_2_ = bf16[512,512]{1,0:T(8,128)(2,1)S(1)} collective-permute-done((bf16[512,512]{1,0:T(8,128)(2,1)S(1)}, bf16[512,512]{1,0:T(8,128)(2,1)S(1)}, u32[]{:S(2)}, u32[]{:S(2)}) %collective-permute-start.7) | collective-permute-done | bytes 524320 | tf_op jit(solution)/shard_map/ppermute | solution.py:18
  71.6 2.5 %collective-permute-start.14 = (bf16[64,2048]{1,0:T(8,128)(2,1)S(1)}, bf16[64,2048]{1,0:T(8,128)(2,1)S(1)}, u32[]{:S(2)}, u32[]{:S(2)}) collective-permute-start(bf16[64,2048]{1,0:T(8,128)(2,1)S(1)} %get-tuple-element.68), channel_id=1, source_target_pairs={{0,2},{1,3},{2,0},{3,1},{4,6},{5,7},{6,4},{7,5},{8,10},{9,11},{10,... | collective-permute-start | bytes 786440 | tf_op jit(solution)/shard_map/ppermute | solution.py:18
  74.1 6.0 %collective-permute-done.8.refs_3_ = bf16[512,512]{1,0:T(8,128)(2,1)S(1)} collective-permute-done((bf16[512,512]{1,0:T(8,128)(2,1)S(1)}, bf16[512,512]{1,0:T(8,128)(2,1)S(1)}, u32[]{:S(2)}, u32[]{:S(2)}) %collective-permute-start.8) | collective-permute-done | bytes 524320 | tf_op jit(solution)/shard_map/ppermute | solution.py:18
  80.1 1.9 %collective-permute-done.10.refs_6_ = bf16[512,1024]{1,0:T(8,128)(2,1)S(1)} collective-permute-done((bf16[512,1024]{1,0:T(8,128)(2,1)S(1)}, bf16[512,1024]{1,0:T(8,128)(2,1)S(1)}, u32[]{:S(2)}, u32[]{:S(2)}) %collective-permute-start.10) | collective-permute-done | bytes 1048608 | tf_op jit(solution)/shard_map/ppermute | solution.py:23
  82.0 1.2 collective-permute-done.9.refs_5_
  83.2 2.7 %weight_product.1 = (bf16[272,1024]{1,0:T(8,128)(2,1)S(1)}, bf16[272,1024]{1,0:T(8,128)(2,1)S(1)}) custom-call(s32[1]{0:T(128)} %bitcast.3.rep_ref, bf16[512,512]{1,0:T(8,128)(2,1)S(1)} %get-tuple-element.53.refs_0_, bf16[512,512]{1,0:T(8,128)(2,1)S(1)} %collective-permute-done.6.refs_1_, bf16[512,512]{1,0:T(8,128)(2,1)S(1)} %collective-permute-done.7.refs_2_, ...), custom_call_target="tpu_custom_call" | custom-call | flops 2147483648 | bytes 8388608 | tf_op jit(solution)/shard_map/weight_product/pallas_call | solution.py:215
  85.9 1.5 %collective-permute-start.13 = (bf16[272,1024]{1,0:T(8,128)(2,1)S(1)}, bf16[272,1024]{1,0:T(8,128)(2,1)S(1)}, u32[]{:S(2)}, u32[]{:S(2)}) collective-permute-start(bf16[272,1024]{1,0:T(8,128)(2,1)S(1)} %get-tuple-element.60.refs_0_), channel_id=1, source_target_pairs={{0,4},{4,0},{8,12},{12,8},{1,5},{5,1},{9,13},{13,9},{2,6},{6,2},{1... | collective-permute-start | bytes 1671176 | tf_op jit(solution)/shard_map/ppermute | solution.py:23
  87.4 1.2 collective-permute-start.12
  88.6 6.3 %collective-permute-start.16 = (bf16[128,2048]{1,0:T(8,128)(2,1)S(1)}, bf16[128,2048]{1,0:T(8,128)(2,1)S(1)}, u32[]{:S(2)}, u32[]{:S(2)}) collective-permute-start(bf16[128,2048]{1,0:T(8,128)(2,1)S(1)} %get-tuple-element.71), channel_id=1, source_target_pairs={{0,1},{1,2},{2,3},{3,0},{4,5},{5,6},{6,7},{7,4},{8,9},{9,10},{10,1... | collective-permute-start | bytes 1572872 | tf_op jit(solution)/shard_map/ppermute | solution.py:18
  95.0 8.3 %collective-permute-done.14.refs_2_ = bf16[64,2048]{1,0:T(8,128)(2,1)S(1)} collective-permute-done((bf16[64,2048]{1,0:T(8,128)(2,1)S(1)}, bf16[64,2048]{1,0:T(8,128)(2,1)S(1)}, u32[]{:S(2)}, u32[]{:S(2)}) %collective-permute-start.14) | collective-permute-done | bytes 262176 | tf_op jit(solution)/shard_map/ppermute | solution.py:18
  103.3 0.2 joined.5.sum_ref
  103.5 3.4 %collective-permute-start.19 = (bf16[544,1024]{1,0:T(8,128)(2,1)S(1)}, bf16[544,1024]{1,0:T(8,128)(2,1)S(1)}, u32[]{:S(2)}, u32[]{:S(2)}) collective-permute-start(bf16[544,1024]{1,0:T(8,128)(2,1)S(1)} %joined.5.sum_ref), channel_id=1, source_target_pairs={{0,8},{4,12},{8,0},{12,4},{1,9},{5,13},{9,1},{13,5},{2,10},{6,14},... | collective-permute-start | bytes 3342344 | tf_op jit(solution)/shard_map/ppermute | solution.py:23
  107.0 0.2 joined.4.sum_ref
  107.1 2.7 %collective-permute-start.18 = (bf16[544,1024]{1,0:T(8,128)(2,1)S(1)}, bf16[544,1024]{1,0:T(8,128)(2,1)S(1)}, u32[]{:S(2)}, u32[]{:S(2)}) collective-permute-start(bf16[544,1024]{1,0:T(8,128)(2,1)S(1)} %joined.4.sum_ref), channel_id=1, source_target_pairs={{0,4},{4,0},{8,12},{12,8},{1,5},{5,1},{9,13},{13,9},{2,6},{6,2},{1... | collective-permute-start | bytes 3342344 | tf_op jit(solution)/shard_map/ppermute | solution.py:23
  109.8 1.4 %finished_half.4 = (f32[2048,1024]{1,0:T(8,128)}, f32[1,2048]{1,0:T(1,128)}) custom-call(s32[1]{0:T(128)} %bitcast.3.rep_ref, bf16[544,1024]{1,0:T(8,128)(2,1)S(1)} %joined.5.sum_ref), custom_call_target="tpu_custom_call" | custom-call | flops 557056 | bytes 3342336 | tf_op jit(solution)/shard_map/finished_half/pallas_call | solution.py:368
  111.2 1.4 %finished_half.5 = (f32[2048,1024]{1,0:T(8,128)}, f32[1,2048]{1,0:T(1,128)}) custom-call(s32[1]{0:T(128)} %bitcast.3.rep_ref, bf16[544,1024]{1,0:T(8,128)(2,1)S(1)} %joined.4.sum_ref, f32[2048,1024]{1,0:T(8,128)} %get-tuple-element.61.refs_0_, f32[1,2048]{1,0:T(1,128)} %get-tuple-element.62.refs_1_), custom_call_target="tpu_custom_call", output_to_operand_aliasing={{0}: (2, {}), {1}: (3, {})} | custom-call | flops 557056 | bytes 3342336 | tf_op jit(solution)/shard_map/finished_half/pallas_call | solution.py:368
  112.7 4.7 %collective-permute-done.15.refs_1_ = bf16[128,2048]{1,0:T(8,128)(2,1)S(1)} collective-permute-done((bf16[128,2048]{1,0:T(8,128)(2,1)S(1)}, bf16[128,2048]{1,0:T(8,128)(2,1)S(1)}, u32[]{:S(2)}, u32[]{:S(2)}) %collective-permute-start.15) | collective-permute-done | bytes 524320 | tf_op jit(solution)/shard_map/ppermute | solution.py:18
  117.3 1.5 %row_gradient.2 = (bf16[64,8192]{1,0:T(8,128)(2,1)S(1)}, bf16[64,8192]{1,0:T(8,128)(2,1)S(1)}) custom-call(s32[1]{0:T(128)} %bitcast.1.me_ref, bf16[1,2,64,8192]{3,2,1,0:T(8,128)(2,1)S(1)} %copy-done, bf16[2,64,8192]{2,1,0:T(8,128)(2,1)S(1)} %copy-done.1, bf16[128,2048]{1,0:T(8,128)(2,1)S(1)} %get-tuple-element.73.refs_0_, ...), custom_call_target="tpu_custom_call" | custom-call | flops 6291456 | bytes 5242880 | tf_op jit(solution)/shard_map/row_gradient/pallas_call | solution.py:302
  118.9 1.3 collective-permute-start.21
  120.2 7.6 %collective-permute-done.17.refs_2_ = bf16[64,2048]{1,0:T(8,128)(2,1)S(1)} collective-permute-done((bf16[64,2048]{1,0:T(8,128)(2,1)S(1)}, bf16[64,2048]{1,0:T(8,128)(2,1)S(1)}, u32[]{:S(2)}, u32[]{:S(2)}) %collective-permute-start.17) | collective-permute-done | bytes 262176 | tf_op jit(solution)/shard_map/ppermute | solution.py:18
  127.7 1.5 %row_gradient.3 = (bf16[64,8192]{1,0:T(8,128)(2,1)S(1)}, bf16[64,8192]{1,0:T(8,128)(2,1)S(1)}) custom-call(s32[1]{0:T(128)} %bitcast.1.me_ref, bf16[1,2,64,8192]{3,2,1,0:T(8,128)(2,1)S(1)} %copy-done, bf16[2,64,8192]{2,1,0:T(8,128)(2,1)S(1)} %copy-done.1, bf16[128,2048]{1,0:T(8,128)(2,1)S(1)} %get-tuple-element.73.refs_0_, ...), custom_call_target="tpu_custom_call" | custom-call | flops 6291456 | bytes 5242880 | tf_op jit(solution)/shard_map/row_gradient/pallas_call | solution.py:302
  129.2 1.3 collective-permute-start.20
  130.5 1.4 %finished_half.6 = (f32[2048,1024]{1,0:T(8,128)}, f32[1,2048]{1,0:T(1,128)}) custom-call(s32[1]{0:T(128)} %bitcast.3.rep_ref, bf16[544,1024]{1,0:T(8,128)(2,1)S(1)} %collective-permute-done.19.sum_ref, f32[2048,1024]{1,0:T(8,128)} %get-tuple-element.63.refs_0_, f32[1,2048]{1,0:T(1,128)} %get-tuple-element.64.refs_1_), custom_call_target="tpu_custom_call", output_to_operand_aliasing={{0}: (2, {}), {1}: (3, {})} | custom-call | flops 557056 | bytes 3342336 | tf_op jit(solution)/shard_map/finished_half/pallas_call | solution.py:368
  132.0 1.4 %finished_half.7 = (f32[2048,1024]{1,0:T(8,128)}, f32[1,2048]{1,0:T(1,128)}) custom-call(s32[1]{0:T(128)} %bitcast.3.rep_ref, bf16[544,1024]{1,0:T(8,128)(2,1)S(1)} %collective-permute-done.18.sum_ref, f32[2048,1024]{1,0:T(8,128)} %get-tuple-element.78.refs_0_, f32[1,2048]{1,0:T(1,128)} %get-tuple-element.79.refs_1_), custom_call_target="tpu_custom_call", output_to_operand_aliasing={{0}: (2, {}), {1}: (3, {})} | custom-call | flops 557056 | bytes 3342336 | tf_op jit(solution)/shard_map/finished_half/pallas_call | solution.py:368
  133.4 1.1 input_gradient.2.refs_0_
  134.5 1.1 input_gradient.3
  (23 shorter events, 0.1 us)
Async XLA Ops:
  0.6 8.7 %copy-start.4 = (bf16[1,2,64,1024]{3,2,1,0:T(8,128)(2,1)S(1)}, bf16[1,2,64,1024]{3,2,1,0:T(8,128)(2,1)}, u32[]{:S(2)}) copy-start(bf16[1,2,64,1024]{3,2,1,0:T(8,128)(2,1)} %param.6) | copy-start | bytes 786436
  4.8 38.3 %copy-start.5 = (bf16[1,2048]{1,0:T(2,128)(2,1)S(1)}, bf16[1,2048]{1,0:T(2,128)(2,1)}, u32[]{:S(2)}) copy-start(bf16[1,2048]{1,0:T(2,128)(2,1)} %refs_9_.1) | copy-start | bytes 12292
  4.8 15.9 %collective-permute-start.2 = (bf16[128,2048]{1,0:T(8,128)(2,1)}, bf16[128,2048]{1,0:T(8,128)(2,1)S(1)}, u32[]{:S(2)}, u32[]{:S(2)}) collective-permute-start(bf16[128,2048]{1,0:T(8,128)(2,1)} %get-tuple-element.47), channel_id=1, source_target_pairs={{0,4},{4,0},{8,12},{12,8},{1,5},{5,1},{9,13},{13,9},{2,6},{6,2},{1... | collective-permute-start | bytes 1572872 | tf_op jit(solution)/shard_map/ppermute | solution.py:23
  7.8 24.8 %collective-permute-start.4 = (bf16[128,2048]{1,0:T(8,128)(2,1)}, bf16[128,2048]{1,0:T(8,128)(2,1)S(1)}, u32[]{:S(2)}, u32[]{:S(2)}) collective-permute-start(bf16[128,2048]{1,0:T(8,128)(2,1)} %get-tuple-element.51), channel_id=1, source_target_pairs={{0,8},{4,12},{8,0},{12,4},{1,9},{5,13},{9,1},{13,5},{2,10},{6,14},... | collective-permute-start | bytes 1572872 | tf_op jit(solution)/shard_map/ppermute | solution.py:23
  9.3 23.3 %collective-permute-start.5 = (bf16[128,2048]{1,0:T(8,128)(2,1)}, bf16[128,2048]{1,0:T(8,128)(2,1)S(1)}, u32[]{:S(2)}, u32[]{:S(2)}) collective-permute-start(bf16[128,2048]{1,0:T(8,128)(2,1)} %get-tuple-element.52), channel_id=1, source_target_pairs={{0,12},{4,8},{8,4},{12,0},{1,13},{5,9},{9,5},{13,1},{2,14},{6,10},... | collective-permute-start | bytes 1572872 | tf_op jit(solution)/shard_map/ppermute | solution.py:23
  9.3 33.8 %copy-start.2 = (bf16[1,2048,1024]{2,1,0:T(8,128)(2,1)S(1)}, bf16[1,2048,1024]{2,1,0:T(8,128)(2,1)}, u32[]{:S(2)}) copy-start(bf16[1,2048,1024]{2,1,0:T(8,128)(2,1)} %param.7) | copy-start | bytes 12582916
  9.3 15.6 %collective-permute-start = (bf16[128,1024]{1,0:T(8,128)(2,1)S(1)}, bf16[128,1024]{1,0:T(8,128)(2,1)S(1)}, u32[]{:S(2)}, u32[]{:S(2)}) collective-permute-start(bf16[128,1024]{1,0:T(8,128)(2,1)S(1)} %bitcast.10), channel_id=1, source_target_pairs={{0,1},{1,2},{2,3},{3,0},{4,5},{5,6},{6,7},{7,4},{8,9},{9,10},{10,1... | collective-permute-start | bytes 786440 | tf_op jit(solution)/shard_map/ppermute | solution.py:18
  11.4 18.9 %collective-permute-start.1 = (bf16[128,1024]{1,0:T(8,128)(2,1)S(1)}, bf16[128,1024]{1,0:T(8,128)(2,1)S(1)}, u32[]{:S(2)}, u32[]{:S(2)}) collective-permute-start(bf16[128,1024]{1,0:T(8,128)(2,1)S(1)} %bitcast.11), channel_id=1, source_target_pairs={{0,2},{1,3},{2,0},{3,1},{4,6},{5,7},{6,4},{7,5},{8,10},{9,11},{10,... | collective-permute-start | bytes 786440 | tf_op jit(solution)/shard_map/ppermute | solution.py:18
  20.7 15.4 %collective-permute-start.3 = (bf16[128,1024]{1,0:T(8,128)(2,1)S(1)}, bf16[128,1024]{1,0:T(8,128)(2,1)S(1)}, u32[]{:S(2)}, u32[]{:S(2)}) collective-permute-start(bf16[128,1024]{1,0:T(8,128)(2,1)S(1)} %bitcast.12), channel_id=1, source_target_pairs={{0,3},{1,0},{2,1},{3,2},{4,7},{5,4},{6,5},{7,6},{8,11},{9,8},{10,9... | collective-permute-start | bytes 786440 | tf_op jit(solution)/shard_map/ppermute | solution.py:18
  32.6 1.0 copy-start.3
  34.1 17.7 %collective-permute-start.6 = (bf16[512,512]{1,0:T(8,128)(2,1)S(1)}, bf16[512,512]{1,0:T(8,128)(2,1)S(1)}, u32[]{:S(2)}, u32[]{:S(2)}) collective-permute-start(bf16[512,512]{1,0:T(8,128)(2,1)S(1)} %get-tuple-element.54), channel_id=1, source_target_pairs={{0,1},{1,2},{2,3},{3,0},{4,5},{5,6},{6,7},{7,4},{8,9},{9,10},{10,1... | collective-permute-start | bytes 1572872 | tf_op jit(solution)/shard_map/ppermute | solution.py:18
  36.2 45.7 %collective-permute-start.10 = (bf16[512,1024]{1,0:T(8,128)(2,1)S(1)}, bf16[512,1024]{1,0:T(8,128)(2,1)S(1)}, u32[]{:S(2)}, u32[]{:S(2)}) collective-permute-start(bf16[512,1024]{1,0:T(8,128)(2,1)S(1)} %joined.3.refs_4_), channel_id=1, source_target_pairs={{0,8},{4,12},{8,0},{12,4},{1,9},{5,13},{9,1},{13,5},{2,10},{6,14},... | collective-permute-start | bytes 3145736 | tf_op jit(solution)/shard_map/ppermute | solution.py:23
  37.8 44.2 %collective-permute-start.11 = (bf16[512,1024]{1,0:T(8,128)(2,1)S(1)}, bf16[512,1024]{1,0:T(8,128)(2,1)S(1)}, u32[]{:S(2)}, u32[]{:S(2)}) collective-permute-start(bf16[512,1024]{1,0:T(8,128)(2,1)S(1)} %joined.3.refs_4_), channel_id=1, source_target_pairs={{0,12},{4,8},{8,4},{12,0},{1,13},{5,9},{9,5},{13,1},{2,14},{6,10},... | collective-permute-start | bytes 3145736 | tf_op jit(solution)/shard_map/ppermute | solution.py:23
  39.2 43.9 %collective-permute-start.9 = (bf16[512,1024]{1,0:T(8,128)(2,1)S(1)}, bf16[512,1024]{1,0:T(8,128)(2,1)S(1)}, u32[]{:S(2)}, u32[]{:S(2)}) collective-permute-start(bf16[512,1024]{1,0:T(8,128)(2,1)S(1)} %joined.3.refs_4_), channel_id=1, source_target_pairs={{0,4},{4,0},{8,12},{12,8},{1,5},{5,1},{9,13},{13,9},{2,6},{6,2},{1... | collective-permute-start | bytes 3145736 | tf_op jit(solution)/shard_map/ppermute | solution.py:23
  39.8 31.9 %collective-permute-start.7 = (bf16[512,512]{1,0:T(8,128)(2,1)S(1)}, bf16[512,512]{1,0:T(8,128)(2,1)S(1)}, u32[]{:S(2)}, u32[]{:S(2)}) collective-permute-start(bf16[512,512]{1,0:T(8,128)(2,1)S(1)} %get-tuple-element.55), channel_id=1, source_target_pairs={{0,2},{1,3},{2,0},{3,1},{4,6},{5,7},{6,4},{7,5},{8,10},{9,11},{10,... | collective-permute-start | bytes 1572872 | tf_op jit(solution)/shard_map/ppermute | solution.py:18
  51.8 28.2 %collective-permute-start.8 = (bf16[512,512]{1,0:T(8,128)(2,1)S(1)}, bf16[512,512]{1,0:T(8,128)(2,1)S(1)}, u32[]{:S(2)}, u32[]{:S(2)}) collective-permute-start(bf16[512,512]{1,0:T(8,128)(2,1)S(1)} %get-tuple-element.57), channel_id=1, source_target_pairs={{0,3},{1,0},{2,1},{3,2},{4,7},{5,4},{6,5},{7,6},{8,11},{9,8},{10,9... | collective-permute-start | bytes 1572872 | tf_op jit(solution)/shard_map/ppermute | solution.py:18
  71.6 31.7 %collective-permute-start.14 = (bf16[64,2048]{1,0:T(8,128)(2,1)S(1)}, bf16[64,2048]{1,0:T(8,128)(2,1)S(1)}, u32[]{:S(2)}, u32[]{:S(2)}) collective-permute-start(bf16[64,2048]{1,0:T(8,128)(2,1)S(1)} %get-tuple-element.68), channel_id=1, source_target_pairs={{0,2},{1,3},{2,0},{3,1},{4,6},{5,7},{6,4},{7,5},{8,10},{9,11},{10,... | collective-permute-start | bytes 786440 | tf_op jit(solution)/shard_map/ppermute | solution.py:18
  85.9 17.4 %collective-permute-start.13 = (bf16[272,1024]{1,0:T(8,128)(2,1)S(1)}, bf16[272,1024]{1,0:T(8,128)(2,1)S(1)}, u32[]{:S(2)}, u32[]{:S(2)}) collective-permute-start(bf16[272,1024]{1,0:T(8,128)(2,1)S(1)} %get-tuple-element.60.refs_0_), channel_id=1, source_target_pairs={{0,4},{4,0},{8,12},{12,8},{1,5},{5,1},{9,13},{13,9},{2,6},{6,2},{1... | collective-permute-start | bytes 1671176 | tf_op jit(solution)/shard_map/ppermute | solution.py:23
  87.4 19.5 %collective-permute-start.12 = (bf16[272,1024]{1,0:T(8,128)(2,1)S(1)}, bf16[272,1024]{1,0:T(8,128)(2,1)S(1)}, u32[]{:S(2)}, u32[]{:S(2)}) collective-permute-start(bf16[272,1024]{1,0:T(8,128)(2,1)S(1)} %get-tuple-element.59.refs_0_), channel_id=1, source_target_pairs={{0,8},{4,12},{8,0},{12,4},{1,9},{5,13},{9,1},{13,5},{2,10},{6,14},... | collective-permute-start | bytes 1671176 | tf_op jit(solution)/shard_map/ppermute | solution.py:23
  88.6 24.0 %collective-permute-start.16 = (bf16[128,2048]{1,0:T(8,128)(2,1)S(1)}, bf16[128,2048]{1,0:T(8,128)(2,1)S(1)}, u32[]{:S(2)}, u32[]{:S(2)}) collective-permute-start(bf16[128,2048]{1,0:T(8,128)(2,1)S(1)} %get-tuple-element.71), channel_id=1, source_target_pairs={{0,1},{1,2},{2,3},{3,0},{4,5},{5,6},{6,7},{7,4},{8,9},{9,10},{10,1... | collective-permute-start | bytes 1572872 | tf_op jit(solution)/shard_map/ppermute | solution.py:18
  103.3 14.0 %collective-permute-start.15 = (bf16[128,2048]{1,0:T(8,128)(2,1)S(1)}, bf16[128,2048]{1,0:T(8,128)(2,1)S(1)}, u32[]{:S(2)}, u32[]{:S(2)}) collective-permute-start(bf16[128,2048]{1,0:T(8,128)(2,1)S(1)} %get-tuple-element.69), channel_id=1, source_target_pairs={{0,3},{1,0},{2,1},{3,2},{4,7},{5,4},{6,5},{7,6},{8,11},{9,8},{10,9... | collective-permute-start | bytes 1572872 | tf_op jit(solution)/shard_map/ppermute | solution.py:18
  103.3 24.4 %collective-permute-start.17 = (bf16[64,2048]{1,0:T(8,128)(2,1)S(1)}, bf16[64,2048]{1,0:T(8,128)(2,1)S(1)}, u32[]{:S(2)}, u32[]{:S(2)}) collective-permute-start(bf16[64,2048]{1,0:T(8,128)(2,1)S(1)} %get-tuple-element.75), channel_id=1, source_target_pairs={{0,2},{1,3},{2,0},{3,1},{4,6},{5,7},{6,4},{7,5},{8,10},{9,11},{10,... | collective-permute-start | bytes 786440 | tf_op jit(solution)/shard_map/ppermute | solution.py:18
  103.5 27.0 %collective-permute-start.19 = (bf16[544,1024]{1,0:T(8,128)(2,1)S(1)}, bf16[544,1024]{1,0:T(8,128)(2,1)S(1)}, u32[]{:S(2)}, u32[]{:S(2)}) collective-permute-start(bf16[544,1024]{1,0:T(8,128)(2,1)S(1)} %joined.5.sum_ref), channel_id=1, source_target_pairs={{0,8},{4,12},{8,0},{12,4},{1,9},{5,13},{9,1},{13,5},{2,10},{6,14},... | collective-permute-start | bytes 3342344 | tf_op jit(solution)/shard_map/ppermute | solution.py:23
  107.1 24.8 %collective-permute-start.18 = (bf16[544,1024]{1,0:T(8,128)(2,1)S(1)}, bf16[544,1024]{1,0:T(8,128)(2,1)S(1)}, u32[]{:S(2)}, u32[]{:S(2)}) collective-permute-start(bf16[544,1024]{1,0:T(8,128)(2,1)S(1)} %joined.4.sum_ref), channel_id=1, source_target_pairs={{0,4},{4,0},{8,12},{12,8},{1,5},{5,1},{9,13},{13,9},{2,6},{6,2},{1... | collective-permute-start | bytes 3342344 | tf_op jit(solution)/shard_map/ppermute | solution.py:23
  111.2 6.1 %copy-start = (bf16[1,2,64,8192]{3,2,1,0:T(8,128)(2,1)S(1)}, bf16[1,2,64,8192]{3,2,1,0:T(8,128)(2,1)}, u32[]{:S(2)}) copy-start(bf16[1,2,64,8192]{3,2,1,0:T(8,128)(2,1)} %x_ref.3) | copy-start | bytes 6291460
  111.2 6.1 %copy-start.1 = (bf16[2,64,8192]{2,1,0:T(8,128)(2,1)S(1)}, bf16[2,64,8192]{2,1,0:T(8,128)(2,1)}, u32[]{:S(2)}) copy-start(bf16[2,64,8192]{2,1,0:T(8,128)(2,1)} %top_ref.3) | copy-start | bytes 6291460
  118.9 14.6 %collective-permute-start.21 = (bf16[64,8192]{1,0:T(8,128)(2,1)S(1)}, bf16[64,8192]{1,0:T(8,128)(2,1)S(1)}, u32[]{:S(2)}, u32[]{:S(2)}) collective-permute-start(bf16[64,8192]{1,0:T(8,128)(2,1)S(1)} %get-tuple-element.72.upper_ref), channel_id=1, source_target_pairs={{16,0},{17,1},{18,2},{19,3},{20,4},{21,5},{22,6},{23,7},{24,8},{25... | collective-permute-start | bytes 3145736 | tf_op jit(solution)/shard_map/ppermute | solution.py:452
  129.2 5.3 %collective-permute-start.20 = (bf16[64,8192]{1,0:T(8,128)(2,1)S(1)}, bf16[64,8192]{1,0:T(8,128)(2,1)S(1)}, u32[]{:S(2)}, u32[]{:S(2)}) collective-permute-start(bf16[64,8192]{1,0:T(8,128)(2,1)S(1)} %get-tuple-element.76.upper_ref), channel_id=1, source_target_pairs={{16,0},{17,1},{18,2},{19,3},{20,4},{21,5},{22,6},{23,7},{24,8},{25... | collective-permute-start | bytes 3145736 | tf_op jit(solution)/shard_map/ppermute | solution.py:452

commit v14 on v12

--- a/solution.py
+++ b/solution.py
@@ -268,7 +268,7 @@
     shard = blocks[0].shape[1]
     rows = x.shape[2]
     width = shard * groups
-    step = 16
+    step = min(rows, 32)
 
     def block_spec(block):
         base = m * rows // step if block.shape[0] > rows else 0

time: 134 us -> 134 us (level)
  no operation moved by 1% of the time
where the time goes in v14:
time: 134 us; the launch traced here: 133 us
  waiting for transfers between devices  70.3 us (52%)
  starting transfers between devices  41.9 us (31%)
  Pallas kernels  18.3 us (14%)
  local copies, waits for them, and re-layouts  1.6 us (1%)
    ppermute x10, waiting for transfers between devices, cyclic(): lax.ppermute(value, axis, [(i, (i + steps) % count) for i in range(count)])  58 us
    ppermute x10, starting transfers between devices, cyclic(): lax.ppermute(value, axis, [(i, (i + steps) % count) for i in range(count)])  23.3 us
    ppermute x10, starting transfers between devices, flipped(): return lax.ppermute(value, axis, [(i, i ^ mask) for i in range(count)])  16 us
    ppermute x10, waiting for transfers between devices, flipped(): return lax.ppermute(value, axis, [(i, i ^ mask) for i in range(count)])  12.3 us
    pallas_call x4, Pallas kernels, finished_half(): pl.pallas_call(kernel, grid_spec=pltpu.PrefetchScalarGridSpec(num_scalar_...  5.7 us
    pallas_call x1, Pallas kernels, returned_blocks(): pl.pallas_call(kernel, grid=(shard // tile,), out_shape=[jax.ShapeDtypeSt...  3.17 us
    pallas_call x1, Pallas kernels, weight_product(): pl.pallas_call(kernel, out_shape=[jax.ShapeDtypeStruct((chunk + 16, featu...  2.73 us
  transfers between devices with their start and end apart: 22, of which 11 were waited for; matrix products, arithmetic and copies ran while one was open for 0% of the time, Pallas kernels for 12%

profile of v14, /device:TPU:0, one launch (start us, length us, event | category | flops | bytes accessed | tf_op | source)
XLA Modules:
  0.0 132.9 jit_solution(9445977899882093607)
XLA Ops:
  0.6 0.0 copy-start
  0.6 1.6 %copy-done = bf16[1,2,64,8192]{3,2,1,0:T(8,128)(2,1)S(1)} copy-done((bf16[1,2,64,8192]{3,2,1,0:T(8,128)(2,1)S(1)}, bf16[1,2,64,8192]{3,2,1,0:T(8,128)(2,1)}, u32[]{:S(2)}) %copy-start) | copy-done | bytes 2097176
  2.2 1.1 scaled_blocks.1
  3.3 3.0 %collective-permute-start.2 = (bf16[128,2048]{1,0:T(8,128)(2,1)S(1)}, bf16[128,2048]{1,0:T(8,128)(2,1)S(1)}, u32[]{:S(2)}, u32[]{:S(2)}) collective-permute-start(bf16[128,2048]{1,0:T(8,128)(2,1)S(1)} %get-tuple-element.47), channel_id=1, source_target_pairs={{0,4},{4,0},{8,12},{12,8},{1,5},{5,1},{9,13},{13,9},{2,6},{6,2},{1... | collective-permute-start | bytes 1572872 | tf_op jit(solution)/shard_map/ppermute | solution.py:23
  6.3 1.5 %collective-permute-start.4 = (bf16[128,2048]{1,0:T(8,128)(2,1)S(1)}, bf16[128,2048]{1,0:T(8,128)(2,1)S(1)}, u32[]{:S(2)}, u32[]{:S(2)}) collective-permute-start(bf16[128,2048]{1,0:T(8,128)(2,1)S(1)} %get-tuple-element.51), channel_id=1, source_target_pairs={{0,8},{4,12},{8,0},{12,4},{1,9},{5,13},{9,1},{13,5},{2,10},{6,14},... | collective-permute-start | bytes 1572872 | tf_op jit(solution)/shard_map/ppermute | solution.py:23
  7.8 0.0 collective-permute-start.5
  7.9 2.0 %collective-permute-start = (bf16[128,1024]{1,0:T(8,128)(2,1)S(1)}, bf16[128,1024]{1,0:T(8,128)(2,1)S(1)}, u32[]{:S(2)}, u32[]{:S(2)}) collective-permute-start(bf16[128,1024]{1,0:T(8,128)(2,1)S(1)} %bitcast.10), channel_id=1, source_target_pairs={{0,1},{1,2},{2,3},{3,0},{4,5},{5,6},{6,7},{7,4},{8,9},{9,10},{10,1... | collective-permute-start | bytes 786440 | tf_op jit(solution)/shard_map/ppermute | solution.py:18
  9.9 2.6 %collective-permute-start.1 = (bf16[128,1024]{1,0:T(8,128)(2,1)S(1)}, bf16[128,1024]{1,0:T(8,128)(2,1)S(1)}, u32[]{:S(2)}, u32[]{:S(2)}) collective-permute-start(bf16[128,1024]{1,0:T(8,128)(2,1)S(1)} %bitcast.11), channel_id=1, source_target_pairs={{0,2},{1,3},{2,0},{3,1},{4,6},{5,7},{6,4},{7,5},{8,10},{9,11},{10,... | collective-permute-start | bytes 786440 | tf_op jit(solution)/shard_map/ppermute | solution.py:18
  12.5 6.6 %collective-permute-done.2.refs_1_ = bf16[128,2048]{1,0:T(8,128)(2,1)S(1)} collective-permute-done((bf16[128,2048]{1,0:T(8,128)(2,1)S(1)}, bf16[128,2048]{1,0:T(8,128)(2,1)S(1)}, u32[]{:S(2)}, u32[]{:S(2)}) %collective-permute-start.2) | collective-permute-done | bytes 524320 | tf_op jit(solution)/shard_map/ppermute | solution.py:23
  19.1 4.2 %collective-permute-start.3 = (bf16[128,1024]{1,0:T(8,128)(2,1)S(1)}, bf16[128,1024]{1,0:T(8,128)(2,1)S(1)}, u32[]{:S(2)}, u32[]{:S(2)}) collective-permute-start(bf16[128,1024]{1,0:T(8,128)(2,1)S(1)} %bitcast.12), channel_id=1, source_target_pairs={{0,3},{1,0},{2,1},{3,2},{4,7},{5,4},{6,5},{7,6},{8,11},{9,8},{10,9... | collective-permute-start | bytes 786440 | tf_op jit(solution)/shard_map/ppermute | solution.py:18
  23.2 5.5 %collective-permute-done.1.refs_2_ = bf16[128,1024]{1,0:T(8,128)(2,1)S(1)} collective-permute-done((bf16[128,1024]{1,0:T(8,128)(2,1)S(1)}, bf16[128,1024]{1,0:T(8,128)(2,1)S(1)}, u32[]{:S(2)}, u32[]{:S(2)}) %collective-permute-start.1) | collective-permute-done | bytes 262176 | tf_op jit(solution)/shard_map/ppermute | solution.py:18
  28.7 2.2 %collective-permute-done.4.refs_2_ = bf16[128,2048]{1,0:T(8,128)(2,1)S(1)} collective-permute-done((bf16[128,2048]{1,0:T(8,128)(2,1)S(1)}, bf16[128,2048]{1,0:T(8,128)(2,1)S(1)}, u32[]{:S(2)}, u32[]{:S(2)}) %collective-permute-start.4) | collective-permute-done | bytes 524320 | tf_op jit(solution)/shard_map/ppermute | solution.py:23
  30.9 0.5 regrouped.1
  31.4 2.2 %collective-permute-start.6 = (bf16[512,512]{1,0:T(8,128)(2,1)S(1)}, bf16[512,512]{1,0:T(8,128)(2,1)S(1)}, u32[]{:S(2)}, u32[]{:S(2)}) collective-permute-start(bf16[512,512]{1,0:T(8,128)(2,1)S(1)} %get-tuple-element.54), channel_id=1, source_target_pairs={{0,1},{1,2},{2,3},{3,0},{4,5},{5,6},{6,7},{7,4},{8,9},{9,10},{10,1... | collective-permute-start | bytes 1572872 | tf_op jit(solution)/shard_map/ppermute | solution.py:18
  33.6 0.0 collective-permute-done.3.refs_3_
  33.6 0.1 joined.3.refs_4_
  33.7 2.1 %collective-permute-start.10 = (bf16[512,1024]{1,0:T(8,128)(2,1)S(1)}, bf16[512,1024]{1,0:T(8,128)(2,1)S(1)}, u32[]{:S(2)}, u32[]{:S(2)}) collective-permute-start(bf16[512,1024]{1,0:T(8,128)(2,1)S(1)} %joined.3.refs_4_), channel_id=1, source_target_pairs={{0,8},{4,12},{8,0},{12,4},{1,9},{5,13},{9,1},{13,5},{2,10},{6,14},... | collective-permute-start | bytes 3145736 | tf_op jit(solution)/shard_map/ppermute | solution.py:23
  35.8 1.0 collective-permute-start.11
  36.8 0.5 collective-permute-start.9
  37.3 3.4 %collective-permute-start.7 = (bf16[512,512]{1,0:T(8,128)(2,1)S(1)}, bf16[512,512]{1,0:T(8,128)(2,1)S(1)}, u32[]{:S(2)}, u32[]{:S(2)}) collective-permute-start(bf16[512,512]{1,0:T(8,128)(2,1)S(1)} %get-tuple-element.55), channel_id=1, source_target_pairs={{0,2},{1,3},{2,0},{3,1},{4,6},{5,7},{6,4},{7,5},{8,10},{9,11},{10,... | collective-permute-start | bytes 1572872 | tf_op jit(solution)/shard_map/ppermute | solution.py:18
  40.7 3.2 %returned_blocks.1 = (bf16[128,2048]{1,0:T(8,128)(2,1)S(1)}, bf16[128,2048]{1,0:T(8,128)(2,1)S(1)}, bf16[64,2048]{1,0:T(8,128)(2,1)S(1)}, bf16[64,2048]{1,0:T(8,128)(2,1)S(1)}, bf16[128,2048]{1,0:T(8,128)(2,1)S(1)}) custom-call(bf16[128,1024]{1,0:T(8,128)(2,1)S(1)} %bitcast.14, bf16[128,1024]{1,0:T(8,128)(2,1)S(1)} %collective-permute-done.refs_1_, ...), custom_call_target="tpu_custom_call" | custom-call | flops 2147483648 | bytes 7340032 | tf_op jit(solution)/shard_map/returned_blocks/pallas_call | solution.py:252
  43.9 5.4 %collective-permute-done.6.refs_1_ = bf16[512,512]{1,0:T(8,128)(2,1)S(1)} collective-permute-done((bf16[512,512]{1,0:T(8,128)(2,1)S(1)}, bf16[512,512]{1,0:T(8,128)(2,1)S(1)}, u32[]{:S(2)}, u32[]{:S(2)}) %collective-permute-start.6) | collective-permute-done | bytes 524320 | tf_op jit(solution)/shard_map/ppermute | solution.py:18
  49.3 19.8 %collective-permute-done.7.refs_2_ = bf16[512,512]{1,0:T(8,128)(2,1)S(1)} collective-permute-done((bf16[512,512]{1,0:T(8,128)(2,1)S(1)}, bf16[512,512]{1,0:T(8,128)(2,1)S(1)}, u32[]{:S(2)}, u32[]{:S(2)}) %collective-permute-start.7) | collective-permute-done | bytes 524320 | tf_op jit(solution)/shard_map/ppermute | solution.py:18
  69.1 2.3 %collective-permute-start.14 = (bf16[64,2048]{1,0:T(8,128)(2,1)S(1)}, bf16[64,2048]{1,0:T(8,128)(2,1)S(1)}, u32[]{:S(2)}, u32[]{:S(2)}) collective-permute-start(bf16[64,2048]{1,0:T(8,128)(2,1)S(1)} %get-tuple-element.68), channel_id=1, source_target_pairs={{0,2},{1,3},{2,0},{3,1},{4,6},{5,7},{6,4},{7,5},{8,10},{9,11},{10,... | collective-permute-start | bytes 786440 | tf_op jit(solution)/shard_map/ppermute | solution.py:18
  71.4 5.6 %collective-permute-done.8.refs_3_ = bf16[512,512]{1,0:T(8,128)(2,1)S(1)} collective-permute-done((bf16[512,512]{1,0:T(8,128)(2,1)S(1)}, bf16[512,512]{1,0:T(8,128)(2,1)S(1)}, u32[]{:S(2)}, u32[]{:S(2)}) %collective-permute-start.8) | collective-permute-done | bytes 524320 | tf_op jit(solution)/shard_map/ppermute | solution.py:18
  76.9 2.3 %collective-permute-done.10.refs_6_ = bf16[512,1024]{1,0:T(8,128)(2,1)S(1)} collective-permute-done((bf16[512,1024]{1,0:T(8,128)(2,1)S(1)}, bf16[512,1024]{1,0:T(8,128)(2,1)S(1)}, u32[]{:S(2)}, u32[]{:S(2)}) %collective-permute-start.10) | collective-permute-done | bytes 1048608 | tf_op jit(solution)/shard_map/ppermute | solution.py:23
  79.2 1.2 collective-permute-done.9.refs_5_
  80.5 2.7 %weight_product.1 = (bf16[272,1024]{1,0:T(8,128)(2,1)S(1)}, bf16[272,1024]{1,0:T(8,128)(2,1)S(1)}) custom-call(s32[1]{0:T(128)} %bitcast.3.rep_ref, bf16[512,512]{1,0:T(8,128)(2,1)S(1)} %get-tuple-element.53.refs_0_, bf16[512,512]{1,0:T(8,128)(2,1)S(1)} %collective-permute-done.6.refs_1_, bf16[512,512]{1,0:T(8,128)(2,1)S(1)} %collective-permute-done.7.refs_2_, ...), custom_call_target="tpu_custom_call" | custom-call | flops 2147483648 | bytes 8388608 | tf_op jit(solution)/shard_map/weight_product/pallas_call | solution.py:215
  83.2 1.5 %collective-permute-start.13 = (bf16[272,1024]{1,0:T(8,128)(2,1)S(1)}, bf16[272,1024]{1,0:T(8,128)(2,1)S(1)}, u32[]{:S(2)}, u32[]{:S(2)}) collective-permute-start(bf16[272,1024]{1,0:T(8,128)(2,1)S(1)} %get-tuple-element.60.refs_0_), channel_id=1, source_target_pairs={{0,4},{4,0},{8,12},{12,8},{1,5},{5,1},{9,13},{13,9},{2,6},{6,2},{1... | collective-permute-start | bytes 1671176 | tf_op jit(solution)/shard_map/ppermute | solution.py:23
  84.7 1.4 %collective-permute-start.12 = (bf16[272,1024]{1,0:T(8,128)(2,1)S(1)}, bf16[272,1024]{1,0:T(8,128)(2,1)S(1)}, u32[]{:S(2)}, u32[]{:S(2)}) collective-permute-start(bf16[272,1024]{1,0:T(8,128)(2,1)S(1)} %get-tuple-element.59.refs_0_), channel_id=1, source_target_pairs={{0,8},{4,12},{8,0},{12,4},{1,9},{5,13},{9,1},{13,5},{2,10},{6,14},... | collective-permute-start | bytes 1671176 | tf_op jit(solution)/shard_map/ppermute | solution.py:23
  86.1 6.7 %collective-permute-start.16 = (bf16[128,2048]{1,0:T(8,128)(2,1)S(1)}, bf16[128,2048]{1,0:T(8,128)(2,1)S(1)}, u32[]{:S(2)}, u32[]{:S(2)}) collective-permute-start(bf16[128,2048]{1,0:T(8,128)(2,1)S(1)} %get-tuple-element.71), channel_id=1, source_target_pairs={{0,1},{1,2},{2,3},{3,0},{4,5},{5,6},{6,7},{7,4},{8,9},{9,10},{10,1... | collective-permute-start | bytes 1572872 | tf_op jit(solution)/shard_map/ppermute | solution.py:18
  92.8 7.9 %collective-permute-done.14.refs_2_ = bf16[64,2048]{1,0:T(8,128)(2,1)S(1)} collective-permute-done((bf16[64,2048]{1,0:T(8,128)(2,1)S(1)}, bf16[64,2048]{1,0:T(8,128)(2,1)S(1)}, u32[]{:S(2)}, u32[]{:S(2)}) %collective-permute-start.14) | collective-permute-done | bytes 262176 | tf_op jit(solution)/shard_map/ppermute | solution.py:18
  100.8 0.2 joined.5.sum_ref
  100.9 3.2 %collective-permute-start.19 = (bf16[544,1024]{1,0:T(8,128)(2,1)S(1)}, bf16[544,1024]{1,0:T(8,128)(2,1)S(1)}, u32[]{:S(2)}, u32[]{:S(2)}) collective-permute-start(bf16[544,1024]{1,0:T(8,128)(2,1)S(1)} %joined.5.sum_ref), channel_id=1, source_target_pairs={{0,8},{4,12},{8,0},{12,4},{1,9},{5,13},{9,1},{13,5},{2,10},{6,14},... | collective-permute-start | bytes 3342344 | tf_op jit(solution)/shard_map/ppermute | solution.py:23
  104.2 0.2 joined.4.sum_ref
  104.3 1.7 %collective-permute-start.18 = (bf16[544,1024]{1,0:T(8,128)(2,1)S(1)}, bf16[544,1024]{1,0:T(8,128)(2,1)S(1)}, u32[]{:S(2)}, u32[]{:S(2)}) collective-permute-start(bf16[544,1024]{1,0:T(8,128)(2,1)S(1)} %joined.4.sum_ref), channel_id=1, source_target_pairs={{0,4},{4,0},{8,12},{12,8},{1,5},{5,1},{9,13},{13,9},{2,6},{6,2},{1... | collective-permute-start | bytes 3342344 | tf_op jit(solution)/shard_map/ppermute | solution.py:23
  106.0 1.4 %finished_half.4 = (f32[2048,1024]{1,0:T(8,128)}, f32[1,2048]{1,0:T(1,128)}) custom-call(s32[1]{0:T(128)} %bitcast.3.rep_ref, bf16[544,1024]{1,0:T(8,128)(2,1)S(1)} %joined.5.sum_ref), custom_call_target="tpu_custom_call" | custom-call | flops 557056 | bytes 3342336 | tf_op jit(solution)/shard_map/finished_half/pallas_call | solution.py:368
  107.4 1.4 %finished_half.5 = (f32[2048,1024]{1,0:T(8,128)}, f32[1,2048]{1,0:T(1,128)}) custom-call(s32[1]{0:T(128)} %bitcast.3.rep_ref, bf16[544,1024]{1,0:T(8,128)(2,1)S(1)} %joined.4.sum_ref, f32[2048,1024]{1,0:T(8,128)} %get-tuple-element.61.refs_0_, f32[1,2048]{1,0:T(1,128)} %get-tuple-element.62.refs_1_), custom_call_target="tpu_custom_call", output_to_operand_aliasing={{0}: (2, {}), {1}: (3, {})} | custom-call | flops 557056 | bytes 3342336 | tf_op jit(solution)/shard_map/finished_half/pallas_call | solution.py:368
  108.8 6.5 %collective-permute-done.15.refs_1_ = bf16[128,2048]{1,0:T(8,128)(2,1)S(1)} collective-permute-done((bf16[128,2048]{1,0:T(8,128)(2,1)S(1)}, bf16[128,2048]{1,0:T(8,128)(2,1)S(1)}, u32[]{:S(2)}, u32[]{:S(2)}) %collective-permute-start.15) | collective-permute-done | bytes 524320 | tf_op jit(solution)/shard_map/ppermute | solution.py:18
  115.3 1.2 row_gradient.2
  116.6 1.3 collective-permute-start.21
  117.9 7.4 %collective-permute-done.17.refs_2_ = bf16[64,2048]{1,0:T(8,128)(2,1)S(1)} collective-permute-done((bf16[64,2048]{1,0:T(8,128)(2,1)S(1)}, bf16[64,2048]{1,0:T(8,128)(2,1)S(1)}, u32[]{:S(2)}, u32[]{:S(2)}) %collective-permute-start.17) | collective-permute-done | bytes 262176 | tf_op jit(solution)/shard_map/ppermute | solution.py:18
  125.2 1.2 row_gradient.3
  126.5 1.3 collective-permute-start.20
  127.8 1.4 %finished_half.6 = (f32[2048,1024]{1,0:T(8,128)}, f32[1,2048]{1,0:T(1,128)}) custom-call(s32[1]{0:T(128)} %bitcast.3.rep_ref, bf16[544,1024]{1,0:T(8,128)(2,1)S(1)} %collective-permute-done.19.sum_ref, f32[2048,1024]{1,0:T(8,128)} %get-tuple-element.63.refs_0_, f32[1,2048]{1,0:T(1,128)} %get-tuple-element.64.refs_1_), custom_call_target="tpu_custom_call", output_to_operand_aliasing={{0}: (2, {}), {1}: (3, {})} | custom-call | flops 557056 | bytes 3342336 | tf_op jit(solution)/shard_map/finished_half/pallas_call | solution.py:368
  129.2 1.4 %finished_half.7 = (f32[2048,1024]{1,0:T(8,128)}, f32[1,2048]{1,0:T(1,128)}) custom-call(s32[1]{0:T(128)} %bitcast.3.rep_ref, bf16[544,1024]{1,0:T(8,128)(2,1)S(1)} %collective-permute-done.18.sum_ref, f32[2048,1024]{1,0:T(8,128)} %get-tuple-element.78.refs_0_, f32[1,2048]{1,0:T(1,128)} %get-tuple-element.79.refs_1_), custom_call_target="tpu_custom_call", output_to_operand_aliasing={{0}: (2, {}), {1}: (3, {})} | custom-call | flops 557056 | bytes 3342336 | tf_op jit(solution)/shard_map/finished_half/pallas_call | solution.py:368
  130.7 1.1 input_gradient.2.refs_0_
  131.8 1.1 input_gradient.3
  (23 shorter events, 0.1 us)
Async XLA Ops:
  0.6 1.6 %copy-start = (bf16[1,2,64,8192]{3,2,1,0:T(8,128)(2,1)S(1)}, bf16[1,2,64,8192]{3,2,1,0:T(8,128)(2,1)}, u32[]{:S(2)}) copy-start(bf16[1,2,64,8192]{3,2,1,0:T(8,128)(2,1)} %x_ref.3) | copy-start | bytes 6291460
  2.2 5.6 %copy-start.4 = (bf16[1,2,64,1024]{3,2,1,0:T(8,128)(2,1)S(1)}, bf16[1,2,64,1024]{3,2,1,0:T(8,128)(2,1)}, u32[]{:S(2)}) copy-start(bf16[1,2,64,1024]{3,2,1,0:T(8,128)(2,1)} %param.6) | copy-start | bytes 786436
  3.3 15.8 %collective-permute-start.2 = (bf16[128,2048]{1,0:T(8,128)(2,1)S(1)}, bf16[128,2048]{1,0:T(8,128)(2,1)S(1)}, u32[]{:S(2)}, u32[]{:S(2)}) collective-permute-start(bf16[128,2048]{1,0:T(8,128)(2,1)S(1)} %get-tuple-element.47), channel_id=1, source_target_pairs={{0,4},{4,0},{8,12},{12,8},{1,5},{5,1},{9,13},{13,9},{2,6},{6,2},{1... | collective-permute-start | bytes 1572872 | tf_op jit(solution)/shard_map/ppermute | solution.py:23
  6.3 24.6 %collective-permute-start.4 = (bf16[128,2048]{1,0:T(8,128)(2,1)S(1)}, bf16[128,2048]{1,0:T(8,128)(2,1)S(1)}, u32[]{:S(2)}, u32[]{:S(2)}) collective-permute-start(bf16[128,2048]{1,0:T(8,128)(2,1)S(1)} %get-tuple-element.51), channel_id=1, source_target_pairs={{0,8},{4,12},{8,0},{12,4},{1,9},{5,13},{9,1},{13,5},{2,10},{6,14},... | collective-permute-start | bytes 1572872 | tf_op jit(solution)/shard_map/ppermute | solution.py:23
  7.8 23.1 %collective-permute-start.5 = (bf16[128,2048]{1,0:T(8,128)(2,1)S(1)}, bf16[128,2048]{1,0:T(8,128)(2,1)S(1)}, u32[]{:S(2)}, u32[]{:S(2)}) collective-permute-start(bf16[128,2048]{1,0:T(8,128)(2,1)S(1)} %get-tuple-element.52), channel_id=1, source_target_pairs={{0,12},{4,8},{8,4},{12,0},{1,13},{5,9},{9,5},{13,1},{2,14},{6,10},... | collective-permute-start | bytes 1572872 | tf_op jit(solution)/shard_map/ppermute | solution.py:23
  7.8 32.9 %copy-start.5 = (bf16[1,2048]{1,0:T(2,128)(2,1)S(1)}, bf16[1,2048]{1,0:T(2,128)(2,1)}, u32[]{:S(2)}) copy-start(bf16[1,2048]{1,0:T(2,128)(2,1)} %refs_9_.1) | copy-start | bytes 12292
  7.8 32.9 %copy-start.3 = (bf16[1,2048,1024]{2,1,0:T(8,128)(2,1)S(1)}, bf16[1,2048,1024]{2,1,0:T(8,128)(2,1)}, u32[]{:S(2)}) copy-start(bf16[1,2048,1024]{2,1,0:T(8,128)(2,1)} %param.7) | copy-start | bytes 12582916
  7.9 15.4 %collective-permute-start = (bf16[128,1024]{1,0:T(8,128)(2,1)S(1)}, bf16[128,1024]{1,0:T(8,128)(2,1)S(1)}, u32[]{:S(2)}, u32[]{:S(2)}) collective-permute-start(bf16[128,1024]{1,0:T(8,128)(2,1)S(1)} %bitcast.10), channel_id=1, source_target_pairs={{0,1},{1,2},{2,3},{3,0},{4,5},{5,6},{6,7},{7,4},{8,9},{9,10},{10,1... | collective-permute-start | bytes 786440 | tf_op jit(solution)/shard_map/ppermute | solution.py:18
  9.9 18.9 %collective-permute-start.1 = (bf16[128,1024]{1,0:T(8,128)(2,1)S(1)}, bf16[128,1024]{1,0:T(8,128)(2,1)S(1)}, u32[]{:S(2)}, u32[]{:S(2)}) collective-permute-start(bf16[128,1024]{1,0:T(8,128)(2,1)S(1)} %bitcast.11), channel_id=1, source_target_pairs={{0,2},{1,3},{2,0},{3,1},{4,6},{5,7},{6,4},{7,5},{8,10},{9,11},{10,... | collective-permute-start | bytes 786440 | tf_op jit(solution)/shard_map/ppermute | solution.py:18
  19.1 14.5 %collective-permute-start.3 = (bf16[128,1024]{1,0:T(8,128)(2,1)S(1)}, bf16[128,1024]{1,0:T(8,128)(2,1)S(1)}, u32[]{:S(2)}, u32[]{:S(2)}) collective-permute-start(bf16[128,1024]{1,0:T(8,128)(2,1)S(1)} %bitcast.12), channel_id=1, source_target_pairs={{0,3},{1,0},{2,1},{3,2},{4,7},{5,4},{6,5},{7,6},{8,11},{9,8},{10,9... | collective-permute-start | bytes 786440 | tf_op jit(solution)/shard_map/ppermute | solution.py:18
  31.4 17.9 %collective-permute-start.6 = (bf16[512,512]{1,0:T(8,128)(2,1)S(1)}, bf16[512,512]{1,0:T(8,128)(2,1)S(1)}, u32[]{:S(2)}, u32[]{:S(2)}) collective-permute-start(bf16[512,512]{1,0:T(8,128)(2,1)S(1)} %get-tuple-element.54), channel_id=1, source_target_pairs={{0,1},{1,2},{2,3},{3,0},{4,5},{5,6},{6,7},{7,4},{8,9},{9,10},{10,1... | collective-permute-start | bytes 1572872 | tf_op jit(solution)/shard_map/ppermute | solution.py:18
  33.7 45.5 %collective-permute-start.10 = (bf16[512,1024]{1,0:T(8,128)(2,1)S(1)}, bf16[512,1024]{1,0:T(8,128)(2,1)S(1)}, u32[]{:S(2)}, u32[]{:S(2)}) collective-permute-start(bf16[512,1024]{1,0:T(8,128)(2,1)S(1)} %joined.3.refs_4_), channel_id=1, source_target_pairs={{0,8},{4,12},{8,0},{12,4},{1,9},{5,13},{9,1},{13,5},{2,10},{6,14},... | collective-permute-start | bytes 3145736 | tf_op jit(solution)/shard_map/ppermute | solution.py:23
  35.8 43.4 %collective-permute-start.11 = (bf16[512,1024]{1,0:T(8,128)(2,1)S(1)}, bf16[512,1024]{1,0:T(8,128)(2,1)S(1)}, u32[]{:S(2)}, u32[]{:S(2)}) collective-permute-start(bf16[512,1024]{1,0:T(8,128)(2,1)S(1)} %joined.3.refs_4_), channel_id=1, source_target_pairs={{0,12},{4,8},{8,4},{12,0},{1,13},{5,9},{9,5},{13,1},{2,14},{6,10},... | collective-permute-start | bytes 3145736 | tf_op jit(solution)/shard_map/ppermute | solution.py:23
  36.8 43.7 %collective-permute-start.9 = (bf16[512,1024]{1,0:T(8,128)(2,1)S(1)}, bf16[512,1024]{1,0:T(8,128)(2,1)S(1)}, u32[]{:S(2)}, u32[]{:S(2)}) collective-permute-start(bf16[512,1024]{1,0:T(8,128)(2,1)S(1)} %joined.3.refs_4_), channel_id=1, source_target_pairs={{0,4},{4,0},{8,12},{12,8},{1,5},{5,1},{9,13},{13,9},{2,6},{6,2},{1... | collective-permute-start | bytes 3145736 | tf_op jit(solution)/shard_map/ppermute | solution.py:23
  37.3 31.8 %collective-permute-start.7 = (bf16[512,512]{1,0:T(8,128)(2,1)S(1)}, bf16[512,512]{1,0:T(8,128)(2,1)S(1)}, u32[]{:S(2)}, u32[]{:S(2)}) collective-permute-start(bf16[512,512]{1,0:T(8,128)(2,1)S(1)} %get-tuple-element.55), channel_id=1, source_target_pairs={{0,2},{1,3},{2,0},{3,1},{4,6},{5,7},{6,4},{7,5},{8,10},{9,11},{10,... | collective-permute-start | bytes 1572872 | tf_op jit(solution)/shard_map/ppermute | solution.py:18
  49.3 27.6 %collective-permute-start.8 = (bf16[512,512]{1,0:T(8,128)(2,1)S(1)}, bf16[512,512]{1,0:T(8,128)(2,1)S(1)}, u32[]{:S(2)}, u32[]{:S(2)}) collective-permute-start(bf16[512,512]{1,0:T(8,128)(2,1)S(1)} %get-tuple-element.57), channel_id=1, source_target_pairs={{0,3},{1,0},{2,1},{3,2},{4,7},{5,4},{6,5},{7,6},{8,11},{9,8},{10,9... | collective-permute-start | bytes 1572872 | tf_op jit(solution)/shard_map/ppermute | solution.py:18
  69.1 31.6 %collective-permute-start.14 = (bf16[64,2048]{1,0:T(8,128)(2,1)S(1)}, bf16[64,2048]{1,0:T(8,128)(2,1)S(1)}, u32[]{:S(2)}, u32[]{:S(2)}) collective-permute-start(bf16[64,2048]{1,0:T(8,128)(2,1)S(1)} %get-tuple-element.68), channel_id=1, source_target_pairs={{0,2},{1,3},{2,0},{3,1},{4,6},{5,7},{6,4},{7,5},{8,10},{9,11},{10,... | collective-permute-start | bytes 786440 | tf_op jit(solution)/shard_map/ppermute | solution.py:18
  83.2 17.6 %collective-permute-start.13 = (bf16[272,1024]{1,0:T(8,128)(2,1)S(1)}, bf16[272,1024]{1,0:T(8,128)(2,1)S(1)}, u32[]{:S(2)}, u32[]{:S(2)}) collective-permute-start(bf16[272,1024]{1,0:T(8,128)(2,1)S(1)} %get-tuple-element.60.refs_0_), channel_id=1, source_target_pairs={{0,4},{4,0},{8,12},{12,8},{1,5},{5,1},{9,13},{13,9},{2,6},{6,2},{1... | collective-permute-start | bytes 1671176 | tf_op jit(solution)/shard_map/ppermute | solution.py:23
  84.7 19.5 %collective-permute-start.12 = (bf16[272,1024]{1,0:T(8,128)(2,1)S(1)}, bf16[272,1024]{1,0:T(8,128)(2,1)S(1)}, u32[]{:S(2)}, u32[]{:S(2)}) collective-permute-start(bf16[272,1024]{1,0:T(8,128)(2,1)S(1)} %get-tuple-element.59.refs_0_), channel_id=1, source_target_pairs={{0,8},{4,12},{8,0},{12,4},{1,9},{5,13},{9,1},{13,5},{2,10},{6,14},... | collective-permute-start | bytes 1671176 | tf_op jit(solution)/shard_map/ppermute | solution.py:23
  86.1 22.7 %collective-permute-start.16 = (bf16[128,2048]{1,0:T(8,128)(2,1)S(1)}, bf16[128,2048]{1,0:T(8,128)(2,1)S(1)}, u32[]{:S(2)}, u32[]{:S(2)}) collective-permute-start(bf16[128,2048]{1,0:T(8,128)(2,1)S(1)} %get-tuple-element.71), channel_id=1, source_target_pairs={{0,1},{1,2},{2,3},{3,0},{4,5},{5,6},{6,7},{7,4},{8,9},{9,10},{10,1... | collective-permute-start | bytes 1572872 | tf_op jit(solution)/shard_map/ppermute | solution.py:18
  100.7 14.6 %collective-permute-start.15 = (bf16[128,2048]{1,0:T(8,128)(2,1)S(1)}, bf16[128,2048]{1,0:T(8,128)(2,1)S(1)}, u32[]{:S(2)}, u32[]{:S(2)}) collective-permute-start(bf16[128,2048]{1,0:T(8,128)(2,1)S(1)} %get-tuple-element.69), channel_id=1, source_target_pairs={{0,3},{1,0},{2,1},{3,2},{4,7},{5,4},{6,5},{7,6},{8,11},{9,8},{10,9... | collective-permute-start | bytes 1572872 | tf_op jit(solution)/shard_map/ppermute | solution.py:18
  100.7 24.5 %collective-permute-start.17 = (bf16[64,2048]{1,0:T(8,128)(2,1)S(1)}, bf16[64,2048]{1,0:T(8,128)(2,1)S(1)}, u32[]{:S(2)}, u32[]{:S(2)}) collective-permute-start(bf16[64,2048]{1,0:T(8,128)(2,1)S(1)} %get-tuple-element.75), channel_id=1, source_target_pairs={{0,2},{1,3},{2,0},{3,1},{4,6},{5,7},{6,4},{7,5},{8,10},{9,11},{10,... | collective-permute-start | bytes 786440 | tf_op jit(solution)/shard_map/ppermute | solution.py:18
  100.9 26.8 %collective-permute-start.19 = (bf16[544,1024]{1,0:T(8,128)(2,1)S(1)}, bf16[544,1024]{1,0:T(8,128)(2,1)S(1)}, u32[]{:S(2)}, u32[]{:S(2)}) collective-permute-start(bf16[544,1024]{1,0:T(8,128)(2,1)S(1)} %joined.5.sum_ref), channel_id=1, source_target_pairs={{0,8},{4,12},{8,0},{12,4},{1,9},{5,13},{9,1},{13,5},{2,10},{6,14},... | collective-permute-start | bytes 3342344 | tf_op jit(solution)/shard_map/ppermute | solution.py:23
  104.3 24.9 %collective-permute-start.18 = (bf16[544,1024]{1,0:T(8,128)(2,1)S(1)}, bf16[544,1024]{1,0:T(8,128)(2,1)S(1)}, u32[]{:S(2)}, u32[]{:S(2)}) collective-permute-start(bf16[544,1024]{1,0:T(8,128)(2,1)S(1)} %joined.4.sum_ref), channel_id=1, source_target_pairs={{0,4},{4,0},{8,12},{12,8},{1,5},{5,1},{9,13},{13,9},{2,6},{6,2},{1... | collective-permute-start | bytes 3342344 | tf_op jit(solution)/shard_map/ppermute | solution.py:23
  107.4 7.9 %copy-start.1 = (bf16[1,2,64,8192]{3,2,1,0:T(8,128)(2,1)S(1)}, bf16[1,2,64,8192]{3,2,1,0:T(8,128)(2,1)}, u32[]{:S(2)}) copy-start(bf16[1,2,64,8192]{3,2,1,0:T(8,128)(2,1)} %x_ref.3) | copy-start | bytes 6291460
  107.4 7.9 %copy-start.2 = (bf16[2,64,8192]{2,1,0:T(8,128)(2,1)S(1)}, bf16[2,64,8192]{2,1,0:T(8,128)(2,1)}, u32[]{:S(2)}) copy-start(bf16[2,64,8192]{2,1,0:T(8,128)(2,1)} %top_ref.3) | copy-start | bytes 6291460
  116.6 14.1 %collective-permute-start.21 = (bf16[64,8192]{1,0:T(8,128)(2,1)S(1)}, bf16[64,8192]{1,0:T(8,128)(2,1)S(1)}, u32[]{:S(2)}, u32[]{:S(2)}) collective-permute-start(bf16[64,8192]{1,0:T(8,128)(2,1)S(1)} %get-tuple-element.72.upper_ref), channel_id=1, source_target_pairs={{16,0},{17,1},{18,2},{19,3},{20,4},{21,5},{22,6},{23,7},{24,8},{25... | collective-permute-start | bytes 3145736 | tf_op jit(solution)/shard_map/ppermute | solution.py:452
  126.5 5.3 %collective-permute-start.20 = (bf16[64,8192]{1,0:T(8,128)(2,1)S(1)}, bf16[64,8192]{1,0:T(8,128)(2,1)S(1)}, u32[]{:S(2)}, u32[]{:S(2)}) collective-permute-start(bf16[64,8192]{1,0:T(8,128)(2,1)S(1)} %get-tuple-element.76.upper_ref), channel_id=1, source_target_pairs={{16,0},{17,1},{18,2},{19,3},{20,4},{21,5},{22,6},{23,7},{24,8},{25... | collective-permute-start | bytes 3145736 | tf_op jit(solution)/shard_map/ppermute | solution.py:452

commit v15 on v14

--- a/solution.py
+++ b/solution.py
@@ -318,7 +318,7 @@
 
 def input_gradient(upper, piece, passed, is_upper, shape, m, earlier):
     rows, width = upper.shape
-    step = min(rows, 32)
+    step = min(rows, 64)
 
     def kernel(is_upper_ref, upper_ref, piece_ref, passed_ref, *refs):
         lower = (passed_ref[...].astype(f32) + piece_ref[...].astype(f32)).astype(bf16)
@@ -332,7 +332,7 @@
         in_specs=[SMEM_ARG, spec, spec, spec] + [ANY_ARG] * len(earlier),
         out_specs=pl.BlockSpec((1, 1, step, width), lambda i: (0, m, i, 0)),
         input_output_aliases={4: 0} if earlier else {},
-        compiler_params=params(8),
+        compiler_params=params(12),
         cost_estimate=cost(4 * rows * width, 8 * rows * width),
         name="input_gradient",
     )(is_upper, upper, piece, passed, *earlier)

time: 134 us -> 134 us (level)
  no operation moved by 1% of the time
where the time goes in v15:
time: 134 us; the launch traced here: 133 us
  waiting for transfers between devices  70.3 us (52%)
  starting transfers between devices  41.9 us (31%)
  Pallas kernels  18.6 us (14%)
  local copies, waits for them, and re-layouts  1.6 us (1%)
    ppermute x10, waiting for transfers between devices, cyclic(): lax.ppermute(value, axis, [(i, (i + steps) % count) for i in range(count)])  58 us
    ppermute x10, starting transfers between devices, cyclic(): lax.ppermute(value, axis, [(i, (i + steps) % count) for i in range(count)])  23.3 us
    ppermute x10, starting transfers between devices, flipped(): return lax.ppermute(value, axis, [(i, i ^ mask) for i in range(count)])  16 us
    ppermute x10, waiting for transfers between devices, flipped(): return lax.ppermute(value, axis, [(i, i ^ mask) for i in range(count)])  12.3 us
    pallas_call x4, Pallas kernels, finished_half(): pl.pallas_call(kernel, grid_spec=pltpu.PrefetchScalarGridSpec(num_scalar_...  5.7 us
    pallas_call x1, Pallas kernels, returned_blocks(): pl.pallas_call(kernel, grid=(shard // tile,), out_shape=[jax.ShapeDtypeSt...  3.17 us
    pallas_call x1, Pallas kernels, weight_product(): pl.pallas_call(kernel, out_shape=[jax.ShapeDtypeStruct((chunk + 16, featu...  2.73 us
  transfers between devices with their start and end apart: 22, of which 11 were waited for; matrix products, arithmetic and copies ran while one was open for 0% of the time, Pallas kernels for 12%

profile of v15, /device:TPU:0, one launch (start us, length us, event | category | flops | bytes accessed | tf_op | source)
XLA Modules:
  0.0 133.2 jit_solution(8821579883495780740)
XLA Ops:
  0.6 0.0 copy-start
  0.6 1.6 %copy-done = bf16[1,2,64,8192]{3,2,1,0:T(8,128)(2,1)S(1)} copy-done((bf16[1,2,64,8192]{3,2,1,0:T(8,128)(2,1)S(1)}, bf16[1,2,64,8192]{3,2,1,0:T(8,128)(2,1)}, u32[]{:S(2)}) %copy-start) | copy-done | bytes 2097176
  2.2 1.1 scaled_blocks.1
  3.3 3.0 %collective-permute-start.2 = (bf16[128,2048]{1,0:T(8,128)(2,1)S(1)}, bf16[128,2048]{1,0:T(8,128)(2,1)S(1)}, u32[]{:S(2)}, u32[]{:S(2)}) collective-permute-start(bf16[128,2048]{1,0:T(8,128)(2,1)S(1)} %get-tuple-element.47), channel_id=1, source_target_pairs={{0,4},{4,0},{8,12},{12,8},{1,5},{5,1},{9,13},{13,9},{2,6},{6,2},{1... | collective-permute-start | bytes 1572872 | tf_op jit(solution)/shard_map/ppermute | solution.py:23
  6.3 1.5 %collective-permute-start.4 = (bf16[128,2048]{1,0:T(8,128)(2,1)S(1)}, bf16[128,2048]{1,0:T(8,128)(2,1)S(1)}, u32[]{:S(2)}, u32[]{:S(2)}) collective-permute-start(bf16[128,2048]{1,0:T(8,128)(2,1)S(1)} %get-tuple-element.51), channel_id=1, source_target_pairs={{0,8},{4,12},{8,0},{12,4},{1,9},{5,13},{9,1},{13,5},{2,10},{6,14},... | collective-permute-start | bytes 1572872 | tf_op jit(solution)/shard_map/ppermute | solution.py:23
  7.8 0.0 collective-permute-start.5
  7.9 2.0 %collective-permute-start = (bf16[128,1024]{1,0:T(8,128)(2,1)S(1)}, bf16[128,1024]{1,0:T(8,128)(2,1)S(1)}, u32[]{:S(2)}, u32[]{:S(2)}) collective-permute-start(bf16[128,1024]{1,0:T(8,128)(2,1)S(1)} %bitcast.10), channel_id=1, source_target_pairs={{0,1},{1,2},{2,3},{3,0},{4,5},{5,6},{6,7},{7,4},{8,9},{9,10},{10,1... | collective-permute-start | bytes 786440 | tf_op jit(solution)/shard_map/ppermute | solution.py:18
  9.9 2.6 %collective-permute-start.1 = (bf16[128,1024]{1,0:T(8,128)(2,1)S(1)}, bf16[128,1024]{1,0:T(8,128)(2,1)S(1)}, u32[]{:S(2)}, u32[]{:S(2)}) collective-permute-start(bf16[128,1024]{1,0:T(8,128)(2,1)S(1)} %bitcast.11), channel_id=1, source_target_pairs={{0,2},{1,3},{2,0},{3,1},{4,6},{5,7},{6,4},{7,5},{8,10},{9,11},{10,... | collective-permute-start | bytes 786440 | tf_op jit(solution)/shard_map/ppermute | solution.py:18
  12.5 6.6 %collective-permute-done.2.refs_1_ = bf16[128,2048]{1,0:T(8,128)(2,1)S(1)} collective-permute-done((bf16[128,2048]{1,0:T(8,128)(2,1)S(1)}, bf16[128,2048]{1,0:T(8,128)(2,1)S(1)}, u32[]{:S(2)}, u32[]{:S(2)}) %collective-permute-start.2) | collective-permute-done | bytes 524320 | tf_op jit(solution)/shard_map/ppermute | solution.py:23
  19.1 4.2 %collective-permute-start.3 = (bf16[128,1024]{1,0:T(8,128)(2,1)S(1)}, bf16[128,1024]{1,0:T(8,128)(2,1)S(1)}, u32[]{:S(2)}, u32[]{:S(2)}) collective-permute-start(bf16[128,1024]{1,0:T(8,128)(2,1)S(1)} %bitcast.12), channel_id=1, source_target_pairs={{0,3},{1,0},{2,1},{3,2},{4,7},{5,4},{6,5},{7,6},{8,11},{9,8},{10,9... | collective-permute-start | bytes 786440 | tf_op jit(solution)/shard_map/ppermute | solution.py:18
  23.2 5.5 %collective-permute-done.1.refs_2_ = bf16[128,1024]{1,0:T(8,128)(2,1)S(1)} collective-permute-done((bf16[128,1024]{1,0:T(8,128)(2,1)S(1)}, bf16[128,1024]{1,0:T(8,128)(2,1)S(1)}, u32[]{:S(2)}, u32[]{:S(2)}) %collective-permute-start.1) | collective-permute-done | bytes 262176 | tf_op jit(solution)/shard_map/ppermute | solution.py:18
  28.7 2.2 %collective-permute-done.4.refs_2_ = bf16[128,2048]{1,0:T(8,128)(2,1)S(1)} collective-permute-done((bf16[128,2048]{1,0:T(8,128)(2,1)S(1)}, bf16[128,2048]{1,0:T(8,128)(2,1)S(1)}, u32[]{:S(2)}, u32[]{:S(2)}) %collective-permute-start.4) | collective-permute-done | bytes 524320 | tf_op jit(solution)/shard_map/ppermute | solution.py:23
  30.9 0.5 regrouped.1
  31.4 2.2 %collective-permute-start.6 = (bf16[512,512]{1,0:T(8,128)(2,1)S(1)}, bf16[512,512]{1,0:T(8,128)(2,1)S(1)}, u32[]{:S(2)}, u32[]{:S(2)}) collective-permute-start(bf16[512,512]{1,0:T(8,128)(2,1)S(1)} %get-tuple-element.54), channel_id=1, source_target_pairs={{0,1},{1,2},{2,3},{3,0},{4,5},{5,6},{6,7},{7,4},{8,9},{9,10},{10,1... | collective-permute-start | bytes 1572872 | tf_op jit(solution)/shard_map/ppermute | solution.py:18
  33.6 0.0 collective-permute-done.3.refs_3_
  33.6 0.1 joined.3.refs_4_
  33.7 2.1 %collective-permute-start.10 = (bf16[512,1024]{1,0:T(8,128)(2,1)S(1)}, bf16[512,1024]{1,0:T(8,128)(2,1)S(1)}, u32[]{:S(2)}, u32[]{:S(2)}) collective-permute-start(bf16[512,1024]{1,0:T(8,128)(2,1)S(1)} %joined.3.refs_4_), channel_id=1, source_target_pairs={{0,8},{4,12},{8,0},{12,4},{1,9},{5,13},{9,1},{13,5},{2,10},{6,14},... | collective-permute-start | bytes 3145736 | tf_op jit(solution)/shard_map/ppermute | solution.py:23
  35.8 1.0 collective-permute-start.11
  36.8 0.5 collective-permute-start.9
  37.3 3.4 %collective-permute-start.7 = (bf16[512,512]{1,0:T(8,128)(2,1)S(1)}, bf16[512,512]{1,0:T(8,128)(2,1)S(1)}, u32[]{:S(2)}, u32[]{:S(2)}) collective-permute-start(bf16[512,512]{1,0:T(8,128)(2,1)S(1)} %get-tuple-element.55), channel_id=1, source_target_pairs={{0,2},{1,3},{2,0},{3,1},{4,6},{5,7},{6,4},{7,5},{8,10},{9,11},{10,... | collective-permute-start | bytes 1572872 | tf_op jit(solution)/shard_map/ppermute | solution.py:18
  40.7 3.2 %returned_blocks.1 = (bf16[128,2048]{1,0:T(8,128)(2,1)S(1)}, bf16[128,2048]{1,0:T(8,128)(2,1)S(1)}, bf16[64,2048]{1,0:T(8,128)(2,1)S(1)}, bf16[64,2048]{1,0:T(8,128)(2,1)S(1)}, bf16[128,2048]{1,0:T(8,128)(2,1)S(1)}) custom-call(bf16[128,1024]{1,0:T(8,128)(2,1)S(1)} %bitcast.14, bf16[128,1024]{1,0:T(8,128)(2,1)S(1)} %collective-permute-done.refs_1_, ...), custom_call_target="tpu_custom_call" | custom-call | flops 2147483648 | bytes 7340032 | tf_op jit(solution)/shard_map/returned_blocks/pallas_call | solution.py:252
  43.9 5.4 %collective-permute-done.6.refs_1_ = bf16[512,512]{1,0:T(8,128)(2,1)S(1)} collective-permute-done((bf16[512,512]{1,0:T(8,128)(2,1)S(1)}, bf16[512,512]{1,0:T(8,128)(2,1)S(1)}, u32[]{:S(2)}, u32[]{:S(2)}) %collective-permute-start.6) | collective-permute-done | bytes 524320 | tf_op jit(solution)/shard_map/ppermute | solution.py:18
  49.3 19.8 %collective-permute-done.7.refs_2_ = bf16[512,512]{1,0:T(8,128)(2,1)S(1)} collective-permute-done((bf16[512,512]{1,0:T(8,128)(2,1)S(1)}, bf16[512,512]{1,0:T(8,128)(2,1)S(1)}, u32[]{:S(2)}, u32[]{:S(2)}) %collective-permute-start.7) | collective-permute-done | bytes 524320 | tf_op jit(solution)/shard_map/ppermute | solution.py:18
  69.1 2.3 %collective-permute-start.14 = (bf16[64,2048]{1,0:T(8,128)(2,1)S(1)}, bf16[64,2048]{1,0:T(8,128)(2,1)S(1)}, u32[]{:S(2)}, u32[]{:S(2)}) collective-permute-start(bf16[64,2048]{1,0:T(8,128)(2,1)S(1)} %get-tuple-element.68), channel_id=1, source_target_pairs={{0,2},{1,3},{2,0},{3,1},{4,6},{5,7},{6,4},{7,5},{8,10},{9,11},{10,... | collective-permute-start | bytes 786440 | tf_op jit(solution)/shard_map/ppermute | solution.py:18
  71.4 5.6 %collective-permute-done.8.refs_3_ = bf16[512,512]{1,0:T(8,128)(2,1)S(1)} collective-permute-done((bf16[512,512]{1,0:T(8,128)(2,1)S(1)}, bf16[512,512]{1,0:T(8,128)(2,1)S(1)}, u32[]{:S(2)}, u32[]{:S(2)}) %collective-permute-start.8) | collective-permute-done | bytes 524320 | tf_op jit(solution)/shard_map/ppermute | solution.py:18
  76.9 2.3 %collective-permute-done.10.refs_6_ = bf16[512,1024]{1,0:T(8,128)(2,1)S(1)} collective-permute-done((bf16[512,1024]{1,0:T(8,128)(2,1)S(1)}, bf16[512,1024]{1,0:T(8,128)(2,1)S(1)}, u32[]{:S(2)}, u32[]{:S(2)}) %collective-permute-start.10) | collective-permute-done | bytes 1048608 | tf_op jit(solution)/shard_map/ppermute | solution.py:23
  79.2 1.2 collective-permute-done.9.refs_5_
  80.5 2.7 %weight_product.1 = (bf16[272,1024]{1,0:T(8,128)(2,1)S(1)}, bf16[272,1024]{1,0:T(8,128)(2,1)S(1)}) custom-call(s32[1]{0:T(128)} %bitcast.3.rep_ref, bf16[512,512]{1,0:T(8,128)(2,1)S(1)} %get-tuple-element.53.refs_0_, bf16[512,512]{1,0:T(8,128)(2,1)S(1)} %collective-permute-done.6.refs_1_, bf16[512,512]{1,0:T(8,128)(2,1)S(1)} %collective-permute-done.7.refs_2_, ...), custom_call_target="tpu_custom_call" | custom-call | flops 2147483648 | bytes 8388608 | tf_op jit(solution)/shard_map/weight_product/pallas_call | solution.py:215
  83.2 1.5 %collective-permute-start.13 = (bf16[272,1024]{1,0:T(8,128)(2,1)S(1)}, bf16[272,1024]{1,0:T(8,128)(2,1)S(1)}, u32[]{:S(2)}, u32[]{:S(2)}) collective-permute-start(bf16[272,1024]{1,0:T(8,128)(2,1)S(1)} %get-tuple-element.60.refs_0_), channel_id=1, source_target_pairs={{0,4},{4,0},{8,12},{12,8},{1,5},{5,1},{9,13},{13,9},{2,6},{6,2},{1... | collective-permute-start | bytes 1671176 | tf_op jit(solution)/shard_map/ppermute | solution.py:23
  84.7 1.4 %collective-permute-start.12 = (bf16[272,1024]{1,0:T(8,128)(2,1)S(1)}, bf16[272,1024]{1,0:T(8,128)(2,1)S(1)}, u32[]{:S(2)}, u32[]{:S(2)}) collective-permute-start(bf16[272,1024]{1,0:T(8,128)(2,1)S(1)} %get-tuple-element.59.refs_0_), channel_id=1, source_target_pairs={{0,8},{4,12},{8,0},{12,4},{1,9},{5,13},{9,1},{13,5},{2,10},{6,14},... | collective-permute-start | bytes 1671176 | tf_op jit(solution)/shard_map/ppermute | solution.py:23
  86.1 6.7 %collective-permute-start.16 = (bf16[128,2048]{1,0:T(8,128)(2,1)S(1)}, bf16[128,2048]{1,0:T(8,128)(2,1)S(1)}, u32[]{:S(2)}, u32[]{:S(2)}) collective-permute-start(bf16[128,2048]{1,0:T(8,128)(2,1)S(1)} %get-tuple-element.71), channel_id=1, source_target_pairs={{0,1},{1,2},{2,3},{3,0},{4,5},{5,6},{6,7},{7,4},{8,9},{9,10},{10,1... | collective-permute-start | bytes 1572872 | tf_op jit(solution)/shard_map/ppermute | solution.py:18
  92.8 7.9 %collective-permute-done.14.refs_2_ = bf16[64,2048]{1,0:T(8,128)(2,1)S(1)} collective-permute-done((bf16[64,2048]{1,0:T(8,128)(2,1)S(1)}, bf16[64,2048]{1,0:T(8,128)(2,1)S(1)}, u32[]{:S(2)}, u32[]{:S(2)}) %collective-permute-start.14) | collective-permute-done | bytes 262176 | tf_op jit(solution)/shard_map/ppermute | solution.py:18
  100.8 0.2 joined.5.sum_ref
  100.9 3.2 %collective-permute-start.19 = (bf16[544,1024]{1,0:T(8,128)(2,1)S(1)}, bf16[544,1024]{1,0:T(8,128)(2,1)S(1)}, u32[]{:S(2)}, u32[]{:S(2)}) collective-permute-start(bf16[544,1024]{1,0:T(8,128)(2,1)S(1)} %joined.5.sum_ref), channel_id=1, source_target_pairs={{0,8},{4,12},{8,0},{12,4},{1,9},{5,13},{9,1},{13,5},{2,10},{6,14},... | collective-permute-start | bytes 3342344 | tf_op jit(solution)/shard_map/ppermute | solution.py:23
  104.2 0.2 joined.4.sum_ref
  104.3 1.7 %collective-permute-start.18 = (bf16[544,1024]{1,0:T(8,128)(2,1)S(1)}, bf16[544,1024]{1,0:T(8,128)(2,1)S(1)}, u32[]{:S(2)}, u32[]{:S(2)}) collective-permute-start(bf16[544,1024]{1,0:T(8,128)(2,1)S(1)} %joined.4.sum_ref), channel_id=1, source_target_pairs={{0,4},{4,0},{8,12},{12,8},{1,5},{5,1},{9,13},{13,9},{2,6},{6,2},{1... | collective-permute-start | bytes 3342344 | tf_op jit(solution)/shard_map/ppermute | solution.py:23
  106.0 1.4 %finished_half.4 = (f32[2048,1024]{1,0:T(8,128)}, f32[1,2048]{1,0:T(1,128)}) custom-call(s32[1]{0:T(128)} %bitcast.3.rep_ref, bf16[544,1024]{1,0:T(8,128)(2,1)S(1)} %joined.5.sum_ref), custom_call_target="tpu_custom_call" | custom-call | flops 557056 | bytes 3342336 | tf_op jit(solution)/shard_map/finished_half/pallas_call | solution.py:368
  107.4 1.4 %finished_half.5 = (f32[2048,1024]{1,0:T(8,128)}, f32[1,2048]{1,0:T(1,128)}) custom-call(s32[1]{0:T(128)} %bitcast.3.rep_ref, bf16[544,1024]{1,0:T(8,128)(2,1)S(1)} %joined.4.sum_ref, f32[2048,1024]{1,0:T(8,128)} %get-tuple-element.61.refs_0_, f32[1,2048]{1,0:T(1,128)} %get-tuple-element.62.refs_1_), custom_call_target="tpu_custom_call", output_to_operand_aliasing={{0}: (2, {}), {1}: (3, {})} | custom-call | flops 557056 | bytes 3342336 | tf_op jit(solution)/shard_map/finished_half/pallas_call | solution.py:368
  108.8 6.5 %collective-permute-done.15.refs_1_ = bf16[128,2048]{1,0:T(8,128)(2,1)S(1)} collective-permute-done((bf16[128,2048]{1,0:T(8,128)(2,1)S(1)}, bf16[128,2048]{1,0:T(8,128)(2,1)S(1)}, u32[]{:S(2)}, u32[]{:S(2)}) %collective-permute-start.15) | collective-permute-done | bytes 524320 | tf_op jit(solution)/shard_map/ppermute | solution.py:18
  115.3 1.2 row_gradient.2
  116.6 1.3 collective-permute-start.21
  117.9 7.4 %collective-permute-done.17.refs_2_ = bf16[64,2048]{1,0:T(8,128)(2,1)S(1)} collective-permute-done((bf16[64,2048]{1,0:T(8,128)(2,1)S(1)}, bf16[64,2048]{1,0:T(8,128)(2,1)S(1)}, u32[]{:S(2)}, u32[]{:S(2)}) %collective-permute-start.17) | collective-permute-done | bytes 262176 | tf_op jit(solution)/shard_map/ppermute | solution.py:18
  125.2 1.2 row_gradient.3
  126.5 1.3 collective-permute-start.20
  127.8 1.4 %finished_half.6 = (f32[2048,1024]{1,0:T(8,128)}, f32[1,2048]{1,0:T(1,128)}) custom-call(s32[1]{0:T(128)} %bitcast.3.rep_ref, bf16[544,1024]{1,0:T(8,128)(2,1)S(1)} %collective-permute-done.19.sum_ref, f32[2048,1024]{1,0:T(8,128)} %get-tuple-element.63.refs_0_, f32[1,2048]{1,0:T(1,128)} %get-tuple-element.64.refs_1_), custom_call_target="tpu_custom_call", output_to_operand_aliasing={{0}: (2, {}), {1}: (3, {})} | custom-call | flops 557056 | bytes 3342336 | tf_op jit(solution)/shard_map/finished_half/pallas_call | solution.py:368
  129.2 1.4 %finished_half.7 = (f32[2048,1024]{1,0:T(8,128)}, f32[1,2048]{1,0:T(1,128)}) custom-call(s32[1]{0:T(128)} %bitcast.3.rep_ref, bf16[544,1024]{1,0:T(8,128)(2,1)S(1)} %collective-permute-done.18.sum_ref, f32[2048,1024]{1,0:T(8,128)} %get-tuple-element.78.refs_0_, f32[1,2048]{1,0:T(1,128)} %get-tuple-element.79.refs_1_), custom_call_target="tpu_custom_call", output_to_operand_aliasing={{0}: (2, {}), {1}: (3, {})} | custom-call | flops 557056 | bytes 3342336 | tf_op jit(solution)/shard_map/finished_half/pallas_call | solution.py:368
  130.7 1.2 input_gradient.2.refs_0_
  131.9 1.2 input_gradient.3
  (23 shorter events, 0.1 us)
Async XLA Ops:
  0.6 1.6 %copy-start = (bf16[1,2,64,8192]{3,2,1,0:T(8,128)(2,1)S(1)}, bf16[1,2,64,8192]{3,2,1,0:T(8,128)(2,1)}, u32[]{:S(2)}) copy-start(bf16[1,2,64,8192]{3,2,1,0:T(8,128)(2,1)} %x_ref.3) | copy-start | bytes 6291460
  2.2 5.6 %copy-start.4 = (bf16[1,2,64,1024]{3,2,1,0:T(8,128)(2,1)S(1)}, bf16[1,2,64,1024]{3,2,1,0:T(8,128)(2,1)}, u32[]{:S(2)}) copy-start(bf16[1,2,64,1024]{3,2,1,0:T(8,128)(2,1)} %param.6) | copy-start | bytes 786436
  3.3 15.8 %collective-permute-start.2 = (bf16[128,2048]{1,0:T(8,128)(2,1)S(1)}, bf16[128,2048]{1,0:T(8,128)(2,1)S(1)}, u32[]{:S(2)}, u32[]{:S(2)}) collective-permute-start(bf16[128,2048]{1,0:T(8,128)(2,1)S(1)} %get-tuple-element.47), channel_id=1, source_target_pairs={{0,4},{4,0},{8,12},{12,8},{1,5},{5,1},{9,13},{13,9},{2,6},{6,2},{1... | collective-permute-start | bytes 1572872 | tf_op jit(solution)/shard_map/ppermute | solution.py:23
  6.3 24.6 %collective-permute-start.4 = (bf16[128,2048]{1,0:T(8,128)(2,1)S(1)}, bf16[128,2048]{1,0:T(8,128)(2,1)S(1)}, u32[]{:S(2)}, u32[]{:S(2)}) collective-permute-start(bf16[128,2048]{1,0:T(8,128)(2,1)S(1)} %get-tuple-element.51), channel_id=1, source_target_pairs={{0,8},{4,12},{8,0},{12,4},{1,9},{5,13},{9,1},{13,5},{2,10},{6,14},... | collective-permute-start | bytes 1572872 | tf_op jit(solution)/shard_map/ppermute | solution.py:23
  7.8 23.1 %collective-permute-start.5 = (bf16[128,2048]{1,0:T(8,128)(2,1)S(1)}, bf16[128,2048]{1,0:T(8,128)(2,1)S(1)}, u32[]{:S(2)}, u32[]{:S(2)}) collective-permute-start(bf16[128,2048]{1,0:T(8,128)(2,1)S(1)} %get-tuple-element.52), channel_id=1, source_target_pairs={{0,12},{4,8},{8,4},{12,0},{1,13},{5,9},{9,5},{13,1},{2,14},{6,10},... | collective-permute-start | bytes 1572872 | tf_op jit(solution)/shard_map/ppermute | solution.py:23
  7.8 32.9 %copy-start.5 = (bf16[1,2048]{1,0:T(2,128)(2,1)S(1)}, bf16[1,2048]{1,0:T(2,128)(2,1)}, u32[]{:S(2)}) copy-start(bf16[1,2048]{1,0:T(2,128)(2,1)} %refs_9_.1) | copy-start | bytes 12292
  7.8 32.9 %copy-start.3 = (bf16[1,2048,1024]{2,1,0:T(8,128)(2,1)S(1)}, bf16[1,2048,1024]{2,1,0:T(8,128)(2,1)}, u32[]{:S(2)}) copy-start(bf16[1,2048,1024]{2,1,0:T(8,128)(2,1)} %param.7) | copy-start | bytes 12582916
  7.9 15.4 %collective-permute-start = (bf16[128,1024]{1,0:T(8,128)(2,1)S(1)}, bf16[128,1024]{1,0:T(8,128)(2,1)S(1)}, u32[]{:S(2)}, u32[]{:S(2)}) collective-permute-start(bf16[128,1024]{1,0:T(8,128)(2,1)S(1)} %bitcast.10), channel_id=1, source_target_pairs={{0,1},{1,2},{2,3},{3,0},{4,5},{5,6},{6,7},{7,4},{8,9},{9,10},{10,1... | collective-permute-start | bytes 786440 | tf_op jit(solution)/shard_map/ppermute | solution.py:18
  9.9 18.9 %collective-permute-start.1 = (bf16[128,1024]{1,0:T(8,128)(2,1)S(1)}, bf16[128,1024]{1,0:T(8,128)(2,1)S(1)}, u32[]{:S(2)}, u32[]{:S(2)}) collective-permute-start(bf16[128,1024]{1,0:T(8,128)(2,1)S(1)} %bitcast.11), channel_id=1, source_target_pairs={{0,2},{1,3},{2,0},{3,1},{4,6},{5,7},{6,4},{7,5},{8,10},{9,11},{10,... | collective-permute-start | bytes 786440 | tf_op jit(solution)/shard_map/ppermute | solution.py:18
  19.1 14.5 %collective-permute-start.3 = (bf16[128,1024]{1,0:T(8,128)(2,1)S(1)}, bf16[128,1024]{1,0:T(8,128)(2,1)S(1)}, u32[]{:S(2)}, u32[]{:S(2)}) collective-permute-start(bf16[128,1024]{1,0:T(8,128)(2,1)S(1)} %bitcast.12), channel_id=1, source_target_pairs={{0,3},{1,0},{2,1},{3,2},{4,7},{5,4},{6,5},{7,6},{8,11},{9,8},{10,9... | collective-permute-start | bytes 786440 | tf_op jit(solution)/shard_map/ppermute | solution.py:18
  31.4 17.9 %collective-permute-start.6 = (bf16[512,512]{1,0:T(8,128)(2,1)S(1)}, bf16[512,512]{1,0:T(8,128)(2,1)S(1)}, u32[]{:S(2)}, u32[]{:S(2)}) collective-permute-start(bf16[512,512]{1,0:T(8,128)(2,1)S(1)} %get-tuple-element.54), channel_id=1, source_target_pairs={{0,1},{1,2},{2,3},{3,0},{4,5},{5,6},{6,7},{7,4},{8,9},{9,10},{10,1... | collective-permute-start | bytes 1572872 | tf_op jit(solution)/shard_map/ppermute | solution.py:18
  33.7 45.5 %collective-permute-start.10 = (bf16[512,1024]{1,0:T(8,128)(2,1)S(1)}, bf16[512,1024]{1,0:T(8,128)(2,1)S(1)}, u32[]{:S(2)}, u32[]{:S(2)}) collective-permute-start(bf16[512,1024]{1,0:T(8,128)(2,1)S(1)} %joined.3.refs_4_), channel_id=1, source_target_pairs={{0,8},{4,12},{8,0},{12,4},{1,9},{5,13},{9,1},{13,5},{2,10},{6,14},... | collective-permute-start | bytes 3145736 | tf_op jit(solution)/shard_map/ppermute | solution.py:23
  35.8 43.4 %collective-permute-start.11 = (bf16[512,1024]{1,0:T(8,128)(2,1)S(1)}, bf16[512,1024]{1,0:T(8,128)(2,1)S(1)}, u32[]{:S(2)}, u32[]{:S(2)}) collective-permute-start(bf16[512,1024]{1,0:T(8,128)(2,1)S(1)} %joined.3.refs_4_), channel_id=1, source_target_pairs={{0,12},{4,8},{8,4},{12,0},{1,13},{5,9},{9,5},{13,1},{2,14},{6,10},... | collective-permute-start | bytes 3145736 | tf_op jit(solution)/shard_map/ppermute | solution.py:23
  36.8 43.7 %collective-permute-start.9 = (bf16[512,1024]{1,0:T(8,128)(2,1)S(1)}, bf16[512,1024]{1,0:T(8,128)(2,1)S(1)}, u32[]{:S(2)}, u32[]{:S(2)}) collective-permute-start(bf16[512,1024]{1,0:T(8,128)(2,1)S(1)} %joined.3.refs_4_), channel_id=1, source_target_pairs={{0,4},{4,0},{8,12},{12,8},{1,5},{5,1},{9,13},{13,9},{2,6},{6,2},{1... | collective-permute-start | bytes 3145736 | tf_op jit(solution)/shard_map/ppermute | solution.py:23
  37.3 31.8 %collective-permute-start.7 = (bf16[512,512]{1,0:T(8,128)(2,1)S(1)}, bf16[512,512]{1,0:T(8,128)(2,1)S(1)}, u32[]{:S(2)}, u32[]{:S(2)}) collective-permute-start(bf16[512,512]{1,0:T(8,128)(2,1)S(1)} %get-tuple-element.55), channel_id=1, source_target_pairs={{0,2},{1,3},{2,0},{3,1},{4,6},{5,7},{6,4},{7,5},{8,10},{9,11},{10,... | collective-permute-start | bytes 1572872 | tf_op jit(solution)/shard_map/ppermute | solution.py:18
  49.3 27.6 %collective-permute-start.8 = (bf16[512,512]{1,0:T(8,128)(2,1)S(1)}, bf16[512,512]{1,0:T(8,128)(2,1)S(1)}, u32[]{:S(2)}, u32[]{:S(2)}) collective-permute-start(bf16[512,512]{1,0:T(8,128)(2,1)S(1)} %get-tuple-element.57), channel_id=1, source_target_pairs={{0,3},{1,0},{2,1},{3,2},{4,7},{5,4},{6,5},{7,6},{8,11},{9,8},{10,9... | collective-permute-start | bytes 1572872 | tf_op jit(solution)/shard_map/ppermute | solution.py:18
  69.1 31.6 %collective-permute-start.14 = (bf16[64,2048]{1,0:T(8,128)(2,1)S(1)}, bf16[64,2048]{1,0:T(8,128)(2,1)S(1)}, u32[]{:S(2)}, u32[]{:S(2)}) collective-permute-start(bf16[64,2048]{1,0:T(8,128)(2,1)S(1)} %get-tuple-element.68), channel_id=1, source_target_pairs={{0,2},{1,3},{2,0},{3,1},{4,6},{5,7},{6,4},{7,5},{8,10},{9,11},{10,... | collective-permute-start | bytes 786440 | tf_op jit(solution)/shard_map/ppermute | solution.py:18
  83.2 17.6 %collective-permute-start.13 = (bf16[272,1024]{1,0:T(8,128)(2,1)S(1)}, bf16[272,1024]{1,0:T(8,128)(2,1)S(1)}, u32[]{:S(2)}, u32[]{:S(2)}) collective-permute-start(bf16[272,1024]{1,0:T(8,128)(2,1)S(1)} %get-tuple-element.60.refs_0_), channel_id=1, source_target_pairs={{0,4},{4,0},{8,12},{12,8},{1,5},{5,1},{9,13},{13,9},{2,6},{6,2},{1... | collective-permute-start | bytes 1671176 | tf_op jit(solution)/shard_map/ppermute | solution.py:23
  84.7 19.5 %collective-permute-start.12 = (bf16[272,1024]{1,0:T(8,128)(2,1)S(1)}, bf16[272,1024]{1,0:T(8,128)(2,1)S(1)}, u32[]{:S(2)}, u32[]{:S(2)}) collective-permute-start(bf16[272,1024]{1,0:T(8,128)(2,1)S(1)} %get-tuple-element.59.refs_0_), channel_id=1, source_target_pairs={{0,8},{4,12},{8,0},{12,4},{1,9},{5,13},{9,1},{13,5},{2,10},{6,14},... | collective-permute-start | bytes 1671176 | tf_op jit(solution)/shard_map/ppermute | solution.py:23
  86.1 22.7 %collective-permute-start.16 = (bf16[128,2048]{1,0:T(8,128)(2,1)S(1)}, bf16[128,2048]{1,0:T(8,128)(2,1)S(1)}, u32[]{:S(2)}, u32[]{:S(2)}) collective-permute-start(bf16[128,2048]{1,0:T(8,128)(2,1)S(1)} %get-tuple-element.71), channel_id=1, source_target_pairs={{0,1},{1,2},{2,3},{3,0},{4,5},{5,6},{6,7},{7,4},{8,9},{9,10},{10,1... | collective-permute-start | bytes 1572872 | tf_op jit(solution)/shard_map/ppermute | solution.py:18
  100.7 14.6 %collective-permute-start.15 = (bf16[128,2048]{1,0:T(8,128)(2,1)S(1)}, bf16[128,2048]{1,0:T(8,128)(2,1)S(1)}, u32[]{:S(2)}, u32[]{:S(2)}) collective-permute-start(bf16[128,2048]{1,0:T(8,128)(2,1)S(1)} %get-tuple-element.69), channel_id=1, source_target_pairs={{0,3},{1,0},{2,1},{3,2},{4,7},{5,4},{6,5},{7,6},{8,11},{9,8},{10,9... | collective-permute-start | bytes 1572872 | tf_op jit(solution)/shard_map/ppermute | solution.py:18
  100.7 24.5 %collective-permute-start.17 = (bf16[64,2048]{1,0:T(8,128)(2,1)S(1)}, bf16[64,2048]{1,0:T(8,128)(2,1)S(1)}, u32[]{:S(2)}, u32[]{:S(2)}) collective-permute-start(bf16[64,2048]{1,0:T(8,128)(2,1)S(1)} %get-tuple-element.75), channel_id=1, source_target_pairs={{0,2},{1,3},{2,0},{3,1},{4,6},{5,7},{6,4},{7,5},{8,10},{9,11},{10,... | collective-permute-start | bytes 786440 | tf_op jit(solution)/shard_map/ppermute | solution.py:18
  100.9 26.8 %collective-permute-start.19 = (bf16[544,1024]{1,0:T(8,128)(2,1)S(1)}, bf16[544,1024]{1,0:T(8,128)(2,1)S(1)}, u32[]{:S(2)}, u32[]{:S(2)}) collective-permute-start(bf16[544,1024]{1,0:T(8,128)(2,1)S(1)} %joined.5.sum_ref), channel_id=1, source_target_pairs={{0,8},{4,12},{8,0},{12,4},{1,9},{5,13},{9,1},{13,5},{2,10},{6,14},... | collective-permute-start | bytes 3342344 | tf_op jit(solution)/shard_map/ppermute | solution.py:23
  104.3 24.9 %collective-permute-start.18 = (bf16[544,1024]{1,0:T(8,128)(2,1)S(1)}, bf16[544,1024]{1,0:T(8,128)(2,1)S(1)}, u32[]{:S(2)}, u32[]{:S(2)}) collective-permute-start(bf16[544,1024]{1,0:T(8,128)(2,1)S(1)} %joined.4.sum_ref), channel_id=1, source_target_pairs={{0,4},{4,0},{8,12},{12,8},{1,5},{5,1},{9,13},{13,9},{2,6},{6,2},{1... | collective-permute-start | bytes 3342344 | tf_op jit(solution)/shard_map/ppermute | solution.py:23
  107.4 7.9 %copy-start.1 = (bf16[1,2,64,8192]{3,2,1,0:T(8,128)(2,1)S(1)}, bf16[1,2,64,8192]{3,2,1,0:T(8,128)(2,1)}, u32[]{:S(2)}) copy-start(bf16[1,2,64,8192]{3,2,1,0:T(8,128)(2,1)} %x_ref.3) | copy-start | bytes 6291460
  107.4 7.9 %copy-start.2 = (bf16[2,64,8192]{2,1,0:T(8,128)(2,1)S(1)}, bf16[2,64,8192]{2,1,0:T(8,128)(2,1)}, u32[]{:S(2)}) copy-start(bf16[2,64,8192]{2,1,0:T(8,128)(2,1)} %top_ref.3) | copy-start | bytes 6291460
  116.6 14.1 %collective-permute-start.21 = (bf16[64,8192]{1,0:T(8,128)(2,1)S(1)}, bf16[64,8192]{1,0:T(8,128)(2,1)S(1)}, u32[]{:S(2)}, u32[]{:S(2)}) collective-permute-start(bf16[64,8192]{1,0:T(8,128)(2,1)S(1)} %get-tuple-element.72.upper_ref), channel_id=1, source_target_pairs={{16,0},{17,1},{18,2},{19,3},{20,4},{21,5},{22,6},{23,7},{24,8},{25... | collective-permute-start | bytes 3145736 | tf_op jit(solution)/shard_map/ppermute | solution.py:452
  126.5 5.4 %collective-permute-start.20 = (bf16[64,8192]{1,0:T(8,128)(2,1)S(1)}, bf16[64,8192]{1,0:T(8,128)(2,1)S(1)}, u32[]{:S(2)}, u32[]{:S(2)}) collective-permute-start(bf16[64,8192]{1,0:T(8,128)(2,1)S(1)} %get-tuple-element.76.upper_ref), channel_id=1, source_target_pairs={{16,0},{17,1},{18,2},{19,3},{20,4},{21,5},{22,6},{23,7},{24,8},{25... | collective-permute-start | bytes 3145736 | tf_op jit(solution)/shard_map/ppermute | solution.py:452
